TPU v7x, 32 devices: a whole 2x2x4 slice. The times are simulated.
32 devices in a mesh: section: 4 (over y, core), dom: 8 (over z, x).
Axes of the slice: x: 2, y: 2, z: 4, core: 2. Of those that a mesh axis runs over, the one named last changes fastest.
Arguments:
- right_sides: float32 [256, 32, 128], P(('section', 'dom')), may hold values from -6 to 6
- diag_inverse: bfloat16 [256, 128, 128], P(('section', 'dom')), as said below
- diag_blocks: bfloat16 [256, 128, 128], P(('section', 'dom')), as said below
- lower_blocks: bfloat16 [256, 3, 128, 128], P(('section', 'dom'))
- upper_blocks: bfloat16 [256, 3, 128, 128], P(('section', 'dom'))
- halo_blocks: bfloat16 [256, 2, 128, 128], P(('section', 'dom')), may hold values from -0.1875 to 0.1875
- lower_index: int32 [256, 3], P(('section', 'dom')), may hold values from 0 to 7, as said below
- upper_index: int32 [256, 3], P(('section', 'dom')), may hold values from 0 to 7, as said below
- halo_index: int32 [256, 2], P(('section', 'dom')), may hold values from 0 to 7, as said below
Outputs:
- solution: float32 [256, 32, 128], P(('section', 'dom'))
- product: float32 [256, 32, 128], P(('section', 'dom'))
Inputs may be any that keep to these rules, and one draw needn't show every extreme that they name: `lower_index`: for block row g with k = g mod 8, every entry lies in 0 to k, and the first entry equals k. `upper_index`: for block row g with k = g mod 8, every entry lies in k to 7, and the first entry equals k. `halo_index`: for block row g the first entry equals g mod 8. `diag_inverse`: each block is the identity scaled row by row plus a full block. `diag_blocks`: each block is the identity scaled row by row plus a full block.
All inputs are finite; a program needn't handle non-finite values.
Results may differ from a plain program's by a relative error of at most 0.029.
Values may be sent and summed in bfloat16 or wider, within the bound.
No kernel may reach another device: no remote copies, remote signals or barrier semaphores. Data moves between devices by JAX's collectives and lax.ppermute only.
A program may use at most 64 MiB of HBM per device.

v0:
```python
import jax
import jax.numpy as jnp
from jax import lax
from jax.experimental import pallas as pl
from jax.experimental.pallas import tpu as pltpu
from jax.sharding import PartitionSpec as P

RIM = 4

VMEM = pl.BlockSpec(memory_space=pltpu.VMEM)
SMEM = pl.BlockSpec(memory_space=pltpu.SMEM)
HBM = pl.BlockSpec(memory_space=pltpu.HBM)
SMALL = pltpu.CompilerParams(vmem_limit_bytes=16 * 1024 * 1024)


def mul(a, b):
    return jnp.dot(a, b, preferred_element_type=jnp.float32)


def narrow(a):
    return a.astype(jnp.bfloat16)


def sweep_kernel(
    rhs_far,
    inverse_far,
    lower_far,
    upper_far,
    lower_at_far,
    upper_at_far,
    base,
    response,
    payload,
    rhs,
    inverse,
    lower,
    upper,
    lower_at,
    upper_at,
    low,
    upp,
    down,
    exact,
    arrived,
):
    rows, count, width = rhs.shape
    slots = lower.shape[1]
    upper_slots = upper.shape[1]
    near = count + width
    last = rows - 1
    half = rows // 2
    parts = [
        (inverse_far, inverse),
        (rhs_far, rhs),
        (lower_far.at[:half], lower.at[:half]),
        (lower_at_far, lower_at),
        (lower_far.at[half:], lower.at[half:]),
        (upper_far, upper),
        (upper_at_far, upper_at),
    ]
    copies = [
        pltpu.make_async_copy(far, here, arrived.at[i]) for i, (far, here) in enumerate(parts)
    ]
    for copy in copies:
        copy.start()
    eye = narrow(
        lax.broadcasted_iota(jnp.int32, (width, width), 0)
        == lax.broadcasted_iota(jnp.int32, (width, width), 1)
    )
    down[:, :count] = jnp.zeros((rows, count, width), jnp.bfloat16)
    response[:, :near] = jnp.zeros((rows, near, width), jnp.bfloat16)
    for k in range(rows):
        down[k, count:] = eye
        response[k, near:] = eye

    for k in range(rows):
        if k == 0:
            for copy in copies[:4]:
                copy.wait()
        if k == half:
            for copy in copies[4:]:
                copy.wait()
            for j in range(rows):
                blocks = upper[j].reshape(upper_slots * width, width)
                upp[j] = narrow(mul(blocks, inverse[j]))
        own = inverse[k]
        scaled = mul(narrow(rhs[k]), own)
        low[k] = narrow(mul(lower[k].reshape(slots * width, width), own))
        if k == 0:
            total = low[k, :width].astype(jnp.float32)
            for m in range(1, slots):
                total = total + low[k, m * width : (m + 1) * width].astype(jnp.float32)
            exact[k, :count] = scaled
            exact[k, count:] = -total
        else:
            source = jnp.concatenate([down[lower_at[m, k]] for m in range(1, slots)], axis=1)
            summed = mul(source, low[k, width:])
            exact[k, :count] = scaled - summed[:count]
            exact[k, count:] = -low[k, :width].astype(jnp.float32) - summed[count:]
        down[k] = narrow(exact[k])

    for k in range(last, -1, -1):
        if k == last:
            total = upp[k, :width].astype(jnp.float32)
            for m in range(1, upper_slots):
                total = total + upp[k, m * width : (m + 1) * width].astype(jnp.float32)
            base[k] = exact[k, :count]
            response[k, :near] = narrow(exact[k])
            response[k, near:] = narrow(-total)
        else:
            source = jnp.concatenate(
                [response[upper_at[m, k]] for m in range(1, upper_slots)], axis=1
            )
            summed = mul(source, upp[k, width:])
            solved = exact[k] - summed[:near]
            base[k] = solved[:count]
            response[k, :near] = narrow(solved)
            response[k, near:] = narrow(-upp[k, :width].astype(jnp.float32) - summed[near:])

    far = near + width
    payload[:near] = down[last]
    payload[near : near + far] = response[0]
    payload[near + far :] = response[last, near:]


def chain_kernel(
    groups, axes, gathered, base, response, solution, rounded, inner, outer, flow
):
    rows, count, width = base.shape
    near = count + width
    far = near + width
    me = lax.axis_index(axes[0])
    side = lax.rem(lax.axis_index(axes[1]), 2)
    zero = jnp.zeros((count, width), jnp.bfloat16)

    inflow = [zero]
    for t in range(1, groups):
        add = gathered[t - 1, :count].astype(jnp.float32)
        if t > 1:
            add = add + mul(inflow[-1], gathered[t - 1, count:near])
        inflow.append(narrow(add))
    outflow = [zero]
    for t in range(groups - 1, 0, -1):
        add = gathered[t, near : near + count].astype(jnp.float32)
        add = add + mul(inflow[t], gathered[t, near + count : 2 * near])
        if t < groups - 1:
            add = add + mul(outflow[0], gathered[t, 2 * near : near + far])
        outflow.insert(0, narrow(add))
    for t in range(groups):
        flow[0, t] = inflow[t]
        flow[1, t] = outflow[t]

    both = jnp.concatenate([flow[0, me], flow[1, me]], axis=1)
    for k in range(rows):
        value = base[k] + mul(both, response[k, count:])
        solution[k] = value
        rounded[k] = narrow(value)
    rounded[rows + 1] = flow[1, me]
    prior = lax.max(me - 1, 0)
    before = flow[0, me].astype(jnp.float32) + mul(flow[1, prior], gathered[prior, near + far :])
    rounded[rows] = narrow(jnp.where(me > 0, before, 0.0))
    rim = inner.shape[0]
    for e in range(rim):
        inner[e] = rounded[(1 - side) * (rows - rim) + e]
        outer[e] = rounded[side * (rows - rim) + e]


def local_kernel(rounded, diagonal, lower, upper, lower_at, upper_at, partial):
    rows, slots, width, _ = lower.shape
    upper_slots = upper.shape[1]
    for k in range(rows):
        total = mul(rounded[k], diagonal[k])
        source = [rounded[rows]]
        for m in range(1, slots):
            at = lower_at[m, k]
            source.append(rounded[jnp.where(at == k, rows, at)])
        total = total + mul(
            jnp.concatenate(source, axis=1), lower[k].reshape(slots * width, width)
        )
        source = [rounded[rows + 1]]
        for m in range(1, upper_slots):
            at = upper_at[m, k]
            source.append(rounded[jnp.where(at == k, rows + 1, at)])
        total = total + mul(
            jnp.concatenate(source, axis=1), upper[k].reshape(upper_slots * width, width)
        )
        partial[k] = total


def halo_kernel(axis, partial, inner, outer, halo, halo_at, product, rim_rows):
    rows, slots, width, _ = halo.shape
    rim = inner.shape[0]
    turn = rim * (1 - lax.rem(lax.axis_index(axis), 2))
    rim_rows[:rim] = inner[...]
    rim_rows[rim:] = outer[...]
    for k in range(rows):
        source = [
            rim_rows[lax.rem(halo_at[m, k] + turn, 2 * rim)] for m in range(slots)
        ]
        product[k] = partial[k] + mul(
            jnp.concatenate(source, axis=1), halo[k].reshape(slots * width, width)
        )


def swaps(block, axis, first):
    count = lax.axis_size(axis)
    pairs = []
    for low in range(first, count - 1, 2):
        pairs += [(low, low + 1), (low + 1, low)]
    return lax.ppermute(block, axis, pairs)


def on_device(
    right_sides,
    diag_inverse,
    diag_blocks,
    lower_blocks,
    upper_blocks,
    halo_blocks,
    lower_index,
    upper_index,
    halo_index,
):
    rows, count, width = right_sides.shape
    lower_at, upper_at, halo_at = lower_index.T, upper_index.T, halo_index.T
    slots = lower_blocks.shape[1]
    upper_slots = upper_blocks.shape[1]
    groups = lax.axis_size("section")
    near = count + width
    far = near + width
    wide = jax.ShapeDtypeStruct((rows, count, width), jnp.float32)

    base, response, payload = pl.pallas_call(
        sweep_kernel,
        out_shape=(
            wide,
            jax.ShapeDtypeStruct((rows, far, width), jnp.bfloat16),
            jax.ShapeDtypeStruct((near + far + width, width), jnp.bfloat16),
        ),
        in_specs=[HBM] * 6,
        out_specs=(VMEM, VMEM, VMEM),
        scratch_shapes=[
            pltpu.VMEM(right_sides.shape, right_sides.dtype),
            pltpu.VMEM(diag_inverse.shape, diag_inverse.dtype),
            pltpu.VMEM(lower_blocks.shape, lower_blocks.dtype),
            pltpu.VMEM(upper_blocks.shape, upper_blocks.dtype),
            pltpu.SMEM(lower_at.shape, jnp.int32),
            pltpu.SMEM(upper_at.shape, jnp.int32),
            pltpu.VMEM((rows, slots * width, width), jnp.bfloat16),
            pltpu.VMEM((rows, upper_slots * width, width), jnp.bfloat16),
            pltpu.VMEM((rows, near, width), jnp.bfloat16),
            pltpu.VMEM((rows, near, width), jnp.float32),
            pltpu.SemaphoreType.DMA((7,)),
        ],
        compiler_params=SMALL,
        name="sweeps",
    )(
        *(
            pltpu.with_memory_space_constraint(a, pltpu.HBM)
            for a in (right_sides, diag_inverse, lower_blocks, upper_blocks, lower_at, upper_at)
        )
    )

    gathered = lax.all_gather(payload, "section")

    def chain(*refs):
        chain_kernel(groups, ("section", "dom"), *refs)

    solution, rounded, inner, outer = pl.pallas_call(
        chain,
        out_shape=(
            wide,
            jax.ShapeDtypeStruct((rows + 2, count, width), jnp.bfloat16),
            jax.ShapeDtypeStruct((RIM, count, width), jnp.bfloat16),
            jax.ShapeDtypeStruct((RIM, count, width), jnp.bfloat16),
        ),
        in_specs=[VMEM] * 3,
        out_specs=(VMEM,) * 4,
        scratch_shapes=[pltpu.VMEM((2, groups, count, width), jnp.bfloat16)],
        compiler_params=SMALL,
        name="chain",
    )(gathered, base, response)

    outer = swaps(outer, "dom", 1)
    inner = swaps(inner, "dom", 0)

    partial = pl.pallas_call(
        local_kernel,
        out_shape=wide,
        in_specs=[VMEM] * 4 + [SMEM] * 2,
        out_specs=VMEM,
        compiler_params=SMALL,
        name="local_product",
    )(rounded, diag_blocks, lower_blocks, upper_blocks, lower_at, upper_at)

    def halo(*refs):
        halo_kernel("dom", *refs)

    product = pl.pallas_call(
        halo,
        out_shape=wide,
        in_specs=[VMEM] * 4 + [SMEM],
        out_specs=VMEM,
        scratch_shapes=[pltpu.VMEM((2 * RIM, count, width), jnp.bfloat16)],
        compiler_params=SMALL,
        name="halo_product",
    )(partial, inner, outer, halo_blocks, halo_at)
    return (solution, product)


def solution(mesh):
    in_specs = (
        P(("section", "dom"), None, None),
        P(("section", "dom"), None, None),
        P(("section", "dom"), None, None),
        P(("section", "dom"), None, None, None),
        P(("section", "dom"), None, None, None),
        P(("section", "dom"), None, None, None),
        P(("section", "dom"), None),
        P(("section", "dom"), None),
        P(("section", "dom"), None),
    )
    out_specs = (P(("section", "dom"), None, None), P(("section", "dom"), None, None))
    return jax.shard_map(
        on_device, mesh=mesh, in_specs=in_specs, out_specs=out_specs, check_vma=False
    )
```

profile of v0, /device:TPU:8, one launch (start us, length us, event | category | flops | bytes accessed | tf_op | source)
XLA Modules:
  0.0 24.1 jit_solution(5148225476825092920)
XLA Ops:
  0.6 4.7 %sweeps.1 = (f32[8,32,128]{2,1,0:T(8,128)S(1)}, bf16[8,288,128]{2,1,0:T(8,128)(2,1)S(1)}, bf16[576,128]{1,0:T(8,128)(2,1)S(1)}) custom-call(f32[8,32,128]{2,1,0:T(8,128)} %rhs_far.1, bf16[8,128,128]{2,1,0:T(8,128)(2,1)} %inverse_far.1, bf16[8,3,128,128]{3,2,1,0:T(8,128)(2,1)} %lower.1, bf16[8,3,128,128]{3,2,1,0:T(8,128)(2,1)} %upper.1, s32[3,8]{1,0:T(4,128)} %bitcast.5, ...), custom_call_target="tpu_custom_call" | custom-call | tf_op jit(solution)/shard_map/sweeps/pallas_call | solution.py:233
  5.3 0.0 copy-start.1
  5.3 7.7 %all-gather = bf16[2304,128]{1,0:T(8,128)(2,1)S(1)} all-gather(bf16[576,128]{1,0:T(8,128)(2,1)S(1)} %get-tuple-element.9), channel_id=2, replica_groups=mesh['section'=4,'dom'=8] {'section'}, dimensions={0}, use_global_device_ids=true | all-gather | bytes 737280 | tf_op jit(solution)/shard_map/all_gather | solution.py:264
  13.0 0.0 copy-start
  13.0 0.0 copy-start.3
  13.0 1.5 %chain.1 = (f32[8,32,128]{2,1,0:T(8,128)}, bf16[10,32,128]{2,1,0:T(8,128)(2,1)S(1)}, bf16[4,32,128]{2,1,0:T(8,128)(2,1)S(1)}, bf16[4,32,128]{2,1,0:T(8,128)(2,1)S(1)}) custom-call(bf16[4,576,128]{2,1,0:T(8,128)(2,1)S(1)} %bitcast.4, f32[8,32,128]{2,1,0:T(8,128)S(1)} %get-tuple-element.10.refs_1_, bf16[8,288,128]{2,1,0:T(8,128)(2,1)S(1)} %get-tuple-element.11.refs_2_), custom_call_target="tpu_custom_call" | custom-call | tf_op jit(solution)/shard_map/chain/pallas_call | solution.py:269
  14.5 0.0 copy-start.5
  14.5 0.0 copy-start.4
  14.5 1.5 %collective-permute-start = (bf16[4,32,128]{2,1,0:T(8,128)(2,1)S(1)}, bf16[4,32,128]{2,1,0:T(8,128)(2,1)S(1)}, u32[]{:S(2)}, u32[]{:S(2)}) collective-permute-start(bf16[4,32,128]{2,1,0:T(8,128)(2,1)S(1)} %get-tuple-element.14), channel_id=1, source_target_pairs={{0,1},{1,0},{2,3},{3,2},{4,5},{5,4},{6,7},{7,6},{8,9},{9,8},{10,11... | collective-permute-start | bytes 98312 | tf_op jit(solution)/shard_map/ppermute | solution.py:210
  16.0 2.3 %collective-permute-start.1 = (bf16[4,32,128]{2,1,0:T(8,128)(2,1)S(1)}, bf16[4,32,128]{2,1,0:T(8,128)(2,1)S(1)}, u32[]{:S(2)}, u32[]{:S(2)}) collective-permute-start(bf16[4,32,128]{2,1,0:T(8,128)(2,1)S(1)} %get-tuple-element.15), channel_id=1, source_target_pairs={{1,2},{2,1},{3,4},{4,3},{5,6},{6,5},{9,10},{10,9},{11,12},{12,11},... | collective-permute-start | bytes 98312 | tf_op jit(solution)/shard_map/ppermute | solution.py:210
  18.3 0.0 copy-done.1
  18.3 0.0 copy-done
  18.3 0.0 copy-done.3
  18.3 0.0 copy-done.5
  18.3 0.0 copy-done.4
  18.3 0.0 copy-start.2
  18.3 1.0 %local_product.1.refs_0_ = f32[8,32,128]{2,1,0:T(8,128)S(1)} custom-call(bf16[10,32,128]{2,1,0:T(8,128)(2,1)S(1)} %get-tuple-element.13.rounded, bf16[8,128,128]{2,1,0:T(8,128)(2,1)S(1)} %copy-done.3, bf16[8,3,128,128]{3,2,1,0:T(8,128)(2,1)S(1)} %copy-done, bf16[8,3,128,128]{3,2,1,0:T(8,128)(2,1)S(1)} %copy-done.1, s32[3,8]{1,0:T(4,128)S(1)} %bitcast.6, ...), custom_call_target="tpu_custom_call" | custom-call | tf_op jit(solution)/shard_map/local_product/pallas_call | solution.py:287
  19.4 0.0 copy-start.6
  19.4 0.0 collective-permute-done.refs_1_
  19.4 3.2 %collective-permute-done.1.refs_2_ = bf16[4,32,128]{2,1,0:T(8,128)(2,1)S(1)} collective-permute-done((bf16[4,32,128]{2,1,0:T(8,128)(2,1)S(1)}, bf16[4,32,128]{2,1,0:T(8,128)(2,1)S(1)}, u32[]{:S(2)}, u32[]{:S(2)}) %collective-permute-start.1) | collective-permute-done | bytes 32800 | tf_op jit(solution)/shard_map/ppermute | solution.py:210
  22.7 0.0 copy-done.2
  22.7 0.0 copy-done.6
  22.7 1.4 %halo_product.1 = f32[8,32,128]{2,1,0:T(8,128)} custom-call(f32[8,32,128]{2,1,0:T(8,128)S(1)} %local_product.1.refs_0_, bf16[4,32,128]{2,1,0:T(8,128)(2,1)S(1)} %collective-permute-done.refs_1_, bf16[4,32,128]{2,1,0:T(8,128)(2,1)S(1)} %collective-permute-done.1.refs_2_, bf16[8,2,128,128]{3,2,1,0:T(8,128)(2,1)S(1)} %copy-done.2, s32[2,8]{1,0:T(2,128)S(1)} %bitcast.9), custom_call_target="tpu_custom_call" | custom-call | tf_op jit(solution)/shard_map/halo_product/pallas_call | solution.py:299
Async XLA Ops:
  5.3 13.0 %copy-start.1 = (bf16[8,3,128,128]{3,2,1,0:T(8,128)(2,1)S(1)}, bf16[8,3,128,128]{3,2,1,0:T(8,128)(2,1)}, u32[]{:S(2)}) copy-start(bf16[8,3,128,128]{3,2,1,0:T(8,128)(2,1)} %upper.1) | copy-start | bytes 2359300
  13.0 5.3 %copy-start = (bf16[8,3,128,128]{3,2,1,0:T(8,128)(2,1)S(1)}, bf16[8,3,128,128]{3,2,1,0:T(8,128)(2,1)}, u32[]{:S(2)}) copy-start(bf16[8,3,128,128]{3,2,1,0:T(8,128)(2,1)} %lower.1) | copy-start | bytes 2359300
  13.0 5.3 %copy-start.3 = (bf16[8,128,128]{2,1,0:T(8,128)(2,1)S(1)}, bf16[8,128,128]{2,1,0:T(8,128)(2,1)}, u32[]{:S(2)}) copy-start(bf16[8,128,128]{2,1,0:T(8,128)(2,1)} %diagonal.1) | copy-start | bytes 786436
  14.5 3.9 %copy-start.5 = (s32[8,3]{0,1:T(4,128)S(1)}, s32[8,3]{0,1:T(4,128)}, u32[]{:S(2)}) copy-start(s32[8,3]{0,1:T(4,128)} %param.16) | copy-start | bytes 292
  14.5 3.9 %copy-start.4 = (s32[8,3]{0,1:T(4,128)S(1)}, s32[8,3]{0,1:T(4,128)}, u32[]{:S(2)}) copy-start(s32[8,3]{0,1:T(4,128)} %param.15) | copy-start | bytes 292
  14.5 4.9 %collective-permute-start = (bf16[4,32,128]{2,1,0:T(8,128)(2,1)S(1)}, bf16[4,32,128]{2,1,0:T(8,128)(2,1)S(1)}, u32[]{:S(2)}, u32[]{:S(2)}) collective-permute-start(bf16[4,32,128]{2,1,0:T(8,128)(2,1)S(1)} %get-tuple-element.14), channel_id=1, source_target_pairs={{0,1},{1,0},{2,3},{3,2},{4,5},{5,4},{6,7},{7,6},{8,9},{9,8},{10,11... | collective-permute-start | bytes 98312 | tf_op jit(solution)/shard_map/ppermute | solution.py:210
  16.0 6.7 %collective-permute-start.1 = (bf16[4,32,128]{2,1,0:T(8,128)(2,1)S(1)}, bf16[4,32,128]{2,1,0:T(8,128)(2,1)S(1)}, u32[]{:S(2)}, u32[]{:S(2)}) collective-permute-start(bf16[4,32,128]{2,1,0:T(8,128)(2,1)S(1)} %get-tuple-element.15), channel_id=1, source_target_pairs={{1,2},{2,1},{3,4},{4,3},{5,6},{6,5},{9,10},{10,9},{11,12},{12,11},... | collective-permute-start | bytes 98312 | tf_op jit(solution)/shard_map/ppermute | solution.py:210
  18.3 4.3 %copy-start.2 = (bf16[8,2,128,128]{3,2,1,0:T(8,128)(2,1)S(1)}, bf16[8,2,128,128]{3,2,1,0:T(8,128)(2,1)}, u32[]{:S(2)}) copy-start(bf16[8,2,128,128]{3,2,1,0:T(8,128)(2,1)} %refs_3_.1) | copy-start | bytes 1572868
  19.4 3.3 %copy-start.6 = (s32[8,2]{0,1:T(2,128)S(1)}, s32[8,2]{0,1:T(2,128)}, u32[]{:S(2)}) copy-start(s32[8,2]{0,1:T(2,128)} %param.17) | copy-start | bytes 196
where the time goes:
time: 24.3 us; the launch traced here: 24.1 us
  Pallas kernels  8.58 us (35%)
  blocking collectives  7.69 us (32%)
  starting transfers between devices  3.81 us (16%)
  waiting for transfers between devices  3.24 us (13%)
  between operations  0.73 us (3%)
    all_gather x1, blocking collectives, on_device(): gathered = lax.all_gather(payload, 'section')  7.69 us
    pallas_call x1, Pallas kernels, on_device(): pl.pallas_call(sweep_kernel, out_shape=(wide, jax.ShapeDtypeStruct((rows,...  4.66 us
    ppermute x2, starting transfers between devices, swaps(): return lax.ppermute(block, axis, pairs)  3.81 us
    ppermute x2, waiting for transfers between devices, swaps(): return lax.ppermute(block, axis, pairs)  3.24 us
    pallas_call x1, Pallas kernels, on_device(): pl.pallas_call(chain, out_shape=(wide, jax.ShapeDtypeStruct((rows + 2, co...  1.46 us
    pallas_call x1, Pallas kernels, on_device(): pl.pallas_call(halo, out_shape=wide, in_specs=[VMEM] * 4 + [SMEM], out_sp...  1.41 us
    pallas_call x1, Pallas kernels, on_device(): pl.pallas_call(local_kernel, out_shape=wide, in_specs=[VMEM] * 4 + [SMEM]...  1.05 us
  transfers between devices with their start and end apart: 2, of which 1 were waited for; matrix products, arithmetic and copies ran while one was open for 0% of the time, Pallas kernels for 4%

commit v1 on v0

--- a/solution.py
+++ b/solution.py
@@ -123,57 +123,134 @@
     payload[near + far :] = response[last, near:]
 
 
-def chain_kernel(
-    groups, axes, gathered, base, response, solution, rounded, inner, outer, flow
-):
+def compose_kernel(axis, bit, final, mine, theirs, *refs):
+    prior, sent, inner, prior_out = refs[:4] if bit > 1 else (None, *refs[:3])
+    pair = refs[-1]
+    width = mine.shape[1]
+    count = (mine.shape[0] - 4 * width) // 2
+    near = count + width
+    me = lax.axis_index(axis)
+    place = lax.rem(lax.div(me, bit), 2)
+    mid = near + count
+    far = near + near + width
+
+    pair[place] = mine[...]
+    pair[1 - place] = theirs[...]
+    a = pair[0]
+    b = pair[1]
+    across = mul(a[:near], jnp.concatenate([b[count:near], b[mid : mid + width]], axis=1))
+    ahead = b[:near].astype(jnp.float32)
+    joined = across[:, :width] + jnp.concatenate(
+        [ahead[:count], jnp.zeros((width, width), jnp.float32)], axis=0
+    )
+    between = across[:, width:] + jnp.concatenate(
+        [b[near:mid].astype(jnp.float32), jnp.zeros((width, width), jnp.float32)], axis=0
+    )
+    between = jnp.concatenate([narrow(between), b[mid + width : far]], axis=0)
+    first = mul(between, a[mid + width : far])
+    first = narrow(first[:near] + a[near : 2 * near].astype(jnp.float32)), narrow(first[near:])
+    joined = narrow(joined)
+    inner[:near] = a[:near]
+    inner[near:] = between
+    prior_out[...] = a[far:]
+    if prior is not None:
+        lowest = jnp.logical_and(place == 1, lax.rem(me, bit) == 0)
+
+        @pl.when(jnp.logical_not(lowest))
+        def _():
+            prior_out[...] = prior[...]
+
+    if final:
+        refs[-2][...] = joined[:count]
+        above = lax.rem(lax.div(me, 2 * bit), 2) == 1
+
+        @pl.when(above)
+        def _():
+            sent[...] = first[0]
+
+        @pl.when(jnp.logical_not(above))
+        def _():
+            sent[:count] = joined[:count]
+            sent[count:] = b[far:]
+
+    else:
+        sent[:near] = joined
+        sent[near : 2 * near] = first[0]
+        sent[2 * near : far] = first[1]
+        sent[far:] = b[far:]
+
+
+def chain_kernel(axes, levels, *refs):
+    own, theirs, base, response, prior = refs[:5]
+    inner = refs[5 : 4 + levels]
+    solution, rounded, prior_out, near_rows, far_rows = refs[4 + levels :]
     rows, count, width = base.shape
     near = count + width
-    far = near + width
     me = lax.axis_index(axes[0])
     side = lax.rem(lax.axis_index(axes[1]), 2)
-    zero = jnp.zeros((count, width), jnp.bfloat16)
-
-    inflow = [zero]
-    for t in range(1, groups):
-        add = gathered[t - 1, :count].astype(jnp.float32)
-        if t > 1:
-            add = add + mul(inflow[-1], gathered[t - 1, count:near])
-        inflow.append(narrow(add))
-    outflow = [zero]
-    for t in range(groups - 1, 0, -1):
-        add = gathered[t, near : near + count].astype(jnp.float32)
-        add = add + mul(inflow[t], gathered[t, near + count : 2 * near])
-        if t < groups - 1:
-            add = add + mul(outflow[0], gathered[t, 2 * near : near + far])
-        outflow.insert(0, narrow(add))
-    for t in range(groups):
-        flow[0, t] = inflow[t]
-        flow[1, t] = outflow[t]
-
-    both = jnp.concatenate([flow[0, me], flow[1, me]], axis=1)
+
+    bit = 1 << (levels - 1)
+    upper = lax.div(me, bit) == 1
+    down = theirs[:count].astype(jnp.float32)
+    up = down + mul(own[...], theirs[count:])
+    inflow = narrow(jnp.where(upper, down, 0.0))
+    outflow = narrow(jnp.where(upper, 0.0, up))
+    prior_out[...] = prior[...]
+
+    @pl.when(me == bit)
+    def _():
+        prior_out[...] = theirs[count:]
+
+    for level in range(levels - 2, -1, -1):
+        part = inner[level]
+        upper = lax.rem(lax.div(me, 1 << level), 2) == 1
+        down = part[:count].astype(jnp.float32) + mul(inflow, part[count:near])
+        both = jnp.concatenate([inflow, outflow], axis=1)
+        up = part[near : near + count].astype(jnp.float32) + mul(both, part[near + count :])
+        inflow, outflow = (
+            narrow(jnp.where(upper, down, inflow.astype(jnp.float32))),
+            narrow(jnp.where(upper, outflow.astype(jnp.float32), up)),
+        )
+
+    both = jnp.concatenate([inflow, outflow], axis=1)
     for k in range(rows):
         value = base[k] + mul(both, response[k, count:])
         solution[k] = value
         rounded[k] = narrow(value)
-    rounded[rows + 1] = flow[1, me]
-    prior = lax.max(me - 1, 0)
-    before = flow[0, me].astype(jnp.float32) + mul(flow[1, prior], gathered[prior, near + far :])
-    rounded[rows] = narrow(jnp.where(me > 0, before, 0.0))
-    rim = inner.shape[0]
+    rounded[rows] = inflow
+    rounded[rows + 1] = outflow
+    rim = near_rows.shape[0]
     for e in range(rim):
-        inner[e] = rounded[(1 - side) * (rows - rim) + e]
-        outer[e] = rounded[side * (rows - rim) + e]
-
-
-def local_kernel(rounded, diagonal, lower, upper, lower_at, upper_at, partial):
+        near_rows[e] = rounded[(1 - side) * (rows - rim) + e]
+        far_rows[e] = rounded[side * (rows - rim) + e]
+
+
+def local_kernel(
+    axis,
+    rounded,
+    prior,
+    solved,
+    diagonal,
+    lower,
+    upper,
+    lower_at,
+    upper_at,
+    partial,
+    solution,
+    held,
+):
+    solution[...] = solved[...]
     rows, slots, width, _ = lower.shape
     upper_slots = upper.shape[1]
+    before = rounded[rows].astype(jnp.float32) + mul(rounded[0], prior[...])
+    held[...] = rounded[...]
+    held[rows] = narrow(jnp.where(lax.axis_index(axis) > 0, before, 0.0))
     for k in range(rows):
         total = mul(rounded[k], diagonal[k])
-        source = [rounded[rows]]
+        source = [held[rows]]
         for m in range(1, slots):
             at = lower_at[m, k]
-            source.append(rounded[jnp.where(at == k, rows, at)])
+            source.append(held[jnp.where(at == k, rows, at)])
         total = total + mul(
             jnp.concatenate(source, axis=1), lower[k].reshape(slots * width, width)
         )
@@ -187,7 +264,7 @@
         partial[k] = total
 
 
-def halo_kernel(axis, partial, inner, outer, halo, halo_at, product, rim_rows):
+def halo_kernel(axis, partial, outer, inner, halo, halo_at, product, rim_rows):
     rows, slots, width, _ = halo.shape
     rim = inner.shape[0]
     turn = rim * (1 - lax.rem(lax.axis_index(axis), 2))
@@ -200,6 +277,11 @@
         product[k] = partial[k] + mul(
             jnp.concatenate(source, axis=1), halo[k].reshape(slots * width, width)
         )
+
+
+def trade(block, axis, bit):
+    count = lax.axis_size(axis)
+    return lax.ppermute(block, axis, [(i, i ^ bit) for i in range(count)])
 
 
 def swaps(block, axis, first):
@@ -261,37 +343,69 @@
         )
     )
 
-    gathered = lax.all_gather(payload, "section")
+    levels = groups.bit_length() - 1
+    segment = payload.shape[0]
+    bits = jnp.bfloat16
+    prior = []
+    inner = []
+    for level in range(levels - 1):
+        theirs = trade(payload, "section", 1 << level)
+        final = level == levels - 2
+
+        def compose(*refs, bit=1 << level, final=final):
+            compose_kernel("section", bit, final, *refs)
+
+        payload, between, *prior = pl.pallas_call(
+            compose,
+            out_shape=(
+                jax.ShapeDtypeStruct((near if final else segment, width), bits),
+                jax.ShapeDtypeStruct((near + far, width), bits),
+                jax.ShapeDtypeStruct((width, width), bits),
+            )
+            + (jax.ShapeDtypeStruct((count, width), bits),) * final,
+            in_specs=[VMEM] * (2 + len(prior)),
+            out_specs=(VMEM,) * (3 + final),
+            scratch_shapes=[pltpu.VMEM((2, segment, width), bits)],
+            compiler_params=SMALL,
+            name="compose",
+        )(payload, theirs, *prior)
+        inner.append(between)
+    prior, own = prior
+    theirs = trade(payload, "section", 1 << (levels - 1))
 
     def chain(*refs):
-        chain_kernel(groups, ("section", "dom"), *refs)
-
-    solution, rounded, inner, outer = pl.pallas_call(
+        chain_kernel(("section", "dom"), levels, *refs)
+
+    solved, rounded, prior, inner, outer = pl.pallas_call(
         chain,
         out_shape=(
             wide,
-            jax.ShapeDtypeStruct((rows + 2, count, width), jnp.bfloat16),
-            jax.ShapeDtypeStruct((RIM, count, width), jnp.bfloat16),
-            jax.ShapeDtypeStruct((RIM, count, width), jnp.bfloat16),
+            jax.ShapeDtypeStruct((rows + 2, count, width), bits),
+            jax.ShapeDtypeStruct((width, width), bits),
+            jax.ShapeDtypeStruct((RIM, count, width), bits),
+            jax.ShapeDtypeStruct((RIM, count, width), bits),
         ),
-        in_specs=[VMEM] * 3,
-        out_specs=(VMEM,) * 4,
-        scratch_shapes=[pltpu.VMEM((2, groups, count, width), jnp.bfloat16)],
+        in_specs=[VMEM] * (4 + levels),
+        out_specs=(VMEM,) * 5,
         compiler_params=SMALL,
         name="chain",
-    )(gathered, base, response)
+    )(own, theirs, base, response, prior, *inner)
 
     outer = swaps(outer, "dom", 1)
     inner = swaps(inner, "dom", 0)
 
-    partial = pl.pallas_call(
-        local_kernel,
-        out_shape=wide,
-        in_specs=[VMEM] * 4 + [SMEM] * 2,
-        out_specs=VMEM,
+    def local(*refs):
+        local_kernel("section", *refs)
+
+    partial, solution = pl.pallas_call(
+        local,
+        out_shape=(wide, wide),
+        in_specs=[VMEM] * 6 + [SMEM] * 2,
+        out_specs=(VMEM, VMEM),
+        scratch_shapes=[pltpu.VMEM((rows + 2, count, width), bits)],
         compiler_params=SMALL,
         name="local_product",
-    )(rounded, diag_blocks, lower_blocks, upper_blocks, lower_at, upper_at)
+    )(rounded, prior, solved, diag_blocks, lower_blocks, upper_blocks, lower_at, upper_at)
 
     def halo(*refs):
         halo_kernel("dom", *refs)
@@ -304,7 +418,7 @@
         scratch_shapes=[pltpu.VMEM((2 * RIM, count, width), jnp.bfloat16)],
         compiler_params=SMALL,
         name="halo_product",
-    )(partial, inner, outer, halo_blocks, halo_at)
+    )(partial, outer, inner, halo_blocks, halo_at)
     return (solution, product)
 
 

time: 24.3 us -> 23 us (0.947)
  the two profiles are of different devices: /device:TPU:8 before, /device:TPU:0 now
where the time goes in v1:
time: 23 us; the launch traced here: 22.8 us
  starting transfers between devices  8.98 us (39%)
  Pallas kernels  8.73 us (38%)
  waiting for transfers between devices  2.99 us (13%)
  local copies, waits for them, and re-layouts  1.36 us (6%)
  between operations  0.7 us (3%)
    ppermute x2, starting transfers between devices, swaps(): return lax.ppermute(block, axis, pairs)  5.52 us
    pallas_call x1, Pallas kernels, on_device(): pl.pallas_call(sweep_kernel, out_shape=(wide, jax.ShapeDtypeStruct((rows,...  4.73 us
    ppermute x2, starting transfers between devices, trade(): return lax.ppermute(block, axis, [(i, i ^ bit) for i in range(count)])  3.46 us
    ppermute x2, waiting for transfers between devices, trade(): return lax.ppermute(block, axis, [(i, i ^ bit) for i in range(count)])  2.99 us
    pallas_call x1, Pallas kernels, on_device(): pl.pallas_call(local, out_shape=(wide, wide), in_specs=[VMEM] * 6 + [SMEM...  1.78 us
    pallas_call x1, Pallas kernels, on_device(): pl.pallas_call(halo, out_shape=wide, in_specs=[VMEM] * 4 + [SMEM], out_sp...  1.41 us
    unnamed x14, local copies, waits for them, and re-layouts  1.36 us
    pallas_call x1, Pallas kernels, on_device(): pl.pallas_call(chain, out_shape=(wide, jax.ShapeDtypeStruct((rows + 2, co...  0.47 us
  transfers between devices with their start and end apart: 4, of which 2 were waited for; matrix products, arithmetic and copies ran while one was open for 0% of the time, Pallas kernels for 8%

profile of v1, /device:TPU:0, one launch (start us, length us, event | category | flops | bytes accessed | tf_op | source)
XLA Modules:
  0.0 22.8 jit_solution(14436668884520847453)
XLA Ops:
  0.6 0.0 copy-start.1
  0.6 4.7 %sweeps.1 = (f32[8,32,128]{2,1,0:T(8,128)S(1)}, bf16[8,288,128]{2,1,0:T(8,128)(2,1)S(1)}, bf16[576,128]{1,0:T(8,128)(2,1)S(1)}) custom-call(f32[8,32,128]{2,1,0:T(8,128)} %rhs_far.1, bf16[8,128,128]{2,1,0:T(8,128)(2,1)} %inverse_far.1, bf16[8,3,128,128]{3,2,1,0:T(8,128)(2,1)} %refs_4_.1, bf16[8,3,128,128]{3,2,1,0:T(8,128)(2,1)} %refs_5_.1, s32[3,8]{1,0:T(4,128)} %bitcast.3, ...), custom_call_target="tpu_custom_call" | custom-call | tf_op jit(solution)/shard_map/sweeps/pallas_call | solution.py:315
  5.4 0.0 copy-start
  5.4 0.5 %collective-permute-start = (bf16[576,128]{1,0:T(8,128)(2,1)S(1)}, bf16[576,128]{1,0:T(8,128)(2,1)S(1)}, u32[]{:S(2)}, u32[]{:S(2)}) collective-permute-start(bf16[576,128]{1,0:T(8,128)(2,1)S(1)} %get-tuple-element.16.refs_0_), channel_id=1, source_target_pairs={{0,8},{8,0},{16,24},{24,16},{1,9},{9,1},{17,25},{25,17},{2,10},{10... | collective-permute-start | bytes 442376 | tf_op jit(solution)/shard_map/ppermute | solution.py:284
  5.9 1.0 %collective-permute-done.refs_1_ = bf16[576,128]{1,0:T(8,128)(2,1)S(1)} collective-permute-done((bf16[576,128]{1,0:T(8,128)(2,1)S(1)}, bf16[576,128]{1,0:T(8,128)(2,1)S(1)}, u32[]{:S(2)}, u32[]{:S(2)}) %collective-permute-start) | collective-permute-done | bytes 147488 | tf_op jit(solution)/shard_map/ppermute | solution.py:284
  6.9 0.3 %compose.1 = (bf16[160,128]{1,0:T(8,128)(2,1)S(1)}, bf16[448,128]{1,0:T(8,128)(2,1)S(1)}, bf16[128,128]{1,0:T(8,128)(2,1)S(1)}, bf16[32,128]{1,0:T(8,128)(2,1)S(1)}) custom-call(bf16[576,128]{1,0:T(8,128)(2,1)S(1)} %get-tuple-element.16.refs_0_, bf16[576,128]{1,0:T(8,128)(2,1)S(1)} %collective-permute-done.refs_1_), custom_call_target="tpu_custom_call" | custom-call | tf_op jit(solution)/shard_map/compose/pallas_call | solution.py:358
  7.3 2.9 %collective-permute-start.1 = (bf16[160,128]{1,0:T(8,128)(2,1)S(1)}, bf16[160,128]{1,0:T(8,128)(2,1)S(1)}, u32[]{:S(2)}, u32[]{:S(2)}) collective-permute-start(bf16[160,128]{1,0:T(8,128)(2,1)S(1)} %get-tuple-element.18), channel_id=1, source_target_pairs={{0,16},{8,24},{16,0},{24,8},{1,17},{9,25},{17,1},{25,9},{2,18},{10... | collective-permute-start | bytes 122888 | tf_op jit(solution)/shard_map/ppermute | solution.py:284
  10.2 2.0 %collective-permute-done.1.refs_1_ = bf16[160,128]{1,0:T(8,128)(2,1)S(1)} collective-permute-done((bf16[160,128]{1,0:T(8,128)(2,1)S(1)}, bf16[160,128]{1,0:T(8,128)(2,1)S(1)}, u32[]{:S(2)}, u32[]{:S(2)}) %collective-permute-start.1) | collective-permute-done | bytes 40992 | tf_op jit(solution)/shard_map/ppermute | solution.py:284
  12.2 0.0 copy-start.3
  12.2 0.5 %chain.1 = (f32[8,32,128]{2,1,0:T(8,128)S(1)}, bf16[10,32,128]{2,1,0:T(8,128)(2,1)S(1)}, bf16[128,128]{1,0:T(8,128)(2,1)S(1)}, bf16[4,32,128]{2,1,0:T(8,128)(2,1)S(1)}, bf16[4,32,128]{2,1,0:T(8,128)(2,1)S(1)}) custom-call(bf16[32,128]{1,0:T(8,128)(2,1)S(1)} %get-tuple-element.17.refs_0_, bf16[160,128]{1,0:T(8,128)(2,1)S(1)} %collective-permute-done.1.refs_1_, ...), custom_call_target="tpu_custom_call" | custom-call | tf_op jit(solution)/shard_map/chain/pallas_call | solution.py:379
  12.7 0.7 %collective-permute-start.2 = (bf16[4,32,128]{2,1,0:T(8,128)(2,1)S(1)}, bf16[4,32,128]{2,1,0:T(8,128)(2,1)S(1)}, u32[]{:S(2)}, u32[]{:S(2)}) collective-permute-start(bf16[4,32,128]{2,1,0:T(8,128)(2,1)S(1)} %get-tuple-element.28), channel_id=1, source_target_pairs={{1,2},{2,1},{3,4},{4,3},{5,6},{6,5},{9,10},{10,9},{11,12},{12,11},... | collective-permute-start | bytes 98312 | tf_op jit(solution)/shard_map/ppermute | solution.py:292
  13.3 4.9 %collective-permute-start.3 = (bf16[4,32,128]{2,1,0:T(8,128)(2,1)S(1)}, bf16[4,32,128]{2,1,0:T(8,128)(2,1)S(1)}, u32[]{:S(2)}, u32[]{:S(2)}) collective-permute-start(bf16[4,32,128]{2,1,0:T(8,128)(2,1)S(1)} %get-tuple-element.29), channel_id=1, source_target_pairs={{0,1},{1,0},{2,3},{3,2},{4,5},{5,4},{6,7},{7,6},{8,9},{9,8},{10,11... | collective-permute-start | bytes 98312 | tf_op jit(solution)/shard_map/ppermute | solution.py:292
  18.2 0.0 copy-start.5
  18.2 0.0 copy-start.4
  18.2 0.0 copy-done.1
  18.2 0.0 copy-done
  18.2 0.0 copy-done.3
  18.2 0.7 %copy-done.5 = s32[8,3]{0,1:T(4,128)S(1)} copy-done((s32[8,3]{0,1:T(4,128)S(1)}, s32[8,3]{0,1:T(4,128)}, u32[]{:S(2)}) %copy-start.5) | copy-done | bytes 120
  18.9 0.0 copy-done.4
  18.9 0.0 copy-start.2
  18.9 1.8 %local_product.1 = (f32[8,32,128]{2,1,0:T(8,128)S(1)}, f32[8,32,128]{2,1,0:T(8,128)}) custom-call(bf16[10,32,128]{2,1,0:T(8,128)(2,1)S(1)} %get-tuple-element.23.refs_0_, bf16[128,128]{1,0:T(8,128)(2,1)S(1)} %get-tuple-element.24.refs_1_, f32[8,32,128]{2,1,0:T(8,128)S(1)} %get-tuple-element.25.refs_2_, bf16[8,128,128]{2,1,0:T(8,128)(2,1)S(1)} %copy-done.3, ...), custom_call_target="tpu_custom_call" | custom-call | tf_op jit(solution)/shard_map/local_product/pallas_call | solution.py:400
  20.7 0.0 collective-permute-done.2.refs_1_
  20.7 0.0 collective-permute-done.3.refs_2_
  20.7 0.0 copy-start.6
  20.7 0.0 copy-done.2
  20.7 0.7 %copy-done.6 = s32[8,2]{0,1:T(2,128)S(1)} copy-done((s32[8,2]{0,1:T(2,128)S(1)}, s32[8,2]{0,1:T(2,128)}, u32[]{:S(2)}) %copy-start.6) | copy-done | bytes 88
  21.4 1.4 %halo_product.1 = f32[8,32,128]{2,1,0:T(8,128)} custom-call(f32[8,32,128]{2,1,0:T(8,128)S(1)} %get-tuple-element.27.refs_0_, bf16[4,32,128]{2,1,0:T(8,128)(2,1)S(1)} %collective-permute-done.2.refs_1_, bf16[4,32,128]{2,1,0:T(8,128)(2,1)S(1)} %collective-permute-done.3.refs_2_, bf16[8,2,128,128]{3,2,1,0:T(8,128)(2,1)S(1)} %copy-done.2, s32[2,8]{1,0:T(2,128)S(1)} %bitcast.7), custom_call_target="tpu_custom_call" | custom-call | tf_op jit(solution)/shard_map/halo_product/pallas_call | solution.py:413
Async XLA Ops:
  0.6 17.6 %copy-start.1 = (bf16[8,3,128,128]{3,2,1,0:T(8,128)(2,1)S(1)}, bf16[8,3,128,128]{3,2,1,0:T(8,128)(2,1)}, u32[]{:S(2)}) copy-start(bf16[8,3,128,128]{3,2,1,0:T(8,128)(2,1)} %refs_5_.1) | copy-start | bytes 2359300
  5.4 12.8 %copy-start = (bf16[8,3,128,128]{3,2,1,0:T(8,128)(2,1)S(1)}, bf16[8,3,128,128]{3,2,1,0:T(8,128)(2,1)}, u32[]{:S(2)}) copy-start(bf16[8,3,128,128]{3,2,1,0:T(8,128)(2,1)} %refs_4_.1) | copy-start | bytes 2359300
  5.4 1.5 %collective-permute-start = (bf16[576,128]{1,0:T(8,128)(2,1)S(1)}, bf16[576,128]{1,0:T(8,128)(2,1)S(1)}, u32[]{:S(2)}, u32[]{:S(2)}) collective-permute-start(bf16[576,128]{1,0:T(8,128)(2,1)S(1)} %get-tuple-element.16.refs_0_), channel_id=1, source_target_pairs={{0,8},{8,0},{16,24},{24,16},{1,9},{9,1},{17,25},{25,17},{2,10},{10... | collective-permute-start | bytes 442376 | tf_op jit(solution)/shard_map/ppermute | solution.py:284
  7.3 4.9 %collective-permute-start.1 = (bf16[160,128]{1,0:T(8,128)(2,1)S(1)}, bf16[160,128]{1,0:T(8,128)(2,1)S(1)}, u32[]{:S(2)}, u32[]{:S(2)}) collective-permute-start(bf16[160,128]{1,0:T(8,128)(2,1)S(1)} %get-tuple-element.18), channel_id=1, source_target_pairs={{0,16},{8,24},{16,0},{24,8},{1,17},{9,25},{17,1},{25,9},{2,18},{10... | collective-permute-start | bytes 122888 | tf_op jit(solution)/shard_map/ppermute | solution.py:284
  12.2 6.0 %copy-start.3 = (bf16[8,128,128]{2,1,0:T(8,128)(2,1)S(1)}, bf16[8,128,128]{2,1,0:T(8,128)(2,1)}, u32[]{:S(2)}) copy-start(bf16[8,128,128]{2,1,0:T(8,128)(2,1)} %refs_3_.2) | copy-start | bytes 786436
  12.7 8.0 %collective-permute-start.2 = (bf16[4,32,128]{2,1,0:T(8,128)(2,1)S(1)}, bf16[4,32,128]{2,1,0:T(8,128)(2,1)S(1)}, u32[]{:S(2)}, u32[]{:S(2)}) collective-permute-start(bf16[4,32,128]{2,1,0:T(8,128)(2,1)S(1)} %get-tuple-element.28), channel_id=1, source_target_pairs={{1,2},{2,1},{3,4},{4,3},{5,6},{6,5},{9,10},{10,9},{11,12},{12,11},... | collective-permute-start | bytes 98312 | tf_op jit(solution)/shard_map/ppermute | solution.py:292
  13.3 7.3 %collective-permute-start.3 = (bf16[4,32,128]{2,1,0:T(8,128)(2,1)S(1)}, bf16[4,32,128]{2,1,0:T(8,128)(2,1)S(1)}, u32[]{:S(2)}, u32[]{:S(2)}) collective-permute-start(bf16[4,32,128]{2,1,0:T(8,128)(2,1)S(1)} %get-tuple-element.29), channel_id=1, source_target_pairs={{0,1},{1,0},{2,3},{3,2},{4,5},{5,4},{6,7},{7,6},{8,9},{9,8},{10,11... | collective-permute-start | bytes 98312 | tf_op jit(solution)/shard_map/ppermute | solution.py:292
  18.2 0.7 %copy-start.5 = (s32[8,3]{0,1:T(4,128)S(1)}, s32[8,3]{0,1:T(4,128)}, u32[]{:S(2)}) copy-start(s32[8,3]{0,1:T(4,128)} %param.16) | copy-start | bytes 292
  18.2 0.7 %copy-start.4 = (s32[8,3]{0,1:T(4,128)S(1)}, s32[8,3]{0,1:T(4,128)}, u32[]{:S(2)}) copy-start(s32[8,3]{0,1:T(4,128)} %param.15) | copy-start | bytes 292
  18.9 1.8 %copy-start.2 = (bf16[8,2,128,128]{3,2,1,0:T(8,128)(2,1)S(1)}, bf16[8,2,128,128]{3,2,1,0:T(8,128)(2,1)}, u32[]{:S(2)}) copy-start(bf16[8,2,128,128]{3,2,1,0:T(8,128)(2,1)} %refs_3_.3) | copy-start | bytes 1572868
  20.7 0.7 %copy-start.6 = (s32[8,2]{0,1:T(2,128)S(1)}, s32[8,2]{0,1:T(2,128)}, u32[]{:S(2)}) copy-start(s32[8,2]{0,1:T(2,128)} %param.17) | copy-start | bytes 196

commit v2 on v1

--- a/solution.py
+++ b/solution.py
@@ -28,9 +28,13 @@
     upper_far,
     lower_at_far,
     upper_at_far,
+    halo_at_far,
     base,
     response,
     payload,
+    lower_at_kept,
+    upper_at_kept,
+    halo_at_kept,
     rhs,
     inverse,
     lower,
@@ -57,6 +61,9 @@
         (lower_far.at[half:], lower.at[half:]),
         (upper_far, upper),
         (upper_at_far, upper_at),
+        (lower_at_far, lower_at_kept),
+        (upper_at_far, upper_at_kept),
+        (halo_at_far, halo_at_kept),
     ]
     copies = [
         pltpu.make_async_copy(far, here, arrived.at[i]) for i, (far, here) in enumerate(parts)
@@ -238,8 +245,10 @@
     partial,
     solution,
     held,
+    out,
 ):
-    solution[...] = solved[...]
+    copy = pltpu.make_async_copy(solved, solution, out)
+    copy.start()
     rows, slots, width, _ = lower.shape
     upper_slots = upper.shape[1]
     before = rounded[rows].astype(jnp.float32) + mul(rounded[0], prior[...])
@@ -262,6 +271,7 @@
             jnp.concatenate(source, axis=1), upper[k].reshape(upper_slots * width, width)
         )
         partial[k] = total
+    copy.wait()
 
 
 def halo_kernel(axis, partial, outer, inner, halo, halo_at, product, rim_rows):
@@ -312,15 +322,17 @@
     far = near + width
     wide = jax.ShapeDtypeStruct((rows, count, width), jnp.float32)
 
-    base, response, payload = pl.pallas_call(
+    indices = (lower_at, upper_at, halo_at)
+    base, response, payload, *indices = pl.pallas_call(
         sweep_kernel,
         out_shape=(
             wide,
             jax.ShapeDtypeStruct((rows, far, width), jnp.bfloat16),
             jax.ShapeDtypeStruct((near + far + width, width), jnp.bfloat16),
-        ),
-        in_specs=[HBM] * 6,
-        out_specs=(VMEM, VMEM, VMEM),
+        )
+        + tuple(jax.ShapeDtypeStruct(a.shape, a.dtype) for a in indices),
+        in_specs=[HBM] * 7,
+        out_specs=(VMEM,) * 6,
         scratch_shapes=[
             pltpu.VMEM(right_sides.shape, right_sides.dtype),
             pltpu.VMEM(diag_inverse.shape, diag_inverse.dtype),
@@ -332,14 +344,14 @@
             pltpu.VMEM((rows, upper_slots * width, width), jnp.bfloat16),
             pltpu.VMEM((rows, near, width), jnp.bfloat16),
             pltpu.VMEM((rows, near, width), jnp.float32),
-            pltpu.SemaphoreType.DMA((7,)),
+            pltpu.SemaphoreType.DMA((10,)),
         ],
         compiler_params=SMALL,
         name="sweeps",
     )(
         *(
             pltpu.with_memory_space_constraint(a, pltpu.HBM)
-            for a in (right_sides, diag_inverse, lower_blocks, upper_blocks, lower_at, upper_at)
+            for a in (right_sides, diag_inverse, lower_blocks, upper_blocks, *indices)
         )
     )
 
@@ -401,11 +413,14 @@
         local,
         out_shape=(wide, wide),
         in_specs=[VMEM] * 6 + [SMEM] * 2,
-        out_specs=(VMEM, VMEM),
-        scratch_shapes=[pltpu.VMEM((rows + 2, count, width), bits)],
+        out_specs=(VMEM, HBM),
+        scratch_shapes=[
+            pltpu.VMEM((rows + 2, count, width), bits),
+            pltpu.SemaphoreType.DMA(()),
+        ],
         compiler_params=SMALL,
         name="local_product",
-    )(rounded, prior, solved, diag_blocks, lower_blocks, upper_blocks, lower_at, upper_at)
+    )(rounded, prior, solved, diag_blocks, lower_blocks, upper_blocks, *indices[:2])
 
     def halo(*refs):
         halo_kernel("dom", *refs)
@@ -418,7 +433,7 @@
         scratch_shapes=[pltpu.VMEM((2 * RIM, count, width), jnp.bfloat16)],
         compiler_params=SMALL,
         name="halo_product",
-    )(partial, outer, inner, halo_blocks, halo_at)
+    )(partial, outer, inner, halo_blocks, indices[2])
     return (solution, product)
 
 

time: 23 us -> 21.7 us (0.943)
  local copies, waits for them, and re-layouts: 1.36 us -> 0.02 us
    unnamed x14 -> x8, local copies, waits for them, and re-layouts: 1.36 us -> 0.02 us
  transfers between devices with their start and end apart: 4 -> 4, of which waited for: 2 -> 3; matrix products, arithmetic and copies ran while one was open for 0% -> 0% of each run, Pallas kernels for 8% -> 8%
where the time goes in v2:
time: 21.7 us; the launch traced here: 21.5 us
  starting transfers between devices  8.97 us (41%)
  Pallas kernels  8.64 us (40%)
  waiting for transfers between devices  3.21 us (15%)
  between operations  0.7 us (3%)
    ppermute x2, starting transfers between devices, swaps(): return lax.ppermute(block, axis, pairs)  5.51 us
    pallas_call x1, Pallas kernels, on_device(): pl.pallas_call(sweep_kernel, out_shape=(wide, jax.ShapeDtypeStruct((rows,...  4.78 us
    ppermute x2, starting transfers between devices, trade(): return lax.ppermute(block, axis, [(i, i ^ bit) for i in range(count)])  3.46 us
    ppermute x2, waiting for transfers between devices, trade(): return lax.ppermute(block, axis, [(i, i ^ bit) for i in range(count)])  2.99 us
    pallas_call x1, Pallas kernels, on_device(): pl.pallas_call(local, out_shape=(wide, wide), in_specs=[VMEM] * 6 + [SMEM...  1.64 us
    pallas_call x1, Pallas kernels, on_device(): pl.pallas_call(halo, out_shape=wide, in_specs=[VMEM] * 4 + [SMEM], out_sp...  1.41 us
    pallas_call x1, Pallas kernels, on_device(): pl.pallas_call(chain, out_shape=(wide, jax.ShapeDtypeStruct((rows + 2, co...  0.48 us
  transfers between devices with their start and end apart: 4, of which 3 were waited for; matrix products, arithmetic and copies ran while one was open for 0% of the time, Pallas kernels for 8%

profile of v2, /device:TPU:0, one launch (start us, length us, event | category | flops | bytes accessed | tf_op | source)
XLA Modules:
  0.0 21.5 jit_solution(13730964850823018152)
XLA Ops:
  0.6 0.0 copy-start.1
  0.6 4.8 %sweeps.1 = (f32[8,32,128]{2,1,0:T(8,128)S(1)}, bf16[8,288,128]{2,1,0:T(8,128)(2,1)S(1)}, bf16[576,128]{1,0:T(8,128)(2,1)S(1)}, s32[3,8]{1,0:T(4,128)S(1)}, s32[3,8]{1,0:T(4,128)S(1)}, /*index=5*/s32[2,8]{1,0:T(2,128)S(1)}) custom-call(f32[8,32,128]{2,1,0:T(8,128)} %rhs_far.1, bf16[8,128,128]{2,1,0:T(8,128)(2,1)} %inverse_far.1, ...), custom_call_target="tpu_custom_call" | custom-call | tf_op jit(solution)/shard_map/sweeps/pallas_call | solution.py:326
  5.4 0.0 copy-start
  5.4 0.5 %collective-permute-start = (bf16[576,128]{1,0:T(8,128)(2,1)S(1)}, bf16[576,128]{1,0:T(8,128)(2,1)S(1)}, u32[]{:S(2)}, u32[]{:S(2)}) collective-permute-start(bf16[576,128]{1,0:T(8,128)(2,1)S(1)} %get-tuple-element.19.refs_0_), channel_id=1, source_target_pairs={{0,8},{8,0},{16,24},{24,16},{1,9},{9,1},{17,25},{25,17},{2,10},{10... | collective-permute-start | bytes 442376 | tf_op jit(solution)/shard_map/ppermute | solution.py:294
  6.0 1.0 %collective-permute-done.refs_1_ = bf16[576,128]{1,0:T(8,128)(2,1)S(1)} collective-permute-done((bf16[576,128]{1,0:T(8,128)(2,1)S(1)}, bf16[576,128]{1,0:T(8,128)(2,1)S(1)}, u32[]{:S(2)}, u32[]{:S(2)}) %collective-permute-start) | collective-permute-done | bytes 147488 | tf_op jit(solution)/shard_map/ppermute | solution.py:294
  7.0 0.3 %compose.1 = (bf16[160,128]{1,0:T(8,128)(2,1)S(1)}, bf16[448,128]{1,0:T(8,128)(2,1)S(1)}, bf16[128,128]{1,0:T(8,128)(2,1)S(1)}, bf16[32,128]{1,0:T(8,128)(2,1)S(1)}) custom-call(bf16[576,128]{1,0:T(8,128)(2,1)S(1)} %get-tuple-element.19.refs_0_, bf16[576,128]{1,0:T(8,128)(2,1)S(1)} %collective-permute-done.refs_1_), custom_call_target="tpu_custom_call" | custom-call | tf_op jit(solution)/shard_map/compose/pallas_call | solution.py:370
  7.3 2.9 %collective-permute-start.1 = (bf16[160,128]{1,0:T(8,128)(2,1)S(1)}, bf16[160,128]{1,0:T(8,128)(2,1)S(1)}, u32[]{:S(2)}, u32[]{:S(2)}) collective-permute-start(bf16[160,128]{1,0:T(8,128)(2,1)S(1)} %get-tuple-element.21), channel_id=1, source_target_pairs={{0,16},{8,24},{16,0},{24,8},{1,17},{9,25},{17,1},{25,9},{2,18},{10... | collective-permute-start | bytes 122888 | tf_op jit(solution)/shard_map/ppermute | solution.py:294
  10.3 2.0 %collective-permute-done.1.refs_1_ = bf16[160,128]{1,0:T(8,128)(2,1)S(1)} collective-permute-done((bf16[160,128]{1,0:T(8,128)(2,1)S(1)}, bf16[160,128]{1,0:T(8,128)(2,1)S(1)}, u32[]{:S(2)}, u32[]{:S(2)}) %collective-permute-start.1) | collective-permute-done | bytes 40992 | tf_op jit(solution)/shard_map/ppermute | solution.py:294
  12.2 0.0 copy-start.3
  12.2 0.5 %chain.1 = (f32[8,32,128]{2,1,0:T(8,128)S(1)}, bf16[10,32,128]{2,1,0:T(8,128)(2,1)S(1)}, bf16[128,128]{1,0:T(8,128)(2,1)S(1)}, bf16[4,32,128]{2,1,0:T(8,128)(2,1)S(1)}, bf16[4,32,128]{2,1,0:T(8,128)(2,1)S(1)}) custom-call(bf16[32,128]{1,0:T(8,128)(2,1)S(1)} %get-tuple-element.20.refs_0_, bf16[160,128]{1,0:T(8,128)(2,1)S(1)} %collective-permute-done.1.refs_1_, ...), custom_call_target="tpu_custom_call" | custom-call | tf_op jit(solution)/shard_map/chain/pallas_call | solution.py:391
  12.7 0.7 %collective-permute-start.2 = (bf16[4,32,128]{2,1,0:T(8,128)(2,1)S(1)}, bf16[4,32,128]{2,1,0:T(8,128)(2,1)S(1)}, u32[]{:S(2)}, u32[]{:S(2)}) collective-permute-start(bf16[4,32,128]{2,1,0:T(8,128)(2,1)S(1)} %get-tuple-element.33), channel_id=1, source_target_pairs={{1,2},{2,1},{3,4},{4,3},{5,6},{6,5},{9,10},{10,9},{11,12},{12,11},... | collective-permute-start | bytes 98312 | tf_op jit(solution)/shard_map/ppermute | solution.py:302
  13.4 4.8 %collective-permute-start.3 = (bf16[4,32,128]{2,1,0:T(8,128)(2,1)S(1)}, bf16[4,32,128]{2,1,0:T(8,128)(2,1)S(1)}, u32[]{:S(2)}, u32[]{:S(2)}) collective-permute-start(bf16[4,32,128]{2,1,0:T(8,128)(2,1)S(1)} %get-tuple-element.34), channel_id=1, source_target_pairs={{0,1},{1,0},{2,3},{3,2},{4,5},{5,4},{6,7},{7,6},{8,9},{9,8},{10,11... | collective-permute-start | bytes 98312 | tf_op jit(solution)/shard_map/ppermute | solution.py:302
  18.2 0.0 copy-done.1
  18.2 0.0 copy-done
  18.2 0.0 copy-done.3
  18.2 0.0 copy-start.2
  18.2 1.6 %local_product.1 = (f32[8,32,128]{2,1,0:T(8,128)S(1)}, f32[8,32,128]{2,1,0:T(8,128)}) custom-call(bf16[10,32,128]{2,1,0:T(8,128)(2,1)S(1)} %get-tuple-element.26.refs_0_, bf16[128,128]{1,0:T(8,128)(2,1)S(1)} %get-tuple-element.27.refs_1_, f32[8,32,128]{2,1,0:T(8,128)S(1)} %get-tuple-element.28.refs_2_, bf16[8,128,128]{2,1,0:T(8,128)(2,1)S(1)} %copy-done.3, ...), custom_call_target="tpu_custom_call" | custom-call | tf_op jit(solution)/shard_map/local_product/pallas_call | solution.py:412
  19.9 0.0 collective-permute-done.2.refs_1_
  19.9 0.2 %collective-permute-done.3.refs_2_ = bf16[4,32,128]{2,1,0:T(8,128)(2,1)S(1)} collective-permute-done((bf16[4,32,128]{2,1,0:T(8,128)(2,1)S(1)}, bf16[4,32,128]{2,1,0:T(8,128)(2,1)S(1)}, u32[]{:S(2)}, u32[]{:S(2)}) %collective-permute-start.3) | collective-permute-done | bytes 32800 | tf_op jit(solution)/shard_map/ppermute | solution.py:302
  20.1 0.0 copy-done.2
  20.1 1.4 %halo_product.1 = f32[8,32,128]{2,1,0:T(8,128)} custom-call(f32[8,32,128]{2,1,0:T(8,128)S(1)} %get-tuple-element.32.refs_0_, bf16[4,32,128]{2,1,0:T(8,128)(2,1)S(1)} %collective-permute-done.2.refs_1_, bf16[4,32,128]{2,1,0:T(8,128)(2,1)S(1)} %collective-permute-done.3.refs_2_, bf16[8,2,128,128]{3,2,1,0:T(8,128)(2,1)S(1)} %copy-done.2, ...), custom_call_target="tpu_custom_call" | custom-call | tf_op jit(solution)/shard_map/halo_product/pallas_call | solution.py:428
Async XLA Ops:
  0.6 17.6 %copy-start.1 = (bf16[8,3,128,128]{3,2,1,0:T(8,128)(2,1)S(1)}, bf16[8,3,128,128]{3,2,1,0:T(8,128)(2,1)}, u32[]{:S(2)}) copy-start(bf16[8,3,128,128]{3,2,1,0:T(8,128)(2,1)} %refs_5_.1) | copy-start | bytes 2359300
  5.4 12.8 %copy-start = (bf16[8,3,128,128]{3,2,1,0:T(8,128)(2,1)S(1)}, bf16[8,3,128,128]{3,2,1,0:T(8,128)(2,1)}, u32[]{:S(2)}) copy-start(bf16[8,3,128,128]{3,2,1,0:T(8,128)(2,1)} %refs_4_.1) | copy-start | bytes 2359300
  5.4 1.5 %collective-permute-start = (bf16[576,128]{1,0:T(8,128)(2,1)S(1)}, bf16[576,128]{1,0:T(8,128)(2,1)S(1)}, u32[]{:S(2)}, u32[]{:S(2)}) collective-permute-start(bf16[576,128]{1,0:T(8,128)(2,1)S(1)} %get-tuple-element.19.refs_0_), channel_id=1, source_target_pairs={{0,8},{8,0},{16,24},{24,16},{1,9},{9,1},{17,25},{25,17},{2,10},{10... | collective-permute-start | bytes 442376 | tf_op jit(solution)/shard_map/ppermute | solution.py:294
  7.3 4.9 %collective-permute-start.1 = (bf16[160,128]{1,0:T(8,128)(2,1)S(1)}, bf16[160,128]{1,0:T(8,128)(2,1)S(1)}, u32[]{:S(2)}, u32[]{:S(2)}) collective-permute-start(bf16[160,128]{1,0:T(8,128)(2,1)S(1)} %get-tuple-element.21), channel_id=1, source_target_pairs={{0,16},{8,24},{16,0},{24,8},{1,17},{9,25},{17,1},{25,9},{2,18},{10... | collective-permute-start | bytes 122888 | tf_op jit(solution)/shard_map/ppermute | solution.py:294
  12.2 6.0 %copy-start.3 = (bf16[8,128,128]{2,1,0:T(8,128)(2,1)S(1)}, bf16[8,128,128]{2,1,0:T(8,128)(2,1)}, u32[]{:S(2)}) copy-start(bf16[8,128,128]{2,1,0:T(8,128)(2,1)} %refs_3_.2) | copy-start | bytes 786436
  12.7 7.2 %collective-permute-start.2 = (bf16[4,32,128]{2,1,0:T(8,128)(2,1)S(1)}, bf16[4,32,128]{2,1,0:T(8,128)(2,1)S(1)}, u32[]{:S(2)}, u32[]{:S(2)}) collective-permute-start(bf16[4,32,128]{2,1,0:T(8,128)(2,1)S(1)} %get-tuple-element.33), channel_id=1, source_target_pairs={{1,2},{2,1},{3,4},{4,3},{5,6},{6,5},{9,10},{10,9},{11,12},{12,11},... | collective-permute-start | bytes 98312 | tf_op jit(solution)/shard_map/ppermute | solution.py:302
  13.4 6.7 %collective-permute-start.3 = (bf16[4,32,128]{2,1,0:T(8,128)(2,1)S(1)}, bf16[4,32,128]{2,1,0:T(8,128)(2,1)S(1)}, u32[]{:S(2)}, u32[]{:S(2)}) collective-permute-start(bf16[4,32,128]{2,1,0:T(8,128)(2,1)S(1)} %get-tuple-element.34), channel_id=1, source_target_pairs={{0,1},{1,0},{2,3},{3,2},{4,5},{5,4},{6,7},{7,6},{8,9},{9,8},{10,11... | collective-permute-start | bytes 98312 | tf_op jit(solution)/shard_map/ppermute | solution.py:302
  18.2 1.9 %copy-start.2 = (bf16[8,2,128,128]{3,2,1,0:T(8,128)(2,1)S(1)}, bf16[8,2,128,128]{3,2,1,0:T(8,128)(2,1)}, u32[]{:S(2)}) copy-start(bf16[8,2,128,128]{3,2,1,0:T(8,128)(2,1)} %refs_3_.3) | copy-start | bytes 1572868

commit v3 on v2

--- a/solution.py
+++ b/solution.py
@@ -41,10 +41,13 @@
     upper,
     lower_at,
     upper_at,
-    low,
-    upp,
+    low_pair,
+    low_second,
+    upp_pair,
+    upp_second,
     down,
     exact,
+    fixed,
     arrived,
 ):
     rows, count, width = rhs.shape
@@ -74,55 +77,119 @@
         lax.broadcasted_iota(jnp.int32, (width, width), 0)
         == lax.broadcasted_iota(jnp.int32, (width, width), 1)
     )
-    down[:, :count] = jnp.zeros((rows, count, width), jnp.bfloat16)
-    response[:, :near] = jnp.zeros((rows, near, width), jnp.bfloat16)
+    down[:, :count] = jnp.zeros((rows + 1, count, width), jnp.bfloat16)
+    response[:, :near] = jnp.zeros((rows + 1, near, width), jnp.bfloat16)
     for k in range(rows):
         down[k, count:] = eye
         response[k, near:] = eye
-
-    for k in range(rows):
-        if k == 0:
-            for copy in copies[:4]:
-                copy.wait()
-        if k == half:
+    down[rows, count:] = jnp.zeros_like(eye)
+    response[rows, near:] = jnp.zeros_like(eye)
+
+    def piece(blocks, m):
+        return blocks[m * width : (m + 1) * width]
+
+    def named(at, k, row, blocks, many):
+        return sum(
+            jnp.where(at[m, k] == row, piece(blocks, m), 0.0) for m in range(1, many)
+        )
+
+    def sources(held, at, k, skipped, many):
+        picked = []
+        for m in range(1, many):
+            row = at[m, k]
+            picked.append(held[row if skipped is None else jnp.where(row == skipped, rows, row)])
+        return jnp.concatenate(picked, axis=1)
+
+    def ready_down(p):
+        a, b = 2 * p, 2 * p + 1
+        both = []
+        for k in (a, b):
+            blocks = lower[k].reshape(slots * width, width)
+            both.append(mul(jnp.concatenate([narrow(rhs[k]), blocks], axis=0), inverse[k]))
+        of_a, of_b = both
+        link = narrow(named(lower_at, b, a, of_b[count:], slots))
+        of_a_narrow = narrow(of_a)
+        through = mul(of_a_narrow, link)
+        exact[a, :count] = of_a[:count]
+        exact[a, count:] = -of_a[count:near]
+        exact[b, :count] = of_b[:count] - through[:count]
+        exact[b, count:] = through[count:near] - of_b[count:near]
+        if p == 0:
+            inner = sum(piece(of_a[count:], m) for m in range(1, slots))
+            exact[a, count:] += -inner
+            inner = sum(piece(through[count:], m) for m in range(1, slots))
+            exact[b, count:] += inner - named(lower_at, b, b, of_b[count:], slots)
+        else:
+            low_pair[p, :, :width] = of_a_narrow[near:]
+            low_pair[p, :, width:] = narrow(through[near:])
+            low_second[p] = narrow(of_b[near:])
+
+    def go_down(p):
+        a, b = 2 * p, 2 * p + 1
+        if p > 0:
+            first = mul(sources(down, lower_at, a, None, slots), low_pair[p])
+            second = mul(sources(down, lower_at, b, a, slots), low_second[p])
+            exact[a] -= first[:, :width]
+            exact[b] += first[:, width:] - second
+        down[a] = narrow(exact[a])
+        down[b] = narrow(exact[b])
+
+    def ready_up(p):
+        a = last - 2 * p
+        b = a - 1
+        of_a = mul(upper[a].reshape(upper_slots * width, width), inverse[a])
+        of_b = mul(upper[b].reshape(upper_slots * width, width), inverse[b])
+        link = narrow(named(upper_at, b, a, of_b, upper_slots))
+        of_a_narrow = narrow(of_a)
+        through = mul(of_a_narrow, link)
+        fixed[a] = -of_a[:width]
+        fixed[b] = through[:width] - of_b[:width]
+        if p == 0:
+            fixed[a] += -sum(piece(of_a, m) for m in range(1, upper_slots))
+            inner = sum(piece(through, m) for m in range(1, upper_slots))
+            fixed[b] += inner - named(upper_at, b, b, of_b, upper_slots)
+        else:
+            upp_pair[p, :, :width] = of_a_narrow[width:]
+            upp_pair[p, :, width:] = narrow(through[width:])
+            upp_second[p] = narrow(of_b[width:])
+        return link
+
+    def go_up(p, link):
+        a = last - 2 * p
+        b = a - 1
+        of_a = exact[a]
+        of_b = exact[b] - mul(down[a], link)
+        free_a = fixed[a]
+        free_b = fixed[b]
+        if p > 0:
+            first = mul(sources(response, upper_at, a, None, upper_slots), upp_pair[p])
+            second = mul(sources(response, upper_at, b, a, upper_slots), upp_second[p])
+            of_a = of_a - first[:near, :width]
+            of_b = of_b + first[:near, width:] - second[:near]
+            free_a = free_a - first[near:, :width]
+            free_b = free_b + first[near:, width:] - second[near:]
+        for k, value, free in ((a, of_a, free_a), (b, of_b, free_b)):
+            base[k] = value[:count]
+            response[k, :near] = narrow(value)
+            response[k, near:] = narrow(free)
+
+    pairs = rows // 2
+    for copy in copies[:4]:
+        copy.wait()
+    links = []
+    for p in range(pairs):
+        if 2 * p + 2 > half and len(links) == 0:
             for copy in copies[4:]:
                 copy.wait()
-            for j in range(rows):
-                blocks = upper[j].reshape(upper_slots * width, width)
-                upp[j] = narrow(mul(blocks, inverse[j]))
-        own = inverse[k]
-        scaled = mul(narrow(rhs[k]), own)
-        low[k] = narrow(mul(lower[k].reshape(slots * width, width), own))
-        if k == 0:
-            total = low[k, :width].astype(jnp.float32)
-            for m in range(1, slots):
-                total = total + low[k, m * width : (m + 1) * width].astype(jnp.float32)
-            exact[k, :count] = scaled
-            exact[k, count:] = -total
-        else:
-            source = jnp.concatenate([down[lower_at[m, k]] for m in range(1, slots)], axis=1)
-            summed = mul(source, low[k, width:])
-            exact[k, :count] = scaled - summed[:count]
-            exact[k, count:] = -low[k, :width].astype(jnp.float32) - summed[count:]
-        down[k] = narrow(exact[k])
-
-    for k in range(last, -1, -1):
-        if k == last:
-            total = upp[k, :width].astype(jnp.float32)
-            for m in range(1, upper_slots):
-                total = total + upp[k, m * width : (m + 1) * width].astype(jnp.float32)
-            base[k] = exact[k, :count]
-            response[k, :near] = narrow(exact[k])
-            response[k, near:] = narrow(-total)
-        else:
-            source = jnp.concatenate(
-                [response[upper_at[m, k]] for m in range(1, upper_slots)], axis=1
-            )
-            summed = mul(source, upp[k, width:])
-            solved = exact[k] - summed[:near]
-            base[k] = solved[:count]
-            response[k, :near] = narrow(solved)
-            response[k, near:] = narrow(-upp[k, :width].astype(jnp.float32) - summed[near:])
+            links.append(ready_up(0))
+        ready_down(p)
+        go_down(p)
+        if 0 < len(links) < pairs:
+            links.append(ready_up(len(links)))
+    while len(links) < pairs:
+        links.append(ready_up(len(links)))
+    for p in range(pairs):
+        go_up(p, links[p])
 
     far = near + width
     payload[:near] = down[last]
@@ -327,7 +394,7 @@
         sweep_kernel,
         out_shape=(
             wide,
-            jax.ShapeDtypeStruct((rows, far, width), jnp.bfloat16),
+            jax.ShapeDtypeStruct((rows + 1, far, width), jnp.bfloat16),
             jax.ShapeDtypeStruct((near + far + width, width), jnp.bfloat16),
         )
         + tuple(jax.ShapeDtypeStruct(a.shape, a.dtype) for a in indices),
@@ -340,10 +407,13 @@
             pltpu.VMEM(upper_blocks.shape, upper_blocks.dtype),
             pltpu.SMEM(lower_at.shape, jnp.int32),
             pltpu.SMEM(upper_at.shape, jnp.int32),
-            pltpu.VMEM((rows, slots * width, width), jnp.bfloat16),
-            pltpu.VMEM((rows, upper_slots * width, width), jnp.bfloat16),
-            pltpu.VMEM((rows, near, width), jnp.bfloat16),
+            pltpu.VMEM((rows // 2, (slots - 1) * width, 2 * width), jnp.bfloat16),
+            pltpu.VMEM((rows // 2, (slots - 1) * width, width), jnp.bfloat16),
+            pltpu.VMEM((rows // 2, (upper_slots - 1) * width, 2 * width), jnp.bfloat16),
+            pltpu.VMEM((rows // 2, (upper_slots - 1) * width, width), jnp.bfloat16),
+            pltpu.VMEM((rows + 1, near, width), jnp.bfloat16),
             pltpu.VMEM((rows, near, width), jnp.float32),
+            pltpu.VMEM((rows, width, width), jnp.float32),
             pltpu.SemaphoreType.DMA((10,)),
         ],
         compiler_params=SMALL,

time: 21.7 us -> 21.4 us (0.986)
  Pallas kernels: 8.64 us -> 8.33 us
    pallas_call x1, Pallas kernels: 4.78 us -> 4.47 us  [on_device(): pl.pallas_call(sweep_kernel, out_shape=(wide, jax.ShapeDtypeStruct((rows...]
where the time goes in v3:
time: 21.4 us; the launch traced here: 21.2 us
  starting transfers between devices  8.98 us (42%)
  Pallas kernels  8.33 us (39%)
  waiting for transfers between devices  3.21 us (15%)
  between operations  0.7 us (3%)
    ppermute x2, starting transfers between devices, swaps(): return lax.ppermute(block, axis, pairs)  5.52 us
    pallas_call x1, Pallas kernels, on_device(): pl.pallas_call(sweep_kernel, out_shape=(wide, jax.ShapeDtypeStruct((rows...  4.47 us
    ppermute x2, starting transfers between devices, trade(): return lax.ppermute(block, axis, [(i, i ^ bit) for i in range(count)])  3.46 us
    ppermute x2, waiting for transfers between devices, trade(): return lax.ppermute(block, axis, [(i, i ^ bit) for i in range(count)])  2.99 us
    pallas_call x1, Pallas kernels, on_device(): pl.pallas_call(local, out_shape=(wide, wide), in_specs=[VMEM] * 6 + [SMEM...  1.64 us
    pallas_call x1, Pallas kernels, on_device(): pl.pallas_call(halo, out_shape=wide, in_specs=[VMEM] * 4 + [SMEM], out_sp...  1.41 us
    pallas_call x1, Pallas kernels, on_device(): pl.pallas_call(chain, out_shape=(wide, jax.ShapeDtypeStruct((rows + 2, co...  0.47 us
  transfers between devices with their start and end apart: 4, of which 3 were waited for; matrix products, arithmetic and copies ran while one was open for 0% of the time, Pallas kernels for 8%

profile of v3, /device:TPU:0, one launch (start us, length us, event | category | flops | bytes accessed | tf_op | source)
XLA Modules:
  0.0 21.2 jit_solution(1125915315721547453)
XLA Ops:
  0.6 0.0 copy-start.1
  0.6 4.5 %sweeps.1 = (f32[8,32,128]{2,1,0:T(8,128)S(1)}, bf16[9,288,128]{2,1,0:T(8,128)(2,1)S(1)}, bf16[576,128]{1,0:T(8,128)(2,1)S(1)}, s32[3,8]{1,0:T(4,128)S(1)}, s32[3,8]{1,0:T(4,128)S(1)}, /*index=5*/s32[2,8]{1,0:T(2,128)S(1)}) custom-call(f32[8,32,128]{2,1,0:T(8,128)} %rhs_far.1, bf16[8,128,128]{2,1,0:T(8,128)(2,1)} %inverse_far.1, ...), custom_call_target="tpu_custom_call" | custom-call | tf_op jit(solution)/shard_map/sweeps/pallas_call | solution.py:393
  5.1 0.0 copy-start
  5.1 0.5 %collective-permute-start = (bf16[576,128]{1,0:T(8,128)(2,1)S(1)}, bf16[576,128]{1,0:T(8,128)(2,1)S(1)}, u32[]{:S(2)}, u32[]{:S(2)}) collective-permute-start(bf16[576,128]{1,0:T(8,128)(2,1)S(1)} %get-tuple-element.19.refs_0_), channel_id=1, source_target_pairs={{0,8},{8,0},{16,24},{24,16},{1,9},{9,1},{17,25},{25,17},{2,10},{10... | collective-permute-start | bytes 442376 | tf_op jit(solution)/shard_map/ppermute | solution.py:361
  5.6 1.0 %collective-permute-done.refs_1_ = bf16[576,128]{1,0:T(8,128)(2,1)S(1)} collective-permute-done((bf16[576,128]{1,0:T(8,128)(2,1)S(1)}, bf16[576,128]{1,0:T(8,128)(2,1)S(1)}, u32[]{:S(2)}, u32[]{:S(2)}) %collective-permute-start) | collective-permute-done | bytes 147488 | tf_op jit(solution)/shard_map/ppermute | solution.py:361
  6.7 0.3 %compose.1 = (bf16[160,128]{1,0:T(8,128)(2,1)S(1)}, bf16[448,128]{1,0:T(8,128)(2,1)S(1)}, bf16[128,128]{1,0:T(8,128)(2,1)S(1)}, bf16[32,128]{1,0:T(8,128)(2,1)S(1)}) custom-call(bf16[576,128]{1,0:T(8,128)(2,1)S(1)} %get-tuple-element.19.refs_0_, bf16[576,128]{1,0:T(8,128)(2,1)S(1)} %collective-permute-done.refs_1_), custom_call_target="tpu_custom_call" | custom-call | tf_op jit(solution)/shard_map/compose/pallas_call | solution.py:440
  7.0 2.9 %collective-permute-start.1 = (bf16[160,128]{1,0:T(8,128)(2,1)S(1)}, bf16[160,128]{1,0:T(8,128)(2,1)S(1)}, u32[]{:S(2)}, u32[]{:S(2)}) collective-permute-start(bf16[160,128]{1,0:T(8,128)(2,1)S(1)} %get-tuple-element.21), channel_id=1, source_target_pairs={{0,16},{8,24},{16,0},{24,8},{1,17},{9,25},{17,1},{25,9},{2,18},{10... | collective-permute-start | bytes 122888 | tf_op jit(solution)/shard_map/ppermute | solution.py:361
  9.9 2.0 %collective-permute-done.1.refs_1_ = bf16[160,128]{1,0:T(8,128)(2,1)S(1)} collective-permute-done((bf16[160,128]{1,0:T(8,128)(2,1)S(1)}, bf16[160,128]{1,0:T(8,128)(2,1)S(1)}, u32[]{:S(2)}, u32[]{:S(2)}) %collective-permute-start.1) | collective-permute-done | bytes 40992 | tf_op jit(solution)/shard_map/ppermute | solution.py:361
  11.9 0.0 copy-start.3
  11.9 0.5 %chain.1 = (f32[8,32,128]{2,1,0:T(8,128)S(1)}, bf16[10,32,128]{2,1,0:T(8,128)(2,1)S(1)}, bf16[128,128]{1,0:T(8,128)(2,1)S(1)}, bf16[4,32,128]{2,1,0:T(8,128)(2,1)S(1)}, bf16[4,32,128]{2,1,0:T(8,128)(2,1)S(1)}) custom-call(bf16[32,128]{1,0:T(8,128)(2,1)S(1)} %get-tuple-element.20.refs_0_, bf16[160,128]{1,0:T(8,128)(2,1)S(1)} %collective-permute-done.1.refs_1_, ...), custom_call_target="tpu_custom_call" | custom-call | tf_op jit(solution)/shard_map/chain/pallas_call | solution.py:461
  12.4 0.7 %collective-permute-start.2 = (bf16[4,32,128]{2,1,0:T(8,128)(2,1)S(1)}, bf16[4,32,128]{2,1,0:T(8,128)(2,1)S(1)}, u32[]{:S(2)}, u32[]{:S(2)}) collective-permute-start(bf16[4,32,128]{2,1,0:T(8,128)(2,1)S(1)} %get-tuple-element.33), channel_id=1, source_target_pairs={{1,2},{2,1},{3,4},{4,3},{5,6},{6,5},{9,10},{10,9},{11,12},{12,11},... | collective-permute-start | bytes 98312 | tf_op jit(solution)/shard_map/ppermute | solution.py:369
  13.1 4.9 %collective-permute-start.3 = (bf16[4,32,128]{2,1,0:T(8,128)(2,1)S(1)}, bf16[4,32,128]{2,1,0:T(8,128)(2,1)S(1)}, u32[]{:S(2)}, u32[]{:S(2)}) collective-permute-start(bf16[4,32,128]{2,1,0:T(8,128)(2,1)S(1)} %get-tuple-element.34), channel_id=1, source_target_pairs={{0,1},{1,0},{2,3},{3,2},{4,5},{5,4},{6,7},{7,6},{8,9},{9,8},{10,11... | collective-permute-start | bytes 98312 | tf_op jit(solution)/shard_map/ppermute | solution.py:369
  17.9 0.0 copy-done.1
  17.9 0.0 copy-done
  17.9 0.0 copy-done.3
  17.9 0.0 copy-start.2
  17.9 1.6 %local_product.1 = (f32[8,32,128]{2,1,0:T(8,128)S(1)}, f32[8,32,128]{2,1,0:T(8,128)}) custom-call(bf16[10,32,128]{2,1,0:T(8,128)(2,1)S(1)} %get-tuple-element.26.refs_0_, bf16[128,128]{1,0:T(8,128)(2,1)S(1)} %get-tuple-element.27.refs_1_, f32[8,32,128]{2,1,0:T(8,128)S(1)} %get-tuple-element.28.refs_2_, bf16[8,128,128]{2,1,0:T(8,128)(2,1)S(1)} %copy-done.3, ...), custom_call_target="tpu_custom_call" | custom-call | tf_op jit(solution)/shard_map/local_product/pallas_call | solution.py:482
  19.6 0.0 collective-permute-done.2.refs_1_
  19.6 0.2 %collective-permute-done.3.refs_2_ = bf16[4,32,128]{2,1,0:T(8,128)(2,1)S(1)} collective-permute-done((bf16[4,32,128]{2,1,0:T(8,128)(2,1)S(1)}, bf16[4,32,128]{2,1,0:T(8,128)(2,1)S(1)}, u32[]{:S(2)}, u32[]{:S(2)}) %collective-permute-start.3) | collective-permute-done | bytes 32800 | tf_op jit(solution)/shard_map/ppermute | solution.py:369
  19.8 0.0 copy-done.2
  19.8 1.4 %halo_product.1 = f32[8,32,128]{2,1,0:T(8,128)} custom-call(f32[8,32,128]{2,1,0:T(8,128)S(1)} %get-tuple-element.32.refs_0_, bf16[4,32,128]{2,1,0:T(8,128)(2,1)S(1)} %collective-permute-done.2.refs_1_, bf16[4,32,128]{2,1,0:T(8,128)(2,1)S(1)} %collective-permute-done.3.refs_2_, bf16[8,2,128,128]{3,2,1,0:T(8,128)(2,1)S(1)} %copy-done.2, ...), custom_call_target="tpu_custom_call" | custom-call | tf_op jit(solution)/shard_map/halo_product/pallas_call | solution.py:498
Async XLA Ops:
  0.6 17.3 %copy-start.1 = (bf16[8,3,128,128]{3,2,1,0:T(8,128)(2,1)S(1)}, bf16[8,3,128,128]{3,2,1,0:T(8,128)(2,1)}, u32[]{:S(2)}) copy-start(bf16[8,3,128,128]{3,2,1,0:T(8,128)(2,1)} %refs_5_.1) | copy-start | bytes 2359300
  5.1 12.8 %copy-start = (bf16[8,3,128,128]{3,2,1,0:T(8,128)(2,1)S(1)}, bf16[8,3,128,128]{3,2,1,0:T(8,128)(2,1)}, u32[]{:S(2)}) copy-start(bf16[8,3,128,128]{3,2,1,0:T(8,128)(2,1)} %refs_4_.1) | copy-start | bytes 2359300
  5.1 1.5 %collective-permute-start = (bf16[576,128]{1,0:T(8,128)(2,1)S(1)}, bf16[576,128]{1,0:T(8,128)(2,1)S(1)}, u32[]{:S(2)}, u32[]{:S(2)}) collective-permute-start(bf16[576,128]{1,0:T(8,128)(2,1)S(1)} %get-tuple-element.19.refs_0_), channel_id=1, source_target_pairs={{0,8},{8,0},{16,24},{24,16},{1,9},{9,1},{17,25},{25,17},{2,10},{10... | collective-permute-start | bytes 442376 | tf_op jit(solution)/shard_map/ppermute | solution.py:361
  7.0 4.9 %collective-permute-start.1 = (bf16[160,128]{1,0:T(8,128)(2,1)S(1)}, bf16[160,128]{1,0:T(8,128)(2,1)S(1)}, u32[]{:S(2)}, u32[]{:S(2)}) collective-permute-start(bf16[160,128]{1,0:T(8,128)(2,1)S(1)} %get-tuple-element.21), channel_id=1, source_target_pairs={{0,16},{8,24},{16,0},{24,8},{1,17},{9,25},{17,1},{25,9},{2,18},{10... | collective-permute-start | bytes 122888 | tf_op jit(solution)/shard_map/ppermute | solution.py:361
  11.9 6.0 %copy-start.3 = (bf16[8,128,128]{2,1,0:T(8,128)(2,1)S(1)}, bf16[8,128,128]{2,1,0:T(8,128)(2,1)}, u32[]{:S(2)}) copy-start(bf16[8,128,128]{2,1,0:T(8,128)(2,1)} %refs_3_.2) | copy-start | bytes 786436
  12.4 7.2 %collective-permute-start.2 = (bf16[4,32,128]{2,1,0:T(8,128)(2,1)S(1)}, bf16[4,32,128]{2,1,0:T(8,128)(2,1)S(1)}, u32[]{:S(2)}, u32[]{:S(2)}) collective-permute-start(bf16[4,32,128]{2,1,0:T(8,128)(2,1)S(1)} %get-tuple-element.33), channel_id=1, source_target_pairs={{1,2},{2,1},{3,4},{4,3},{5,6},{6,5},{9,10},{10,9},{11,12},{12,11},... | collective-permute-start | bytes 98312 | tf_op jit(solution)/shard_map/ppermute | solution.py:369
  13.1 6.8 %collective-permute-start.3 = (bf16[4,32,128]{2,1,0:T(8,128)(2,1)S(1)}, bf16[4,32,128]{2,1,0:T(8,128)(2,1)S(1)}, u32[]{:S(2)}, u32[]{:S(2)}) collective-permute-start(bf16[4,32,128]{2,1,0:T(8,128)(2,1)S(1)} %get-tuple-element.34), channel_id=1, source_target_pairs={{0,1},{1,0},{2,3},{3,2},{4,5},{5,4},{6,7},{7,6},{8,9},{9,8},{10,11... | collective-permute-start | bytes 98312 | tf_op jit(solution)/shard_map/ppermute | solution.py:369
  17.9 1.9 %copy-start.2 = (bf16[8,2,128,128]{3,2,1,0:T(8,128)(2,1)S(1)}, bf16[8,2,128,128]{3,2,1,0:T(8,128)(2,1)}, u32[]{:S(2)}) copy-start(bf16[8,2,128,128]{3,2,1,0:T(8,128)(2,1)} %refs_3_.3) | copy-start | bytes 1572868

commit v4 on v3

--- a/solution.py
+++ b/solution.py
@@ -100,29 +100,48 @@
             picked.append(held[row if skipped is None else jnp.where(row == skipped, rows, row)])
         return jnp.concatenate(picked, axis=1)
 
+    def apart(left, right, own, other):
+        zero = jnp.zeros_like(own)
+        sides = [jnp.concatenate([own, zero], axis=1), jnp.concatenate([zero, other], axis=1)]
+        return mul(jnp.concatenate([left, right], axis=1), jnp.concatenate(sides, axis=0))
+
+    def ready(at, blocks, many, first, step, heads):
+        of_a, of_b, links = [], [], []
+        for a in (first, first + 2 * step):
+            b = a + step
+            lefts = [
+                jnp.concatenate(heads(k) + [blocks[k].reshape(many * width, width)], axis=0)
+                for k in (a, b)
+            ]
+            both = apart(*lefts, inverse[a], inverse[b])
+            of_a.append(both[:, :width])
+            of_b.append(both[:, width:])
+            tail = both[both.shape[0] - many * width :, width:]
+            links.append(narrow(named(at, b, a, tail, many)))
+        narrow_a = [narrow(value) for value in of_a]
+        both = apart(*narrow_a, *links)
+        through = [both[:, :width], both[:, width:]]
+        return of_a, narrow_a, of_b, through, links
+
     def ready_down(p):
-        a, b = 2 * p, 2 * p + 1
-        both = []
-        for k in (a, b):
-            blocks = lower[k].reshape(slots * width, width)
-            both.append(mul(jnp.concatenate([narrow(rhs[k]), blocks], axis=0), inverse[k]))
-        of_a, of_b = both
-        link = narrow(named(lower_at, b, a, of_b[count:], slots))
-        of_a_narrow = narrow(of_a)
-        through = mul(of_a_narrow, link)
-        exact[a, :count] = of_a[:count]
-        exact[a, count:] = -of_a[count:near]
-        exact[b, :count] = of_b[:count] - through[:count]
-        exact[b, count:] = through[count:near] - of_b[count:near]
-        if p == 0:
-            inner = sum(piece(of_a[count:], m) for m in range(1, slots))
-            exact[a, count:] += -inner
-            inner = sum(piece(through[count:], m) for m in range(1, slots))
-            exact[b, count:] += inner - named(lower_at, b, b, of_b[count:], slots)
-        else:
-            low_pair[p, :, :width] = of_a_narrow[near:]
-            low_pair[p, :, width:] = narrow(through[near:])
-            low_second[p] = narrow(of_b[near:])
+        of_a, narrow_a, of_b, through, _ = ready(
+            lower_at, lower, slots, 2 * p, 1, lambda k: [narrow(rhs[k])]
+        )
+        for i in range(2):
+            a, b = 2 * (p + i), 2 * (p + i) + 1
+            exact[a, :count] = of_a[i][:count]
+            exact[a, count:] = -of_a[i][count:near]
+            exact[b, :count] = of_b[i][:count] - through[i][:count]
+            exact[b, count:] = through[i][count:near] - of_b[i][count:near]
+            if p + i == 0:
+                inner = sum(piece(of_a[i][count:], m) for m in range(1, slots))
+                exact[a, count:] += -inner
+                inner = sum(piece(through[i][count:], m) for m in range(1, slots))
+                exact[b, count:] += inner - named(lower_at, b, b, of_b[i][count:], slots)
+            else:
+                low_pair[p + i, :, :width] = narrow_a[i][near:]
+                low_pair[p + i, :, width:] = narrow(through[i][near:])
+                low_second[p + i] = narrow(of_b[i][near:])
 
     def go_down(p):
         a, b = 2 * p, 2 * p + 1
@@ -135,24 +154,23 @@
         down[b] = narrow(exact[b])
 
     def ready_up(p):
-        a = last - 2 * p
-        b = a - 1
-        of_a = mul(upper[a].reshape(upper_slots * width, width), inverse[a])
-        of_b = mul(upper[b].reshape(upper_slots * width, width), inverse[b])
-        link = narrow(named(upper_at, b, a, of_b, upper_slots))
-        of_a_narrow = narrow(of_a)
-        through = mul(of_a_narrow, link)
-        fixed[a] = -of_a[:width]
-        fixed[b] = through[:width] - of_b[:width]
-        if p == 0:
-            fixed[a] += -sum(piece(of_a, m) for m in range(1, upper_slots))
-            inner = sum(piece(through, m) for m in range(1, upper_slots))
-            fixed[b] += inner - named(upper_at, b, b, of_b, upper_slots)
-        else:
-            upp_pair[p, :, :width] = of_a_narrow[width:]
-            upp_pair[p, :, width:] = narrow(through[width:])
-            upp_second[p] = narrow(of_b[width:])
-        return link
+        of_a, narrow_a, of_b, through, links = ready(
+            upper_at, upper, upper_slots, last - 2 * p, -1, lambda k: []
+        )
+        for i in range(2):
+            a = last - 2 * (p + i)
+            b = a - 1
+            fixed[a] = -of_a[i][:width]
+            fixed[b] = through[i][:width] - of_b[i][:width]
+            if p + i == 0:
+                fixed[a] += -sum(piece(of_a[i], m) for m in range(1, upper_slots))
+                inner = sum(piece(through[i], m) for m in range(1, upper_slots))
+                fixed[b] += inner - named(upper_at, b, b, of_b[i], upper_slots)
+            else:
+                upp_pair[p + i, :, :width] = narrow_a[i][width:]
+                upp_pair[p + i, :, width:] = narrow(through[i][width:])
+                upp_second[p + i] = narrow(of_b[i][width:])
+        return links
 
     def go_up(p, link):
         a = last - 2 * p
@@ -176,18 +194,17 @@
     pairs = rows // 2
     for copy in copies[:4]:
         copy.wait()
+    ready_down(0)
+    go_down(0)
+    for copy in copies[4:]:
+        copy.wait()
     links = []
-    for p in range(pairs):
-        if 2 * p + 2 > half and len(links) == 0:
-            for copy in copies[4:]:
-                copy.wait()
-            links.append(ready_up(0))
-        ready_down(p)
+    for p in range(1, pairs):
+        if p % 2 == 1 and p + 1 < pairs:
+            ready_down(p + 1)
         go_down(p)
-        if 0 < len(links) < pairs:
-            links.append(ready_up(len(links)))
-    while len(links) < pairs:
-        links.append(ready_up(len(links)))
+        if p % 2 == 1:
+            links += ready_up(p - 1)
     for p in range(pairs):
         go_up(p, links[p])
 

time: 21.4 us -> 20.7 us (0.967)
  Pallas kernels: 8.33 us -> 7.6 us
    pallas_call x1, Pallas kernels: 4.47 us -> 3.75 us  [on_device(): pl.pallas_call(sweep_kernel, out_shape=(wide, jax.ShapeDtypeStruct((rows...]
where the time goes in v4:
time: 20.7 us; the launch traced here: 20.5 us
  starting transfers between devices  8.97 us (43%)
  Pallas kernels  7.6 us (37%)
  waiting for transfers between devices  3.21 us (16%)
  between operations  0.7 us (3%)
    ppermute x2, starting transfers between devices, swaps(): return lax.ppermute(block, axis, pairs)  5.51 us
    pallas_call x1, Pallas kernels, on_device(): pl.pallas_call(sweep_kernel, out_shape=(wide, jax.ShapeDtypeStruct((rows...  3.75 us
    ppermute x2, starting transfers between devices, trade(): return lax.ppermute(block, axis, [(i, i ^ bit) for i in range(count)])  3.46 us
    ppermute x2, waiting for transfers between devices, trade(): return lax.ppermute(block, axis, [(i, i ^ bit) for i in range(count)])  2.99 us
    pallas_call x1, Pallas kernels, on_device(): pl.pallas_call(local, out_shape=(wide, wide), in_specs=[VMEM] * 6 + [SMEM...  1.64 us
    pallas_call x1, Pallas kernels, on_device(): pl.pallas_call(halo, out_shape=wide, in_specs=[VMEM] * 4 + [SMEM], out_sp...  1.41 us
    pallas_call x1, Pallas kernels, on_device(): pl.pallas_call(chain, out_shape=(wide, jax.ShapeDtypeStruct((rows + 2, co...  0.47 us
  transfers between devices with their start and end apart: 4, of which 3 were waited for; matrix products, arithmetic and copies ran while one was open for 0% of the time, Pallas kernels for 8%

profile of v4, /device:TPU:0, one launch (start us, length us, event | category | flops | bytes accessed | tf_op | source)
XLA Modules:
  0.0 20.5 jit_solution(48270738983598603)
XLA Ops:
  0.6 0.0 copy-start.1
  0.6 3.7 %sweeps.1 = (f32[8,32,128]{2,1,0:T(8,128)S(1)}, bf16[9,288,128]{2,1,0:T(8,128)(2,1)S(1)}, bf16[576,128]{1,0:T(8,128)(2,1)S(1)}, s32[3,8]{1,0:T(4,128)S(1)}, s32[3,8]{1,0:T(4,128)S(1)}, /*index=5*/s32[2,8]{1,0:T(2,128)S(1)}) custom-call(f32[8,32,128]{2,1,0:T(8,128)} %rhs_far.1, bf16[8,128,128]{2,1,0:T(8,128)(2,1)} %inverse_far.1, ...), custom_call_target="tpu_custom_call" | custom-call | tf_op jit(solution)/shard_map/sweeps/pallas_call | solution.py:410
  4.4 0.0 copy-start
  4.4 0.5 %collective-permute-start = (bf16[576,128]{1,0:T(8,128)(2,1)S(1)}, bf16[576,128]{1,0:T(8,128)(2,1)S(1)}, u32[]{:S(2)}, u32[]{:S(2)}) collective-permute-start(bf16[576,128]{1,0:T(8,128)(2,1)S(1)} %get-tuple-element.19.refs_0_), channel_id=1, source_target_pairs={{0,8},{8,0},{16,24},{24,16},{1,9},{9,1},{17,25},{25,17},{2,10},{10... | collective-permute-start | bytes 442376 | tf_op jit(solution)/shard_map/ppermute | solution.py:378
  4.9 1.0 %collective-permute-done.refs_1_ = bf16[576,128]{1,0:T(8,128)(2,1)S(1)} collective-permute-done((bf16[576,128]{1,0:T(8,128)(2,1)S(1)}, bf16[576,128]{1,0:T(8,128)(2,1)S(1)}, u32[]{:S(2)}, u32[]{:S(2)}) %collective-permute-start) | collective-permute-done | bytes 147488 | tf_op jit(solution)/shard_map/ppermute | solution.py:378
  5.9 0.3 %compose.1 = (bf16[160,128]{1,0:T(8,128)(2,1)S(1)}, bf16[448,128]{1,0:T(8,128)(2,1)S(1)}, bf16[128,128]{1,0:T(8,128)(2,1)S(1)}, bf16[32,128]{1,0:T(8,128)(2,1)S(1)}) custom-call(bf16[576,128]{1,0:T(8,128)(2,1)S(1)} %get-tuple-element.19.refs_0_, bf16[576,128]{1,0:T(8,128)(2,1)S(1)} %collective-permute-done.refs_1_), custom_call_target="tpu_custom_call" | custom-call | tf_op jit(solution)/shard_map/compose/pallas_call | solution.py:457
  6.3 2.9 %collective-permute-start.1 = (bf16[160,128]{1,0:T(8,128)(2,1)S(1)}, bf16[160,128]{1,0:T(8,128)(2,1)S(1)}, u32[]{:S(2)}, u32[]{:S(2)}) collective-permute-start(bf16[160,128]{1,0:T(8,128)(2,1)S(1)} %get-tuple-element.21), channel_id=1, source_target_pairs={{0,16},{8,24},{16,0},{24,8},{1,17},{9,25},{17,1},{25,9},{2,18},{10... | collective-permute-start | bytes 122888 | tf_op jit(solution)/shard_map/ppermute | solution.py:378
  9.2 2.0 %collective-permute-done.1.refs_1_ = bf16[160,128]{1,0:T(8,128)(2,1)S(1)} collective-permute-done((bf16[160,128]{1,0:T(8,128)(2,1)S(1)}, bf16[160,128]{1,0:T(8,128)(2,1)S(1)}, u32[]{:S(2)}, u32[]{:S(2)}) %collective-permute-start.1) | collective-permute-done | bytes 40992 | tf_op jit(solution)/shard_map/ppermute | solution.py:378
  11.2 0.0 copy-start.3
  11.2 0.5 %chain.1 = (f32[8,32,128]{2,1,0:T(8,128)S(1)}, bf16[10,32,128]{2,1,0:T(8,128)(2,1)S(1)}, bf16[128,128]{1,0:T(8,128)(2,1)S(1)}, bf16[4,32,128]{2,1,0:T(8,128)(2,1)S(1)}, bf16[4,32,128]{2,1,0:T(8,128)(2,1)S(1)}) custom-call(bf16[32,128]{1,0:T(8,128)(2,1)S(1)} %get-tuple-element.20.refs_0_, bf16[160,128]{1,0:T(8,128)(2,1)S(1)} %collective-permute-done.1.refs_1_, ...), custom_call_target="tpu_custom_call" | custom-call | tf_op jit(solution)/shard_map/chain/pallas_call | solution.py:478
  11.7 0.7 %collective-permute-start.2 = (bf16[4,32,128]{2,1,0:T(8,128)(2,1)S(1)}, bf16[4,32,128]{2,1,0:T(8,128)(2,1)S(1)}, u32[]{:S(2)}, u32[]{:S(2)}) collective-permute-start(bf16[4,32,128]{2,1,0:T(8,128)(2,1)S(1)} %get-tuple-element.33), channel_id=1, source_target_pairs={{1,2},{2,1},{3,4},{4,3},{5,6},{6,5},{9,10},{10,9},{11,12},{12,11},... | collective-permute-start | bytes 98312 | tf_op jit(solution)/shard_map/ppermute | solution.py:386
  12.3 4.8 %collective-permute-start.3 = (bf16[4,32,128]{2,1,0:T(8,128)(2,1)S(1)}, bf16[4,32,128]{2,1,0:T(8,128)(2,1)S(1)}, u32[]{:S(2)}, u32[]{:S(2)}) collective-permute-start(bf16[4,32,128]{2,1,0:T(8,128)(2,1)S(1)} %get-tuple-element.34), channel_id=1, source_target_pairs={{0,1},{1,0},{2,3},{3,2},{4,5},{5,4},{6,7},{7,6},{8,9},{9,8},{10,11... | collective-permute-start | bytes 98312 | tf_op jit(solution)/shard_map/ppermute | solution.py:386
  17.2 0.0 copy-done.1
  17.2 0.0 copy-done
  17.2 0.0 copy-done.3
  17.2 0.0 copy-start.2
  17.2 1.6 %local_product.1 = (f32[8,32,128]{2,1,0:T(8,128)S(1)}, f32[8,32,128]{2,1,0:T(8,128)}) custom-call(bf16[10,32,128]{2,1,0:T(8,128)(2,1)S(1)} %get-tuple-element.26.refs_0_, bf16[128,128]{1,0:T(8,128)(2,1)S(1)} %get-tuple-element.27.refs_1_, f32[8,32,128]{2,1,0:T(8,128)S(1)} %get-tuple-element.28.refs_2_, bf16[8,128,128]{2,1,0:T(8,128)(2,1)S(1)} %copy-done.3, ...), custom_call_target="tpu_custom_call" | custom-call | tf_op jit(solution)/shard_map/local_product/pallas_call | solution.py:499
  18.9 0.0 collective-permute-done.2.refs_1_
  18.9 0.2 %collective-permute-done.3.refs_2_ = bf16[4,32,128]{2,1,0:T(8,128)(2,1)S(1)} collective-permute-done((bf16[4,32,128]{2,1,0:T(8,128)(2,1)S(1)}, bf16[4,32,128]{2,1,0:T(8,128)(2,1)S(1)}, u32[]{:S(2)}, u32[]{:S(2)}) %collective-permute-start.3) | collective-permute-done | bytes 32800 | tf_op jit(solution)/shard_map/ppermute | solution.py:386
  19.1 0.0 copy-done.2
  19.1 1.4 %halo_product.1 = f32[8,32,128]{2,1,0:T(8,128)} custom-call(f32[8,32,128]{2,1,0:T(8,128)S(1)} %get-tuple-element.32.refs_0_, bf16[4,32,128]{2,1,0:T(8,128)(2,1)S(1)} %collective-permute-done.2.refs_1_, bf16[4,32,128]{2,1,0:T(8,128)(2,1)S(1)} %collective-permute-done.3.refs_2_, bf16[8,2,128,128]{3,2,1,0:T(8,128)(2,1)S(1)} %copy-done.2, ...), custom_call_target="tpu_custom_call" | custom-call | tf_op jit(solution)/shard_map/halo_product/pallas_call | solution.py:515
Async XLA Ops:
  0.6 16.6 %copy-start.1 = (bf16[8,3,128,128]{3,2,1,0:T(8,128)(2,1)S(1)}, bf16[8,3,128,128]{3,2,1,0:T(8,128)(2,1)}, u32[]{:S(2)}) copy-start(bf16[8,3,128,128]{3,2,1,0:T(8,128)(2,1)} %refs_5_.1) | copy-start | bytes 2359300
  4.4 12.8 %copy-start = (bf16[8,3,128,128]{3,2,1,0:T(8,128)(2,1)S(1)}, bf16[8,3,128,128]{3,2,1,0:T(8,128)(2,1)}, u32[]{:S(2)}) copy-start(bf16[8,3,128,128]{3,2,1,0:T(8,128)(2,1)} %refs_4_.1) | copy-start | bytes 2359300
  4.4 1.5 %collective-permute-start = (bf16[576,128]{1,0:T(8,128)(2,1)S(1)}, bf16[576,128]{1,0:T(8,128)(2,1)S(1)}, u32[]{:S(2)}, u32[]{:S(2)}) collective-permute-start(bf16[576,128]{1,0:T(8,128)(2,1)S(1)} %get-tuple-element.19.refs_0_), channel_id=1, source_target_pairs={{0,8},{8,0},{16,24},{24,16},{1,9},{9,1},{17,25},{25,17},{2,10},{10... | collective-permute-start | bytes 442376 | tf_op jit(solution)/shard_map/ppermute | solution.py:378
  6.3 4.9 %collective-permute-start.1 = (bf16[160,128]{1,0:T(8,128)(2,1)S(1)}, bf16[160,128]{1,0:T(8,128)(2,1)S(1)}, u32[]{:S(2)}, u32[]{:S(2)}) collective-permute-start(bf16[160,128]{1,0:T(8,128)(2,1)S(1)} %get-tuple-element.21), channel_id=1, source_target_pairs={{0,16},{8,24},{16,0},{24,8},{1,17},{9,25},{17,1},{25,9},{2,18},{10... | collective-permute-start | bytes 122888 | tf_op jit(solution)/shard_map/ppermute | solution.py:378
  11.2 6.0 %copy-start.3 = (bf16[8,128,128]{2,1,0:T(8,128)(2,1)S(1)}, bf16[8,128,128]{2,1,0:T(8,128)(2,1)}, u32[]{:S(2)}) copy-start(bf16[8,128,128]{2,1,0:T(8,128)(2,1)} %refs_3_.2) | copy-start | bytes 786436
  11.7 7.2 %collective-permute-start.2 = (bf16[4,32,128]{2,1,0:T(8,128)(2,1)S(1)}, bf16[4,32,128]{2,1,0:T(8,128)(2,1)S(1)}, u32[]{:S(2)}, u32[]{:S(2)}) collective-permute-start(bf16[4,32,128]{2,1,0:T(8,128)(2,1)S(1)} %get-tuple-element.33), channel_id=1, source_target_pairs={{1,2},{2,1},{3,4},{4,3},{5,6},{6,5},{9,10},{10,9},{11,12},{12,11},... | collective-permute-start | bytes 98312 | tf_op jit(solution)/shard_map/ppermute | solution.py:386
  12.3 6.7 %collective-permute-start.3 = (bf16[4,32,128]{2,1,0:T(8,128)(2,1)S(1)}, bf16[4,32,128]{2,1,0:T(8,128)(2,1)S(1)}, u32[]{:S(2)}, u32[]{:S(2)}) collective-permute-start(bf16[4,32,128]{2,1,0:T(8,128)(2,1)S(1)} %get-tuple-element.34), channel_id=1, source_target_pairs={{0,1},{1,0},{2,3},{3,2},{4,5},{5,4},{6,7},{7,6},{8,9},{9,8},{10,11... | collective-permute-start | bytes 98312 | tf_op jit(solution)/shard_map/ppermute | solution.py:386
  17.2 1.9 %copy-start.2 = (bf16[8,2,128,128]{3,2,1,0:T(8,128)(2,1)S(1)}, bf16[8,2,128,128]{3,2,1,0:T(8,128)(2,1)}, u32[]{:S(2)}) copy-start(bf16[8,2,128,128]{3,2,1,0:T(8,128)(2,1)} %refs_3_.3) | copy-start | bytes 1572868

commit v5 on v4

--- a/solution.py
+++ b/solution.py
@@ -172,11 +172,11 @@
                 upp_second[p + i] = narrow(of_b[i][width:])
         return links
 
-    def go_up(p, link):
+    def go_up(p, passed):
         a = last - 2 * p
         b = a - 1
         of_a = exact[a]
-        of_b = exact[b] - mul(down[a], link)
+        of_b = exact[b] - passed
         free_a = fixed[a]
         free_b = fixed[b]
         if p > 0:
@@ -205,8 +205,11 @@
         go_down(p)
         if p % 2 == 1:
             links += ready_up(p - 1)
-    for p in range(pairs):
-        go_up(p, links[p])
+    for p in range(0, pairs, 2):
+        a = last - 2 * p
+        passed = apart(down[a], down[a - 2], links[p], links[p + 1])
+        go_up(p, passed[:, :width])
+        go_up(p + 1, passed[:, width:])
 
     far = near + width
     payload[:near] = down[last]
@@ -317,7 +320,7 @@
 
 
 def local_kernel(
-    axis,
+    axes,
     rounded,
     prior,
     solved,
@@ -326,8 +329,10 @@
     upper,
     lower_at,
     upper_at,
+    halo_at,
     partial,
     solution,
+    masks,
     held,
     out,
 ):
@@ -337,7 +342,7 @@
     upper_slots = upper.shape[1]
     before = rounded[rows].astype(jnp.float32) + mul(rounded[0], prior[...])
     held[...] = rounded[...]
-    held[rows] = narrow(jnp.where(lax.axis_index(axis) > 0, before, 0.0))
+    held[rows] = narrow(jnp.where(lax.axis_index(axes[0]) > 0, before, 0.0))
     for k in range(rows):
         total = mul(rounded[k], diagonal[k])
         source = [held[rows]]
@@ -355,19 +360,27 @@
             jnp.concatenate(source, axis=1), upper[k].reshape(upper_slots * width, width)
         )
         partial[k] = total
+    _, picked, places, count, _ = masks.shape
+    turn = places // 2 * (1 - lax.rem(lax.axis_index(axes[1]), 2))
+    for k in range(rows):
+        for m in range(picked):
+            at = lax.rem(halo_at[m + 1, k] + turn, places)
+            for j in range(places):
+                mask = jnp.where(at == j, 1.0, 0.0)
+                masks[k, m, j] = narrow(jnp.full((count, width), mask, jnp.float32))
     copy.wait()
 
 
-def halo_kernel(axis, partial, outer, inner, halo, halo_at, product, rim_rows):
+def halo_kernel(axis, partial, outer, inner, halo, masks, product, rim_rows):
     rows, slots, width, _ = halo.shape
     rim = inner.shape[0]
     turn = rim * (1 - lax.rem(lax.axis_index(axis), 2))
     rim_rows[:rim] = inner[...]
     rim_rows[rim:] = outer[...]
     for k in range(rows):
-        source = [
-            rim_rows[lax.rem(halo_at[m, k] + turn, 2 * rim)] for m in range(slots)
-        ]
+        source = [rim_rows[lax.rem(k + turn, 2 * rim)]]
+        for m in range(1, slots):
+            source.append(sum(masks[k, m - 1, j] * rim_rows[j] for j in range(2 * rim)))
         product[k] = partial[k] + mul(
             jnp.concatenate(source, axis=1), halo[k].reshape(slots * width, width)
         )
@@ -494,20 +507,21 @@
     inner = swaps(inner, "dom", 0)
 
     def local(*refs):
-        local_kernel("section", *refs)
-
-    partial, solution = pl.pallas_call(
+        local_kernel(("section", "dom"), *refs)
+
+    masks = (rows, halo_blocks.shape[1] - 1, 2 * RIM, count, width)
+    partial, solution, masks = pl.pallas_call(
         local,
-        out_shape=(wide, wide),
-        in_specs=[VMEM] * 6 + [SMEM] * 2,
-        out_specs=(VMEM, HBM),
+        out_shape=(wide, wide, jax.ShapeDtypeStruct(masks, bits)),
+        in_specs=[VMEM] * 6 + [SMEM] * 3,
+        out_specs=(VMEM, HBM, VMEM),
         scratch_shapes=[
             pltpu.VMEM((rows + 2, count, width), bits),
             pltpu.SemaphoreType.DMA(()),
         ],
         compiler_params=SMALL,
         name="local_product",
-    )(rounded, prior, solved, diag_blocks, lower_blocks, upper_blocks, *indices[:2])
+    )(rounded, prior, solved, diag_blocks, lower_blocks, upper_blocks, *indices)
 
     def halo(*refs):
         halo_kernel("dom", *refs)
@@ -515,12 +529,12 @@
     product = pl.pallas_call(
         halo,
         out_shape=wide,
-        in_specs=[VMEM] * 4 + [SMEM],
+        in_specs=[VMEM] * 5,
         out_specs=VMEM,
-        scratch_shapes=[pltpu.VMEM((2 * RIM, count, width), jnp.bfloat16)],
+        scratch_shapes=[pltpu.VMEM((2 * RIM, count, width), bits)],
         compiler_params=SMALL,
         name="halo_product",
-    )(partial, outer, inner, halo_blocks, indices[2])
+    )(partial, outer, inner, halo_blocks, masks)
     return (solution, product)
 
 

time: 20.7 us -> 20.1 us (0.971)
  Pallas kernels: 7.6 us -> 7.17 us
    pallas_call x2, Pallas kernels: 3.05 us -> 2.63 us  [the longest x1 1.74 us: on_device(): pl.pallas_call(local, out_shape=(wide, wide, jax.ShapeDtypeStruct(masks,...]
  transfers between devices with their start and end apart: 4 -> 4, of which waited for: 3 -> 3; matrix products, arithmetic and copies ran while one was open for 0% -> 0% of each run, Pallas kernels for 8% -> 9%
where the time goes in v5:
time: 20.1 us; the launch traced here: 20 us
  starting transfers between devices  8.97 us (45%)
  Pallas kernels  7.17 us (36%)
  waiting for transfers between devices  3.12 us (16%)
  between operations  0.7 us (3%)
    ppermute x2, starting transfers between devices, swaps(): return lax.ppermute(block, axis, pairs)  5.51 us
    pallas_call x1, Pallas kernels, on_device(): pl.pallas_call(sweep_kernel, out_shape=(wide, jax.ShapeDtypeStruct((rows...  3.73 us
    ppermute x2, starting transfers between devices, trade(): return lax.ppermute(block, axis, [(i, i ^ bit) for i in range(count)])  3.46 us
    ppermute x2, waiting for transfers between devices, trade(): return lax.ppermute(block, axis, [(i, i ^ bit) for i in range(count)])  2.99 us
    pallas_call x1, Pallas kernels, on_device(): pl.pallas_call(local, out_shape=(wide, wide, jax.ShapeDtypeStruct(masks,...  1.74 us
    pallas_call x1, Pallas kernels, on_device(): pl.pallas_call(halo, out_shape=wide, in_specs=[VMEM] * 5, out_specs=VMEM,...  0.89 us
    pallas_call x1, Pallas kernels, on_device(): pl.pallas_call(chain, out_shape=(wide, jax.ShapeDtypeStruct((rows + 2, co...  0.48 us
  transfers between devices with their start and end apart: 4, of which 3 were waited for; matrix products, arithmetic and copies ran while one was open for 0% of the time, Pallas kernels for 9%

profile of v5, /device:TPU:0, one launch (start us, length us, event | category | flops | bytes accessed | tf_op | source)
XLA Modules:
  0.0 20.0 jit_solution(6460584632967521468)
XLA Ops:
  0.6 0.0 copy-start.1
  0.6 3.7 %sweeps.1 = (f32[8,32,128]{2,1,0:T(8,128)S(1)}, bf16[9,288,128]{2,1,0:T(8,128)(2,1)S(1)}, bf16[576,128]{1,0:T(8,128)(2,1)S(1)}, s32[3,8]{1,0:T(4,128)S(1)}, s32[3,8]{1,0:T(4,128)S(1)}, /*index=5*/s32[2,8]{1,0:T(2,128)S(1)}) custom-call(f32[8,32,128]{2,1,0:T(8,128)} %rhs_far.1, bf16[8,128,128]{2,1,0:T(8,128)(2,1)} %inverse_far.1, ...), custom_call_target="tpu_custom_call" | custom-call | tf_op jit(solution)/shard_map/sweeps/pallas_call | solution.py:423
  4.4 0.0 copy-start
  4.4 0.5 %collective-permute-start = (bf16[576,128]{1,0:T(8,128)(2,1)S(1)}, bf16[576,128]{1,0:T(8,128)(2,1)S(1)}, u32[]{:S(2)}, u32[]{:S(2)}) collective-permute-start(bf16[576,128]{1,0:T(8,128)(2,1)S(1)} %get-tuple-element.20.refs_0_), channel_id=1, source_target_pairs={{0,8},{8,0},{16,24},{24,16},{1,9},{9,1},{17,25},{25,17},{2,10},{10... | collective-permute-start | bytes 442376 | tf_op jit(solution)/shard_map/ppermute | solution.py:391
  4.9 1.0 %collective-permute-done.refs_1_ = bf16[576,128]{1,0:T(8,128)(2,1)S(1)} collective-permute-done((bf16[576,128]{1,0:T(8,128)(2,1)S(1)}, bf16[576,128]{1,0:T(8,128)(2,1)S(1)}, u32[]{:S(2)}, u32[]{:S(2)}) %collective-permute-start) | collective-permute-done | bytes 147488 | tf_op jit(solution)/shard_map/ppermute | solution.py:391
  5.9 0.3 %compose.1 = (bf16[160,128]{1,0:T(8,128)(2,1)S(1)}, bf16[448,128]{1,0:T(8,128)(2,1)S(1)}, bf16[128,128]{1,0:T(8,128)(2,1)S(1)}, bf16[32,128]{1,0:T(8,128)(2,1)S(1)}) custom-call(bf16[576,128]{1,0:T(8,128)(2,1)S(1)} %get-tuple-element.20.refs_0_, bf16[576,128]{1,0:T(8,128)(2,1)S(1)} %collective-permute-done.refs_1_), custom_call_target="tpu_custom_call" | custom-call | tf_op jit(solution)/shard_map/compose/pallas_call | solution.py:470
  6.3 2.9 %collective-permute-start.1 = (bf16[160,128]{1,0:T(8,128)(2,1)S(1)}, bf16[160,128]{1,0:T(8,128)(2,1)S(1)}, u32[]{:S(2)}, u32[]{:S(2)}) collective-permute-start(bf16[160,128]{1,0:T(8,128)(2,1)S(1)} %get-tuple-element.22), channel_id=1, source_target_pairs={{0,16},{8,24},{16,0},{24,8},{1,17},{9,25},{17,1},{25,9},{2,18},{10... | collective-permute-start | bytes 122888 | tf_op jit(solution)/shard_map/ppermute | solution.py:391
  9.2 2.0 %collective-permute-done.1.refs_1_ = bf16[160,128]{1,0:T(8,128)(2,1)S(1)} collective-permute-done((bf16[160,128]{1,0:T(8,128)(2,1)S(1)}, bf16[160,128]{1,0:T(8,128)(2,1)S(1)}, u32[]{:S(2)}, u32[]{:S(2)}) %collective-permute-start.1) | collective-permute-done | bytes 40992 | tf_op jit(solution)/shard_map/ppermute | solution.py:391
  11.2 0.0 copy-start.3
  11.2 0.5 %chain.1 = (f32[8,32,128]{2,1,0:T(8,128)S(1)}, bf16[10,32,128]{2,1,0:T(8,128)(2,1)S(1)}, bf16[128,128]{1,0:T(8,128)(2,1)S(1)}, bf16[4,32,128]{2,1,0:T(8,128)(2,1)S(1)}, bf16[4,32,128]{2,1,0:T(8,128)(2,1)S(1)}) custom-call(bf16[32,128]{1,0:T(8,128)(2,1)S(1)} %get-tuple-element.21.refs_0_, bf16[160,128]{1,0:T(8,128)(2,1)S(1)} %collective-permute-done.1.refs_1_, ...), custom_call_target="tpu_custom_call" | custom-call | tf_op jit(solution)/shard_map/chain/pallas_call | solution.py:491
  11.7 0.7 %collective-permute-start.2 = (bf16[4,32,128]{2,1,0:T(8,128)(2,1)S(1)}, bf16[4,32,128]{2,1,0:T(8,128)(2,1)S(1)}, u32[]{:S(2)}, u32[]{:S(2)}) collective-permute-start(bf16[4,32,128]{2,1,0:T(8,128)(2,1)S(1)} %get-tuple-element.35), channel_id=1, source_target_pairs={{1,2},{2,1},{3,4},{4,3},{5,6},{6,5},{9,10},{10,9},{11,12},{12,11},... | collective-permute-start | bytes 98312 | tf_op jit(solution)/shard_map/ppermute | solution.py:399
  12.3 4.8 %collective-permute-start.3 = (bf16[4,32,128]{2,1,0:T(8,128)(2,1)S(1)}, bf16[4,32,128]{2,1,0:T(8,128)(2,1)S(1)}, u32[]{:S(2)}, u32[]{:S(2)}) collective-permute-start(bf16[4,32,128]{2,1,0:T(8,128)(2,1)S(1)} %get-tuple-element.36), channel_id=1, source_target_pairs={{0,1},{1,0},{2,3},{3,2},{4,5},{5,4},{6,7},{7,6},{8,9},{9,8},{10,11... | collective-permute-start | bytes 98312 | tf_op jit(solution)/shard_map/ppermute | solution.py:399
  17.2 0.0 copy-done.1
  17.2 0.0 copy-done
  17.2 0.0 copy-done.3
  17.2 0.0 copy-start.2
  17.2 1.7 %local_product.1 = (f32[8,32,128]{2,1,0:T(8,128)S(1)}, f32[8,32,128]{2,1,0:T(8,128)}, bf16[8,1,8,32,128]{4,3,2,1,0:T(8,128)(2,1)S(1)}) custom-call(bf16[10,32,128]{2,1,0:T(8,128)(2,1)S(1)} %get-tuple-element.27.refs_0_, bf16[128,128]{1,0:T(8,128)(2,1)S(1)} %get-tuple-element.28.refs_1_, f32[8,32,128]{2,1,0:T(8,128)S(1)} %get-tuple-element.29.refs_2_, ...), custom_call_target="tpu_custom_call" | custom-call | tf_op jit(solution)/shard_map/local_product/pallas_call | solution.py:513
  18.9 0.0 collective-permute-done.2.refs_1_
  19.0 0.1 collective-permute-done.3.refs_2_
  19.1 0.0 copy-done.2
  19.1 0.9 %halo_product.1 = f32[8,32,128]{2,1,0:T(8,128)} custom-call(f32[8,32,128]{2,1,0:T(8,128)S(1)} %get-tuple-element.34.refs_0_, bf16[4,32,128]{2,1,0:T(8,128)(2,1)S(1)} %collective-permute-done.2.refs_1_, bf16[4,32,128]{2,1,0:T(8,128)(2,1)S(1)} %collective-permute-done.3.refs_2_, bf16[8,2,128,128]{3,2,1,0:T(8,128)(2,1)S(1)} %copy-done.2, ...), custom_call_target="tpu_custom_call" | custom-call | tf_op jit(solution)/shard_map/halo_product/pallas_call | solution.py:529
Async XLA Ops:
  0.6 16.6 %copy-start.1 = (bf16[8,3,128,128]{3,2,1,0:T(8,128)(2,1)S(1)}, bf16[8,3,128,128]{3,2,1,0:T(8,128)(2,1)}, u32[]{:S(2)}) copy-start(bf16[8,3,128,128]{3,2,1,0:T(8,128)(2,1)} %refs_5_.1) | copy-start | bytes 2359300
  4.4 12.8 %copy-start = (bf16[8,3,128,128]{3,2,1,0:T(8,128)(2,1)S(1)}, bf16[8,3,128,128]{3,2,1,0:T(8,128)(2,1)}, u32[]{:S(2)}) copy-start(bf16[8,3,128,128]{3,2,1,0:T(8,128)(2,1)} %refs_4_.1) | copy-start | bytes 2359300
  4.4 1.5 %collective-permute-start = (bf16[576,128]{1,0:T(8,128)(2,1)S(1)}, bf16[576,128]{1,0:T(8,128)(2,1)S(1)}, u32[]{:S(2)}, u32[]{:S(2)}) collective-permute-start(bf16[576,128]{1,0:T(8,128)(2,1)S(1)} %get-tuple-element.20.refs_0_), channel_id=1, source_target_pairs={{0,8},{8,0},{16,24},{24,16},{1,9},{9,1},{17,25},{25,17},{2,10},{10... | collective-permute-start | bytes 442376 | tf_op jit(solution)/shard_map/ppermute | solution.py:391
  6.3 4.9 %collective-permute-start.1 = (bf16[160,128]{1,0:T(8,128)(2,1)S(1)}, bf16[160,128]{1,0:T(8,128)(2,1)S(1)}, u32[]{:S(2)}, u32[]{:S(2)}) collective-permute-start(bf16[160,128]{1,0:T(8,128)(2,1)S(1)} %get-tuple-element.22), channel_id=1, source_target_pairs={{0,16},{8,24},{16,0},{24,8},{1,17},{9,25},{17,1},{25,9},{2,18},{10... | collective-permute-start | bytes 122888 | tf_op jit(solution)/shard_map/ppermute | solution.py:391
  11.2 6.0 %copy-start.3 = (bf16[8,128,128]{2,1,0:T(8,128)(2,1)S(1)}, bf16[8,128,128]{2,1,0:T(8,128)(2,1)}, u32[]{:S(2)}) copy-start(bf16[8,128,128]{2,1,0:T(8,128)(2,1)} %refs_3_.2) | copy-start | bytes 786436
  11.7 7.3 %collective-permute-start.2 = (bf16[4,32,128]{2,1,0:T(8,128)(2,1)S(1)}, bf16[4,32,128]{2,1,0:T(8,128)(2,1)S(1)}, u32[]{:S(2)}, u32[]{:S(2)}) collective-permute-start(bf16[4,32,128]{2,1,0:T(8,128)(2,1)S(1)} %get-tuple-element.35), channel_id=1, source_target_pairs={{1,2},{2,1},{3,4},{4,3},{5,6},{6,5},{9,10},{10,9},{11,12},{12,11},... | collective-permute-start | bytes 98312 | tf_op jit(solution)/shard_map/ppermute | solution.py:399
  12.3 6.7 %collective-permute-start.3 = (bf16[4,32,128]{2,1,0:T(8,128)(2,1)S(1)}, bf16[4,32,128]{2,1,0:T(8,128)(2,1)S(1)}, u32[]{:S(2)}, u32[]{:S(2)}) collective-permute-start(bf16[4,32,128]{2,1,0:T(8,128)(2,1)S(1)} %get-tuple-element.36), channel_id=1, source_target_pairs={{0,1},{1,0},{2,3},{3,2},{4,5},{5,4},{6,7},{7,6},{8,9},{9,8},{10,11... | collective-permute-start | bytes 98312 | tf_op jit(solution)/shard_map/ppermute | solution.py:399
  17.2 1.9 %copy-start.2 = (bf16[8,2,128,128]{3,2,1,0:T(8,128)(2,1)S(1)}, bf16[8,2,128,128]{3,2,1,0:T(8,128)(2,1)}, u32[]{:S(2)}) copy-start(bf16[8,2,128,128]{3,2,1,0:T(8,128)(2,1)} %refs_3_.3) | copy-start | bytes 1572868

commit v6 on v5

--- a/solution.py
+++ b/solution.py
@@ -375,8 +375,10 @@
     rows, slots, width, _ = halo.shape
     rim = inner.shape[0]
     turn = rim * (1 - lax.rem(lax.axis_index(axis), 2))
+    place = lax.axis_index(axis)
+    lone = jnp.logical_or(place == 0, place == lax.axis_size(axis) - 1)
     rim_rows[:rim] = inner[...]
-    rim_rows[rim:] = outer[...]
+    rim_rows[rim:] = narrow(jnp.where(lone, 0.0, outer[...].astype(jnp.float32)))
     for k in range(rows):
         source = [rim_rows[lax.rem(k + turn, 2 * rim)]]
         for m in range(1, slots):
@@ -393,10 +395,10 @@
 
 def swaps(block, axis, first):
     count = lax.axis_size(axis)
-    pairs = []
+    partner = list(range(count))
     for low in range(first, count - 1, 2):
-        pairs += [(low, low + 1), (low + 1, low)]
-    return lax.ppermute(block, axis, pairs)
+        partner[low], partner[low + 1] = low + 1, low
+    return lax.ppermute(block, axis, list(enumerate(partner)))
 
 
 def on_device(

time: 20.1 us -> 20.1 us (level)
  no operation moved by 1% of the time
where the time goes in v6:
time: 20.1 us; the launch traced here: 20 us
  starting transfers between devices  8.97 us (45%)
  Pallas kernels  7.18 us (36%)
  waiting for transfers between devices  3.12 us (16%)
  between operations  0.7 us (3%)
    ppermute x2, starting transfers between devices, swaps(): return lax.ppermute(block, axis, list(enumerate(partner)))  5.52 us
    pallas_call x1, Pallas kernels, on_device(): pl.pallas_call(sweep_kernel, out_shape=(wide, jax.ShapeDtypeStruct((rows...  3.73 us
    ppermute x2, starting transfers between devices, trade(): return lax.ppermute(block, axis, [(i, i ^ bit) for i in range(count)])  3.46 us
    ppermute x2, waiting for transfers between devices, trade(): return lax.ppermute(block, axis, [(i, i ^ bit) for i in range(count)])  2.99 us
    pallas_call x1, Pallas kernels, on_device(): pl.pallas_call(local, out_shape=(wide, wide, jax.ShapeDtypeStruct(masks,...  1.74 us
    pallas_call x1, Pallas kernels, on_device(): pl.pallas_call(halo, out_shape=wide, in_specs=[VMEM] * 5, out_specs=VMEM,...  0.9 us
    pallas_call x1, Pallas kernels, on_device(): pl.pallas_call(chain, out_shape=(wide, jax.ShapeDtypeStruct((rows + 2, co...  0.47 us
  transfers between devices with their start and end apart: 4, of which 3 were waited for; matrix products, arithmetic and copies ran while one was open for 0% of the time, Pallas kernels for 9%

profile of v6, /device:TPU:0, one launch (start us, length us, event | category | flops | bytes accessed | tf_op | source)
XLA Modules:
  0.0 20.0 jit_solution(7649637354880733855)
XLA Ops:
  0.6 0.0 copy-start.1
  0.6 3.7 %sweeps.1 = (f32[8,32,128]{2,1,0:T(8,128)S(1)}, bf16[9,288,128]{2,1,0:T(8,128)(2,1)S(1)}, bf16[576,128]{1,0:T(8,128)(2,1)S(1)}, s32[3,8]{1,0:T(4,128)S(1)}, s32[3,8]{1,0:T(4,128)S(1)}, /*index=5*/s32[2,8]{1,0:T(2,128)S(1)}) custom-call(f32[8,32,128]{2,1,0:T(8,128)} %rhs_far.1, bf16[8,128,128]{2,1,0:T(8,128)(2,1)} %inverse_far.1, ...), custom_call_target="tpu_custom_call" | custom-call | tf_op jit(solution)/shard_map/sweeps/pallas_call | solution.py:425
  4.4 0.0 copy-start
  4.4 0.5 %collective-permute-start = (bf16[576,128]{1,0:T(8,128)(2,1)S(1)}, bf16[576,128]{1,0:T(8,128)(2,1)S(1)}, u32[]{:S(2)}, u32[]{:S(2)}) collective-permute-start(bf16[576,128]{1,0:T(8,128)(2,1)S(1)} %get-tuple-element.20.refs_0_), channel_id=1, source_target_pairs={{0,8},{8,0},{16,24},{24,16},{1,9},{9,1},{17,25},{25,17},{2,10},{10... | collective-permute-start | bytes 442376 | tf_op jit(solution)/shard_map/ppermute | solution.py:393
  4.9 1.0 %collective-permute-done.refs_1_ = bf16[576,128]{1,0:T(8,128)(2,1)S(1)} collective-permute-done((bf16[576,128]{1,0:T(8,128)(2,1)S(1)}, bf16[576,128]{1,0:T(8,128)(2,1)S(1)}, u32[]{:S(2)}, u32[]{:S(2)}) %collective-permute-start) | collective-permute-done | bytes 147488 | tf_op jit(solution)/shard_map/ppermute | solution.py:393
  5.9 0.3 %compose.1 = (bf16[160,128]{1,0:T(8,128)(2,1)S(1)}, bf16[448,128]{1,0:T(8,128)(2,1)S(1)}, bf16[128,128]{1,0:T(8,128)(2,1)S(1)}, bf16[32,128]{1,0:T(8,128)(2,1)S(1)}) custom-call(bf16[576,128]{1,0:T(8,128)(2,1)S(1)} %get-tuple-element.20.refs_0_, bf16[576,128]{1,0:T(8,128)(2,1)S(1)} %collective-permute-done.refs_1_), custom_call_target="tpu_custom_call" | custom-call | tf_op jit(solution)/shard_map/compose/pallas_call | solution.py:472
  6.3 2.9 %collective-permute-start.1 = (bf16[160,128]{1,0:T(8,128)(2,1)S(1)}, bf16[160,128]{1,0:T(8,128)(2,1)S(1)}, u32[]{:S(2)}, u32[]{:S(2)}) collective-permute-start(bf16[160,128]{1,0:T(8,128)(2,1)S(1)} %get-tuple-element.22), channel_id=1, source_target_pairs={{0,16},{8,24},{16,0},{24,8},{1,17},{9,25},{17,1},{25,9},{2,18},{10... | collective-permute-start | bytes 122888 | tf_op jit(solution)/shard_map/ppermute | solution.py:393
  9.2 2.0 %collective-permute-done.1.refs_1_ = bf16[160,128]{1,0:T(8,128)(2,1)S(1)} collective-permute-done((bf16[160,128]{1,0:T(8,128)(2,1)S(1)}, bf16[160,128]{1,0:T(8,128)(2,1)S(1)}, u32[]{:S(2)}, u32[]{:S(2)}) %collective-permute-start.1) | collective-permute-done | bytes 40992 | tf_op jit(solution)/shard_map/ppermute | solution.py:393
  11.2 0.0 copy-start.3
  11.2 0.5 %chain.1 = (f32[8,32,128]{2,1,0:T(8,128)S(1)}, bf16[10,32,128]{2,1,0:T(8,128)(2,1)S(1)}, bf16[128,128]{1,0:T(8,128)(2,1)S(1)}, bf16[4,32,128]{2,1,0:T(8,128)(2,1)S(1)}, bf16[4,32,128]{2,1,0:T(8,128)(2,1)S(1)}) custom-call(bf16[32,128]{1,0:T(8,128)(2,1)S(1)} %get-tuple-element.21.refs_0_, bf16[160,128]{1,0:T(8,128)(2,1)S(1)} %collective-permute-done.1.refs_1_, ...), custom_call_target="tpu_custom_call" | custom-call | tf_op jit(solution)/shard_map/chain/pallas_call | solution.py:493
  11.7 0.7 %collective-permute-start.2 = (bf16[4,32,128]{2,1,0:T(8,128)(2,1)S(1)}, bf16[4,32,128]{2,1,0:T(8,128)(2,1)S(1)}, u32[]{:S(2)}, u32[]{:S(2)}) collective-permute-start(bf16[4,32,128]{2,1,0:T(8,128)(2,1)S(1)} %get-tuple-element.35), channel_id=1, source_target_pairs={{0,0},{1,2},{2,1},{3,4},{4,3},{5,6},{6,5},{7,7},{8,8},{9,10},{10,9... | collective-permute-start | bytes 98312 | tf_op jit(solution)/shard_map/ppermute | solution.py:401
  12.3 4.9 %collective-permute-start.3 = (bf16[4,32,128]{2,1,0:T(8,128)(2,1)S(1)}, bf16[4,32,128]{2,1,0:T(8,128)(2,1)S(1)}, u32[]{:S(2)}, u32[]{:S(2)}) collective-permute-start(bf16[4,32,128]{2,1,0:T(8,128)(2,1)S(1)} %get-tuple-element.36), channel_id=1, source_target_pairs={{0,1},{1,0},{2,3},{3,2},{4,5},{5,4},{6,7},{7,6},{8,9},{9,8},{10,11... | collective-permute-start | bytes 98312 | tf_op jit(solution)/shard_map/ppermute | solution.py:401
  17.2 0.0 copy-done.1
  17.2 0.0 copy-done
  17.2 0.0 copy-done.3
  17.2 0.0 copy-start.2
  17.2 1.7 %local_product.1 = (f32[8,32,128]{2,1,0:T(8,128)S(1)}, f32[8,32,128]{2,1,0:T(8,128)}, bf16[8,1,8,32,128]{4,3,2,1,0:T(8,128)(2,1)S(1)}) custom-call(bf16[10,32,128]{2,1,0:T(8,128)(2,1)S(1)} %get-tuple-element.27.refs_0_, bf16[128,128]{1,0:T(8,128)(2,1)S(1)} %get-tuple-element.28.refs_1_, f32[8,32,128]{2,1,0:T(8,128)S(1)} %get-tuple-element.29.refs_2_, ...), custom_call_target="tpu_custom_call" | custom-call | tf_op jit(solution)/shard_map/local_product/pallas_call | solution.py:515
  18.9 0.0 collective-permute-done.2.refs_1_
  19.0 0.1 collective-permute-done.3.refs_2_
  19.1 0.0 copy-done.2
  19.1 0.9 %halo_product.1 = f32[8,32,128]{2,1,0:T(8,128)} custom-call(f32[8,32,128]{2,1,0:T(8,128)S(1)} %get-tuple-element.34.refs_0_, bf16[4,32,128]{2,1,0:T(8,128)(2,1)S(1)} %collective-permute-done.2.refs_1_, bf16[4,32,128]{2,1,0:T(8,128)(2,1)S(1)} %collective-permute-done.3.refs_2_, bf16[8,2,128,128]{3,2,1,0:T(8,128)(2,1)S(1)} %copy-done.2, ...), custom_call_target="tpu_custom_call" | custom-call | tf_op jit(solution)/shard_map/halo_product/pallas_call | solution.py:531
Async XLA Ops:
  0.6 16.6 %copy-start.1 = (bf16[8,3,128,128]{3,2,1,0:T(8,128)(2,1)S(1)}, bf16[8,3,128,128]{3,2,1,0:T(8,128)(2,1)}, u32[]{:S(2)}) copy-start(bf16[8,3,128,128]{3,2,1,0:T(8,128)(2,1)} %refs_5_.1) | copy-start | bytes 2359300
  4.4 12.8 %copy-start = (bf16[8,3,128,128]{3,2,1,0:T(8,128)(2,1)S(1)}, bf16[8,3,128,128]{3,2,1,0:T(8,128)(2,1)}, u32[]{:S(2)}) copy-start(bf16[8,3,128,128]{3,2,1,0:T(8,128)(2,1)} %refs_4_.1) | copy-start | bytes 2359300
  4.4 1.5 %collective-permute-start = (bf16[576,128]{1,0:T(8,128)(2,1)S(1)}, bf16[576,128]{1,0:T(8,128)(2,1)S(1)}, u32[]{:S(2)}, u32[]{:S(2)}) collective-permute-start(bf16[576,128]{1,0:T(8,128)(2,1)S(1)} %get-tuple-element.20.refs_0_), channel_id=1, source_target_pairs={{0,8},{8,0},{16,24},{24,16},{1,9},{9,1},{17,25},{25,17},{2,10},{10... | collective-permute-start | bytes 442376 | tf_op jit(solution)/shard_map/ppermute | solution.py:393
  6.3 4.9 %collective-permute-start.1 = (bf16[160,128]{1,0:T(8,128)(2,1)S(1)}, bf16[160,128]{1,0:T(8,128)(2,1)S(1)}, u32[]{:S(2)}, u32[]{:S(2)}) collective-permute-start(bf16[160,128]{1,0:T(8,128)(2,1)S(1)} %get-tuple-element.22), channel_id=1, source_target_pairs={{0,16},{8,24},{16,0},{24,8},{1,17},{9,25},{17,1},{25,9},{2,18},{10... | collective-permute-start | bytes 122888 | tf_op jit(solution)/shard_map/ppermute | solution.py:393
  11.2 6.0 %copy-start.3 = (bf16[8,128,128]{2,1,0:T(8,128)(2,1)S(1)}, bf16[8,128,128]{2,1,0:T(8,128)(2,1)}, u32[]{:S(2)}) copy-start(bf16[8,128,128]{2,1,0:T(8,128)(2,1)} %refs_3_.2) | copy-start | bytes 786436
  11.7 7.3 %collective-permute-start.2 = (bf16[4,32,128]{2,1,0:T(8,128)(2,1)S(1)}, bf16[4,32,128]{2,1,0:T(8,128)(2,1)S(1)}, u32[]{:S(2)}, u32[]{:S(2)}) collective-permute-start(bf16[4,32,128]{2,1,0:T(8,128)(2,1)S(1)} %get-tuple-element.35), channel_id=1, source_target_pairs={{0,0},{1,2},{2,1},{3,4},{4,3},{5,6},{6,5},{7,7},{8,8},{9,10},{10,9... | collective-permute-start | bytes 98312 | tf_op jit(solution)/shard_map/ppermute | solution.py:401
  12.3 6.7 %collective-permute-start.3 = (bf16[4,32,128]{2,1,0:T(8,128)(2,1)S(1)}, bf16[4,32,128]{2,1,0:T(8,128)(2,1)S(1)}, u32[]{:S(2)}, u32[]{:S(2)}) collective-permute-start(bf16[4,32,128]{2,1,0:T(8,128)(2,1)S(1)} %get-tuple-element.36), channel_id=1, source_target_pairs={{0,1},{1,0},{2,3},{3,2},{4,5},{5,4},{6,7},{7,6},{8,9},{9,8},{10,11... | collective-permute-start | bytes 98312 | tf_op jit(solution)/shard_map/ppermute | solution.py:401
  17.2 1.9 %copy-start.2 = (bf16[8,2,128,128]{3,2,1,0:T(8,128)(2,1)S(1)}, bf16[8,2,128,128]{3,2,1,0:T(8,128)(2,1)}, u32[]{:S(2)}) copy-start(bf16[8,2,128,128]{3,2,1,0:T(8,128)(2,1)} %refs_3_.3) | copy-start | bytes 1572868

commit v7 on v5

--- a/solution.py
+++ b/solution.py
@@ -10,6 +10,7 @@
 VMEM = pl.BlockSpec(memory_space=pltpu.VMEM)
 SMEM = pl.BlockSpec(memory_space=pltpu.SMEM)
 HBM = pl.BlockSpec(memory_space=pltpu.HBM)
+ANY = pl.BlockSpec(memory_space=pl.ANY)
 SMALL = pltpu.CompilerParams(vmem_limit_bytes=16 * 1024 * 1024)
 
 
@@ -330,6 +331,7 @@
     lower_at,
     upper_at,
     halo_at,
+    relayed,
     partial,
     solution,
     masks,
@@ -391,12 +393,15 @@
     return lax.ppermute(block, axis, [(i, i ^ bit) for i in range(count)])
 
 
-def swaps(block, axis, first):
+def swaps(block, axis):
     count = lax.axis_size(axis)
-    pairs = []
-    for low in range(first, count - 1, 2):
-        pairs += [(low, low + 1), (low + 1, low)]
-    return lax.ppermute(block, axis, pairs)
+    return lax.ppermute(block, axis, [(i, i ^ 1) for i in range(count)])
+
+
+def relay(block, axis):
+    count = lax.axis_size(axis)
+    pairs = [(i, i + 2 if i % 2 else i - 2) for i in range(count)]
+    return lax.ppermute(block, axis, [(i, j) for i, j in pairs if 0 <= j < count])
 
 
 def on_device(
@@ -503,8 +508,9 @@
         name="chain",
     )(own, theirs, base, response, prior, *inner)
 
-    outer = swaps(outer, "dom", 1)
-    inner = swaps(inner, "dom", 0)
+    relayed = relay(outer, "dom")
+    inner = swaps(inner, "dom")
+    outer = swaps(relayed, "dom")
 
     def local(*refs):
         local_kernel(("section", "dom"), *refs)
@@ -513,7 +519,7 @@
     partial, solution, masks = pl.pallas_call(
         local,
         out_shape=(wide, wide, jax.ShapeDtypeStruct(masks, bits)),
-        in_specs=[VMEM] * 6 + [SMEM] * 3,
+        in_specs=[VMEM] * 6 + [SMEM] * 3 + [ANY],
         out_specs=(VMEM, HBM, VMEM),
         scratch_shapes=[
             pltpu.VMEM((rows + 2, count, width), bits),
@@ -521,7 +527,7 @@
         ],
         compiler_params=SMALL,
         name="local_product",
-    )(rounded, prior, solved, diag_blocks, lower_blocks, upper_blocks, *indices)
+    )(rounded, prior, solved, diag_blocks, lower_blocks, upper_blocks, *indices, relayed)
 
     def halo(*refs):
         halo_kernel("dom", *refs)

time: 20.1 us -> 22.5 us (1.12)
  starting transfers between devices: 8.97 us -> 10.2 us
  waiting for transfers between devices: 3.12 us -> 4.26 us
    ppermute x2 -> x3, starting transfers between devices: 5.51 us -> 6.73 us  [the longest x2 5.44 us: swaps(): return lax.ppermute(block, axis, [(i, i ^ 1) for i in range(count)])]
    ppermute x2 -> x3, waiting for transfers between devices: 0.13 us -> 1.27 us  [the longest x2 0.95 us: swaps(): return lax.ppermute(block, axis, [(i, i ^ 1) for i in range(count)])]
  transfers between devices with their start and end apart: 4 -> 5, of which waited for: 3 -> 4; matrix products, arithmetic and copies ran while one was open for 0% -> 0% of each run, Pallas kernels for 9% -> 8%
where the time goes in v7:
time: 22.5 us; the launch traced here: 22.4 us
  starting transfers between devices  10.2 us (45%)
  Pallas kernels  7.18 us (32%)
  waiting for transfers between devices  4.26 us (19%)
  between operations  0.7 us (3%)
    ppermute x2, starting transfers between devices, swaps(): return lax.ppermute(block, axis, [(i, i ^ 1) for i in range(count)])  5.44 us
    pallas_call x1, Pallas kernels, on_device(): pl.pallas_call(sweep_kernel, out_shape=(wide, jax.ShapeDtypeStruct((rows...  3.74 us
    ppermute x2, starting transfers between devices, trade(): return lax.ppermute(block, axis, [(i, i ^ bit) for i in range(count)])  3.46 us
    ppermute x2, waiting for transfers between devices, trade(): return lax.ppermute(block, axis, [(i, i ^ bit) for i in range(count)])  2.99 us
    pallas_call x1, Pallas kernels, on_device(): pl.pallas_call(local, out_shape=(wide, wide, jax.ShapeDtypeStruct(masks,...  1.74 us
    ppermute x1, starting transfers between devices, relay(): lax.ppermute(block, axis, [(i, j) for i, j in pairs if 0 <= j < count])  1.29 us
    ppermute x2, waiting for transfers between devices, swaps(): return lax.ppermute(block, axis, [(i, i ^ 1) for i in range(count)])  0.95 us
    pallas_call x1, Pallas kernels, on_device(): pl.pallas_call(halo, out_shape=wide, in_specs=[VMEM] * 5, out_specs=VMEM,...  0.89 us
  transfers between devices with their start and end apart: 5, of which 4 were waited for; matrix products, arithmetic and copies ran while one was open for 0% of the time, Pallas kernels for 8%

profile of v7, /device:TPU:0, one launch (start us, length us, event | category | flops | bytes accessed | tf_op | source)
XLA Modules:
  0.0 22.4 jit_solution(824037570981312697)
XLA Ops:
  0.6 0.0 copy-start.1
  0.6 3.7 %sweeps.1 = (f32[8,32,128]{2,1,0:T(8,128)S(1)}, bf16[9,288,128]{2,1,0:T(8,128)(2,1)S(1)}, bf16[576,128]{1,0:T(8,128)(2,1)S(1)}, s32[3,8]{1,0:T(4,128)S(1)}, s32[3,8]{1,0:T(4,128)S(1)}, /*index=5*/s32[2,8]{1,0:T(2,128)S(1)}) custom-call(f32[8,32,128]{2,1,0:T(8,128)} %rhs_far.1, bf16[8,128,128]{2,1,0:T(8,128)(2,1)} %inverse_far.1, ...), custom_call_target="tpu_custom_call" | custom-call | tf_op jit(solution)/shard_map/sweeps/pallas_call | solution.py:428
  4.4 0.0 copy-start
  4.4 0.5 %collective-permute-start = (bf16[576,128]{1,0:T(8,128)(2,1)S(1)}, bf16[576,128]{1,0:T(8,128)(2,1)S(1)}, u32[]{:S(2)}, u32[]{:S(2)}) collective-permute-start(bf16[576,128]{1,0:T(8,128)(2,1)S(1)} %get-tuple-element.20.refs_0_), channel_id=1, source_target_pairs={{0,8},{8,0},{16,24},{24,16},{1,9},{9,1},{17,25},{25,17},{2,10},{10... | collective-permute-start | bytes 442376 | tf_op jit(solution)/shard_map/ppermute | solution.py:393
  4.9 1.0 %collective-permute-done.refs_1_ = bf16[576,128]{1,0:T(8,128)(2,1)S(1)} collective-permute-done((bf16[576,128]{1,0:T(8,128)(2,1)S(1)}, bf16[576,128]{1,0:T(8,128)(2,1)S(1)}, u32[]{:S(2)}, u32[]{:S(2)}) %collective-permute-start) | collective-permute-done | bytes 147488 | tf_op jit(solution)/shard_map/ppermute | solution.py:393
  5.9 0.3 %compose.1 = (bf16[160,128]{1,0:T(8,128)(2,1)S(1)}, bf16[448,128]{1,0:T(8,128)(2,1)S(1)}, bf16[128,128]{1,0:T(8,128)(2,1)S(1)}, bf16[32,128]{1,0:T(8,128)(2,1)S(1)}) custom-call(bf16[576,128]{1,0:T(8,128)(2,1)S(1)} %get-tuple-element.20.refs_0_, bf16[576,128]{1,0:T(8,128)(2,1)S(1)} %collective-permute-done.refs_1_), custom_call_target="tpu_custom_call" | custom-call | tf_op jit(solution)/shard_map/compose/pallas_call | solution.py:475
  6.3 2.9 %collective-permute-start.1 = (bf16[160,128]{1,0:T(8,128)(2,1)S(1)}, bf16[160,128]{1,0:T(8,128)(2,1)S(1)}, u32[]{:S(2)}, u32[]{:S(2)}) collective-permute-start(bf16[160,128]{1,0:T(8,128)(2,1)S(1)} %get-tuple-element.22), channel_id=1, source_target_pairs={{0,16},{8,24},{16,0},{24,8},{1,17},{9,25},{17,1},{25,9},{2,18},{10... | collective-permute-start | bytes 122888 | tf_op jit(solution)/shard_map/ppermute | solution.py:393
  9.2 2.0 %collective-permute-done.1.refs_1_ = bf16[160,128]{1,0:T(8,128)(2,1)S(1)} collective-permute-done((bf16[160,128]{1,0:T(8,128)(2,1)S(1)}, bf16[160,128]{1,0:T(8,128)(2,1)S(1)}, u32[]{:S(2)}, u32[]{:S(2)}) %collective-permute-start.1) | collective-permute-done | bytes 40992 | tf_op jit(solution)/shard_map/ppermute | solution.py:393
  11.2 0.0 copy-start.3
  11.2 0.5 %chain.1 = (f32[8,32,128]{2,1,0:T(8,128)S(1)}, bf16[10,32,128]{2,1,0:T(8,128)(2,1)S(1)}, bf16[128,128]{1,0:T(8,128)(2,1)S(1)}, bf16[4,32,128]{2,1,0:T(8,128)(2,1)S(1)}, bf16[4,32,128]{2,1,0:T(8,128)(2,1)S(1)}) custom-call(bf16[32,128]{1,0:T(8,128)(2,1)S(1)} %get-tuple-element.21.refs_0_, bf16[160,128]{1,0:T(8,128)(2,1)S(1)} %collective-permute-done.1.refs_1_, ...), custom_call_target="tpu_custom_call" | custom-call | tf_op jit(solution)/shard_map/chain/pallas_call | solution.py:496
  11.7 1.3 %collective-permute-start.2 = (bf16[4,32,128]{2,1,0:T(8,128)(2,1)S(1)}, bf16[4,32,128]{2,1,0:T(8,128)(2,1)S(1)}, u32[]{:S(2)}, u32[]{:S(2)}) collective-permute-start(bf16[4,32,128]{2,1,0:T(8,128)(2,1)S(1)} %get-tuple-element.33), channel_id=1, source_target_pairs={{1,3},{2,0},{3,5},{4,2},{5,7},{6,4},{9,11},{10,8},{11,13},{12,10},... | collective-permute-start | bytes 98312 | tf_op jit(solution)/shard_map/ppermute | solution.py:404
  13.0 4.2 %collective-permute-start.4 = (bf16[4,32,128]{2,1,0:T(8,128)(2,1)S(1)}, bf16[4,32,128]{2,1,0:T(8,128)(2,1)S(1)}, u32[]{:S(2)}, u32[]{:S(2)}) collective-permute-start(bf16[4,32,128]{2,1,0:T(8,128)(2,1)S(1)} %get-tuple-element.36), channel_id=1, source_target_pairs={{0,1},{1,0},{2,3},{3,2},{4,5},{5,4},{6,7},{7,6},{8,9},{9,8},{10,11... | collective-permute-start | bytes 98312 | tf_op jit(solution)/shard_map/ppermute | solution.py:398
  17.2 0.3 %collective-permute-done.2.refs_9_ = bf16[4,32,128]{2,1,0:T(8,128)(2,1)S(1)} collective-permute-done((bf16[4,32,128]{2,1,0:T(8,128)(2,1)S(1)}, bf16[4,32,128]{2,1,0:T(8,128)(2,1)S(1)}, u32[]{:S(2)}, u32[]{:S(2)}) %collective-permute-start.2) | collective-permute-done | bytes 32800 | tf_op jit(solution)/shard_map/ppermute | solution.py:404
  17.5 1.2 %collective-permute-start.3 = (bf16[4,32,128]{2,1,0:T(8,128)(2,1)S(1)}, bf16[4,32,128]{2,1,0:T(8,128)(2,1)S(1)}, u32[]{:S(2)}, u32[]{:S(2)}) collective-permute-start(bf16[4,32,128]{2,1,0:T(8,128)(2,1)S(1)} %collective-permute-done.2.refs_9_), channel_id=1, source_target_pairs={{0,1},{1,0},{2,3},{3,2},{4,5},{5,4},{6,7},{7,6},{8,9},{9,8},{10,11... | collective-permute-start | bytes 98312 | tf_op jit(solution)/shard_map/ppermute | solution.py:398
  18.7 0.0 copy-done.1
  18.7 0.0 copy-done
  18.7 0.0 copy-done.3
  18.7 0.0 copy-start.2
  18.7 1.7 %local_product.1 = (f32[8,32,128]{2,1,0:T(8,128)S(1)}, f32[8,32,128]{2,1,0:T(8,128)}, bf16[8,1,8,32,128]{4,3,2,1,0:T(8,128)(2,1)S(1)}) custom-call(bf16[10,32,128]{2,1,0:T(8,128)(2,1)S(1)} %get-tuple-element.27.refs_0_, bf16[128,128]{1,0:T(8,128)(2,1)S(1)} %get-tuple-element.28.refs_1_, f32[8,32,128]{2,1,0:T(8,128)S(1)} %get-tuple-element.29.refs_2_, ...), custom_call_target="tpu_custom_call" | custom-call | tf_op jit(solution)/shard_map/local_product/pallas_call | solution.py:519
  20.5 0.0 collective-permute-done.4.refs_2_
  20.5 1.0 %collective-permute-done.3.refs_1_ = bf16[4,32,128]{2,1,0:T(8,128)(2,1)S(1)} collective-permute-done((bf16[4,32,128]{2,1,0:T(8,128)(2,1)S(1)}, bf16[4,32,128]{2,1,0:T(8,128)(2,1)S(1)}, u32[]{:S(2)}, u32[]{:S(2)}) %collective-permute-start.3) | collective-permute-done | bytes 32800 | tf_op jit(solution)/shard_map/ppermute | solution.py:398
  21.5 0.0 copy-done.2
  21.5 0.9 %halo_product.1 = f32[8,32,128]{2,1,0:T(8,128)} custom-call(f32[8,32,128]{2,1,0:T(8,128)S(1)} %get-tuple-element.35.refs_0_, bf16[4,32,128]{2,1,0:T(8,128)(2,1)S(1)} %collective-permute-done.3.refs_1_, bf16[4,32,128]{2,1,0:T(8,128)(2,1)S(1)} %collective-permute-done.4.refs_2_, bf16[8,2,128,128]{3,2,1,0:T(8,128)(2,1)S(1)} %copy-done.2, ...), custom_call_target="tpu_custom_call" | custom-call | tf_op jit(solution)/shard_map/halo_product/pallas_call | solution.py:535
Async XLA Ops:
  0.6 18.1 %copy-start.1 = (bf16[8,3,128,128]{3,2,1,0:T(8,128)(2,1)S(1)}, bf16[8,3,128,128]{3,2,1,0:T(8,128)(2,1)}, u32[]{:S(2)}) copy-start(bf16[8,3,128,128]{3,2,1,0:T(8,128)(2,1)} %refs_5_.1) | copy-start | bytes 2359300
  4.4 14.4 %copy-start = (bf16[8,3,128,128]{3,2,1,0:T(8,128)(2,1)S(1)}, bf16[8,3,128,128]{3,2,1,0:T(8,128)(2,1)}, u32[]{:S(2)}) copy-start(bf16[8,3,128,128]{3,2,1,0:T(8,128)(2,1)} %refs_4_.1) | copy-start | bytes 2359300
  4.4 1.5 %collective-permute-start = (bf16[576,128]{1,0:T(8,128)(2,1)S(1)}, bf16[576,128]{1,0:T(8,128)(2,1)S(1)}, u32[]{:S(2)}, u32[]{:S(2)}) collective-permute-start(bf16[576,128]{1,0:T(8,128)(2,1)S(1)} %get-tuple-element.20.refs_0_), channel_id=1, source_target_pairs={{0,8},{8,0},{16,24},{24,16},{1,9},{9,1},{17,25},{25,17},{2,10},{10... | collective-permute-start | bytes 442376 | tf_op jit(solution)/shard_map/ppermute | solution.py:393
  6.3 4.9 %collective-permute-start.1 = (bf16[160,128]{1,0:T(8,128)(2,1)S(1)}, bf16[160,128]{1,0:T(8,128)(2,1)S(1)}, u32[]{:S(2)}, u32[]{:S(2)}) collective-permute-start(bf16[160,128]{1,0:T(8,128)(2,1)S(1)} %get-tuple-element.22), channel_id=1, source_target_pairs={{0,16},{8,24},{16,0},{24,8},{1,17},{9,25},{17,1},{25,9},{2,18},{10... | collective-permute-start | bytes 122888 | tf_op jit(solution)/shard_map/ppermute | solution.py:393
  11.2 7.5 %copy-start.3 = (bf16[8,128,128]{2,1,0:T(8,128)(2,1)S(1)}, bf16[8,128,128]{2,1,0:T(8,128)(2,1)}, u32[]{:S(2)}) copy-start(bf16[8,128,128]{2,1,0:T(8,128)(2,1)} %refs_3_.2) | copy-start | bytes 786436
  11.7 5.9 %collective-permute-start.2 = (bf16[4,32,128]{2,1,0:T(8,128)(2,1)S(1)}, bf16[4,32,128]{2,1,0:T(8,128)(2,1)S(1)}, u32[]{:S(2)}, u32[]{:S(2)}) collective-permute-start(bf16[4,32,128]{2,1,0:T(8,128)(2,1)S(1)} %get-tuple-element.33), channel_id=1, source_target_pairs={{1,3},{2,0},{3,5},{4,2},{5,7},{6,4},{9,11},{10,8},{11,13},{12,10},... | collective-permute-start | bytes 98312 | tf_op jit(solution)/shard_map/ppermute | solution.py:404
  13.0 7.5 %collective-permute-start.4 = (bf16[4,32,128]{2,1,0:T(8,128)(2,1)S(1)}, bf16[4,32,128]{2,1,0:T(8,128)(2,1)S(1)}, u32[]{:S(2)}, u32[]{:S(2)}) collective-permute-start(bf16[4,32,128]{2,1,0:T(8,128)(2,1)S(1)} %get-tuple-element.36), channel_id=1, source_target_pairs={{0,1},{1,0},{2,3},{3,2},{4,5},{5,4},{6,7},{7,6},{8,9},{9,8},{10,11... | collective-permute-start | bytes 98312 | tf_op jit(solution)/shard_map/ppermute | solution.py:398
  17.5 3.9 %collective-permute-start.3 = (bf16[4,32,128]{2,1,0:T(8,128)(2,1)S(1)}, bf16[4,32,128]{2,1,0:T(8,128)(2,1)S(1)}, u32[]{:S(2)}, u32[]{:S(2)}) collective-permute-start(bf16[4,32,128]{2,1,0:T(8,128)(2,1)S(1)} %collective-permute-done.2.refs_9_), channel_id=1, source_target_pairs={{0,1},{1,0},{2,3},{3,2},{4,5},{5,4},{6,7},{7,6},{8,9},{9,8},{10,11... | collective-permute-start | bytes 98312 | tf_op jit(solution)/shard_map/ppermute | solution.py:398
  18.7 2.7 %copy-start.2 = (bf16[8,2,128,128]{3,2,1,0:T(8,128)(2,1)S(1)}, bf16[8,2,128,128]{3,2,1,0:T(8,128)(2,1)}, u32[]{:S(2)}) copy-start(bf16[8,2,128,128]{3,2,1,0:T(8,128)(2,1)} %refs_3_.3) | copy-start | bytes 1572868

commit v8 on v5

--- a/solution.py
+++ b/solution.py
@@ -71,7 +71,7 @@
     copies = [
         pltpu.make_async_copy(far, here, arrived.at[i]) for i, (far, here) in enumerate(parts)
     ]
-    for copy in copies:
+    for copy in copies[:5]:
         copy.start()
     eye = narrow(
         lax.broadcasted_iota(jnp.int32, (width, width), 0)
@@ -194,6 +194,8 @@
     pairs = rows // 2
     for copy in copies[:4]:
         copy.wait()
+    for copy in copies[5:]:
+        copy.start()
     ready_down(0)
     go_down(0)
     for copy in copies[4:]:
@@ -274,45 +276,53 @@
         sent[far:] = b[far:]
 
 
-def chain_kernel(axes, levels, *refs):
-    own, theirs, base, response, prior = refs[:5]
-    inner = refs[5 : 4 + levels]
-    solution, rounded, prior_out, near_rows, far_rows = refs[4 + levels :]
+def fold_kernel(axis, levels, *refs):
+    base, response = refs[:2]
+    inner = refs[2 : 1 + levels]
+    folded, folded_response, inflow_map, outflow_map = refs[1 + levels :]
     rows, count, width = base.shape
     near = count + width
-    me = lax.axis_index(axes[0])
-    side = lax.rem(lax.axis_index(axes[1]), 2)
-
-    bit = 1 << (levels - 1)
-    upper = lax.div(me, bit) == 1
-    down = theirs[:count].astype(jnp.float32)
-    up = down + mul(own[...], theirs[count:])
-    inflow = narrow(jnp.where(upper, down, 0.0))
-    outflow = narrow(jnp.where(upper, 0.0, up))
-    prior_out[...] = prior[...]
-
-    @pl.when(me == bit)
-    def _():
-        prior_out[...] = theirs[count:]
-
+    me = lax.axis_index(axis)
+
+    upper = lax.div(me, 1 << (levels - 1)) == 1
+    across = lax.broadcasted_iota(jnp.int32, (near, width), 1) + count
+    unit = jnp.where(lax.broadcasted_iota(jnp.int32, (near, width), 0) == across, 1.0, 0.0)
+    inflow = jnp.where(upper, unit, 0.0)
+    outflow = jnp.where(upper, 0.0, unit)
+    blank = jnp.zeros((width, width), jnp.float32)
     for level in range(levels - 2, -1, -1):
         part = inner[level]
         upper = lax.rem(lax.div(me, 1 << level), 2) == 1
-        down = part[:count].astype(jnp.float32) + mul(inflow, part[count:near])
-        both = jnp.concatenate([inflow, outflow], axis=1)
-        up = part[near : near + count].astype(jnp.float32) + mul(both, part[near + count :])
-        inflow, outflow = (
-            narrow(jnp.where(upper, down, inflow.astype(jnp.float32))),
-            narrow(jnp.where(upper, outflow.astype(jnp.float32), up)),
-        )
-
-    both = jnp.concatenate([inflow, outflow], axis=1)
+        known = jnp.concatenate([part[:count].astype(jnp.float32), blank], axis=0)
+        down = known + mul(narrow(inflow), part[count:near])
+        both = narrow(jnp.concatenate([inflow, outflow], axis=1))
+        known = jnp.concatenate([part[near : near + count].astype(jnp.float32), blank], axis=0)
+        up = known + mul(both, part[near + count :])
+        inflow, outflow = jnp.where(upper, down, inflow), jnp.where(upper, outflow, up)
+
+    inflow_map[...] = narrow(inflow)
+    outflow_map[...] = narrow(outflow)
+    both = narrow(jnp.concatenate([inflow, outflow], axis=1))
     for k in range(rows):
-        value = base[k] + mul(both, response[k, count:])
+        value = mul(both, response[k, count:])
+        folded[k] = base[k] + value[:count]
+        folded_response[k] = narrow(value[count:])
+
+
+def chain_kernel(
+    axes, levels, own, theirs, base, response, solution, rounded, brought, near_rows, far_rows
+):
+    rows, count, width = base.shape
+    side = lax.rem(lax.axis_index(axes[1]), 2)
+    upper = lax.div(lax.axis_index(axes[0]), 1 << (levels - 1)) == 1
+    down = theirs[:count].astype(jnp.float32)
+    up = down + mul(own[...], theirs[count:])
+    z = narrow(jnp.where(upper, down, up))
+    brought[...] = z
+    for k in range(rows):
+        value = base[k] + mul(z, response[k])
         solution[k] = value
         rounded[k] = narrow(value)
-    rounded[rows] = inflow
-    rounded[rows + 1] = outflow
     rim = near_rows.shape[0]
     for e in range(rim):
         near_rows[e] = rounded[(1 - side) * (rows - rim) + e]
@@ -321,46 +331,83 @@
 
 def local_kernel(
     axes,
+    levels,
     rounded,
+    brought,
+    inflow_map,
+    outflow_map,
     prior,
+    theirs,
     solved,
     diagonal,
     lower,
     upper,
-    lower_at,
-    upper_at,
-    halo_at,
+    lower_at_far,
+    upper_at_far,
+    halo_at_far,
     partial,
     solution,
     masks,
     held,
-    out,
+    last_block,
+    lower_at,
+    upper_at,
+    halo_at,
+    arrived,
 ):
-    copy = pltpu.make_async_copy(solved, solution, out)
-    copy.start()
+    parts = [
+        (lower_at_far, lower_at),
+        (upper_at_far, upper_at),
+        (halo_at_far, halo_at),
+        (solved, solution),
+    ]
+    copies = [
+        pltpu.make_async_copy(source, target, arrived.at[i])
+        for i, (source, target) in enumerate(parts)
+    ]
+    for copy in copies:
+        copy.start()
     rows, slots, width, _ = lower.shape
     upper_slots = upper.shape[1]
-    before = rounded[rows].astype(jnp.float32) + mul(rounded[0], prior[...])
-    held[...] = rounded[...]
-    held[rows] = narrow(jnp.where(lax.axis_index(axes[0]) > 0, before, 0.0))
+    count = brought.shape[0]
+    me = lax.axis_index(axes[0])
+    last_block[...] = prior[...]
+
+    @pl.when(me == 1 << (levels - 1))
+    def _():
+        last_block[...] = theirs[count:]
+
+    z = brought[...]
+    after = narrow(outflow_map[:count].astype(jnp.float32) + mul(z, outflow_map[count:]))
+    before = inflow_map[:count].astype(jnp.float32) + mul(z, inflow_map[count:])
+    before = narrow(before).astype(jnp.float32) + mul(rounded[0], last_block[...])
+    before = narrow(jnp.where(me > 0, before, 0.0))
+    held[:rows] = rounded[...]
+    held[rows] = before
+    held[rows + 1] = after
     for k in range(rows):
-        total = mul(rounded[k], diagonal[k])
-        source = [held[rows]]
+        source = jnp.concatenate([rounded[k], after], axis=1)
+        total = mul(source, jnp.concatenate([diagonal[k], upper[k, 0]], axis=0))
+        partial[k] = total + mul(before, lower[k, 0])
+    for copy in copies[:3]:
+        copy.wait()
+    for k in range(rows):
+        source = []
         for m in range(1, slots):
             at = lower_at[m, k]
             source.append(held[jnp.where(at == k, rows, at)])
-        total = total + mul(
-            jnp.concatenate(source, axis=1), lower[k].reshape(slots * width, width)
-        )
-        source = [rounded[rows + 1]]
+        total = mul(
+            jnp.concatenate(source, axis=1), lower[k, 1:].reshape((slots - 1) * width, width)
+        )
+        source = []
         for m in range(1, upper_slots):
             at = upper_at[m, k]
-            source.append(rounded[jnp.where(at == k, rows + 1, at)])
-        total = total + mul(
-            jnp.concatenate(source, axis=1), upper[k].reshape(upper_slots * width, width)
-        )
-        partial[k] = total
-    _, picked, places, count, _ = masks.shape
+            source.append(held[jnp.where(at == k, rows + 1, at)])
+        partial[k] += total + mul(
+            jnp.concatenate(source, axis=1),
+            upper[k, 1:].reshape((upper_slots - 1) * width, width),
+        )
+    _, picked, places, _, _ = masks.shape
     turn = places // 2 * (1 - lax.rem(lax.axis_index(axes[1]), 2))
     for k in range(rows):
         for m in range(picked):
@@ -368,7 +415,7 @@
             for j in range(places):
                 mask = jnp.where(at == j, 1.0, 0.0)
                 masks[k, m, j] = narrow(jnp.full((count, width), mask, jnp.float32))
-    copy.wait()
+    copies[3].wait()
 
 
 def halo_kernel(axis, partial, outer, inner, halo, masks, product, rim_rows):
@@ -485,43 +532,74 @@
     prior, own = prior
     theirs = trade(payload, "section", 1 << (levels - 1))
 
+    def fold(*refs):
+        fold_kernel("section", levels, *refs)
+
+    base, response, inflow_map, outflow_map = pl.pallas_call(
+        fold,
+        out_shape=(
+            wide,
+            jax.ShapeDtypeStruct((rows, width, width), bits),
+            jax.ShapeDtypeStruct((near, width), bits),
+            jax.ShapeDtypeStruct((near, width), bits),
+        ),
+        in_specs=[VMEM] * (1 + levels),
+        out_specs=(VMEM,) * 4,
+        compiler_params=SMALL,
+        name="fold",
+    )(base, response, *inner)
+
     def chain(*refs):
         chain_kernel(("section", "dom"), levels, *refs)
 
-    solved, rounded, prior, inner, outer = pl.pallas_call(
+    solved, rounded, brought, inner, outer = pl.pallas_call(
         chain,
         out_shape=(
             wide,
-            jax.ShapeDtypeStruct((rows + 2, count, width), bits),
-            jax.ShapeDtypeStruct((width, width), bits),
+            jax.ShapeDtypeStruct((rows, count, width), bits),
+            jax.ShapeDtypeStruct((count, width), bits),
             jax.ShapeDtypeStruct((RIM, count, width), bits),
             jax.ShapeDtypeStruct((RIM, count, width), bits),
         ),
-        in_specs=[VMEM] * (4 + levels),
+        in_specs=[VMEM] * 4,
         out_specs=(VMEM,) * 5,
         compiler_params=SMALL,
         name="chain",
-    )(own, theirs, base, response, prior, *inner)
+    )(own, theirs, base, response)
 
     outer = swaps(outer, "dom", 1)
     inner = swaps(inner, "dom", 0)
 
     def local(*refs):
-        local_kernel(("section", "dom"), *refs)
+        local_kernel(("section", "dom"), levels, *refs)
 
     masks = (rows, halo_blocks.shape[1] - 1, 2 * RIM, count, width)
     partial, solution, masks = pl.pallas_call(
         local,
         out_shape=(wide, wide, jax.ShapeDtypeStruct(masks, bits)),
-        in_specs=[VMEM] * 6 + [SMEM] * 3,
+        in_specs=[VMEM] * 13,
         out_specs=(VMEM, HBM, VMEM),
         scratch_shapes=[
             pltpu.VMEM((rows + 2, count, width), bits),
-            pltpu.SemaphoreType.DMA(()),
-        ],
+            pltpu.VMEM((width, width), bits),
+        ]
+        + [pltpu.SMEM(a.shape, jnp.int32) for a in indices]
+        + [pltpu.SemaphoreType.DMA((4,))],
         compiler_params=SMALL,
         name="local_product",
-    )(rounded, prior, solved, diag_blocks, lower_blocks, upper_blocks, *indices)
+    )(
+        rounded,
+        brought,
+        inflow_map,
+        outflow_map,
+        prior,
+        theirs,
+        solved,
+        diag_blocks,
+        lower_blocks,
+        upper_blocks,
+        *indices,
+    )
 
     def halo(*refs):
         halo_kernel("dom", *refs)

time: 20.1 us -> 20.6 us (1.025)
  waiting for transfers between devices: 3.12 us -> 3.44 us
    ppermute x2, waiting for transfers between devices: 0.13 us -> 0.92 us  [swaps(): return lax.ppermute(block, axis, pairs)]
    pallas_call x1, Pallas kernels: 1.74 us -> 0.94 us  [on_device(): pl.pallas_call(local, out_shape=(wide, wide, jax.ShapeDtypeStruct(masks,...]
    pallas_call x1, Pallas kernels: 3.73 us -> 4.33 us  [on_device(): pl.pallas_call(sweep_kernel, out_shape=(wide, jax.ShapeDtypeStruct((rows...]
    ppermute x2, waiting for transfers between devices: 2.99 us -> 2.52 us  [trade(): return lax.ppermute(block, axis, [(i, i ^ bit) for i in range(count)])]
    pallas_call x1 -> x2, Pallas kernels: 0.48 us -> 0.77 us  [the longest x1 0.46 us: on_device(): pl.pallas_call(fold, out_shape=(wide, jax.ShapeDtypeStruct((rows, width,...]
  transfers between devices with their start and end apart: 4 -> 4, of which waited for: 3 -> 3; matrix products, arithmetic and copies ran while one was open for 0% -> 0% of each run, Pallas kernels for 9% -> 7%
where the time goes in v8:
time: 20.6 us; the launch traced here: 20.4 us
  starting transfers between devices  8.98 us (44%)
  Pallas kernels  7.27 us (35%)
  waiting for transfers between devices  3.44 us (17%)
  between operations  0.71 us (3%)
    ppermute x2, starting transfers between devices, swaps(): return lax.ppermute(block, axis, pairs)  5.52 us
    pallas_call x1, Pallas kernels, on_device(): pl.pallas_call(sweep_kernel, out_shape=(wide, jax.ShapeDtypeStruct((rows...  4.33 us
    ppermute x2, starting transfers between devices, trade(): return lax.ppermute(block, axis, [(i, i ^ bit) for i in range(count)])  3.46 us
    ppermute x2, waiting for transfers between devices, trade(): return lax.ppermute(block, axis, [(i, i ^ bit) for i in range(count)])  2.52 us
    pallas_call x1, Pallas kernels, on_device(): pl.pallas_call(local, out_shape=(wide, wide, jax.ShapeDtypeStruct(masks,...  0.94 us
    ppermute x2, waiting for transfers between devices, swaps(): return lax.ppermute(block, axis, pairs)  0.92 us
    pallas_call x1, Pallas kernels, on_device(): pl.pallas_call(halo, out_shape=wide, in_specs=[VMEM] * 5, out_specs=VMEM,...  0.9 us
    pallas_call x1, Pallas kernels, on_device(): pl.pallas_call(fold, out_shape=(wide, jax.ShapeDtypeStruct((rows, width,...  0.46 us
  transfers between devices with their start and end apart: 4, of which 3 were waited for; matrix products, arithmetic and copies ran while one was open for 0% of the time, Pallas kernels for 7%

profile of v8, /device:TPU:0, one launch (start us, length us, event | category | flops | bytes accessed | tf_op | source)
XLA Modules:
  0.0 20.4 jit_solution(11175975154487659907)
XLA Ops:
  0.6 0.0 copy-start.3
  0.6 4.3 %sweeps.1 = (f32[8,32,128]{2,1,0:T(8,128)S(1)}, bf16[9,288,128]{2,1,0:T(8,128)(2,1)S(1)}, bf16[576,128]{1,0:T(8,128)(2,1)S(1)}, s32[3,8]{1,0:T(4,128)S(1)}, s32[3,8]{1,0:T(4,128)S(1)}, /*index=5*/s32[2,8]{1,0:T(2,128)S(1)}) custom-call(f32[8,32,128]{2,1,0:T(8,128)} %rhs_far.1, bf16[8,128,128]{2,1,0:T(8,128)(2,1)} %inverse_far.1, ...), custom_call_target="tpu_custom_call" | custom-call | tf_op jit(solution)/shard_map/sweeps/pallas_call | solution.py:470
  5.0 0.0 copy-start
  5.0 0.0 copy-start.1
  5.0 0.5 %collective-permute-start = (bf16[576,128]{1,0:T(8,128)(2,1)S(1)}, bf16[576,128]{1,0:T(8,128)(2,1)S(1)}, u32[]{:S(2)}, u32[]{:S(2)}) collective-permute-start(bf16[576,128]{1,0:T(8,128)(2,1)S(1)} %get-tuple-element.24.refs_0_), channel_id=1, source_target_pairs={{0,8},{8,0},{16,24},{24,16},{1,9},{9,1},{17,25},{25,17},{2,10},{10... | collective-permute-start | bytes 442376 | tf_op jit(solution)/shard_map/ppermute | solution.py:438
  5.5 1.0 %collective-permute-done.refs_1_ = bf16[576,128]{1,0:T(8,128)(2,1)S(1)} collective-permute-done((bf16[576,128]{1,0:T(8,128)(2,1)S(1)}, bf16[576,128]{1,0:T(8,128)(2,1)S(1)}, u32[]{:S(2)}, u32[]{:S(2)}) %collective-permute-start) | collective-permute-done | bytes 147488 | tf_op jit(solution)/shard_map/ppermute | solution.py:438
  6.5 0.3 %compose.1 = (bf16[160,128]{1,0:T(8,128)(2,1)S(1)}, bf16[448,128]{1,0:T(8,128)(2,1)S(1)}, bf16[128,128]{1,0:T(8,128)(2,1)S(1)}, bf16[32,128]{1,0:T(8,128)(2,1)S(1)}) custom-call(bf16[576,128]{1,0:T(8,128)(2,1)S(1)} %get-tuple-element.24.refs_0_, bf16[576,128]{1,0:T(8,128)(2,1)S(1)} %collective-permute-done.refs_1_), custom_call_target="tpu_custom_call" | custom-call | tf_op jit(solution)/shard_map/compose/pallas_call | solution.py:517
  6.9 3.0 %collective-permute-start.1 = (bf16[160,128]{1,0:T(8,128)(2,1)S(1)}, bf16[160,128]{1,0:T(8,128)(2,1)S(1)}, u32[]{:S(2)}, u32[]{:S(2)}) collective-permute-start(bf16[160,128]{1,0:T(8,128)(2,1)S(1)} %get-tuple-element.26), channel_id=1, source_target_pairs={{0,16},{8,24},{16,0},{24,8},{1,17},{9,25},{17,1},{25,9},{2,18},{10... | collective-permute-start | bytes 122888 | tf_op jit(solution)/shard_map/ppermute | solution.py:438
  9.8 0.5 %fold.1 = (f32[8,32,128]{2,1,0:T(8,128)S(1)}, bf16[8,128,128]{2,1,0:T(8,128)(2,1)S(1)}, bf16[160,128]{1,0:T(8,128)(2,1)S(1)}, bf16[160,128]{1,0:T(8,128)(2,1)S(1)}) custom-call(f32[8,32,128]{2,1,0:T(8,128)S(1)} %get-tuple-element.27.refs_0_, bf16[9,288,128]{2,1,0:T(8,128)(2,1)S(1)} %get-tuple-element.28.refs_1_, bf16[448,128]{1,0:T(8,128)(2,1)S(1)} %get-tuple-element.29.refs_2_), custom_call_target="tpu_custom_call" | custom-call | tf_op jit(solution)/shard_map/fold/pallas_call | solution.py:538
  10.3 1.5 %collective-permute-done.1.refs_1_.refs_5_ = bf16[160,128]{1,0:T(8,128)(2,1)S(1)} collective-permute-done((bf16[160,128]{1,0:T(8,128)(2,1)S(1)}, bf16[160,128]{1,0:T(8,128)(2,1)S(1)}, u32[]{:S(2)}, u32[]{:S(2)}) %collective-permute-start.1) | collective-permute-done | bytes 40992 | tf_op jit(solution)/shard_map/ppermute | solution.py:438
  11.8 0.3 %chain.1 = (f32[8,32,128]{2,1,0:T(8,128)S(1)}, bf16[8,32,128]{2,1,0:T(8,128)(2,1)S(1)}, bf16[32,128]{1,0:T(8,128)(2,1)S(1)}, bf16[4,32,128]{2,1,0:T(8,128)(2,1)S(1)}, bf16[4,32,128]{2,1,0:T(8,128)(2,1)S(1)}) custom-call(bf16[32,128]{1,0:T(8,128)(2,1)S(1)} %get-tuple-element.25.refs_0_, bf16[160,128]{1,0:T(8,128)(2,1)S(1)} %collective-permute-done.1.refs_1_.refs_5_, ...), custom_call_target="tpu_custom_call" | custom-call | tf_op jit(solution)/shard_map/chain/pallas_call | solution.py:555
  12.1 0.7 %collective-permute-start.2 = (bf16[4,32,128]{2,1,0:T(8,128)(2,1)S(1)}, bf16[4,32,128]{2,1,0:T(8,128)(2,1)S(1)}, u32[]{:S(2)}, u32[]{:S(2)}) collective-permute-start(bf16[4,32,128]{2,1,0:T(8,128)(2,1)S(1)} %get-tuple-element.43), channel_id=1, source_target_pairs={{1,2},{2,1},{3,4},{4,3},{5,6},{6,5},{9,10},{10,9},{11,12},{12,11},... | collective-permute-start | bytes 98312 | tf_op jit(solution)/shard_map/ppermute | solution.py:446
  12.8 4.9 %collective-permute-start.3 = (bf16[4,32,128]{2,1,0:T(8,128)(2,1)S(1)}, bf16[4,32,128]{2,1,0:T(8,128)(2,1)S(1)}, u32[]{:S(2)}, u32[]{:S(2)}) collective-permute-start(bf16[4,32,128]{2,1,0:T(8,128)(2,1)S(1)} %get-tuple-element.44), channel_id=1, source_target_pairs={{0,1},{1,0},{2,3},{3,2},{4,5},{5,4},{6,7},{7,6},{8,9},{9,8},{10,11... | collective-permute-start | bytes 98312 | tf_op jit(solution)/shard_map/ppermute | solution.py:446
  17.6 0.0 copy-done.3
  17.6 0.0 copy-done
  17.6 0.0 copy-done.1
  17.6 0.0 copy-start.2
  17.6 0.9 %local_product.1 = (f32[8,32,128]{2,1,0:T(8,128)S(1)}, f32[8,32,128]{2,1,0:T(8,128)}, bf16[8,1,8,32,128]{4,3,2,1,0:T(8,128)(2,1)S(1)}) custom-call(bf16[8,32,128]{2,1,0:T(8,128)(2,1)S(1)} %get-tuple-element.32.refs_0_, bf16[32,128]{1,0:T(8,128)(2,1)S(1)} %get-tuple-element.33.refs_1_, bf16[160,128]{1,0:T(8,128)(2,1)S(1)} %get-tuple-element.34.refs_2_, ...), custom_call_target="tpu_custom_call" | custom-call | tf_op jit(solution)/shard_map/local_product/pallas_call | solution.py:577
  18.6 0.0 collective-permute-done.2.refs_1_
  18.6 0.9 %collective-permute-done.3.refs_2_ = bf16[4,32,128]{2,1,0:T(8,128)(2,1)S(1)} collective-permute-done((bf16[4,32,128]{2,1,0:T(8,128)(2,1)S(1)}, bf16[4,32,128]{2,1,0:T(8,128)(2,1)S(1)}, u32[]{:S(2)}, u32[]{:S(2)}) %collective-permute-start.3) | collective-permute-done | bytes 32800 | tf_op jit(solution)/shard_map/ppermute | solution.py:446
  19.5 0.0 copy-done.2
  19.5 0.9 %halo_product.1 = f32[8,32,128]{2,1,0:T(8,128)} custom-call(f32[8,32,128]{2,1,0:T(8,128)S(1)} %get-tuple-element.42.refs_0_, bf16[4,32,128]{2,1,0:T(8,128)(2,1)S(1)} %collective-permute-done.2.refs_1_, bf16[4,32,128]{2,1,0:T(8,128)(2,1)S(1)} %collective-permute-done.3.refs_2_, bf16[8,2,128,128]{3,2,1,0:T(8,128)(2,1)S(1)} %copy-done.2, ...), custom_call_target="tpu_custom_call" | custom-call | tf_op jit(solution)/shard_map/halo_product/pallas_call | solution.py:607
Async XLA Ops:
  0.6 17.0 %copy-start.3 = (bf16[8,128,128]{2,1,0:T(8,128)(2,1)S(1)}, bf16[8,128,128]{2,1,0:T(8,128)(2,1)}, u32[]{:S(2)}) copy-start(bf16[8,128,128]{2,1,0:T(8,128)(2,1)} %refs_7_.1) | copy-start | bytes 786436
  5.0 12.7 %copy-start = (bf16[8,3,128,128]{3,2,1,0:T(8,128)(2,1)S(1)}, bf16[8,3,128,128]{3,2,1,0:T(8,128)(2,1)}, u32[]{:S(2)}) copy-start(bf16[8,3,128,128]{3,2,1,0:T(8,128)(2,1)} %refs_8_.1) | copy-start | bytes 2359300
  5.0 12.6 %copy-start.1 = (bf16[8,3,128,128]{3,2,1,0:T(8,128)(2,1)S(1)}, bf16[8,3,128,128]{3,2,1,0:T(8,128)(2,1)}, u32[]{:S(2)}) copy-start(bf16[8,3,128,128]{3,2,1,0:T(8,128)(2,1)} %refs_9_.1) | copy-start | bytes 2359300
  5.0 1.5 %collective-permute-start = (bf16[576,128]{1,0:T(8,128)(2,1)S(1)}, bf16[576,128]{1,0:T(8,128)(2,1)S(1)}, u32[]{:S(2)}, u32[]{:S(2)}) collective-permute-start(bf16[576,128]{1,0:T(8,128)(2,1)S(1)} %get-tuple-element.24.refs_0_), channel_id=1, source_target_pairs={{0,8},{8,0},{16,24},{24,16},{1,9},{9,1},{17,25},{25,17},{2,10},{10... | collective-permute-start | bytes 442376 | tf_op jit(solution)/shard_map/ppermute | solution.py:438
  6.9 4.9 %collective-permute-start.1 = (bf16[160,128]{1,0:T(8,128)(2,1)S(1)}, bf16[160,128]{1,0:T(8,128)(2,1)S(1)}, u32[]{:S(2)}, u32[]{:S(2)}) collective-permute-start(bf16[160,128]{1,0:T(8,128)(2,1)S(1)} %get-tuple-element.26), channel_id=1, source_target_pairs={{0,16},{8,24},{16,0},{24,8},{1,17},{9,25},{17,1},{25,9},{2,18},{10... | collective-permute-start | bytes 122888 | tf_op jit(solution)/shard_map/ppermute | solution.py:438
  12.1 6.5 %collective-permute-start.2 = (bf16[4,32,128]{2,1,0:T(8,128)(2,1)S(1)}, bf16[4,32,128]{2,1,0:T(8,128)(2,1)S(1)}, u32[]{:S(2)}, u32[]{:S(2)}) collective-permute-start(bf16[4,32,128]{2,1,0:T(8,128)(2,1)S(1)} %get-tuple-element.43), channel_id=1, source_target_pairs={{1,2},{2,1},{3,4},{4,3},{5,6},{6,5},{9,10},{10,9},{11,12},{12,11},... | collective-permute-start | bytes 98312 | tf_op jit(solution)/shard_map/ppermute | solution.py:446
  12.8 6.7 %collective-permute-start.3 = (bf16[4,32,128]{2,1,0:T(8,128)(2,1)S(1)}, bf16[4,32,128]{2,1,0:T(8,128)(2,1)S(1)}, u32[]{:S(2)}, u32[]{:S(2)}) collective-permute-start(bf16[4,32,128]{2,1,0:T(8,128)(2,1)S(1)} %get-tuple-element.44), channel_id=1, source_target_pairs={{0,1},{1,0},{2,3},{3,2},{4,5},{5,4},{6,7},{7,6},{8,9},{9,8},{10,11... | collective-permute-start | bytes 98312 | tf_op jit(solution)/shard_map/ppermute | solution.py:446
  17.6 1.9 %copy-start.2 = (bf16[8,2,128,128]{3,2,1,0:T(8,128)(2,1)S(1)}, bf16[8,2,128,128]{3,2,1,0:T(8,128)(2,1)}, u32[]{:S(2)}) copy-start(bf16[8,2,128,128]{3,2,1,0:T(8,128)(2,1)} %refs_3_.1) | copy-start | bytes 1572868

commit v9 on v8

--- a/solution.py
+++ b/solution.py
@@ -57,10 +57,12 @@
     last = rows - 1
     half = rows // 2
     parts = [
-        (inverse_far, inverse),
+        (inverse_far.at[:2], inverse.at[:2]),
+        (lower_far.at[:2], lower.at[:2]),
         (rhs_far, rhs),
-        (lower_far.at[:half], lower.at[:half]),
         (lower_at_far, lower_at),
+        (inverse_far.at[2:], inverse.at[2:]),
+        (lower_far.at[2:half], lower.at[2:half]),
         (lower_far.at[half:], lower.at[half:]),
         (upper_far, upper),
         (upper_at_far, upper_at),
@@ -71,7 +73,7 @@
     copies = [
         pltpu.make_async_copy(far, here, arrived.at[i]) for i, (far, here) in enumerate(parts)
     ]
-    for copy in copies[:5]:
+    for copy in copies[:9]:
         copy.start()
     eye = narrow(
         lax.broadcasted_iota(jnp.int32, (width, width), 0)
@@ -105,9 +107,12 @@
         sides = [jnp.concatenate([own, zero], axis=1), jnp.concatenate([zero, other], axis=1)]
         return mul(jnp.concatenate([left, right], axis=1), jnp.concatenate(sides, axis=0))
 
-    def ready(at, blocks, many, first, step, heads):
+    def ready(at, blocks, many, first, step, heads, later=()):
         of_a, of_b, links = [], [], []
         for a in (first, first + 2 * step):
+            if a != first:
+                for copy in later:
+                    copy.wait()
             b = a + step
             lefts = [
                 jnp.concatenate(heads(k) + [blocks[k].reshape(many * width, width)], axis=0)
@@ -123,9 +128,9 @@
         through = [both[:, :width], both[:, width:]]
         return of_a, narrow_a, of_b, through, links
 
-    def ready_down(p):
+    def ready_down(p, later=()):
         of_a, narrow_a, of_b, through, _ = ready(
-            lower_at, lower, slots, 2 * p, 1, lambda k: [narrow(rhs[k])]
+            lower_at, lower, slots, 2 * p, 1, lambda k: [narrow(rhs[k])], later
         )
         for i in range(2):
             a, b = 2 * (p + i), 2 * (p + i) + 1
@@ -194,11 +199,11 @@
     pairs = rows // 2
     for copy in copies[:4]:
         copy.wait()
-    for copy in copies[5:]:
+    for copy in copies[9:]:
         copy.start()
-    ready_down(0)
+    ready_down(0, copies[4:6])
     go_down(0)
-    for copy in copies[4:]:
+    for copy in copies[6:9]:
         copy.wait()
     links = []
     for p in range(1, pairs):
@@ -217,6 +222,8 @@
     payload[:near] = down[last]
     payload[near : near + far] = response[0]
     payload[near + far :] = response[last, near:]
+    for copy in copies[9:]:
+        copy.wait()
 
 
 def compose_kernel(axis, bit, final, mine, theirs, *refs):
@@ -491,7 +498,7 @@
             pltpu.VMEM((rows + 1, near, width), jnp.bfloat16),
             pltpu.VMEM((rows, near, width), jnp.float32),
             pltpu.VMEM((rows, width, width), jnp.float32),
-            pltpu.SemaphoreType.DMA((10,)),
+            pltpu.SemaphoreType.DMA((12,)),
         ],
         compiler_params=SMALL,
         name="sweeps",

time: 20.6 us -> 20.1 us (0.976)
  Pallas kernels: 7.27 us -> 6.77 us
    pallas_call x1, Pallas kernels: 4.33 us -> 3.83 us  [on_device(): pl.pallas_call(sweep_kernel, out_shape=(wide, jax.ShapeDtypeStruct((rows...]
where the time goes in v9:
time: 20.1 us; the launch traced here: 19.9 us
  starting transfers between devices  8.98 us (45%)
  Pallas kernels  6.77 us (34%)
  waiting for transfers between devices  3.44 us (17%)
  between operations  0.71 us (4%)
    ppermute x2, starting transfers between devices, swaps(): return lax.ppermute(block, axis, pairs)  5.52 us
    pallas_call x1, Pallas kernels, on_device(): pl.pallas_call(sweep_kernel, out_shape=(wide, jax.ShapeDtypeStruct((rows...  3.83 us
    ppermute x2, starting transfers between devices, trade(): return lax.ppermute(block, axis, [(i, i ^ bit) for i in range(count)])  3.46 us
    ppermute x2, waiting for transfers between devices, trade(): return lax.ppermute(block, axis, [(i, i ^ bit) for i in range(count)])  2.52 us
    pallas_call x1, Pallas kernels, on_device(): pl.pallas_call(local, out_shape=(wide, wide, jax.ShapeDtypeStruct(masks,...  0.94 us
    ppermute x2, waiting for transfers between devices, swaps(): return lax.ppermute(block, axis, pairs)  0.92 us
    pallas_call x1, Pallas kernels, on_device(): pl.pallas_call(halo, out_shape=wide, in_specs=[VMEM] * 5, out_specs=VMEM,...  0.9 us
    pallas_call x1, Pallas kernels, on_device(): pl.pallas_call(fold, out_shape=(wide, jax.ShapeDtypeStruct((rows, width,...  0.46 us
  transfers between devices with their start and end apart: 4, of which 3 were waited for; matrix products, arithmetic and copies ran while one was open for 0% of the time, Pallas kernels for 7%

profile of v9, /device:TPU:0, one launch (start us, length us, event | category | flops | bytes accessed | tf_op | source)
XLA Modules:
  0.0 19.9 jit_solution(11416613699287601913)
XLA Ops:
  0.6 0.0 copy-start.3
  0.6 3.8 %sweeps.1 = (f32[8,32,128]{2,1,0:T(8,128)S(1)}, bf16[9,288,128]{2,1,0:T(8,128)(2,1)S(1)}, bf16[576,128]{1,0:T(8,128)(2,1)S(1)}, s32[3,8]{1,0:T(4,128)S(1)}, s32[3,8]{1,0:T(4,128)S(1)}, /*index=5*/s32[2,8]{1,0:T(2,128)S(1)}) custom-call(f32[8,32,128]{2,1,0:T(8,128)} %rhs_far.1, bf16[8,128,128]{2,1,0:T(8,128)(2,1)} %inverse_far.1, ...), custom_call_target="tpu_custom_call" | custom-call | tf_op jit(solution)/shard_map/sweeps/pallas_call | solution.py:477
  4.5 0.0 copy-start
  4.5 0.0 copy-start.1
  4.5 0.5 %collective-permute-start = (bf16[576,128]{1,0:T(8,128)(2,1)S(1)}, bf16[576,128]{1,0:T(8,128)(2,1)S(1)}, u32[]{:S(2)}, u32[]{:S(2)}) collective-permute-start(bf16[576,128]{1,0:T(8,128)(2,1)S(1)} %get-tuple-element.24.refs_0_), channel_id=1, source_target_pairs={{0,8},{8,0},{16,24},{24,16},{1,9},{9,1},{17,25},{25,17},{2,10},{10... | collective-permute-start | bytes 442376 | tf_op jit(solution)/shard_map/ppermute | solution.py:445
  5.0 1.0 %collective-permute-done.refs_1_ = bf16[576,128]{1,0:T(8,128)(2,1)S(1)} collective-permute-done((bf16[576,128]{1,0:T(8,128)(2,1)S(1)}, bf16[576,128]{1,0:T(8,128)(2,1)S(1)}, u32[]{:S(2)}, u32[]{:S(2)}) %collective-permute-start) | collective-permute-done | bytes 147488 | tf_op jit(solution)/shard_map/ppermute | solution.py:445
  6.0 0.3 %compose.1 = (bf16[160,128]{1,0:T(8,128)(2,1)S(1)}, bf16[448,128]{1,0:T(8,128)(2,1)S(1)}, bf16[128,128]{1,0:T(8,128)(2,1)S(1)}, bf16[32,128]{1,0:T(8,128)(2,1)S(1)}) custom-call(bf16[576,128]{1,0:T(8,128)(2,1)S(1)} %get-tuple-element.24.refs_0_, bf16[576,128]{1,0:T(8,128)(2,1)S(1)} %collective-permute-done.refs_1_), custom_call_target="tpu_custom_call" | custom-call | tf_op jit(solution)/shard_map/compose/pallas_call | solution.py:524
  6.4 2.9 %collective-permute-start.1 = (bf16[160,128]{1,0:T(8,128)(2,1)S(1)}, bf16[160,128]{1,0:T(8,128)(2,1)S(1)}, u32[]{:S(2)}, u32[]{:S(2)}) collective-permute-start(bf16[160,128]{1,0:T(8,128)(2,1)S(1)} %get-tuple-element.26), channel_id=1, source_target_pairs={{0,16},{8,24},{16,0},{24,8},{1,17},{9,25},{17,1},{25,9},{2,18},{10... | collective-permute-start | bytes 122888 | tf_op jit(solution)/shard_map/ppermute | solution.py:445
  9.3 0.5 %fold.1 = (f32[8,32,128]{2,1,0:T(8,128)S(1)}, bf16[8,128,128]{2,1,0:T(8,128)(2,1)S(1)}, bf16[160,128]{1,0:T(8,128)(2,1)S(1)}, bf16[160,128]{1,0:T(8,128)(2,1)S(1)}) custom-call(f32[8,32,128]{2,1,0:T(8,128)S(1)} %get-tuple-element.27.refs_0_, bf16[9,288,128]{2,1,0:T(8,128)(2,1)S(1)} %get-tuple-element.28.refs_1_, bf16[448,128]{1,0:T(8,128)(2,1)S(1)} %get-tuple-element.29.refs_2_), custom_call_target="tpu_custom_call" | custom-call | tf_op jit(solution)/shard_map/fold/pallas_call | solution.py:545
  9.8 1.5 %collective-permute-done.1.refs_1_.refs_5_ = bf16[160,128]{1,0:T(8,128)(2,1)S(1)} collective-permute-done((bf16[160,128]{1,0:T(8,128)(2,1)S(1)}, bf16[160,128]{1,0:T(8,128)(2,1)S(1)}, u32[]{:S(2)}, u32[]{:S(2)}) %collective-permute-start.1) | collective-permute-done | bytes 40992 | tf_op jit(solution)/shard_map/ppermute | solution.py:445
  11.3 0.3 %chain.1 = (f32[8,32,128]{2,1,0:T(8,128)S(1)}, bf16[8,32,128]{2,1,0:T(8,128)(2,1)S(1)}, bf16[32,128]{1,0:T(8,128)(2,1)S(1)}, bf16[4,32,128]{2,1,0:T(8,128)(2,1)S(1)}, bf16[4,32,128]{2,1,0:T(8,128)(2,1)S(1)}) custom-call(bf16[32,128]{1,0:T(8,128)(2,1)S(1)} %get-tuple-element.25.refs_0_, bf16[160,128]{1,0:T(8,128)(2,1)S(1)} %collective-permute-done.1.refs_1_.refs_5_, ...), custom_call_target="tpu_custom_call" | custom-call | tf_op jit(solution)/shard_map/chain/pallas_call | solution.py:562
  11.6 0.7 %collective-permute-start.2 = (bf16[4,32,128]{2,1,0:T(8,128)(2,1)S(1)}, bf16[4,32,128]{2,1,0:T(8,128)(2,1)S(1)}, u32[]{:S(2)}, u32[]{:S(2)}) collective-permute-start(bf16[4,32,128]{2,1,0:T(8,128)(2,1)S(1)} %get-tuple-element.43), channel_id=1, source_target_pairs={{1,2},{2,1},{3,4},{4,3},{5,6},{6,5},{9,10},{10,9},{11,12},{12,11},... | collective-permute-start | bytes 98312 | tf_op jit(solution)/shard_map/ppermute | solution.py:453
  12.3 4.9 %collective-permute-start.3 = (bf16[4,32,128]{2,1,0:T(8,128)(2,1)S(1)}, bf16[4,32,128]{2,1,0:T(8,128)(2,1)S(1)}, u32[]{:S(2)}, u32[]{:S(2)}) collective-permute-start(bf16[4,32,128]{2,1,0:T(8,128)(2,1)S(1)} %get-tuple-element.44), channel_id=1, source_target_pairs={{0,1},{1,0},{2,3},{3,2},{4,5},{5,4},{6,7},{7,6},{8,9},{9,8},{10,11... | collective-permute-start | bytes 98312 | tf_op jit(solution)/shard_map/ppermute | solution.py:453
  17.1 0.0 copy-done.3
  17.1 0.0 copy-done
  17.1 0.0 copy-done.1
  17.1 0.0 copy-start.2
  17.1 0.9 %local_product.1 = (f32[8,32,128]{2,1,0:T(8,128)S(1)}, f32[8,32,128]{2,1,0:T(8,128)}, bf16[8,1,8,32,128]{4,3,2,1,0:T(8,128)(2,1)S(1)}) custom-call(bf16[8,32,128]{2,1,0:T(8,128)(2,1)S(1)} %get-tuple-element.32.refs_0_, bf16[32,128]{1,0:T(8,128)(2,1)S(1)} %get-tuple-element.33.refs_1_, bf16[160,128]{1,0:T(8,128)(2,1)S(1)} %get-tuple-element.34.refs_2_, ...), custom_call_target="tpu_custom_call" | custom-call | tf_op jit(solution)/shard_map/local_product/pallas_call | solution.py:584
  18.1 0.0 collective-permute-done.2.refs_1_
  18.1 0.9 %collective-permute-done.3.refs_2_ = bf16[4,32,128]{2,1,0:T(8,128)(2,1)S(1)} collective-permute-done((bf16[4,32,128]{2,1,0:T(8,128)(2,1)S(1)}, bf16[4,32,128]{2,1,0:T(8,128)(2,1)S(1)}, u32[]{:S(2)}, u32[]{:S(2)}) %collective-permute-start.3) | collective-permute-done | bytes 32800 | tf_op jit(solution)/shard_map/ppermute | solution.py:453
  19.0 0.0 copy-done.2
  19.0 0.9 %halo_product.1 = f32[8,32,128]{2,1,0:T(8,128)} custom-call(f32[8,32,128]{2,1,0:T(8,128)S(1)} %get-tuple-element.42.refs_0_, bf16[4,32,128]{2,1,0:T(8,128)(2,1)S(1)} %collective-permute-done.2.refs_1_, bf16[4,32,128]{2,1,0:T(8,128)(2,1)S(1)} %collective-permute-done.3.refs_2_, bf16[8,2,128,128]{3,2,1,0:T(8,128)(2,1)S(1)} %copy-done.2, ...), custom_call_target="tpu_custom_call" | custom-call | tf_op jit(solution)/shard_map/halo_product/pallas_call | solution.py:614
Async XLA Ops:
  0.6 16.5 %copy-start.3 = (bf16[8,128,128]{2,1,0:T(8,128)(2,1)S(1)}, bf16[8,128,128]{2,1,0:T(8,128)(2,1)}, u32[]{:S(2)}) copy-start(bf16[8,128,128]{2,1,0:T(8,128)(2,1)} %refs_7_.1) | copy-start | bytes 786436
  4.5 12.7 %copy-start = (bf16[8,3,128,128]{3,2,1,0:T(8,128)(2,1)S(1)}, bf16[8,3,128,128]{3,2,1,0:T(8,128)(2,1)}, u32[]{:S(2)}) copy-start(bf16[8,3,128,128]{3,2,1,0:T(8,128)(2,1)} %refs_8_.1) | copy-start | bytes 2359300
  4.5 12.6 %copy-start.1 = (bf16[8,3,128,128]{3,2,1,0:T(8,128)(2,1)S(1)}, bf16[8,3,128,128]{3,2,1,0:T(8,128)(2,1)}, u32[]{:S(2)}) copy-start(bf16[8,3,128,128]{3,2,1,0:T(8,128)(2,1)} %refs_9_.1) | copy-start | bytes 2359300
  4.5 1.5 %collective-permute-start = (bf16[576,128]{1,0:T(8,128)(2,1)S(1)}, bf16[576,128]{1,0:T(8,128)(2,1)S(1)}, u32[]{:S(2)}, u32[]{:S(2)}) collective-permute-start(bf16[576,128]{1,0:T(8,128)(2,1)S(1)} %get-tuple-element.24.refs_0_), channel_id=1, source_target_pairs={{0,8},{8,0},{16,24},{24,16},{1,9},{9,1},{17,25},{25,17},{2,10},{10... | collective-permute-start | bytes 442376 | tf_op jit(solution)/shard_map/ppermute | solution.py:445
  6.4 4.9 %collective-permute-start.1 = (bf16[160,128]{1,0:T(8,128)(2,1)S(1)}, bf16[160,128]{1,0:T(8,128)(2,1)S(1)}, u32[]{:S(2)}, u32[]{:S(2)}) collective-permute-start(bf16[160,128]{1,0:T(8,128)(2,1)S(1)} %get-tuple-element.26), channel_id=1, source_target_pairs={{0,16},{8,24},{16,0},{24,8},{1,17},{9,25},{17,1},{25,9},{2,18},{10... | collective-permute-start | bytes 122888 | tf_op jit(solution)/shard_map/ppermute | solution.py:445
  11.6 6.5 %collective-permute-start.2 = (bf16[4,32,128]{2,1,0:T(8,128)(2,1)S(1)}, bf16[4,32,128]{2,1,0:T(8,128)(2,1)S(1)}, u32[]{:S(2)}, u32[]{:S(2)}) collective-permute-start(bf16[4,32,128]{2,1,0:T(8,128)(2,1)S(1)} %get-tuple-element.43), channel_id=1, source_target_pairs={{1,2},{2,1},{3,4},{4,3},{5,6},{6,5},{9,10},{10,9},{11,12},{12,11},... | collective-permute-start | bytes 98312 | tf_op jit(solution)/shard_map/ppermute | solution.py:453
  12.3 6.8 %collective-permute-start.3 = (bf16[4,32,128]{2,1,0:T(8,128)(2,1)S(1)}, bf16[4,32,128]{2,1,0:T(8,128)(2,1)S(1)}, u32[]{:S(2)}, u32[]{:S(2)}) collective-permute-start(bf16[4,32,128]{2,1,0:T(8,128)(2,1)S(1)} %get-tuple-element.44), channel_id=1, source_target_pairs={{0,1},{1,0},{2,3},{3,2},{4,5},{5,4},{6,7},{7,6},{8,9},{9,8},{10,11... | collective-permute-start | bytes 98312 | tf_op jit(solution)/shard_map/ppermute | solution.py:453
  17.1 1.9 %copy-start.2 = (bf16[8,2,128,128]{3,2,1,0:T(8,128)(2,1)S(1)}, bf16[8,2,128,128]{3,2,1,0:T(8,128)(2,1)}, u32[]{:S(2)}) copy-start(bf16[8,2,128,128]{3,2,1,0:T(8,128)(2,1)} %refs_3_.1) | copy-start | bytes 1572868

commit v10 on v8

--- a/solution.py
+++ b/solution.py
@@ -28,13 +28,9 @@
     upper_far,
     lower_at_far,
     upper_at_far,
-    halo_at_far,
     base,
     response,
     payload,
-    lower_at_kept,
-    upper_at_kept,
-    halo_at_kept,
     rhs,
     inverse,
     lower,
@@ -64,14 +60,11 @@
         (lower_far.at[half:], lower.at[half:]),
         (upper_far, upper),
         (upper_at_far, upper_at),
-        (lower_at_far, lower_at_kept),
-        (upper_at_far, upper_at_kept),
-        (halo_at_far, halo_at_kept),
     ]
     copies = [
         pltpu.make_async_copy(far, here, arrived.at[i]) for i, (far, here) in enumerate(parts)
     ]
-    for copy in copies[:5]:
+    for copy in copies:
         copy.start()
     eye = narrow(
         lax.broadcasted_iota(jnp.int32, (width, width), 0)
@@ -129,29 +122,34 @@
         )
         for i in range(2):
             a, b = 2 * (p + i), 2 * (p + i) + 1
-            exact[a, :count] = of_a[i][:count]
-            exact[a, count:] = -of_a[i][count:near]
-            exact[b, :count] = of_b[i][:count] - through[i][:count]
-            exact[b, count:] = through[i][count:near] - of_b[i][count:near]
+            free_a = -of_a[i][count:near]
+            free_b = through[i][count:near] - of_b[i][count:near]
             if p + i == 0:
                 inner = sum(piece(of_a[i][count:], m) for m in range(1, slots))
-                exact[a, count:] += -inner
+                free_a = free_a - inner
                 inner = sum(piece(through[i][count:], m) for m in range(1, slots))
-                exact[b, count:] += inner - named(lower_at, b, b, of_b[i][count:], slots)
+                free_b = free_b + inner - named(lower_at, b, b, of_b[i][count:], slots)
             else:
                 low_pair[p + i, :, :width] = narrow_a[i][near:]
                 low_pair[p + i, :, width:] = narrow(through[i][near:])
                 low_second[p + i] = narrow(of_b[i][near:])
+            exact[a, :count] = of_a[i][:count]
+            exact[a, count:] = free_a
+            exact[b, :count] = of_b[i][:count] - through[i][:count]
+            exact[b, count:] = free_b
 
     def go_down(p):
         a, b = 2 * p, 2 * p + 1
+        of_a, of_b = exact[a], exact[b]
         if p > 0:
             first = mul(sources(down, lower_at, a, None, slots), low_pair[p])
             second = mul(sources(down, lower_at, b, a, slots), low_second[p])
-            exact[a] -= first[:, :width]
-            exact[b] += first[:, width:] - second
-        down[a] = narrow(exact[a])
-        down[b] = narrow(exact[b])
+            of_a = of_a - first[:, :width]
+            of_b = of_b + first[:, width:] - second
+            exact[a] = of_a
+            exact[b] = of_b
+        down[a] = narrow(of_a)
+        down[b] = narrow(of_b)
 
     def ready_up(p):
         of_a, narrow_a, of_b, through, links = ready(
@@ -160,16 +158,18 @@
         for i in range(2):
             a = last - 2 * (p + i)
             b = a - 1
-            fixed[a] = -of_a[i][:width]
-            fixed[b] = through[i][:width] - of_b[i][:width]
+            free_a = -of_a[i][:width]
+            free_b = through[i][:width] - of_b[i][:width]
             if p + i == 0:
-                fixed[a] += -sum(piece(of_a[i], m) for m in range(1, upper_slots))
+                free_a = free_a - sum(piece(of_a[i], m) for m in range(1, upper_slots))
                 inner = sum(piece(through[i], m) for m in range(1, upper_slots))
-                fixed[b] += inner - named(upper_at, b, b, of_b[i], upper_slots)
+                free_b = free_b + inner - named(upper_at, b, b, of_b[i], upper_slots)
             else:
                 upp_pair[p + i, :, :width] = narrow_a[i][width:]
                 upp_pair[p + i, :, width:] = narrow(through[i][width:])
                 upp_second[p + i] = narrow(of_b[i][width:])
+            fixed[a] = free_a
+            fixed[b] = free_b
         return links
 
     def go_up(p, passed):
@@ -194,8 +194,6 @@
     pairs = rows // 2
     for copy in copies[:4]:
         copy.wait()
-    for copy in copies[5:]:
-        copy.start()
     ready_down(0)
     go_down(0)
     for copy in copies[4:]:
@@ -207,16 +205,16 @@
         go_down(p)
         if p % 2 == 1:
             links += ready_up(p - 1)
+    far = near + width
+    payload[:near] = down[last]
     for p in range(0, pairs, 2):
         a = last - 2 * p
         passed = apart(down[a], down[a - 2], links[p], links[p + 1])
         go_up(p, passed[:, :width])
         go_up(p + 1, passed[:, width:])
 
-    far = near + width
-    payload[:near] = down[last]
+    payload[near + far :] = response[last, near:]
     payload[near : near + far] = response[0]
-    payload[near + far :] = response[last, near:]
 
 
 def compose_kernel(axis, bit, final, mine, theirs, *refs):
@@ -466,17 +464,18 @@
     far = near + width
     wide = jax.ShapeDtypeStruct((rows, count, width), jnp.float32)
 
-    indices = (lower_at, upper_at, halo_at)
-    base, response, payload, *indices = pl.pallas_call(
+    indices = [
+        pltpu.with_memory_space_constraint(a, pltpu.HBM) for a in (lower_at, upper_at, halo_at)
+    ]
+    base, response, payload = pl.pallas_call(
         sweep_kernel,
         out_shape=(
             wide,
             jax.ShapeDtypeStruct((rows + 1, far, width), jnp.bfloat16),
             jax.ShapeDtypeStruct((near + far + width, width), jnp.bfloat16),
-        )
-        + tuple(jax.ShapeDtypeStruct(a.shape, a.dtype) for a in indices),
-        in_specs=[HBM] * 7,
-        out_specs=(VMEM,) * 6,
+        ),
+        in_specs=[HBM] * 6,
+        out_specs=(VMEM,) * 3,
         scratch_shapes=[
             pltpu.VMEM(right_sides.shape, right_sides.dtype),
             pltpu.VMEM(diag_inverse.shape, diag_inverse.dtype),
@@ -491,15 +490,16 @@
             pltpu.VMEM((rows + 1, near, width), jnp.bfloat16),
             pltpu.VMEM((rows, near, width), jnp.float32),
             pltpu.VMEM((rows, width, width), jnp.float32),
-            pltpu.SemaphoreType.DMA((10,)),
+            pltpu.SemaphoreType.DMA((7,)),
         ],
         compiler_params=SMALL,
         name="sweeps",
     )(
         *(
             pltpu.with_memory_space_constraint(a, pltpu.HBM)
-            for a in (right_sides, diag_inverse, lower_blocks, upper_blocks, *indices)
-        )
+            for a in (right_sides, diag_inverse, lower_blocks, upper_blocks)
+        ),
+        *indices[:2],
     )
 
     levels = groups.bit_length() - 1
@@ -577,7 +577,7 @@
     partial, solution, masks = pl.pallas_call(
         local,
         out_shape=(wide, wide, jax.ShapeDtypeStruct(masks, bits)),
-        in_specs=[VMEM] * 13,
+        in_specs=[VMEM] * 10 + [HBM] * 3,
         out_specs=(VMEM, HBM, VMEM),
         scratch_shapes=[
             pltpu.VMEM((rows + 2, count, width), bits),

time: 20.6 us -> 19.9 us (0.966)
  Pallas kernels: 7.27 us -> 6.85 us
  waiting for transfers between devices: 3.44 us -> 3.17 us
    pallas_call x1, Pallas kernels: 4.33 us -> 3.64 us  [on_device(): pl.pallas_call(sweep_kernel, out_shape=(wide, jax.ShapeDtypeStruct((rows...]
    ppermute x2, waiting for transfers between devices: 0.92 us -> 0.65 us  [swaps(): return lax.ppermute(block, axis, pairs)]
    pallas_call x1, Pallas kernels: 0.94 us -> 1.21 us  [on_device(): pl.pallas_call(local, out_shape=(wide, wide, jax.ShapeDtypeStruct(masks,...]
  transfers between devices with their start and end apart: 4 -> 4, of which waited for: 3 -> 3; matrix products, arithmetic and copies ran while one was open for 0% -> 0% of each run, Pallas kernels for 7% -> 9%
where the time goes in v10:
time: 19.9 us; the launch traced here: 19.7 us
  starting transfers between devices  8.98 us (45%)
  Pallas kernels  6.85 us (34%)
  waiting for transfers between devices  3.17 us (16%)
  between operations  0.71 us (4%)
    ppermute x2, starting transfers between devices, swaps(): return lax.ppermute(block, axis, pairs)  5.52 us
    pallas_call x1, Pallas kernels, on_device(): pl.pallas_call(sweep_kernel, out_shape=(wide, jax.ShapeDtypeStruct((rows...  3.64 us
    ppermute x2, starting transfers between devices, trade(): return lax.ppermute(block, axis, [(i, i ^ bit) for i in range(count)])  3.46 us
    ppermute x2, waiting for transfers between devices, trade(): return lax.ppermute(block, axis, [(i, i ^ bit) for i in range(count)])  2.52 us
    pallas_call x1, Pallas kernels, on_device(): pl.pallas_call(local, out_shape=(wide, wide, jax.ShapeDtypeStruct(masks,...  1.21 us
    pallas_call x1, Pallas kernels, on_device(): pl.pallas_call(halo, out_shape=wide, in_specs=[VMEM] * 5, out_specs=VMEM,...  0.89 us
    ppermute x2, waiting for transfers between devices, swaps(): return lax.ppermute(block, axis, pairs)  0.65 us
    pallas_call x1, Pallas kernels, on_device(): pl.pallas_call(fold, out_shape=(wide, jax.ShapeDtypeStruct((rows, width,...  0.46 us
  transfers between devices with their start and end apart: 4, of which 3 were waited for; matrix products, arithmetic and copies ran while one was open for 0% of the time, Pallas kernels for 9%

profile of v10, /device:TPU:0, one launch (start us, length us, event | category | flops | bytes accessed | tf_op | source)
XLA Modules:
  0.0 19.7 jit_solution(8968824394557675988)
XLA Ops:
  0.6 0.0 copy-start.3
  0.6 3.6 %sweeps.1 = (f32[8,32,128]{2,1,0:T(8,128)S(1)}, bf16[9,288,128]{2,1,0:T(8,128)(2,1)S(1)}, bf16[576,128]{1,0:T(8,128)(2,1)S(1)}) custom-call(f32[8,32,128]{2,1,0:T(8,128)} %rhs_far.1, bf16[8,128,128]{2,1,0:T(8,128)(2,1)} %inverse_far.1, bf16[8,3,128,128]{3,2,1,0:T(8,128)(2,1)} %refs_8_.1, bf16[8,3,128,128]{3,2,1,0:T(8,128)(2,1)} %refs_9_.1, s32[3,8]{1,0:T(4,128)} %bitcast.3, ...), custom_call_target="tpu_custom_call" | custom-call | tf_op jit(solution)/shard_map/sweeps/pallas_call | solution.py:470
  4.3 0.0 copy-start
  4.3 0.0 copy-start.1
  4.3 0.5 %collective-permute-start = (bf16[576,128]{1,0:T(8,128)(2,1)S(1)}, bf16[576,128]{1,0:T(8,128)(2,1)S(1)}, u32[]{:S(2)}, u32[]{:S(2)}) collective-permute-start(bf16[576,128]{1,0:T(8,128)(2,1)S(1)} %get-tuple-element.21.refs_0_), channel_id=1, source_target_pairs={{0,8},{8,0},{16,24},{24,16},{1,9},{9,1},{17,25},{25,17},{2,10},{10... | collective-permute-start | bytes 442376 | tf_op jit(solution)/shard_map/ppermute | solution.py:436
  4.8 1.0 %collective-permute-done.refs_1_ = bf16[576,128]{1,0:T(8,128)(2,1)S(1)} collective-permute-done((bf16[576,128]{1,0:T(8,128)(2,1)S(1)}, bf16[576,128]{1,0:T(8,128)(2,1)S(1)}, u32[]{:S(2)}, u32[]{:S(2)}) %collective-permute-start) | collective-permute-done | bytes 147488 | tf_op jit(solution)/shard_map/ppermute | solution.py:436
  5.8 0.3 %compose.1 = (bf16[160,128]{1,0:T(8,128)(2,1)S(1)}, bf16[448,128]{1,0:T(8,128)(2,1)S(1)}, bf16[128,128]{1,0:T(8,128)(2,1)S(1)}, bf16[32,128]{1,0:T(8,128)(2,1)S(1)}) custom-call(bf16[576,128]{1,0:T(8,128)(2,1)S(1)} %get-tuple-element.21.refs_0_, bf16[576,128]{1,0:T(8,128)(2,1)S(1)} %collective-permute-done.refs_1_), custom_call_target="tpu_custom_call" | custom-call | tf_op jit(solution)/shard_map/compose/pallas_call | solution.py:517
  6.2 2.9 %collective-permute-start.1 = (bf16[160,128]{1,0:T(8,128)(2,1)S(1)}, bf16[160,128]{1,0:T(8,128)(2,1)S(1)}, u32[]{:S(2)}, u32[]{:S(2)}) collective-permute-start(bf16[160,128]{1,0:T(8,128)(2,1)S(1)} %get-tuple-element.23), channel_id=1, source_target_pairs={{0,16},{8,24},{16,0},{24,8},{1,17},{9,25},{17,1},{25,9},{2,18},{10... | collective-permute-start | bytes 122888 | tf_op jit(solution)/shard_map/ppermute | solution.py:436
  9.1 0.5 %fold.1 = (f32[8,32,128]{2,1,0:T(8,128)S(1)}, bf16[8,128,128]{2,1,0:T(8,128)(2,1)S(1)}, bf16[160,128]{1,0:T(8,128)(2,1)S(1)}, bf16[160,128]{1,0:T(8,128)(2,1)S(1)}) custom-call(f32[8,32,128]{2,1,0:T(8,128)S(1)} %get-tuple-element.24.refs_0_, bf16[9,288,128]{2,1,0:T(8,128)(2,1)S(1)} %get-tuple-element.25.refs_1_, bf16[448,128]{1,0:T(8,128)(2,1)S(1)} %get-tuple-element.26.refs_2_), custom_call_target="tpu_custom_call" | custom-call | tf_op jit(solution)/shard_map/fold/pallas_call | solution.py:538
  9.6 1.5 %collective-permute-done.1.refs_1_.refs_5_ = bf16[160,128]{1,0:T(8,128)(2,1)S(1)} collective-permute-done((bf16[160,128]{1,0:T(8,128)(2,1)S(1)}, bf16[160,128]{1,0:T(8,128)(2,1)S(1)}, u32[]{:S(2)}, u32[]{:S(2)}) %collective-permute-start.1) | collective-permute-done | bytes 40992 | tf_op jit(solution)/shard_map/ppermute | solution.py:436
  11.1 0.3 %chain.1 = (f32[8,32,128]{2,1,0:T(8,128)S(1)}, bf16[8,32,128]{2,1,0:T(8,128)(2,1)S(1)}, bf16[32,128]{1,0:T(8,128)(2,1)S(1)}, bf16[4,32,128]{2,1,0:T(8,128)(2,1)S(1)}, bf16[4,32,128]{2,1,0:T(8,128)(2,1)S(1)}) custom-call(bf16[32,128]{1,0:T(8,128)(2,1)S(1)} %get-tuple-element.22.refs_0_, bf16[160,128]{1,0:T(8,128)(2,1)S(1)} %collective-permute-done.1.refs_1_.refs_5_, ...), custom_call_target="tpu_custom_call" | custom-call | tf_op jit(solution)/shard_map/chain/pallas_call | solution.py:555
  11.4 0.7 %collective-permute-start.2 = (bf16[4,32,128]{2,1,0:T(8,128)(2,1)S(1)}, bf16[4,32,128]{2,1,0:T(8,128)(2,1)S(1)}, u32[]{:S(2)}, u32[]{:S(2)}) collective-permute-start(bf16[4,32,128]{2,1,0:T(8,128)(2,1)S(1)} %get-tuple-element.37), channel_id=1, source_target_pairs={{1,2},{2,1},{3,4},{4,3},{5,6},{6,5},{9,10},{10,9},{11,12},{12,11},... | collective-permute-start | bytes 98312 | tf_op jit(solution)/shard_map/ppermute | solution.py:444
  12.1 4.9 %collective-permute-start.3 = (bf16[4,32,128]{2,1,0:T(8,128)(2,1)S(1)}, bf16[4,32,128]{2,1,0:T(8,128)(2,1)S(1)}, u32[]{:S(2)}, u32[]{:S(2)}) collective-permute-start(bf16[4,32,128]{2,1,0:T(8,128)(2,1)S(1)} %get-tuple-element.38), channel_id=1, source_target_pairs={{0,1},{1,0},{2,3},{3,2},{4,5},{5,4},{6,7},{7,6},{8,9},{9,8},{10,11... | collective-permute-start | bytes 98312 | tf_op jit(solution)/shard_map/ppermute | solution.py:444
  16.9 0.0 copy-done.3
  16.9 0.0 copy-done
  16.9 0.0 copy-done.1
  16.9 0.0 copy-start.2
  17.0 1.2 %local_product.1 = (f32[8,32,128]{2,1,0:T(8,128)S(1)}, f32[8,32,128]{2,1,0:T(8,128)}, bf16[8,1,8,32,128]{4,3,2,1,0:T(8,128)(2,1)S(1)}) custom-call(bf16[8,32,128]{2,1,0:T(8,128)(2,1)S(1)} %get-tuple-element.29.refs_0_, bf16[32,128]{1,0:T(8,128)(2,1)S(1)} %get-tuple-element.30.refs_1_, bf16[160,128]{1,0:T(8,128)(2,1)S(1)} %get-tuple-element.31.refs_2_, ...), custom_call_target="tpu_custom_call" | custom-call | tf_op jit(solution)/shard_map/local_product/pallas_call | solution.py:577
  18.2 0.0 collective-permute-done.2.refs_1_
  18.2 0.6 %collective-permute-done.3.refs_2_ = bf16[4,32,128]{2,1,0:T(8,128)(2,1)S(1)} collective-permute-done((bf16[4,32,128]{2,1,0:T(8,128)(2,1)S(1)}, bf16[4,32,128]{2,1,0:T(8,128)(2,1)S(1)}, u32[]{:S(2)}, u32[]{:S(2)}) %collective-permute-start.3) | collective-permute-done | bytes 32800 | tf_op jit(solution)/shard_map/ppermute | solution.py:444
  18.8 0.0 copy-done.2
  18.8 0.9 %halo_product.1 = f32[8,32,128]{2,1,0:T(8,128)} custom-call(f32[8,32,128]{2,1,0:T(8,128)S(1)} %get-tuple-element.36.refs_0_, bf16[4,32,128]{2,1,0:T(8,128)(2,1)S(1)} %collective-permute-done.2.refs_1_, bf16[4,32,128]{2,1,0:T(8,128)(2,1)S(1)} %collective-permute-done.3.refs_2_, bf16[8,2,128,128]{3,2,1,0:T(8,128)(2,1)S(1)} %copy-done.2, ...), custom_call_target="tpu_custom_call" | custom-call | tf_op jit(solution)/shard_map/halo_product/pallas_call | solution.py:607
Async XLA Ops:
  0.6 16.3 %copy-start.3 = (bf16[8,128,128]{2,1,0:T(8,128)(2,1)S(1)}, bf16[8,128,128]{2,1,0:T(8,128)(2,1)}, u32[]{:S(2)}) copy-start(bf16[8,128,128]{2,1,0:T(8,128)(2,1)} %refs_7_.1) | copy-start | bytes 786436
  4.3 12.7 %copy-start = (bf16[8,3,128,128]{3,2,1,0:T(8,128)(2,1)S(1)}, bf16[8,3,128,128]{3,2,1,0:T(8,128)(2,1)}, u32[]{:S(2)}) copy-start(bf16[8,3,128,128]{3,2,1,0:T(8,128)(2,1)} %refs_8_.1) | copy-start | bytes 2359300
  4.3 12.6 %copy-start.1 = (bf16[8,3,128,128]{3,2,1,0:T(8,128)(2,1)S(1)}, bf16[8,3,128,128]{3,2,1,0:T(8,128)(2,1)}, u32[]{:S(2)}) copy-start(bf16[8,3,128,128]{3,2,1,0:T(8,128)(2,1)} %refs_9_.1) | copy-start | bytes 2359300
  4.3 1.5 %collective-permute-start = (bf16[576,128]{1,0:T(8,128)(2,1)S(1)}, bf16[576,128]{1,0:T(8,128)(2,1)S(1)}, u32[]{:S(2)}, u32[]{:S(2)}) collective-permute-start(bf16[576,128]{1,0:T(8,128)(2,1)S(1)} %get-tuple-element.21.refs_0_), channel_id=1, source_target_pairs={{0,8},{8,0},{16,24},{24,16},{1,9},{9,1},{17,25},{25,17},{2,10},{10... | collective-permute-start | bytes 442376 | tf_op jit(solution)/shard_map/ppermute | solution.py:436
  6.2 4.9 %collective-permute-start.1 = (bf16[160,128]{1,0:T(8,128)(2,1)S(1)}, bf16[160,128]{1,0:T(8,128)(2,1)S(1)}, u32[]{:S(2)}, u32[]{:S(2)}) collective-permute-start(bf16[160,128]{1,0:T(8,128)(2,1)S(1)} %get-tuple-element.23), channel_id=1, source_target_pairs={{0,16},{8,24},{16,0},{24,8},{1,17},{9,25},{17,1},{25,9},{2,18},{10... | collective-permute-start | bytes 122888 | tf_op jit(solution)/shard_map/ppermute | solution.py:436
  11.4 6.8 %collective-permute-start.2 = (bf16[4,32,128]{2,1,0:T(8,128)(2,1)S(1)}, bf16[4,32,128]{2,1,0:T(8,128)(2,1)S(1)}, u32[]{:S(2)}, u32[]{:S(2)}) collective-permute-start(bf16[4,32,128]{2,1,0:T(8,128)(2,1)S(1)} %get-tuple-element.37), channel_id=1, source_target_pairs={{1,2},{2,1},{3,4},{4,3},{5,6},{6,5},{9,10},{10,9},{11,12},{12,11},... | collective-permute-start | bytes 98312 | tf_op jit(solution)/shard_map/ppermute | solution.py:444
  12.1 6.8 %collective-permute-start.3 = (bf16[4,32,128]{2,1,0:T(8,128)(2,1)S(1)}, bf16[4,32,128]{2,1,0:T(8,128)(2,1)S(1)}, u32[]{:S(2)}, u32[]{:S(2)}) collective-permute-start(bf16[4,32,128]{2,1,0:T(8,128)(2,1)S(1)} %get-tuple-element.38), channel_id=1, source_target_pairs={{0,1},{1,0},{2,3},{3,2},{4,5},{5,4},{6,7},{7,6},{8,9},{9,8},{10,11... | collective-permute-start | bytes 98312 | tf_op jit(solution)/shard_map/ppermute | solution.py:444
  16.9 1.9 %copy-start.2 = (bf16[8,2,128,128]{3,2,1,0:T(8,128)(2,1)S(1)}, bf16[8,2,128,128]{3,2,1,0:T(8,128)(2,1)}, u32[]{:S(2)}) copy-start(bf16[8,2,128,128]{3,2,1,0:T(8,128)(2,1)} %refs_3_.1) | copy-start | bytes 1572868

commit v11 on v10

--- a/solution.py
+++ b/solution.py
@@ -138,18 +138,27 @@
             exact[b, :count] = of_b[i][:count] - through[i][:count]
             exact[b, count:] = free_b
 
-    def go_down(p):
+    def ready_turn(link):
+        p = rows // 2 - 1
+        both = narrow(apart(low_pair[p, :, width:], low_second[p], link, link))
+        return both[:, :width], both[:, width:], mul(narrow(exact[last]), link)
+
+    def go_down(p, turn=None):
         a, b = 2 * p, 2 * p + 1
         of_a, of_b = exact[a], exact[b]
         if p > 0:
-            first = mul(sources(down, lower_at, a, None, slots), low_pair[p])
-            second = mul(sources(down, lower_at, b, a, slots), low_second[p])
+            right = [low_pair[p], low_second[p]]
+            if turn is not None:
+                right = [jnp.concatenate(both, axis=1) for both in zip(right, turn)]
+            first = mul(sources(down, lower_at, a, None, slots), right[0])
+            second = mul(sources(down, lower_at, b, a, slots), right[1])
             of_a = of_a - first[:, :width]
-            of_b = of_b + first[:, width:] - second
+            of_b = of_b + first[:, width : 2 * width] - second[:, :width]
             exact[a] = of_a
             exact[b] = of_b
         down[a] = narrow(of_a)
         down[b] = narrow(of_b)
+        return None if turn is None else turn[2] + first[:, 2 * width :] - second[:, width:]
 
     def ready_up(p):
         of_a, narrow_a, of_b, through, links = ready(
@@ -199,19 +208,27 @@
     for copy in copies[4:]:
         copy.wait()
     links = []
+    turn = None
     for p in range(1, pairs):
         if p % 2 == 1 and p + 1 < pairs:
             ready_down(p + 1)
-        go_down(p)
+        if p + 1 < pairs:
+            go_down(p)
+        else:
+            passed = [go_down(p, turn), mul(down[last - 2], links[1])]
         if p % 2 == 1:
             links += ready_up(p - 1)
+        if turn is None:
+            turn = ready_turn(links[0])
     far = near + width
     payload[:near] = down[last]
     for p in range(0, pairs, 2):
-        a = last - 2 * p
-        passed = apart(down[a], down[a - 2], links[p], links[p + 1])
-        go_up(p, passed[:, :width])
-        go_up(p + 1, passed[:, width:])
+        if p > 0:
+            a = last - 2 * p
+            both = apart(down[a], down[a - 2], links[p], links[p + 1])
+            passed = [both[:, :width], both[:, width:]]
+        go_up(p, passed[0])
+        go_up(p + 1, passed[1])
 
     payload[near + far :] = response[last, near:]
     payload[near : near + far] = response[0]

time: 19.9 us -> 20 us (level)
  transfers between devices with their start and end apart: 4 -> 4, of which waited for: 3 -> 3; matrix products, arithmetic and copies ran while one was open for 0% -> 0% of each run, Pallas kernels for 9% -> 8%
where the time goes in v11:
time: 20 us; the launch traced here: 19.9 us
  starting transfers between devices  8.98 us (45%)
  Pallas kernels  6.98 us (35%)
  waiting for transfers between devices  3.17 us (16%)
  between operations  0.71 us (4%)
    ppermute x2, starting transfers between devices, swaps(): return lax.ppermute(block, axis, pairs)  5.52 us
    pallas_call x1, Pallas kernels, on_device(): pl.pallas_call(sweep_kernel, out_shape=(wide, jax.ShapeDtypeStruct((rows...  3.77 us
    ppermute x2, starting transfers between devices, trade(): return lax.ppermute(block, axis, [(i, i ^ bit) for i in range(count)])  3.46 us
    ppermute x2, waiting for transfers between devices, trade(): return lax.ppermute(block, axis, [(i, i ^ bit) for i in range(count)])  2.52 us
    pallas_call x1, Pallas kernels, on_device(): pl.pallas_call(local, out_shape=(wide, wide, jax.ShapeDtypeStruct(masks,...  1.22 us
    pallas_call x1, Pallas kernels, on_device(): pl.pallas_call(halo, out_shape=wide, in_specs=[VMEM] * 5, out_specs=VMEM,...  0.89 us
    ppermute x2, waiting for transfers between devices, swaps(): return lax.ppermute(block, axis, pairs)  0.64 us
    pallas_call x1, Pallas kernels, on_device(): pl.pallas_call(fold, out_shape=(wide, jax.ShapeDtypeStruct((rows, width,...  0.46 us
  transfers between devices with their start and end apart: 4, of which 3 were waited for; matrix products, arithmetic and copies ran while one was open for 0% of the time, Pallas kernels for 8%

profile of v11, /device:TPU:0, one launch (start us, length us, event | category | flops | bytes accessed | tf_op | source)
XLA Modules:
  0.0 19.9 jit_solution(17694833371771266048)
XLA Ops:
  0.6 0.0 copy-start.3
  0.6 3.8 %sweeps.1 = (f32[8,32,128]{2,1,0:T(8,128)S(1)}, bf16[9,288,128]{2,1,0:T(8,128)(2,1)S(1)}, bf16[576,128]{1,0:T(8,128)(2,1)S(1)}) custom-call(f32[8,32,128]{2,1,0:T(8,128)} %rhs_far.1, bf16[8,128,128]{2,1,0:T(8,128)(2,1)} %inverse_far.1, bf16[8,3,128,128]{3,2,1,0:T(8,128)(2,1)} %refs_8_.1, bf16[8,3,128,128]{3,2,1,0:T(8,128)(2,1)} %refs_9_.1, s32[3,8]{1,0:T(4,128)} %bitcast.3, ...), custom_call_target="tpu_custom_call" | custom-call | tf_op jit(solution)/shard_map/sweeps/pallas_call | solution.py:487
  4.4 0.0 copy-start
  4.4 0.0 copy-start.1
  4.4 0.5 %collective-permute-start = (bf16[576,128]{1,0:T(8,128)(2,1)S(1)}, bf16[576,128]{1,0:T(8,128)(2,1)S(1)}, u32[]{:S(2)}, u32[]{:S(2)}) collective-permute-start(bf16[576,128]{1,0:T(8,128)(2,1)S(1)} %get-tuple-element.21.refs_0_), channel_id=1, source_target_pairs={{0,8},{8,0},{16,24},{24,16},{1,9},{9,1},{17,25},{25,17},{2,10},{10... | collective-permute-start | bytes 442376 | tf_op jit(solution)/shard_map/ppermute | solution.py:453
  5.0 1.0 %collective-permute-done.refs_1_ = bf16[576,128]{1,0:T(8,128)(2,1)S(1)} collective-permute-done((bf16[576,128]{1,0:T(8,128)(2,1)S(1)}, bf16[576,128]{1,0:T(8,128)(2,1)S(1)}, u32[]{:S(2)}, u32[]{:S(2)}) %collective-permute-start) | collective-permute-done | bytes 147488 | tf_op jit(solution)/shard_map/ppermute | solution.py:453
  6.0 0.3 %compose.1 = (bf16[160,128]{1,0:T(8,128)(2,1)S(1)}, bf16[448,128]{1,0:T(8,128)(2,1)S(1)}, bf16[128,128]{1,0:T(8,128)(2,1)S(1)}, bf16[32,128]{1,0:T(8,128)(2,1)S(1)}) custom-call(bf16[576,128]{1,0:T(8,128)(2,1)S(1)} %get-tuple-element.21.refs_0_, bf16[576,128]{1,0:T(8,128)(2,1)S(1)} %collective-permute-done.refs_1_), custom_call_target="tpu_custom_call" | custom-call | tf_op jit(solution)/shard_map/compose/pallas_call | solution.py:534
  6.3 2.9 %collective-permute-start.1 = (bf16[160,128]{1,0:T(8,128)(2,1)S(1)}, bf16[160,128]{1,0:T(8,128)(2,1)S(1)}, u32[]{:S(2)}, u32[]{:S(2)}) collective-permute-start(bf16[160,128]{1,0:T(8,128)(2,1)S(1)} %get-tuple-element.23), channel_id=1, source_target_pairs={{0,16},{8,24},{16,0},{24,8},{1,17},{9,25},{17,1},{25,9},{2,18},{10... | collective-permute-start | bytes 122888 | tf_op jit(solution)/shard_map/ppermute | solution.py:453
  9.3 0.5 %fold.1 = (f32[8,32,128]{2,1,0:T(8,128)S(1)}, bf16[8,128,128]{2,1,0:T(8,128)(2,1)S(1)}, bf16[160,128]{1,0:T(8,128)(2,1)S(1)}, bf16[160,128]{1,0:T(8,128)(2,1)S(1)}) custom-call(f32[8,32,128]{2,1,0:T(8,128)S(1)} %get-tuple-element.24.refs_0_, bf16[9,288,128]{2,1,0:T(8,128)(2,1)S(1)} %get-tuple-element.25.refs_1_, bf16[448,128]{1,0:T(8,128)(2,1)S(1)} %get-tuple-element.26.refs_2_), custom_call_target="tpu_custom_call" | custom-call | tf_op jit(solution)/shard_map/fold/pallas_call | solution.py:555
  9.7 1.5 %collective-permute-done.1.refs_1_.refs_5_ = bf16[160,128]{1,0:T(8,128)(2,1)S(1)} collective-permute-done((bf16[160,128]{1,0:T(8,128)(2,1)S(1)}, bf16[160,128]{1,0:T(8,128)(2,1)S(1)}, u32[]{:S(2)}, u32[]{:S(2)}) %collective-permute-start.1) | collective-permute-done | bytes 40992 | tf_op jit(solution)/shard_map/ppermute | solution.py:453
  11.2 0.3 %chain.1 = (f32[8,32,128]{2,1,0:T(8,128)S(1)}, bf16[8,32,128]{2,1,0:T(8,128)(2,1)S(1)}, bf16[32,128]{1,0:T(8,128)(2,1)S(1)}, bf16[4,32,128]{2,1,0:T(8,128)(2,1)S(1)}, bf16[4,32,128]{2,1,0:T(8,128)(2,1)S(1)}) custom-call(bf16[32,128]{1,0:T(8,128)(2,1)S(1)} %get-tuple-element.22.refs_0_, bf16[160,128]{1,0:T(8,128)(2,1)S(1)} %collective-permute-done.1.refs_1_.refs_5_, ...), custom_call_target="tpu_custom_call" | custom-call | tf_op jit(solution)/shard_map/chain/pallas_call | solution.py:572
  11.5 0.7 %collective-permute-start.2 = (bf16[4,32,128]{2,1,0:T(8,128)(2,1)S(1)}, bf16[4,32,128]{2,1,0:T(8,128)(2,1)S(1)}, u32[]{:S(2)}, u32[]{:S(2)}) collective-permute-start(bf16[4,32,128]{2,1,0:T(8,128)(2,1)S(1)} %get-tuple-element.37), channel_id=1, source_target_pairs={{1,2},{2,1},{3,4},{4,3},{5,6},{6,5},{9,10},{10,9},{11,12},{12,11},... | collective-permute-start | bytes 98312 | tf_op jit(solution)/shard_map/ppermute | solution.py:461
  12.2 4.9 %collective-permute-start.3 = (bf16[4,32,128]{2,1,0:T(8,128)(2,1)S(1)}, bf16[4,32,128]{2,1,0:T(8,128)(2,1)S(1)}, u32[]{:S(2)}, u32[]{:S(2)}) collective-permute-start(bf16[4,32,128]{2,1,0:T(8,128)(2,1)S(1)} %get-tuple-element.38), channel_id=1, source_target_pairs={{0,1},{1,0},{2,3},{3,2},{4,5},{5,4},{6,7},{7,6},{8,9},{9,8},{10,11... | collective-permute-start | bytes 98312 | tf_op jit(solution)/shard_map/ppermute | solution.py:461
  17.1 0.0 copy-done.3
  17.1 0.0 copy-done
  17.1 0.0 copy-done.1
  17.1 0.0 copy-start.2
  17.1 1.2 %local_product.1 = (f32[8,32,128]{2,1,0:T(8,128)S(1)}, f32[8,32,128]{2,1,0:T(8,128)}, bf16[8,1,8,32,128]{4,3,2,1,0:T(8,128)(2,1)S(1)}) custom-call(bf16[8,32,128]{2,1,0:T(8,128)(2,1)S(1)} %get-tuple-element.29.refs_0_, bf16[32,128]{1,0:T(8,128)(2,1)S(1)} %get-tuple-element.30.refs_1_, bf16[160,128]{1,0:T(8,128)(2,1)S(1)} %get-tuple-element.31.refs_2_, ...), custom_call_target="tpu_custom_call" | custom-call | tf_op jit(solution)/shard_map/local_product/pallas_call | solution.py:594
  18.3 0.0 collective-permute-done.2.refs_1_
  18.3 0.6 %collective-permute-done.3.refs_2_ = bf16[4,32,128]{2,1,0:T(8,128)(2,1)S(1)} collective-permute-done((bf16[4,32,128]{2,1,0:T(8,128)(2,1)S(1)}, bf16[4,32,128]{2,1,0:T(8,128)(2,1)S(1)}, u32[]{:S(2)}, u32[]{:S(2)}) %collective-permute-start.3) | collective-permute-done | bytes 32800 | tf_op jit(solution)/shard_map/ppermute | solution.py:461
  19.0 0.0 copy-done.2
  19.0 0.9 %halo_product.1 = f32[8,32,128]{2,1,0:T(8,128)} custom-call(f32[8,32,128]{2,1,0:T(8,128)S(1)} %get-tuple-element.36.refs_0_, bf16[4,32,128]{2,1,0:T(8,128)(2,1)S(1)} %collective-permute-done.2.refs_1_, bf16[4,32,128]{2,1,0:T(8,128)(2,1)S(1)} %collective-permute-done.3.refs_2_, bf16[8,2,128,128]{3,2,1,0:T(8,128)(2,1)S(1)} %copy-done.2, ...), custom_call_target="tpu_custom_call" | custom-call | tf_op jit(solution)/shard_map/halo_product/pallas_call | solution.py:624
Async XLA Ops:
  0.6 16.4 %copy-start.3 = (bf16[8,128,128]{2,1,0:T(8,128)(2,1)S(1)}, bf16[8,128,128]{2,1,0:T(8,128)(2,1)}, u32[]{:S(2)}) copy-start(bf16[8,128,128]{2,1,0:T(8,128)(2,1)} %refs_7_.1) | copy-start | bytes 786436
  4.4 12.7 %copy-start = (bf16[8,3,128,128]{3,2,1,0:T(8,128)(2,1)S(1)}, bf16[8,3,128,128]{3,2,1,0:T(8,128)(2,1)}, u32[]{:S(2)}) copy-start(bf16[8,3,128,128]{3,2,1,0:T(8,128)(2,1)} %refs_8_.1) | copy-start | bytes 2359300
  4.4 12.6 %copy-start.1 = (bf16[8,3,128,128]{3,2,1,0:T(8,128)(2,1)S(1)}, bf16[8,3,128,128]{3,2,1,0:T(8,128)(2,1)}, u32[]{:S(2)}) copy-start(bf16[8,3,128,128]{3,2,1,0:T(8,128)(2,1)} %refs_9_.1) | copy-start | bytes 2359300
  4.4 1.5 %collective-permute-start = (bf16[576,128]{1,0:T(8,128)(2,1)S(1)}, bf16[576,128]{1,0:T(8,128)(2,1)S(1)}, u32[]{:S(2)}, u32[]{:S(2)}) collective-permute-start(bf16[576,128]{1,0:T(8,128)(2,1)S(1)} %get-tuple-element.21.refs_0_), channel_id=1, source_target_pairs={{0,8},{8,0},{16,24},{24,16},{1,9},{9,1},{17,25},{25,17},{2,10},{10... | collective-permute-start | bytes 442376 | tf_op jit(solution)/shard_map/ppermute | solution.py:453
  6.3 4.9 %collective-permute-start.1 = (bf16[160,128]{1,0:T(8,128)(2,1)S(1)}, bf16[160,128]{1,0:T(8,128)(2,1)S(1)}, u32[]{:S(2)}, u32[]{:S(2)}) collective-permute-start(bf16[160,128]{1,0:T(8,128)(2,1)S(1)} %get-tuple-element.23), channel_id=1, source_target_pairs={{0,16},{8,24},{16,0},{24,8},{1,17},{9,25},{17,1},{25,9},{2,18},{10... | collective-permute-start | bytes 122888 | tf_op jit(solution)/shard_map/ppermute | solution.py:453
  11.5 6.8 %collective-permute-start.2 = (bf16[4,32,128]{2,1,0:T(8,128)(2,1)S(1)}, bf16[4,32,128]{2,1,0:T(8,128)(2,1)S(1)}, u32[]{:S(2)}, u32[]{:S(2)}) collective-permute-start(bf16[4,32,128]{2,1,0:T(8,128)(2,1)S(1)} %get-tuple-element.37), channel_id=1, source_target_pairs={{1,2},{2,1},{3,4},{4,3},{5,6},{6,5},{9,10},{10,9},{11,12},{12,11},... | collective-permute-start | bytes 98312 | tf_op jit(solution)/shard_map/ppermute | solution.py:461
  12.2 6.8 %collective-permute-start.3 = (bf16[4,32,128]{2,1,0:T(8,128)(2,1)S(1)}, bf16[4,32,128]{2,1,0:T(8,128)(2,1)S(1)}, u32[]{:S(2)}, u32[]{:S(2)}) collective-permute-start(bf16[4,32,128]{2,1,0:T(8,128)(2,1)S(1)} %get-tuple-element.38), channel_id=1, source_target_pairs={{0,1},{1,0},{2,3},{3,2},{4,5},{5,4},{6,7},{7,6},{8,9},{9,8},{10,11... | collective-permute-start | bytes 98312 | tf_op jit(solution)/shard_map/ppermute | solution.py:461
  17.1 1.9 %copy-start.2 = (bf16[8,2,128,128]{3,2,1,0:T(8,128)(2,1)S(1)}, bf16[8,2,128,128]{3,2,1,0:T(8,128)(2,1)}, u32[]{:S(2)}) copy-start(bf16[8,2,128,128]{3,2,1,0:T(8,128)(2,1)} %refs_3_.1) | copy-start | bytes 1572868

commit v12 on v10

--- a/solution.py
+++ b/solution.py
@@ -219,7 +219,6 @@
 
 def compose_kernel(axis, bit, final, mine, theirs, *refs):
     prior, sent, inner, prior_out = refs[:4] if bit > 1 else (None, *refs[:3])
-    pair = refs[-1]
     width = mine.shape[1]
     count = (mine.shape[0] - 4 * width) // 2
     near = count + width
@@ -227,51 +226,53 @@
     place = lax.rem(lax.div(me, bit), 2)
     mid = near + count
     far = near + near + width
-
-    pair[place] = mine[...]
-    pair[1 - place] = theirs[...]
-    a = pair[0]
-    b = pair[1]
-    across = mul(a[:near], jnp.concatenate([b[count:near], b[mid : mid + width]], axis=1))
-    ahead = b[:near].astype(jnp.float32)
-    joined = across[:, :width] + jnp.concatenate(
-        [ahead[:count], jnp.zeros((width, width), jnp.float32)], axis=0
-    )
-    between = across[:, width:] + jnp.concatenate(
-        [b[near:mid].astype(jnp.float32), jnp.zeros((width, width), jnp.float32)], axis=0
-    )
-    between = jnp.concatenate([narrow(between), b[mid + width : far]], axis=0)
-    first = mul(between, a[mid + width : far])
-    first = narrow(first[:near] + a[near : 2 * near].astype(jnp.float32)), narrow(first[near:])
-    joined = narrow(joined)
-    inner[:near] = a[:near]
-    inner[near:] = between
-    prior_out[...] = a[far:]
+    blank = jnp.zeros((width, width), jnp.float32)
+
+    def join(a, b):
+        sides = [b[count:near], b[mid : mid + width]]
+        across = mul(a[:near], jnp.concatenate(sides, axis=1))
+        ahead = jnp.concatenate([b[:count].astype(jnp.float32), blank], axis=0)
+        joined = narrow(across[:, :width] + ahead)
+        ahead = jnp.concatenate([b[near:mid].astype(jnp.float32), blank], axis=0)
+        between = narrow(across[:, width:] + ahead)
+        first = mul(between, a[mid + width : far]) + a[near : 2 * near].astype(jnp.float32)
+        inner[:near] = a[:near]
+        inner[near : 2 * near] = between
+        inner[2 * near :] = b[mid + width : far]
+        prior_out[...] = a[far:]
+        if final:
+            refs[-1][...] = joined[:count]
+            above = lax.rem(lax.div(me, 2 * bit), 2) == 1
+
+            @pl.when(above)
+            def _():
+                sent[...] = narrow(first)
+
+            @pl.when(jnp.logical_not(above))
+            def _():
+                sent[:count] = joined[:count]
+                sent[count:] = b[far:]
+
+        else:
+            sent[:near] = joined
+            sent[near : 2 * near] = narrow(first)
+            sent[2 * near : far] = narrow(mul(b[mid + width : far], a[mid + width : far]))
+            sent[far:] = b[far:]
+
+    @pl.when(place == 0)
+    def _():
+        join(mine, theirs)
+
+    @pl.when(place == 1)
+    def _():
+        join(theirs, mine)
+
     if prior is not None:
         lowest = jnp.logical_and(place == 1, lax.rem(me, bit) == 0)
 
         @pl.when(jnp.logical_not(lowest))
         def _():
             prior_out[...] = prior[...]
-
-    if final:
-        refs[-2][...] = joined[:count]
-        above = lax.rem(lax.div(me, 2 * bit), 2) == 1
-
-        @pl.when(above)
-        def _():
-            sent[...] = first[0]
-
-        @pl.when(jnp.logical_not(above))
-        def _():
-            sent[:count] = joined[:count]
-            sent[count:] = b[far:]
-
-    else:
-        sent[:near] = joined
-        sent[near : 2 * near] = first[0]
-        sent[2 * near : far] = first[1]
-        sent[far:] = b[far:]
 
 
 def fold_kernel(axis, levels, *refs):
@@ -317,14 +318,20 @@
     up = down + mul(own[...], theirs[count:])
     z = narrow(jnp.where(upper, down, up))
     brought[...] = z
+    values = []
     for k in range(rows):
         value = base[k] + mul(z, response[k])
         solution[k] = value
-        rounded[k] = narrow(value)
+        values.append(narrow(value))
+        rounded[k] = values[k]
     rim = near_rows.shape[0]
-    for e in range(rim):
-        near_rows[e] = rounded[(1 - side) * (rows - rim) + e]
-        far_rows[e] = rounded[side * (rows - rim) + e]
+    for odd, to_low, to_high in ((0, far_rows, near_rows), (1, near_rows, far_rows)):
+
+        @pl.when(side == odd)
+        def _(to_low=to_low, to_high=to_high):
+            for e in range(rim):
+                to_low[e] = values[e]
+                to_high[e] = values[rows - rim + e]
 
 
 def local_kernel(
@@ -406,29 +413,37 @@
             upper[k, 1:].reshape((upper_slots - 1) * width, width),
         )
     _, picked, places, _, _ = masks.shape
-    turn = places // 2 * (1 - lax.rem(lax.axis_index(axes[1]), 2))
     for k in range(rows):
         for m in range(picked):
-            at = lax.rem(halo_at[m + 1, k] + turn, places)
+            at = halo_at[m + 1, k]
             for j in range(places):
                 mask = jnp.where(at == j, 1.0, 0.0)
                 masks[k, m, j] = narrow(jnp.full((count, width), mask, jnp.float32))
     copies[3].wait()
 
 
-def halo_kernel(axis, partial, outer, inner, halo, masks, product, rim_rows):
+def halo_kernel(axis, partial, outer, inner, halo, masks, product):
     rows, slots, width, _ = halo.shape
     rim = inner.shape[0]
-    turn = rim * (1 - lax.rem(lax.axis_index(axis), 2))
-    rim_rows[:rim] = inner[...]
-    rim_rows[rim:] = outer[...]
-    for k in range(rows):
-        source = [rim_rows[lax.rem(k + turn, 2 * rim)]]
-        for m in range(1, slots):
-            source.append(sum(masks[k, m - 1, j] * rim_rows[j] for j in range(2 * rim)))
-        product[k] = partial[k] + mul(
-            jnp.concatenate(source, axis=1), halo[k].reshape(slots * width, width)
-        )
+    side = lax.rem(lax.axis_index(axis), 2)
+
+    def add(left, right):
+        rim_rows = [left[e] for e in range(rim)] + [right[e] for e in range(rim)]
+        for k in range(rows):
+            source = [rim_rows[k % (2 * rim)]]
+            for m in range(1, slots):
+                source.append(sum(masks[k, m - 1, j] * rim_rows[j] for j in range(2 * rim)))
+            product[k] = partial[k] + mul(
+                jnp.concatenate(source, axis=1), halo[k].reshape(slots * width, width)
+            )
+
+    @pl.when(side == 0)
+    def _():
+        add(outer, inner)
+
+    @pl.when(side == 1)
+    def _():
+        add(inner, outer)
 
 
 def trade(block, axis, bit):
@@ -524,7 +539,6 @@
             + (jax.ShapeDtypeStruct((count, width), bits),) * final,
             in_specs=[VMEM] * (2 + len(prior)),
             out_specs=(VMEM,) * (3 + final),
-            scratch_shapes=[pltpu.VMEM((2, segment, width), bits)],
             compiler_params=SMALL,
             name="compose",
         )(payload, theirs, *prior)
@@ -609,7 +623,6 @@
         out_shape=wide,
         in_specs=[VMEM] * 5,
         out_specs=VMEM,
-        scratch_shapes=[pltpu.VMEM((2 * RIM, count, width), bits)],
         compiler_params=SMALL,
         name="halo_product",
     )(partial, outer, inner, halo_blocks, masks)

time: 19.9 us -> 19.8 us (level)
  no operation moved by 1% of the time
where the time goes in v12:
time: 19.8 us; the launch traced here: 19.7 us
  starting transfers between devices  8.97 us (45%)
  Pallas kernels  6.8 us (34%)
  waiting for transfers between devices  3.17 us (16%)
  between operations  0.71 us (4%)
    ppermute x2, starting transfers between devices, swaps(): return lax.ppermute(block, axis, pairs)  5.5 us
    pallas_call x1, Pallas kernels, on_device(): pl.pallas_call(sweep_kernel, out_shape=(wide, jax.ShapeDtypeStruct((rows...  3.65 us
    ppermute x2, starting transfers between devices, trade(): return lax.ppermute(block, axis, [(i, i ^ bit) for i in range(count)])  3.47 us
    ppermute x2, waiting for transfers between devices, trade(): return lax.ppermute(block, axis, [(i, i ^ bit) for i in range(count)])  2.52 us
    pallas_call x1, Pallas kernels, on_device(): pl.pallas_call(local, out_shape=(wide, wide, jax.ShapeDtypeStruct(masks,...  1.22 us
    pallas_call x1, Pallas kernels, on_device(): pl.pallas_call(halo, out_shape=wide, in_specs=[VMEM] * 5, out_specs=VMEM,...  0.88 us
    ppermute x2, waiting for transfers between devices, swaps(): return lax.ppermute(block, axis, pairs)  0.65 us
    pallas_call x1, Pallas kernels, on_device(): pl.pallas_call(fold, out_shape=(wide, jax.ShapeDtypeStruct((rows, width,...  0.46 us
  transfers between devices with their start and end apart: 4, of which 3 were waited for; matrix products, arithmetic and copies ran while one was open for 0% of the time, Pallas kernels for 9%

profile of v12, /device:TPU:0, one launch (start us, length us, event | category | flops | bytes accessed | tf_op | source)
XLA Modules:
  0.0 19.7 jit_solution(11262793796723689854)
XLA Ops:
  0.6 0.0 copy-start.3
  0.6 3.6 %sweeps.1 = (f32[8,32,128]{2,1,0:T(8,128)S(1)}, bf16[9,288,128]{2,1,0:T(8,128)(2,1)S(1)}, bf16[576,128]{1,0:T(8,128)(2,1)S(1)}) custom-call(f32[8,32,128]{2,1,0:T(8,128)} %rhs_far.1, bf16[8,128,128]{2,1,0:T(8,128)(2,1)} %inverse_far.1, bf16[8,3,128,128]{3,2,1,0:T(8,128)(2,1)} %refs_8_.1, bf16[8,3,128,128]{3,2,1,0:T(8,128)(2,1)} %refs_9_.1, s32[3,8]{1,0:T(4,128)} %bitcast.3, ...), custom_call_target="tpu_custom_call" | custom-call | tf_op jit(solution)/shard_map/sweeps/pallas_call | solution.py:485
  4.3 0.0 copy-start
  4.3 0.0 copy-start.1
  4.3 0.5 %collective-permute-start = (bf16[576,128]{1,0:T(8,128)(2,1)S(1)}, bf16[576,128]{1,0:T(8,128)(2,1)S(1)}, u32[]{:S(2)}, u32[]{:S(2)}) collective-permute-start(bf16[576,128]{1,0:T(8,128)(2,1)S(1)} %get-tuple-element.21.refs_0_), channel_id=1, source_target_pairs={{0,8},{8,0},{16,24},{24,16},{1,9},{9,1},{17,25},{25,17},{2,10},{10... | collective-permute-start | bytes 442376 | tf_op jit(solution)/shard_map/ppermute | solution.py:451
  4.8 1.0 %collective-permute-done.refs_1_ = bf16[576,128]{1,0:T(8,128)(2,1)S(1)} collective-permute-done((bf16[576,128]{1,0:T(8,128)(2,1)S(1)}, bf16[576,128]{1,0:T(8,128)(2,1)S(1)}, u32[]{:S(2)}, u32[]{:S(2)}) %collective-permute-start) | collective-permute-done | bytes 147488 | tf_op jit(solution)/shard_map/ppermute | solution.py:451
  5.8 0.3 %compose.1 = (bf16[160,128]{1,0:T(8,128)(2,1)S(1)}, bf16[448,128]{1,0:T(8,128)(2,1)S(1)}, bf16[128,128]{1,0:T(8,128)(2,1)S(1)}, bf16[32,128]{1,0:T(8,128)(2,1)S(1)}) custom-call(bf16[576,128]{1,0:T(8,128)(2,1)S(1)} %get-tuple-element.21.refs_0_, bf16[576,128]{1,0:T(8,128)(2,1)S(1)} %collective-permute-done.refs_1_), custom_call_target="tpu_custom_call" | custom-call | tf_op jit(solution)/shard_map/compose/pallas_call | solution.py:532
  6.1 3.0 %collective-permute-start.1 = (bf16[160,128]{1,0:T(8,128)(2,1)S(1)}, bf16[160,128]{1,0:T(8,128)(2,1)S(1)}, u32[]{:S(2)}, u32[]{:S(2)}) collective-permute-start(bf16[160,128]{1,0:T(8,128)(2,1)S(1)} %get-tuple-element.23), channel_id=1, source_target_pairs={{0,16},{8,24},{16,0},{24,8},{1,17},{9,25},{17,1},{25,9},{2,18},{10... | collective-permute-start | bytes 122888 | tf_op jit(solution)/shard_map/ppermute | solution.py:451
  9.1 0.5 %fold.1 = (f32[8,32,128]{2,1,0:T(8,128)S(1)}, bf16[8,128,128]{2,1,0:T(8,128)(2,1)S(1)}, bf16[160,128]{1,0:T(8,128)(2,1)S(1)}, bf16[160,128]{1,0:T(8,128)(2,1)S(1)}) custom-call(f32[8,32,128]{2,1,0:T(8,128)S(1)} %get-tuple-element.24.refs_0_, bf16[9,288,128]{2,1,0:T(8,128)(2,1)S(1)} %get-tuple-element.25.refs_1_, bf16[448,128]{1,0:T(8,128)(2,1)S(1)} %get-tuple-element.26.refs_2_), custom_call_target="tpu_custom_call" | custom-call | tf_op jit(solution)/shard_map/fold/pallas_call | solution.py:552
  9.6 1.5 %collective-permute-done.1.refs_1_.refs_5_ = bf16[160,128]{1,0:T(8,128)(2,1)S(1)} collective-permute-done((bf16[160,128]{1,0:T(8,128)(2,1)S(1)}, bf16[160,128]{1,0:T(8,128)(2,1)S(1)}, u32[]{:S(2)}, u32[]{:S(2)}) %collective-permute-start.1) | collective-permute-done | bytes 40992 | tf_op jit(solution)/shard_map/ppermute | solution.py:451
  11.1 0.3 %chain.1 = (f32[8,32,128]{2,1,0:T(8,128)S(1)}, bf16[8,32,128]{2,1,0:T(8,128)(2,1)S(1)}, bf16[32,128]{1,0:T(8,128)(2,1)S(1)}, bf16[4,32,128]{2,1,0:T(8,128)(2,1)S(1)}, bf16[4,32,128]{2,1,0:T(8,128)(2,1)S(1)}) custom-call(bf16[32,128]{1,0:T(8,128)(2,1)S(1)} %get-tuple-element.22.refs_0_, bf16[160,128]{1,0:T(8,128)(2,1)S(1)} %collective-permute-done.1.refs_1_.refs_5_, ...), custom_call_target="tpu_custom_call" | custom-call | tf_op jit(solution)/shard_map/chain/pallas_call | solution.py:569
  11.4 0.7 %collective-permute-start.2 = (bf16[4,32,128]{2,1,0:T(8,128)(2,1)S(1)}, bf16[4,32,128]{2,1,0:T(8,128)(2,1)S(1)}, u32[]{:S(2)}, u32[]{:S(2)}) collective-permute-start(bf16[4,32,128]{2,1,0:T(8,128)(2,1)S(1)} %get-tuple-element.37), channel_id=1, source_target_pairs={{1,2},{2,1},{3,4},{4,3},{5,6},{6,5},{9,10},{10,9},{11,12},{12,11},... | collective-permute-start | bytes 98312 | tf_op jit(solution)/shard_map/ppermute | solution.py:459
  12.0 4.8 %collective-permute-start.3 = (bf16[4,32,128]{2,1,0:T(8,128)(2,1)S(1)}, bf16[4,32,128]{2,1,0:T(8,128)(2,1)S(1)}, u32[]{:S(2)}, u32[]{:S(2)}) collective-permute-start(bf16[4,32,128]{2,1,0:T(8,128)(2,1)S(1)} %get-tuple-element.38), channel_id=1, source_target_pairs={{0,1},{1,0},{2,3},{3,2},{4,5},{5,4},{6,7},{7,6},{8,9},{9,8},{10,11... | collective-permute-start | bytes 98312 | tf_op jit(solution)/shard_map/ppermute | solution.py:459
  16.9 0.0 copy-done.3
  16.9 0.0 copy-done
  16.9 0.0 copy-done.1
  16.9 0.0 copy-start.2
  16.9 1.2 %local_product.1 = (f32[8,32,128]{2,1,0:T(8,128)S(1)}, f32[8,32,128]{2,1,0:T(8,128)}, bf16[8,1,8,32,128]{4,3,2,1,0:T(8,128)(2,1)S(1)}) custom-call(bf16[8,32,128]{2,1,0:T(8,128)(2,1)S(1)} %get-tuple-element.29.refs_0_, bf16[32,128]{1,0:T(8,128)(2,1)S(1)} %get-tuple-element.30.refs_1_, bf16[160,128]{1,0:T(8,128)(2,1)S(1)} %get-tuple-element.31.refs_2_, ...), custom_call_target="tpu_custom_call" | custom-call | tf_op jit(solution)/shard_map/local_product/pallas_call | solution.py:591
  18.1 0.0 collective-permute-done.2.refs_1_
  18.1 0.6 %collective-permute-done.3.refs_2_ = bf16[4,32,128]{2,1,0:T(8,128)(2,1)S(1)} collective-permute-done((bf16[4,32,128]{2,1,0:T(8,128)(2,1)S(1)}, bf16[4,32,128]{2,1,0:T(8,128)(2,1)S(1)}, u32[]{:S(2)}, u32[]{:S(2)}) %collective-permute-start.3) | collective-permute-done | bytes 32800 | tf_op jit(solution)/shard_map/ppermute | solution.py:459
  18.8 0.0 copy-done.2
  18.8 0.9 %halo_product.1 = f32[8,32,128]{2,1,0:T(8,128)} custom-call(f32[8,32,128]{2,1,0:T(8,128)S(1)} %get-tuple-element.36.refs_0_, bf16[4,32,128]{2,1,0:T(8,128)(2,1)S(1)} %collective-permute-done.2.refs_1_, bf16[4,32,128]{2,1,0:T(8,128)(2,1)S(1)} %collective-permute-done.3.refs_2_, bf16[8,2,128,128]{3,2,1,0:T(8,128)(2,1)S(1)} %copy-done.2, ...), custom_call_target="tpu_custom_call" | custom-call | tf_op jit(solution)/shard_map/halo_product/pallas_call | solution.py:621
Async XLA Ops:
  0.6 16.3 %copy-start.3 = (bf16[8,128,128]{2,1,0:T(8,128)(2,1)S(1)}, bf16[8,128,128]{2,1,0:T(8,128)(2,1)}, u32[]{:S(2)}) copy-start(bf16[8,128,128]{2,1,0:T(8,128)(2,1)} %refs_7_.1) | copy-start | bytes 786436
  4.3 12.6 %copy-start = (bf16[8,3,128,128]{3,2,1,0:T(8,128)(2,1)S(1)}, bf16[8,3,128,128]{3,2,1,0:T(8,128)(2,1)}, u32[]{:S(2)}) copy-start(bf16[8,3,128,128]{3,2,1,0:T(8,128)(2,1)} %refs_8_.1) | copy-start | bytes 2359300
  4.3 12.6 %copy-start.1 = (bf16[8,3,128,128]{3,2,1,0:T(8,128)(2,1)S(1)}, bf16[8,3,128,128]{3,2,1,0:T(8,128)(2,1)}, u32[]{:S(2)}) copy-start(bf16[8,3,128,128]{3,2,1,0:T(8,128)(2,1)} %refs_9_.1) | copy-start | bytes 2359300
  4.3 1.5 %collective-permute-start = (bf16[576,128]{1,0:T(8,128)(2,1)S(1)}, bf16[576,128]{1,0:T(8,128)(2,1)S(1)}, u32[]{:S(2)}, u32[]{:S(2)}) collective-permute-start(bf16[576,128]{1,0:T(8,128)(2,1)S(1)} %get-tuple-element.21.refs_0_), channel_id=1, source_target_pairs={{0,8},{8,0},{16,24},{24,16},{1,9},{9,1},{17,25},{25,17},{2,10},{10... | collective-permute-start | bytes 442376 | tf_op jit(solution)/shard_map/ppermute | solution.py:451
  6.1 4.9 %collective-permute-start.1 = (bf16[160,128]{1,0:T(8,128)(2,1)S(1)}, bf16[160,128]{1,0:T(8,128)(2,1)S(1)}, u32[]{:S(2)}, u32[]{:S(2)}) collective-permute-start(bf16[160,128]{1,0:T(8,128)(2,1)S(1)} %get-tuple-element.23), channel_id=1, source_target_pairs={{0,16},{8,24},{16,0},{24,8},{1,17},{9,25},{17,1},{25,9},{2,18},{10... | collective-permute-start | bytes 122888 | tf_op jit(solution)/shard_map/ppermute | solution.py:451
  11.4 6.8 %collective-permute-start.2 = (bf16[4,32,128]{2,1,0:T(8,128)(2,1)S(1)}, bf16[4,32,128]{2,1,0:T(8,128)(2,1)S(1)}, u32[]{:S(2)}, u32[]{:S(2)}) collective-permute-start(bf16[4,32,128]{2,1,0:T(8,128)(2,1)S(1)} %get-tuple-element.37), channel_id=1, source_target_pairs={{1,2},{2,1},{3,4},{4,3},{5,6},{6,5},{9,10},{10,9},{11,12},{12,11},... | collective-permute-start | bytes 98312 | tf_op jit(solution)/shard_map/ppermute | solution.py:459
  12.0 6.7 %collective-permute-start.3 = (bf16[4,32,128]{2,1,0:T(8,128)(2,1)S(1)}, bf16[4,32,128]{2,1,0:T(8,128)(2,1)S(1)}, u32[]{:S(2)}, u32[]{:S(2)}) collective-permute-start(bf16[4,32,128]{2,1,0:T(8,128)(2,1)S(1)} %get-tuple-element.38), channel_id=1, source_target_pairs={{0,1},{1,0},{2,3},{3,2},{4,5},{5,4},{6,7},{7,6},{8,9},{9,8},{10,11... | collective-permute-start | bytes 98312 | tf_op jit(solution)/shard_map/ppermute | solution.py:459
  16.9 1.9 %copy-start.2 = (bf16[8,2,128,128]{3,2,1,0:T(8,128)(2,1)S(1)}, bf16[8,2,128,128]{3,2,1,0:T(8,128)(2,1)}, u32[]{:S(2)}) copy-start(bf16[8,2,128,128]{3,2,1,0:T(8,128)(2,1)} %refs_3_.1) | copy-start | bytes 1572868

commit v13 on v12

--- a/solution.py
+++ b/solution.py
@@ -278,7 +278,10 @@
 def fold_kernel(axis, levels, *refs):
     base, response = refs[:2]
     inner = refs[2 : 1 + levels]
-    folded, folded_response, inflow_map, outflow_map = refs[1 + levels :]
+    diagonal_far, folded, folded_response, inflow_map, outflow_map = refs[1 + levels : 6 + levels]
+    diagonal, arrived = refs[6 + levels :]
+    copy = pltpu.make_async_copy(diagonal_far, diagonal, arrived)
+    copy.start()
     rows, count, width = base.shape
     near = count + width
     me = lax.axis_index(axis)
@@ -306,6 +309,7 @@
         value = mul(both, response[k, count:])
         folded[k] = base[k] + value[:count]
         folded_response[k] = narrow(value[count:])
+    copy.wait()
 
 
 def chain_kernel(
@@ -549,19 +553,21 @@
     def fold(*refs):
         fold_kernel("section", levels, *refs)
 
-    base, response, inflow_map, outflow_map = pl.pallas_call(
+    base, response, inflow_map, outflow_map, diagonal = pl.pallas_call(
         fold,
         out_shape=(
             wide,
             jax.ShapeDtypeStruct((rows, width, width), bits),
             jax.ShapeDtypeStruct((near, width), bits),
             jax.ShapeDtypeStruct((near, width), bits),
+            jax.ShapeDtypeStruct(diag_blocks.shape, diag_blocks.dtype),
         ),
-        in_specs=[VMEM] * (1 + levels),
-        out_specs=(VMEM,) * 4,
+        in_specs=[VMEM] * (1 + levels) + [HBM],
+        out_specs=(VMEM,) * 5,
+        scratch_shapes=[pltpu.SemaphoreType.DMA(())],
         compiler_params=SMALL,
         name="fold",
-    )(base, response, *inner)
+    )(base, response, *inner, pltpu.with_memory_space_constraint(diag_blocks, pltpu.HBM))
 
     def chain(*refs):
         chain_kernel(("section", "dom"), levels, *refs)
@@ -609,7 +615,7 @@
         prior,
         theirs,
         solved,
-        diag_blocks,
+        diagonal,
         lower_blocks,
         upper_blocks,
         *indices,

time: 19.8 us -> 19.8 us (level)
  waiting for transfers between devices: 3.17 us -> 2.55 us
  Pallas kernels: 6.8 us -> 7.37 us
    ppermute x2, waiting for transfers between devices: 2.52 us -> 1.89 us  [trade(): return lax.ppermute(block, axis, [(i, i ^ bit) for i in range(count)])]
    pallas_call x1, Pallas kernels: 0.46 us -> 1.09 us  [on_device(): pl.pallas_call(fold, out_shape=(wide, jax.ShapeDtypeStruct((rows, width,...]
  transfers between devices with their start and end apart: 4 -> 4, of which waited for: 3 -> 3; matrix products, arithmetic and copies ran while one was open for 0% -> 0% of each run, Pallas kernels for 9% -> 12%
where the time goes in v13:
time: 19.8 us; the launch traced here: 19.6 us
  starting transfers between devices  8.97 us (45%)
  Pallas kernels  7.37 us (37%)
  waiting for transfers between devices  2.55 us (13%)
  between operations  0.69 us (3%)
    ppermute x2, starting transfers between devices, swaps(): return lax.ppermute(block, axis, pairs)  5.5 us
    pallas_call x1, Pallas kernels, on_device(): pl.pallas_call(sweep_kernel, out_shape=(wide, jax.ShapeDtypeStruct((rows...  3.61 us
    ppermute x2, starting transfers between devices, trade(): return lax.ppermute(block, axis, [(i, i ^ bit) for i in range(count)])  3.47 us
    ppermute x2, waiting for transfers between devices, trade(): return lax.ppermute(block, axis, [(i, i ^ bit) for i in range(count)])  1.89 us
    pallas_call x1, Pallas kernels, on_device(): pl.pallas_call(local, out_shape=(wide, wide, jax.ShapeDtypeStruct(masks,...  1.21 us
    pallas_call x1, Pallas kernels, on_device(): pl.pallas_call(fold, out_shape=(wide, jax.ShapeDtypeStruct((rows, width,...  1.09 us
    pallas_call x1, Pallas kernels, on_device(): pl.pallas_call(halo, out_shape=wide, in_specs=[VMEM] * 5, out_specs=VMEM,...  0.88 us
    ppermute x2, waiting for transfers between devices, swaps(): return lax.ppermute(block, axis, pairs)  0.66 us
  transfers between devices with their start and end apart: 4, of which 3 were waited for; matrix products, arithmetic and copies ran while one was open for 0% of the time, Pallas kernels for 12%

profile of v13, /device:TPU:0, one launch (start us, length us, event | category | flops | bytes accessed | tf_op | source)
XLA Modules:
  0.0 19.6 jit_solution(4779172249625791022)
XLA Ops:
  0.6 3.6 %sweeps.1 = (f32[8,32,128]{2,1,0:T(8,128)S(1)}, bf16[9,288,128]{2,1,0:T(8,128)(2,1)S(1)}, bf16[576,128]{1,0:T(8,128)(2,1)S(1)}) custom-call(f32[8,32,128]{2,1,0:T(8,128)} %rhs_far.1, bf16[8,128,128]{2,1,0:T(8,128)(2,1)} %inverse_far.1, bf16[8,3,128,128]{3,2,1,0:T(8,128)(2,1)} %refs_8_.1, bf16[8,3,128,128]{3,2,1,0:T(8,128)(2,1)} %refs_9_.1, s32[3,8]{1,0:T(4,128)} %bitcast.3, ...), custom_call_target="tpu_custom_call" | custom-call | tf_op jit(solution)/shard_map/sweeps/pallas_call | solution.py:489
  4.2 0.5 %collective-permute-start = (bf16[576,128]{1,0:T(8,128)(2,1)S(1)}, bf16[576,128]{1,0:T(8,128)(2,1)S(1)}, u32[]{:S(2)}, u32[]{:S(2)}) collective-permute-start(bf16[576,128]{1,0:T(8,128)(2,1)S(1)} %get-tuple-element.22.refs_0_), channel_id=1, source_target_pairs={{0,8},{8,0},{16,24},{24,16},{1,9},{9,1},{17,25},{25,17},{2,10},{10... | collective-permute-start | bytes 442376 | tf_op jit(solution)/shard_map/ppermute | solution.py:455
  4.8 1.0 %collective-permute-done.refs_1_ = bf16[576,128]{1,0:T(8,128)(2,1)S(1)} collective-permute-done((bf16[576,128]{1,0:T(8,128)(2,1)S(1)}, bf16[576,128]{1,0:T(8,128)(2,1)S(1)}, u32[]{:S(2)}, u32[]{:S(2)}) %collective-permute-start) | collective-permute-done | bytes 147488 | tf_op jit(solution)/shard_map/ppermute | solution.py:455
  5.8 0.3 %compose.1 = (bf16[160,128]{1,0:T(8,128)(2,1)S(1)}, bf16[448,128]{1,0:T(8,128)(2,1)S(1)}, bf16[128,128]{1,0:T(8,128)(2,1)S(1)}, bf16[32,128]{1,0:T(8,128)(2,1)S(1)}) custom-call(bf16[576,128]{1,0:T(8,128)(2,1)S(1)} %get-tuple-element.22.refs_0_, bf16[576,128]{1,0:T(8,128)(2,1)S(1)} %collective-permute-done.refs_1_), custom_call_target="tpu_custom_call" | custom-call | tf_op jit(solution)/shard_map/compose/pallas_call | solution.py:536
  6.1 3.0 %collective-permute-start.1 = (bf16[160,128]{1,0:T(8,128)(2,1)S(1)}, bf16[160,128]{1,0:T(8,128)(2,1)S(1)}, u32[]{:S(2)}, u32[]{:S(2)}) collective-permute-start(bf16[160,128]{1,0:T(8,128)(2,1)S(1)} %get-tuple-element.24), channel_id=1, source_target_pairs={{0,16},{8,24},{16,0},{24,8},{1,17},{9,25},{17,1},{25,9},{2,18},{10... | collective-permute-start | bytes 122888 | tf_op jit(solution)/shard_map/ppermute | solution.py:455
  9.0 0.0 copy-start
  9.0 0.0 copy-start.1
  9.0 1.1 %fold.1 = (f32[8,32,128]{2,1,0:T(8,128)S(1)}, bf16[8,128,128]{2,1,0:T(8,128)(2,1)S(1)}, bf16[160,128]{1,0:T(8,128)(2,1)S(1)}, bf16[160,128]{1,0:T(8,128)(2,1)S(1)}, bf16[8,128,128]{2,1,0:T(8,128)(2,1)S(1)}) custom-call(f32[8,32,128]{2,1,0:T(8,128)S(1)} %get-tuple-element.25.refs_0_, bf16[9,288,128]{2,1,0:T(8,128)(2,1)S(1)} %get-tuple-element.26.refs_1_, ...), custom_call_target="tpu_custom_call" | custom-call | tf_op jit(solution)/shard_map/fold/pallas_call | solution.py:556
  10.1 0.9 %collective-permute-done.1.refs_1_.refs_5_ = bf16[160,128]{1,0:T(8,128)(2,1)S(1)} collective-permute-done((bf16[160,128]{1,0:T(8,128)(2,1)S(1)}, bf16[160,128]{1,0:T(8,128)(2,1)S(1)}, u32[]{:S(2)}, u32[]{:S(2)}) %collective-permute-start.1) | collective-permute-done | bytes 40992 | tf_op jit(solution)/shard_map/ppermute | solution.py:455
  11.0 0.3 %chain.1 = (f32[8,32,128]{2,1,0:T(8,128)S(1)}, bf16[8,32,128]{2,1,0:T(8,128)(2,1)S(1)}, bf16[32,128]{1,0:T(8,128)(2,1)S(1)}, bf16[4,32,128]{2,1,0:T(8,128)(2,1)S(1)}, bf16[4,32,128]{2,1,0:T(8,128)(2,1)S(1)}) custom-call(bf16[32,128]{1,0:T(8,128)(2,1)S(1)} %get-tuple-element.23.refs_0_, bf16[160,128]{1,0:T(8,128)(2,1)S(1)} %collective-permute-done.1.refs_1_.refs_5_, ...), custom_call_target="tpu_custom_call" | custom-call | tf_op jit(solution)/shard_map/chain/pallas_call | solution.py:575
  11.3 0.7 %collective-permute-start.2 = (bf16[4,32,128]{2,1,0:T(8,128)(2,1)S(1)}, bf16[4,32,128]{2,1,0:T(8,128)(2,1)S(1)}, u32[]{:S(2)}, u32[]{:S(2)}) collective-permute-start(bf16[4,32,128]{2,1,0:T(8,128)(2,1)S(1)} %get-tuple-element.39), channel_id=1, source_target_pairs={{1,2},{2,1},{3,4},{4,3},{5,6},{6,5},{9,10},{10,9},{11,12},{12,11},... | collective-permute-start | bytes 98312 | tf_op jit(solution)/shard_map/ppermute | solution.py:463
  12.0 4.8 %collective-permute-start.3 = (bf16[4,32,128]{2,1,0:T(8,128)(2,1)S(1)}, bf16[4,32,128]{2,1,0:T(8,128)(2,1)S(1)}, u32[]{:S(2)}, u32[]{:S(2)}) collective-permute-start(bf16[4,32,128]{2,1,0:T(8,128)(2,1)S(1)} %get-tuple-element.40), channel_id=1, source_target_pairs={{0,1},{1,0},{2,3},{3,2},{4,5},{5,4},{6,7},{7,6},{8,9},{9,8},{10,11... | collective-permute-start | bytes 98312 | tf_op jit(solution)/shard_map/ppermute | solution.py:463
  16.8 0.0 copy-done
  16.8 0.0 copy-done.1
  16.8 0.0 copy-start.2
  16.8 1.2 %local_product.1 = (f32[8,32,128]{2,1,0:T(8,128)S(1)}, f32[8,32,128]{2,1,0:T(8,128)}, bf16[8,1,8,32,128]{4,3,2,1,0:T(8,128)(2,1)S(1)}) custom-call(bf16[8,32,128]{2,1,0:T(8,128)(2,1)S(1)} %get-tuple-element.30.refs_0_, bf16[32,128]{1,0:T(8,128)(2,1)S(1)} %get-tuple-element.31.refs_1_, bf16[160,128]{1,0:T(8,128)(2,1)S(1)} %get-tuple-element.32.refs_2_, ...), custom_call_target="tpu_custom_call" | custom-call | tf_op jit(solution)/shard_map/local_product/pallas_call | solution.py:597
  18.0 0.0 collective-permute-done.2.refs_1_
  18.0 0.7 %collective-permute-done.3.refs_2_ = bf16[4,32,128]{2,1,0:T(8,128)(2,1)S(1)} collective-permute-done((bf16[4,32,128]{2,1,0:T(8,128)(2,1)S(1)}, bf16[4,32,128]{2,1,0:T(8,128)(2,1)S(1)}, u32[]{:S(2)}, u32[]{:S(2)}) %collective-permute-start.3) | collective-permute-done | bytes 32800 | tf_op jit(solution)/shard_map/ppermute | solution.py:463
  18.7 0.0 copy-done.2
  18.7 0.9 %halo_product.1 = f32[8,32,128]{2,1,0:T(8,128)} custom-call(f32[8,32,128]{2,1,0:T(8,128)S(1)} %get-tuple-element.38.refs_0_, bf16[4,32,128]{2,1,0:T(8,128)(2,1)S(1)} %collective-permute-done.2.refs_1_, bf16[4,32,128]{2,1,0:T(8,128)(2,1)S(1)} %collective-permute-done.3.refs_2_, bf16[8,2,128,128]{3,2,1,0:T(8,128)(2,1)S(1)} %copy-done.2, ...), custom_call_target="tpu_custom_call" | custom-call | tf_op jit(solution)/shard_map/halo_product/pallas_call | solution.py:627
Async XLA Ops:
  4.2 1.5 %collective-permute-start = (bf16[576,128]{1,0:T(8,128)(2,1)S(1)}, bf16[576,128]{1,0:T(8,128)(2,1)S(1)}, u32[]{:S(2)}, u32[]{:S(2)}) collective-permute-start(bf16[576,128]{1,0:T(8,128)(2,1)S(1)} %get-tuple-element.22.refs_0_), channel_id=1, source_target_pairs={{0,8},{8,0},{16,24},{24,16},{1,9},{9,1},{17,25},{25,17},{2,10},{10... | collective-permute-start | bytes 442376 | tf_op jit(solution)/shard_map/ppermute | solution.py:455
  6.1 4.9 %collective-permute-start.1 = (bf16[160,128]{1,0:T(8,128)(2,1)S(1)}, bf16[160,128]{1,0:T(8,128)(2,1)S(1)}, u32[]{:S(2)}, u32[]{:S(2)}) collective-permute-start(bf16[160,128]{1,0:T(8,128)(2,1)S(1)} %get-tuple-element.24), channel_id=1, source_target_pairs={{0,16},{8,24},{16,0},{24,8},{1,17},{9,25},{17,1},{25,9},{2,18},{10... | collective-permute-start | bytes 122888 | tf_op jit(solution)/shard_map/ppermute | solution.py:455
  9.0 7.8 %copy-start = (bf16[8,3,128,128]{3,2,1,0:T(8,128)(2,1)S(1)}, bf16[8,3,128,128]{3,2,1,0:T(8,128)(2,1)}, u32[]{:S(2)}) copy-start(bf16[8,3,128,128]{3,2,1,0:T(8,128)(2,1)} %refs_8_.1) | copy-start | bytes 2359300
  9.0 7.8 %copy-start.1 = (bf16[8,3,128,128]{3,2,1,0:T(8,128)(2,1)S(1)}, bf16[8,3,128,128]{3,2,1,0:T(8,128)(2,1)}, u32[]{:S(2)}) copy-start(bf16[8,3,128,128]{3,2,1,0:T(8,128)(2,1)} %refs_9_.1) | copy-start | bytes 2359300
  11.3 6.7 %collective-permute-start.2 = (bf16[4,32,128]{2,1,0:T(8,128)(2,1)S(1)}, bf16[4,32,128]{2,1,0:T(8,128)(2,1)S(1)}, u32[]{:S(2)}, u32[]{:S(2)}) collective-permute-start(bf16[4,32,128]{2,1,0:T(8,128)(2,1)S(1)} %get-tuple-element.39), channel_id=1, source_target_pairs={{1,2},{2,1},{3,4},{4,3},{5,6},{6,5},{9,10},{10,9},{11,12},{12,11},... | collective-permute-start | bytes 98312 | tf_op jit(solution)/shard_map/ppermute | solution.py:463
  12.0 6.7 %collective-permute-start.3 = (bf16[4,32,128]{2,1,0:T(8,128)(2,1)S(1)}, bf16[4,32,128]{2,1,0:T(8,128)(2,1)S(1)}, u32[]{:S(2)}, u32[]{:S(2)}) collective-permute-start(bf16[4,32,128]{2,1,0:T(8,128)(2,1)S(1)} %get-tuple-element.40), channel_id=1, source_target_pairs={{0,1},{1,0},{2,3},{3,2},{4,5},{5,4},{6,7},{7,6},{8,9},{9,8},{10,11... | collective-permute-start | bytes 98312 | tf_op jit(solution)/shard_map/ppermute | solution.py:463
  16.8 1.9 %copy-start.2 = (bf16[8,2,128,128]{3,2,1,0:T(8,128)(2,1)S(1)}, bf16[8,2,128,128]{3,2,1,0:T(8,128)(2,1)}, u32[]{:S(2)}) copy-start(bf16[8,2,128,128]{3,2,1,0:T(8,128)(2,1)} %refs_3_.3) | copy-start | bytes 1572868

commit v14 on v13

--- a/solution.py
+++ b/solution.py
@@ -30,6 +30,7 @@
     upper_at_far,
     base,
     response,
+    free,
     payload,
     rhs,
     inverse,
@@ -71,12 +72,12 @@
         == lax.broadcasted_iota(jnp.int32, (width, width), 1)
     )
     down[:, :count] = jnp.zeros((rows + 1, count, width), jnp.bfloat16)
-    response[:, :near] = jnp.zeros((rows + 1, near, width), jnp.bfloat16)
+    response[...] = jnp.zeros(response.shape, jnp.bfloat16)
     for k in range(rows):
         down[k, count:] = eye
-        response[k, near:] = eye
+        free[k] = eye
     down[rows, count:] = jnp.zeros_like(eye)
-    response[rows, near:] = jnp.zeros_like(eye)
+    free[rows] = jnp.zeros_like(eye)
 
     def piece(blocks, m):
         return blocks[m * width : (m + 1) * width]
@@ -172,24 +173,27 @@
             fixed[b] = free_b
         return links
 
+    def step_up(p, held, of_a, of_b):
+        a = last - 2 * p
+        b = a - 1
+        if p > 0:
+            first = mul(sources(held, upper_at, a, None, upper_slots), upp_pair[p])
+            second = mul(sources(held, upper_at, b, a, upper_slots), upp_second[p])
+            of_a = of_a - first[:, :width]
+            of_b = of_b + first[:, width:] - second
+        held[a] = narrow(of_a)
+        held[b] = narrow(of_b)
+        return of_a, of_b
+
+    def go_free(p):
+        a = last - 2 * p
+        step_up(p, free, fixed[a], fixed[a - 1])
+
     def go_up(p, passed):
         a = last - 2 * p
-        b = a - 1
-        of_a = exact[a]
-        of_b = exact[b] - passed
-        free_a = fixed[a]
-        free_b = fixed[b]
-        if p > 0:
-            first = mul(sources(response, upper_at, a, None, upper_slots), upp_pair[p])
-            second = mul(sources(response, upper_at, b, a, upper_slots), upp_second[p])
-            of_a = of_a - first[:near, :width]
-            of_b = of_b + first[:near, width:] - second[:near]
-            free_a = free_a - first[near:, :width]
-            free_b = free_b + first[near:, width:] - second[near:]
-        for k, value, free in ((a, of_a, free_a), (b, of_b, free_b)):
-            base[k] = value[:count]
-            response[k, :near] = narrow(value)
-            response[k, near:] = narrow(free)
+        of_a, of_b = step_up(p, response, exact[a], exact[a - 1] - passed)
+        base[a] = of_a[:count]
+        base[a - 1] = of_b[:count]
 
     pairs = rows // 2
     for copy in copies[:4]:
@@ -199,22 +203,30 @@
     for copy in copies[4:]:
         copy.wait()
     links = []
+    freed = 0
     for p in range(1, pairs):
         if p % 2 == 1 and p + 1 < pairs:
             ready_down(p + 1)
         go_down(p)
+        while freed < len(links):
+            go_free(freed)
+            freed += 1
         if p % 2 == 1:
             links += ready_up(p - 1)
     far = near + width
     payload[:near] = down[last]
-    for p in range(0, pairs, 2):
+    for p in range(pairs):
         a = last - 2 * p
-        passed = apart(down[a], down[a - 2], links[p], links[p + 1])
-        go_up(p, passed[:, :width])
-        go_up(p + 1, passed[:, width:])
-
-    payload[near + far :] = response[last, near:]
-    payload[near : near + far] = response[0]
+        if p % 2 == 0:
+            passed = apart(down[a], down[a - 2], links[p], links[p + 1])
+        go_up(p, passed[:, width * (p % 2) : width * (p % 2 + 1)])
+        if freed < pairs:
+            go_free(freed)
+            freed += 1
+
+    payload[near + far :] = free[last]
+    payload[2 * near : near + far] = free[0]
+    payload[near : 2 * near] = response[0]
 
 
 def compose_kernel(axis, bit, final, mine, theirs, *refs):
@@ -276,10 +288,10 @@
 
 
 def fold_kernel(axis, levels, *refs):
-    base, response = refs[:2]
-    inner = refs[2 : 1 + levels]
-    diagonal_far, folded, folded_response, inflow_map, outflow_map = refs[1 + levels : 6 + levels]
-    diagonal, arrived = refs[6 + levels :]
+    base, response, free = refs[:3]
+    inner = refs[3 : 2 + levels]
+    diagonal_far, folded, folded_response, inflow_map, outflow_map = refs[2 + levels : 7 + levels]
+    diagonal, arrived = refs[7 + levels :]
     copy = pltpu.make_async_copy(diagonal_far, diagonal, arrived)
     copy.start()
     rows, count, width = base.shape
@@ -306,7 +318,7 @@
     outflow_map[...] = narrow(outflow)
     both = narrow(jnp.concatenate([inflow, outflow], axis=1))
     for k in range(rows):
-        value = mul(both, response[k, count:])
+        value = mul(both, jnp.concatenate([response[k, count:], free[k]], axis=0))
         folded[k] = base[k] + value[:count]
         folded_response[k] = narrow(value[count:])
     copy.wait()
@@ -486,15 +498,16 @@
     indices = [
         pltpu.with_memory_space_constraint(a, pltpu.HBM) for a in (lower_at, upper_at, halo_at)
     ]
-    base, response, payload = pl.pallas_call(
+    base, response, free, payload = pl.pallas_call(
         sweep_kernel,
         out_shape=(
             wide,
-            jax.ShapeDtypeStruct((rows + 1, far, width), jnp.bfloat16),
+            jax.ShapeDtypeStruct((rows + 1, near, width), jnp.bfloat16),
+            jax.ShapeDtypeStruct((rows + 1, width, width), jnp.bfloat16),
             jax.ShapeDtypeStruct((near + far + width, width), jnp.bfloat16),
         ),
         in_specs=[HBM] * 6,
-        out_specs=(VMEM,) * 3,
+        out_specs=(VMEM,) * 4,
         scratch_shapes=[
             pltpu.VMEM(right_sides.shape, right_sides.dtype),
             pltpu.VMEM(diag_inverse.shape, diag_inverse.dtype),
@@ -562,12 +575,12 @@
             jax.ShapeDtypeStruct((near, width), bits),
             jax.ShapeDtypeStruct(diag_blocks.shape, diag_blocks.dtype),
         ),
-        in_specs=[VMEM] * (1 + levels) + [HBM],
+        in_specs=[VMEM] * (2 + levels) + [HBM],
         out_specs=(VMEM,) * 5,
         scratch_shapes=[pltpu.SemaphoreType.DMA(())],
         compiler_params=SMALL,
         name="fold",
-    )(base, response, *inner, pltpu.with_memory_space_constraint(diag_blocks, pltpu.HBM))
+    )(base, response, free, *inner, pltpu.with_memory_space_constraint(diag_blocks, pltpu.HBM))
 
     def chain(*refs):
         chain_kernel(("section", "dom"), levels, *refs)

time: 19.8 us -> 20.1 us (1.015)
  Pallas kernels: 7.37 us -> 7.71 us
    pallas_call x1, Pallas kernels: 3.61 us -> 3.95 us  [on_device(): pl.pallas_call(sweep_kernel, out_shape=(wide, jax.ShapeDtypeStruct((rows...]
where the time goes in v14:
time: 20.1 us; the launch traced here: 19.9 us
  starting transfers between devices  8.97 us (45%)
  Pallas kernels  7.71 us (38%)
  waiting for transfers between devices  2.55 us (13%)
  between operations  0.69 us (3%)
    ppermute x2, starting transfers between devices, swaps(): return lax.ppermute(block, axis, pairs)  5.5 us
    pallas_call x1, Pallas kernels, on_device(): pl.pallas_call(sweep_kernel, out_shape=(wide, jax.ShapeDtypeStruct((rows...  3.95 us
    ppermute x2, starting transfers between devices, trade(): return lax.ppermute(block, axis, [(i, i ^ bit) for i in range(count)])  3.46 us
    ppermute x2, waiting for transfers between devices, trade(): return lax.ppermute(block, axis, [(i, i ^ bit) for i in range(count)])  1.89 us
    pallas_call x1, Pallas kernels, on_device(): pl.pallas_call(local, out_shape=(wide, wide, jax.ShapeDtypeStruct(masks,...  1.21 us
    pallas_call x1, Pallas kernels, on_device(): pl.pallas_call(fold, out_shape=(wide, jax.ShapeDtypeStruct((rows, width,...  1.09 us
    pallas_call x1, Pallas kernels, on_device(): pl.pallas_call(halo, out_shape=wide, in_specs=[VMEM] * 5, out_specs=VMEM,...  0.88 us
    ppermute x2, waiting for transfers between devices, swaps(): return lax.ppermute(block, axis, pairs)  0.67 us
  transfers between devices with their start and end apart: 4, of which 3 were waited for; matrix products, arithmetic and copies ran while one was open for 0% of the time, Pallas kernels for 12%

profile of v14, /device:TPU:0, one launch (start us, length us, event | category | flops | bytes accessed | tf_op | source)
XLA Modules:
  0.0 19.9 jit_solution(15613467489791367104)
XLA Ops:
  0.6 3.9 %sweeps.1 = (f32[8,32,128]{2,1,0:T(8,128)S(1)}, bf16[9,160,128]{2,1,0:T(8,128)(2,1)S(1)}, bf16[9,128,128]{2,1,0:T(8,128)(2,1)S(1)}, bf16[576,128]{1,0:T(8,128)(2,1)S(1)}) custom-call(f32[8,32,128]{2,1,0:T(8,128)} %rhs_far.1, bf16[8,128,128]{2,1,0:T(8,128)(2,1)} %inverse_far.1, bf16[8,3,128,128]{3,2,1,0:T(8,128)(2,1)} %refs_8_.1, ...), custom_call_target="tpu_custom_call" | custom-call | tf_op jit(solution)/shard_map/sweeps/pallas_call | solution.py:501
  4.6 0.5 %collective-permute-start = (bf16[576,128]{1,0:T(8,128)(2,1)S(1)}, bf16[576,128]{1,0:T(8,128)(2,1)S(1)}, u32[]{:S(2)}, u32[]{:S(2)}) collective-permute-start(bf16[576,128]{1,0:T(8,128)(2,1)S(1)} %get-tuple-element.23.refs_0_), channel_id=1, source_target_pairs={{0,8},{8,0},{16,24},{24,16},{1,9},{9,1},{17,25},{25,17},{2,10},{10... | collective-permute-start | bytes 442376 | tf_op jit(solution)/shard_map/ppermute | solution.py:467
  5.1 1.0 %collective-permute-done.refs_1_ = bf16[576,128]{1,0:T(8,128)(2,1)S(1)} collective-permute-done((bf16[576,128]{1,0:T(8,128)(2,1)S(1)}, bf16[576,128]{1,0:T(8,128)(2,1)S(1)}, u32[]{:S(2)}, u32[]{:S(2)}) %collective-permute-start) | collective-permute-done | bytes 147488 | tf_op jit(solution)/shard_map/ppermute | solution.py:467
  6.1 0.3 %compose.1 = (bf16[160,128]{1,0:T(8,128)(2,1)S(1)}, bf16[448,128]{1,0:T(8,128)(2,1)S(1)}, bf16[128,128]{1,0:T(8,128)(2,1)S(1)}, bf16[32,128]{1,0:T(8,128)(2,1)S(1)}) custom-call(bf16[576,128]{1,0:T(8,128)(2,1)S(1)} %get-tuple-element.23.refs_0_, bf16[576,128]{1,0:T(8,128)(2,1)S(1)} %collective-permute-done.refs_1_), custom_call_target="tpu_custom_call" | custom-call | tf_op jit(solution)/shard_map/compose/pallas_call | solution.py:549
  6.4 3.0 %collective-permute-start.1 = (bf16[160,128]{1,0:T(8,128)(2,1)S(1)}, bf16[160,128]{1,0:T(8,128)(2,1)S(1)}, u32[]{:S(2)}, u32[]{:S(2)}) collective-permute-start(bf16[160,128]{1,0:T(8,128)(2,1)S(1)} %get-tuple-element.25), channel_id=1, source_target_pairs={{0,16},{8,24},{16,0},{24,8},{1,17},{9,25},{17,1},{25,9},{2,18},{10... | collective-permute-start | bytes 122888 | tf_op jit(solution)/shard_map/ppermute | solution.py:467
  9.3 0.0 copy-start
  9.3 0.0 copy-start.1
  9.3 1.1 %fold.1 = (f32[8,32,128]{2,1,0:T(8,128)S(1)}, bf16[8,128,128]{2,1,0:T(8,128)(2,1)S(1)}, bf16[160,128]{1,0:T(8,128)(2,1)S(1)}, bf16[160,128]{1,0:T(8,128)(2,1)S(1)}, bf16[8,128,128]{2,1,0:T(8,128)(2,1)S(1)}) custom-call(f32[8,32,128]{2,1,0:T(8,128)S(1)} %get-tuple-element.26.refs_0_, bf16[9,160,128]{2,1,0:T(8,128)(2,1)S(1)} %get-tuple-element.27.refs_1_, ...), custom_call_target="tpu_custom_call" | custom-call | tf_op jit(solution)/shard_map/fold/pallas_call | solution.py:569
  10.4 0.9 %collective-permute-done.1.refs_1_.refs_5_ = bf16[160,128]{1,0:T(8,128)(2,1)S(1)} collective-permute-done((bf16[160,128]{1,0:T(8,128)(2,1)S(1)}, bf16[160,128]{1,0:T(8,128)(2,1)S(1)}, u32[]{:S(2)}, u32[]{:S(2)}) %collective-permute-start.1) | collective-permute-done | bytes 40992 | tf_op jit(solution)/shard_map/ppermute | solution.py:467
  11.3 0.3 %chain.1 = (f32[8,32,128]{2,1,0:T(8,128)S(1)}, bf16[8,32,128]{2,1,0:T(8,128)(2,1)S(1)}, bf16[32,128]{1,0:T(8,128)(2,1)S(1)}, bf16[4,32,128]{2,1,0:T(8,128)(2,1)S(1)}, bf16[4,32,128]{2,1,0:T(8,128)(2,1)S(1)}) custom-call(bf16[32,128]{1,0:T(8,128)(2,1)S(1)} %get-tuple-element.24.refs_0_, bf16[160,128]{1,0:T(8,128)(2,1)S(1)} %collective-permute-done.1.refs_1_.refs_5_, ...), custom_call_target="tpu_custom_call" | custom-call | tf_op jit(solution)/shard_map/chain/pallas_call | solution.py:588
  11.6 0.7 %collective-permute-start.2 = (bf16[4,32,128]{2,1,0:T(8,128)(2,1)S(1)}, bf16[4,32,128]{2,1,0:T(8,128)(2,1)S(1)}, u32[]{:S(2)}, u32[]{:S(2)}) collective-permute-start(bf16[4,32,128]{2,1,0:T(8,128)(2,1)S(1)} %get-tuple-element.41), channel_id=1, source_target_pairs={{1,2},{2,1},{3,4},{4,3},{5,6},{6,5},{9,10},{10,9},{11,12},{12,11},... | collective-permute-start | bytes 98312 | tf_op jit(solution)/shard_map/ppermute | solution.py:475
  12.3 4.8 %collective-permute-start.3 = (bf16[4,32,128]{2,1,0:T(8,128)(2,1)S(1)}, bf16[4,32,128]{2,1,0:T(8,128)(2,1)S(1)}, u32[]{:S(2)}, u32[]{:S(2)}) collective-permute-start(bf16[4,32,128]{2,1,0:T(8,128)(2,1)S(1)} %get-tuple-element.42), channel_id=1, source_target_pairs={{0,1},{1,0},{2,3},{3,2},{4,5},{5,4},{6,7},{7,6},{8,9},{9,8},{10,11... | collective-permute-start | bytes 98312 | tf_op jit(solution)/shard_map/ppermute | solution.py:475
  17.1 0.0 copy-done
  17.1 0.0 copy-done.1
  17.1 0.0 copy-start.2
  17.1 1.2 %local_product.1 = (f32[8,32,128]{2,1,0:T(8,128)S(1)}, f32[8,32,128]{2,1,0:T(8,128)}, bf16[8,1,8,32,128]{4,3,2,1,0:T(8,128)(2,1)S(1)}) custom-call(bf16[8,32,128]{2,1,0:T(8,128)(2,1)S(1)} %get-tuple-element.32.refs_0_, bf16[32,128]{1,0:T(8,128)(2,1)S(1)} %get-tuple-element.33.refs_1_, bf16[160,128]{1,0:T(8,128)(2,1)S(1)} %get-tuple-element.34.refs_2_, ...), custom_call_target="tpu_custom_call" | custom-call | tf_op jit(solution)/shard_map/local_product/pallas_call | solution.py:610
  18.4 0.0 collective-permute-done.2.refs_1_
  18.4 0.7 %collective-permute-done.3.refs_2_ = bf16[4,32,128]{2,1,0:T(8,128)(2,1)S(1)} collective-permute-done((bf16[4,32,128]{2,1,0:T(8,128)(2,1)S(1)}, bf16[4,32,128]{2,1,0:T(8,128)(2,1)S(1)}, u32[]{:S(2)}, u32[]{:S(2)}) %collective-permute-start.3) | collective-permute-done | bytes 32800 | tf_op jit(solution)/shard_map/ppermute | solution.py:475
  19.0 0.0 copy-done.2
  19.0 0.9 %halo_product.1 = f32[8,32,128]{2,1,0:T(8,128)} custom-call(f32[8,32,128]{2,1,0:T(8,128)S(1)} %get-tuple-element.40.refs_0_, bf16[4,32,128]{2,1,0:T(8,128)(2,1)S(1)} %collective-permute-done.2.refs_1_, bf16[4,32,128]{2,1,0:T(8,128)(2,1)S(1)} %collective-permute-done.3.refs_2_, bf16[8,2,128,128]{3,2,1,0:T(8,128)(2,1)S(1)} %copy-done.2, ...), custom_call_target="tpu_custom_call" | custom-call | tf_op jit(solution)/shard_map/halo_product/pallas_call | solution.py:640
Async XLA Ops:
  4.6 1.5 %collective-permute-start = (bf16[576,128]{1,0:T(8,128)(2,1)S(1)}, bf16[576,128]{1,0:T(8,128)(2,1)S(1)}, u32[]{:S(2)}, u32[]{:S(2)}) collective-permute-start(bf16[576,128]{1,0:T(8,128)(2,1)S(1)} %get-tuple-element.23.refs_0_), channel_id=1, source_target_pairs={{0,8},{8,0},{16,24},{24,16},{1,9},{9,1},{17,25},{25,17},{2,10},{10... | collective-permute-start | bytes 442376 | tf_op jit(solution)/shard_map/ppermute | solution.py:467
  6.4 4.9 %collective-permute-start.1 = (bf16[160,128]{1,0:T(8,128)(2,1)S(1)}, bf16[160,128]{1,0:T(8,128)(2,1)S(1)}, u32[]{:S(2)}, u32[]{:S(2)}) collective-permute-start(bf16[160,128]{1,0:T(8,128)(2,1)S(1)} %get-tuple-element.25), channel_id=1, source_target_pairs={{0,16},{8,24},{16,0},{24,8},{1,17},{9,25},{17,1},{25,9},{2,18},{10... | collective-permute-start | bytes 122888 | tf_op jit(solution)/shard_map/ppermute | solution.py:467
  9.3 7.8 %copy-start = (bf16[8,3,128,128]{3,2,1,0:T(8,128)(2,1)S(1)}, bf16[8,3,128,128]{3,2,1,0:T(8,128)(2,1)}, u32[]{:S(2)}) copy-start(bf16[8,3,128,128]{3,2,1,0:T(8,128)(2,1)} %refs_8_.1) | copy-start | bytes 2359300
  9.3 7.8 %copy-start.1 = (bf16[8,3,128,128]{3,2,1,0:T(8,128)(2,1)S(1)}, bf16[8,3,128,128]{3,2,1,0:T(8,128)(2,1)}, u32[]{:S(2)}) copy-start(bf16[8,3,128,128]{3,2,1,0:T(8,128)(2,1)} %refs_9_.1) | copy-start | bytes 2359300
  11.6 6.7 %collective-permute-start.2 = (bf16[4,32,128]{2,1,0:T(8,128)(2,1)S(1)}, bf16[4,32,128]{2,1,0:T(8,128)(2,1)S(1)}, u32[]{:S(2)}, u32[]{:S(2)}) collective-permute-start(bf16[4,32,128]{2,1,0:T(8,128)(2,1)S(1)} %get-tuple-element.41), channel_id=1, source_target_pairs={{1,2},{2,1},{3,4},{4,3},{5,6},{6,5},{9,10},{10,9},{11,12},{12,11},... | collective-permute-start | bytes 98312 | tf_op jit(solution)/shard_map/ppermute | solution.py:475
  12.3 6.7 %collective-permute-start.3 = (bf16[4,32,128]{2,1,0:T(8,128)(2,1)S(1)}, bf16[4,32,128]{2,1,0:T(8,128)(2,1)S(1)}, u32[]{:S(2)}, u32[]{:S(2)}) collective-permute-start(bf16[4,32,128]{2,1,0:T(8,128)(2,1)S(1)} %get-tuple-element.42), channel_id=1, source_target_pairs={{0,1},{1,0},{2,3},{3,2},{4,5},{5,4},{6,7},{7,6},{8,9},{9,8},{10,11... | collective-permute-start | bytes 98312 | tf_op jit(solution)/shard_map/ppermute | solution.py:475
  17.1 1.9 %copy-start.2 = (bf16[8,2,128,128]{3,2,1,0:T(8,128)(2,1)S(1)}, bf16[8,2,128,128]{3,2,1,0:T(8,128)(2,1)}, u32[]{:S(2)}) copy-start(bf16[8,2,128,128]{3,2,1,0:T(8,128)(2,1)} %refs_3_.1) | copy-start | bytes 1572868

commit v15 on v13

--- a/solution.py
+++ b/solution.py
@@ -98,44 +98,41 @@
         sides = [jnp.concatenate([own, zero], axis=1), jnp.concatenate([zero, other], axis=1)]
         return mul(jnp.concatenate([left, right], axis=1), jnp.concatenate(sides, axis=0))
 
-    def ready(at, blocks, many, first, step, heads):
-        of_a, of_b, links = [], [], []
-        for a in (first, first + 2 * step):
-            b = a + step
-            lefts = [
-                jnp.concatenate(heads(k) + [blocks[k].reshape(many * width, width)], axis=0)
-                for k in (a, b)
-            ]
-            both = apart(*lefts, inverse[a], inverse[b])
-            of_a.append(both[:, :width])
-            of_b.append(both[:, width:])
-            tail = both[both.shape[0] - many * width :, width:]
+    def scaled(k, parts):
+        lefts = [jnp.concatenate(parts(j), axis=0) for j in (k, k + 1)]
+        both = apart(*lefts, inverse[k], inverse[k + 1])
+        return {k: both[:, :width], k + 1: both[:, width:]}
+
+    def ready(at, many, places, of, extra=()):
+        links = []
+        for a, b in places:
+            tail = of[b][of[b].shape[0] - many * width :]
             links.append(narrow(named(at, b, a, tail, many)))
-        narrow_a = [narrow(value) for value in of_a]
-        both = apart(*narrow_a, *links)
-        through = [both[:, :width], both[:, width:]]
-        return of_a, narrow_a, of_b, through, links
-
-    def ready_down(p):
-        of_a, narrow_a, of_b, through, _ = ready(
-            lower_at, lower, slots, 2 * p, 1, lambda k: [narrow(rhs[k])]
-        )
-        for i in range(2):
-            a, b = 2 * (p + i), 2 * (p + i) + 1
-            free_a = -of_a[i][count:near]
-            free_b = through[i][count:near] - of_b[i][count:near]
+        narrow_a = [narrow(of[a]) for a, _ in places]
+        lefts = narrow_a
+        if extra:
+            lefts = [jnp.concatenate(both, axis=0) for both in zip(narrow_a, extra)]
+        both = apart(*lefts, *links)
+        return narrow_a, [both[:, :width], both[:, width:]], links
+
+    def ready_down(p, of):
+        places = [(2 * p, 2 * p + 1), (2 * p + 2, 2 * p + 3)]
+        narrow_a, through, _ = ready(lower_at, slots, places, of)
+        for i, (a, b) in enumerate(places):
+            free_a = -of[a][count:near]
+            free_b = through[i][count:near] - of[b][count:near]
             if p + i == 0:
-                inner = sum(piece(of_a[i][count:], m) for m in range(1, slots))
+                inner = sum(piece(of[a][count:], m) for m in range(1, slots))
                 free_a = free_a - inner
                 inner = sum(piece(through[i][count:], m) for m in range(1, slots))
-                free_b = free_b + inner - named(lower_at, b, b, of_b[i][count:], slots)
+                free_b = free_b + inner - named(lower_at, b, b, of[b][count:], slots)
             else:
                 low_pair[p + i, :, :width] = narrow_a[i][near:]
                 low_pair[p + i, :, width:] = narrow(through[i][near:])
-                low_second[p + i] = narrow(of_b[i][near:])
-            exact[a, :count] = of_a[i][:count]
+                low_second[p + i] = narrow(of[b][near:])
+            exact[a, :count] = of[a][:count]
             exact[a, count:] = free_a
-            exact[b, :count] = of_b[i][:count] - through[i][:count]
+            exact[b, :count] = of[b][:count] - through[i][:count]
             exact[b, count:] = free_b
 
     def go_down(p):
@@ -151,26 +148,24 @@
         down[a] = narrow(of_a)
         down[b] = narrow(of_b)
 
-    def ready_up(p):
-        of_a, narrow_a, of_b, through, links = ready(
-            upper_at, upper, upper_slots, last - 2 * p, -1, lambda k: []
-        )
-        for i in range(2):
-            a = last - 2 * (p + i)
-            b = a - 1
-            free_a = -of_a[i][:width]
-            free_b = through[i][:width] - of_b[i][:width]
+    def ready_up(p, of, extra=()):
+        places = [(last - 2 * (p + i), last - 2 * (p + i) - 1) for i in range(2)]
+        narrow_a, through, links = ready(upper_at, upper_slots, places, of, extra)
+        size = upper_slots * width
+        for i, (a, b) in enumerate(places):
+            free_a = -of[a][:width]
+            free_b = through[i][:width] - of[b][:width]
             if p + i == 0:
-                free_a = free_a - sum(piece(of_a[i], m) for m in range(1, upper_slots))
+                free_a = free_a - sum(piece(of[a], m) for m in range(1, upper_slots))
                 inner = sum(piece(through[i], m) for m in range(1, upper_slots))
-                free_b = free_b + inner - named(upper_at, b, b, of_b[i], upper_slots)
+                free_b = free_b + inner - named(upper_at, b, b, of[b], upper_slots)
             else:
                 upp_pair[p + i, :, :width] = narrow_a[i][width:]
-                upp_pair[p + i, :, width:] = narrow(through[i][width:])
-                upp_second[p + i] = narrow(of_b[i][width:])
+                upp_pair[p + i, :, width:] = narrow(through[i][width:size])
+                upp_second[p + i] = narrow(of[b][width:])
             fixed[a] = free_a
             fixed[b] = free_b
-        return links
+        return links, [value[size:] for value in through]
 
     def go_up(p, passed):
         a = last - 2 * p
@@ -192,26 +187,47 @@
             response[k, near:] = narrow(free)
 
     pairs = rows // 2
+    middle = pairs // 2
+
+    def lower_part(k):
+        return [narrow(rhs[k]), lower[k].reshape(slots * width, width)]
+
+    def upper_part(k):
+        return [upper[k].reshape(upper_slots * width, width)]
+
     for copy in copies[:4]:
         copy.wait()
-    ready_down(0)
+    for p in range(0, middle, 2):
+        ready_down(p, scaled(2 * p, lower_part) | scaled(2 * p + 2, lower_part))
     go_down(0)
     for copy in copies[4:]:
         copy.wait()
+    of_low, of_upp = {}, {}
+    for k in range(half, rows, 2):
+        for j, value in scaled(k, lambda j: lower_part(j) + upper_part(j)).items():
+            of_low[j] = value[: count + slots * width]
+            of_upp[j] = value[count + slots * width :]
+    for p in range(middle, pairs, 2):
+        ready_down(p, of_low)
     links = []
     for p in range(1, pairs):
-        if p % 2 == 1 and p + 1 < pairs:
-            ready_down(p + 1)
         go_down(p)
-        if p % 2 == 1:
-            links += ready_up(p - 1)
+        if p % 2 == 1 and p - 1 < middle:
+            links += ready_up(p - 1, of_upp)[0]
     far = near + width
     payload[:near] = down[last]
-    for p in range(0, pairs, 2):
+    passed = []
+    for p in range(middle, pairs, 2):
         a = last - 2 * p
-        passed = apart(down[a], down[a - 2], links[p], links[p + 1])
-        go_up(p, passed[:, :width])
-        go_up(p + 1, passed[:, width:])
+        of_upp = scaled(a - 1, upper_part) | scaled(a - 3, upper_part)
+        passed += ready_up(p, of_upp, (down[a], down[a - 2]))[1]
+    early = []
+    for p in range(0, middle, 2):
+        a = last - 2 * p
+        both = apart(down[a], down[a - 2], links[p], links[p + 1])
+        early += [both[:, :width], both[:, width:]]
+    for p, value in enumerate(early + passed):
+        go_up(p, value)
 
     payload[near + far :] = response[last, near:]
     payload[near : near + far] = response[0]

time: 19.8 us -> 19.8 us (level)
  no operation moved by 1% of the time
where the time goes in v15:
time: 19.8 us; the launch traced here: 19.6 us
  starting transfers between devices  8.97 us (45%)
  Pallas kernels  7.42 us (37%)
  waiting for transfers between devices  2.55 us (13%)
  between operations  0.69 us (3%)
    ppermute x2, starting transfers between devices, swaps(): return lax.ppermute(block, axis, pairs)  5.5 us
    pallas_call x1, Pallas kernels, on_device(): pl.pallas_call(sweep_kernel, out_shape=(wide, jax.ShapeDtypeStruct((rows...  3.66 us
    ppermute x2, starting transfers between devices, trade(): return lax.ppermute(block, axis, [(i, i ^ bit) for i in range(count)])  3.47 us
    ppermute x2, waiting for transfers between devices, trade(): return lax.ppermute(block, axis, [(i, i ^ bit) for i in range(count)])  1.89 us
    pallas_call x1, Pallas kernels, on_device(): pl.pallas_call(local, out_shape=(wide, wide, jax.ShapeDtypeStruct(masks,...  1.21 us
    pallas_call x1, Pallas kernels, on_device(): pl.pallas_call(fold, out_shape=(wide, jax.ShapeDtypeStruct((rows, width,...  1.09 us
    pallas_call x1, Pallas kernels, on_device(): pl.pallas_call(halo, out_shape=wide, in_specs=[VMEM] * 5, out_specs=VMEM,...  0.88 us
    ppermute x2, waiting for transfers between devices, swaps(): return lax.ppermute(block, axis, pairs)  0.66 us
  transfers between devices with their start and end apart: 4, of which 3 were waited for; matrix products, arithmetic and copies ran while one was open for 0% of the time, Pallas kernels for 12%

profile of v15, /device:TPU:0, one launch (start us, length us, event | category | flops | bytes accessed | tf_op | source)
XLA Modules:
  0.0 19.6 jit_solution(9776716450173479666)
XLA Ops:
  0.6 3.7 %sweeps.1 = (f32[8,32,128]{2,1,0:T(8,128)S(1)}, bf16[9,288,128]{2,1,0:T(8,128)(2,1)S(1)}, bf16[576,128]{1,0:T(8,128)(2,1)S(1)}) custom-call(f32[8,32,128]{2,1,0:T(8,128)} %rhs_far.1, bf16[8,128,128]{2,1,0:T(8,128)(2,1)} %inverse_far.1, bf16[8,3,128,128]{3,2,1,0:T(8,128)(2,1)} %refs_8_.1, bf16[8,3,128,128]{3,2,1,0:T(8,128)(2,1)} %refs_9_.1, s32[3,8]{1,0:T(4,128)} %bitcast.3, ...), custom_call_target="tpu_custom_call" | custom-call | tf_op jit(solution)/shard_map/sweeps/pallas_call | solution.py:505
  4.3 0.5 %collective-permute-start = (bf16[576,128]{1,0:T(8,128)(2,1)S(1)}, bf16[576,128]{1,0:T(8,128)(2,1)S(1)}, u32[]{:S(2)}, u32[]{:S(2)}) collective-permute-start(bf16[576,128]{1,0:T(8,128)(2,1)S(1)} %get-tuple-element.22.refs_0_), channel_id=1, source_target_pairs={{0,8},{8,0},{16,24},{24,16},{1,9},{9,1},{17,25},{25,17},{2,10},{10... | collective-permute-start | bytes 442376 | tf_op jit(solution)/shard_map/ppermute | solution.py:471
  4.8 1.0 %collective-permute-done.refs_1_ = bf16[576,128]{1,0:T(8,128)(2,1)S(1)} collective-permute-done((bf16[576,128]{1,0:T(8,128)(2,1)S(1)}, bf16[576,128]{1,0:T(8,128)(2,1)S(1)}, u32[]{:S(2)}, u32[]{:S(2)}) %collective-permute-start) | collective-permute-done | bytes 147488 | tf_op jit(solution)/shard_map/ppermute | solution.py:471
  5.8 0.3 %compose.1 = (bf16[160,128]{1,0:T(8,128)(2,1)S(1)}, bf16[448,128]{1,0:T(8,128)(2,1)S(1)}, bf16[128,128]{1,0:T(8,128)(2,1)S(1)}, bf16[32,128]{1,0:T(8,128)(2,1)S(1)}) custom-call(bf16[576,128]{1,0:T(8,128)(2,1)S(1)} %get-tuple-element.22.refs_0_, bf16[576,128]{1,0:T(8,128)(2,1)S(1)} %collective-permute-done.refs_1_), custom_call_target="tpu_custom_call" | custom-call | tf_op jit(solution)/shard_map/compose/pallas_call | solution.py:552
  6.1 3.0 %collective-permute-start.1 = (bf16[160,128]{1,0:T(8,128)(2,1)S(1)}, bf16[160,128]{1,0:T(8,128)(2,1)S(1)}, u32[]{:S(2)}, u32[]{:S(2)}) collective-permute-start(bf16[160,128]{1,0:T(8,128)(2,1)S(1)} %get-tuple-element.24), channel_id=1, source_target_pairs={{0,16},{8,24},{16,0},{24,8},{1,17},{9,25},{17,1},{25,9},{2,18},{10... | collective-permute-start | bytes 122888 | tf_op jit(solution)/shard_map/ppermute | solution.py:471
  9.1 0.0 copy-start
  9.1 0.0 copy-start.1
  9.1 1.1 %fold.1 = (f32[8,32,128]{2,1,0:T(8,128)S(1)}, bf16[8,128,128]{2,1,0:T(8,128)(2,1)S(1)}, bf16[160,128]{1,0:T(8,128)(2,1)S(1)}, bf16[160,128]{1,0:T(8,128)(2,1)S(1)}, bf16[8,128,128]{2,1,0:T(8,128)(2,1)S(1)}) custom-call(f32[8,32,128]{2,1,0:T(8,128)S(1)} %get-tuple-element.25.refs_0_, bf16[9,288,128]{2,1,0:T(8,128)(2,1)S(1)} %get-tuple-element.26.refs_1_, ...), custom_call_target="tpu_custom_call" | custom-call | tf_op jit(solution)/shard_map/fold/pallas_call | solution.py:572
  10.2 0.9 %collective-permute-done.1.refs_1_.refs_5_ = bf16[160,128]{1,0:T(8,128)(2,1)S(1)} collective-permute-done((bf16[160,128]{1,0:T(8,128)(2,1)S(1)}, bf16[160,128]{1,0:T(8,128)(2,1)S(1)}, u32[]{:S(2)}, u32[]{:S(2)}) %collective-permute-start.1) | collective-permute-done | bytes 40992 | tf_op jit(solution)/shard_map/ppermute | solution.py:471
  11.0 0.3 %chain.1 = (f32[8,32,128]{2,1,0:T(8,128)S(1)}, bf16[8,32,128]{2,1,0:T(8,128)(2,1)S(1)}, bf16[32,128]{1,0:T(8,128)(2,1)S(1)}, bf16[4,32,128]{2,1,0:T(8,128)(2,1)S(1)}, bf16[4,32,128]{2,1,0:T(8,128)(2,1)S(1)}) custom-call(bf16[32,128]{1,0:T(8,128)(2,1)S(1)} %get-tuple-element.23.refs_0_, bf16[160,128]{1,0:T(8,128)(2,1)S(1)} %collective-permute-done.1.refs_1_.refs_5_, ...), custom_call_target="tpu_custom_call" | custom-call | tf_op jit(solution)/shard_map/chain/pallas_call | solution.py:591
  11.4 0.7 %collective-permute-start.2 = (bf16[4,32,128]{2,1,0:T(8,128)(2,1)S(1)}, bf16[4,32,128]{2,1,0:T(8,128)(2,1)S(1)}, u32[]{:S(2)}, u32[]{:S(2)}) collective-permute-start(bf16[4,32,128]{2,1,0:T(8,128)(2,1)S(1)} %get-tuple-element.39), channel_id=1, source_target_pairs={{1,2},{2,1},{3,4},{4,3},{5,6},{6,5},{9,10},{10,9},{11,12},{12,11},... | collective-permute-start | bytes 98312 | tf_op jit(solution)/shard_map/ppermute | solution.py:479
  12.0 4.8 %collective-permute-start.3 = (bf16[4,32,128]{2,1,0:T(8,128)(2,1)S(1)}, bf16[4,32,128]{2,1,0:T(8,128)(2,1)S(1)}, u32[]{:S(2)}, u32[]{:S(2)}) collective-permute-start(bf16[4,32,128]{2,1,0:T(8,128)(2,1)S(1)} %get-tuple-element.40), channel_id=1, source_target_pairs={{0,1},{1,0},{2,3},{3,2},{4,5},{5,4},{6,7},{7,6},{8,9},{9,8},{10,11... | collective-permute-start | bytes 98312 | tf_op jit(solution)/shard_map/ppermute | solution.py:479
  16.9 0.0 copy-done
  16.9 0.0 copy-done.1
  16.9 0.0 copy-start.2
  16.9 1.2 %local_product.1 = (f32[8,32,128]{2,1,0:T(8,128)S(1)}, f32[8,32,128]{2,1,0:T(8,128)}, bf16[8,1,8,32,128]{4,3,2,1,0:T(8,128)(2,1)S(1)}) custom-call(bf16[8,32,128]{2,1,0:T(8,128)(2,1)S(1)} %get-tuple-element.30.refs_0_, bf16[32,128]{1,0:T(8,128)(2,1)S(1)} %get-tuple-element.31.refs_1_, bf16[160,128]{1,0:T(8,128)(2,1)S(1)} %get-tuple-element.32.refs_2_, ...), custom_call_target="tpu_custom_call" | custom-call | tf_op jit(solution)/shard_map/local_product/pallas_call | solution.py:613
  18.1 0.0 collective-permute-done.2.refs_1_
  18.1 0.7 %collective-permute-done.3.refs_2_ = bf16[4,32,128]{2,1,0:T(8,128)(2,1)S(1)} collective-permute-done((bf16[4,32,128]{2,1,0:T(8,128)(2,1)S(1)}, bf16[4,32,128]{2,1,0:T(8,128)(2,1)S(1)}, u32[]{:S(2)}, u32[]{:S(2)}) %collective-permute-start.3) | collective-permute-done | bytes 32800 | tf_op jit(solution)/shard_map/ppermute | solution.py:479
  18.8 0.0 copy-done.2
  18.8 0.9 %halo_product.1 = f32[8,32,128]{2,1,0:T(8,128)} custom-call(f32[8,32,128]{2,1,0:T(8,128)S(1)} %get-tuple-element.38.refs_0_, bf16[4,32,128]{2,1,0:T(8,128)(2,1)S(1)} %collective-permute-done.2.refs_1_, bf16[4,32,128]{2,1,0:T(8,128)(2,1)S(1)} %collective-permute-done.3.refs_2_, bf16[8,2,128,128]{3,2,1,0:T(8,128)(2,1)S(1)} %copy-done.2, ...), custom_call_target="tpu_custom_call" | custom-call | tf_op jit(solution)/shard_map/halo_product/pallas_call | solution.py:643
Async XLA Ops:
  4.3 1.5 %collective-permute-start = (bf16[576,128]{1,0:T(8,128)(2,1)S(1)}, bf16[576,128]{1,0:T(8,128)(2,1)S(1)}, u32[]{:S(2)}, u32[]{:S(2)}) collective-permute-start(bf16[576,128]{1,0:T(8,128)(2,1)S(1)} %get-tuple-element.22.refs_0_), channel_id=1, source_target_pairs={{0,8},{8,0},{16,24},{24,16},{1,9},{9,1},{17,25},{25,17},{2,10},{10... | collective-permute-start | bytes 442376 | tf_op jit(solution)/shard_map/ppermute | solution.py:471
  6.1 4.9 %collective-permute-start.1 = (bf16[160,128]{1,0:T(8,128)(2,1)S(1)}, bf16[160,128]{1,0:T(8,128)(2,1)S(1)}, u32[]{:S(2)}, u32[]{:S(2)}) collective-permute-start(bf16[160,128]{1,0:T(8,128)(2,1)S(1)} %get-tuple-element.24), channel_id=1, source_target_pairs={{0,16},{8,24},{16,0},{24,8},{1,17},{9,25},{17,1},{25,9},{2,18},{10... | collective-permute-start | bytes 122888 | tf_op jit(solution)/shard_map/ppermute | solution.py:471
  9.1 7.8 %copy-start = (bf16[8,3,128,128]{3,2,1,0:T(8,128)(2,1)S(1)}, bf16[8,3,128,128]{3,2,1,0:T(8,128)(2,1)}, u32[]{:S(2)}) copy-start(bf16[8,3,128,128]{3,2,1,0:T(8,128)(2,1)} %refs_8_.1) | copy-start | bytes 2359300
  9.1 7.8 %copy-start.1 = (bf16[8,3,128,128]{3,2,1,0:T(8,128)(2,1)S(1)}, bf16[8,3,128,128]{3,2,1,0:T(8,128)(2,1)}, u32[]{:S(2)}) copy-start(bf16[8,3,128,128]{3,2,1,0:T(8,128)(2,1)} %refs_9_.1) | copy-start | bytes 2359300
  11.4 6.7 %collective-permute-start.2 = (bf16[4,32,128]{2,1,0:T(8,128)(2,1)S(1)}, bf16[4,32,128]{2,1,0:T(8,128)(2,1)S(1)}, u32[]{:S(2)}, u32[]{:S(2)}) collective-permute-start(bf16[4,32,128]{2,1,0:T(8,128)(2,1)S(1)} %get-tuple-element.39), channel_id=1, source_target_pairs={{1,2},{2,1},{3,4},{4,3},{5,6},{6,5},{9,10},{10,9},{11,12},{12,11},... | collective-permute-start | bytes 98312 | tf_op jit(solution)/shard_map/ppermute | solution.py:479
  12.0 6.7 %collective-permute-start.3 = (bf16[4,32,128]{2,1,0:T(8,128)(2,1)S(1)}, bf16[4,32,128]{2,1,0:T(8,128)(2,1)S(1)}, u32[]{:S(2)}, u32[]{:S(2)}) collective-permute-start(bf16[4,32,128]{2,1,0:T(8,128)(2,1)S(1)} %get-tuple-element.40), channel_id=1, source_target_pairs={{0,1},{1,0},{2,3},{3,2},{4,5},{5,4},{6,7},{7,6},{8,9},{9,8},{10,11... | collective-permute-start | bytes 98312 | tf_op jit(solution)/shard_map/ppermute | solution.py:479
  16.9 1.9 %copy-start.2 = (bf16[8,2,128,128]{3,2,1,0:T(8,128)(2,1)S(1)}, bf16[8,2,128,128]{3,2,1,0:T(8,128)(2,1)}, u32[]{:S(2)}) copy-start(bf16[8,2,128,128]{3,2,1,0:T(8,128)(2,1)} %refs_3_.3) | copy-start | bytes 1572868

commit v16 on v15

--- a/solution.py
+++ b/solution.py
@@ -103,16 +103,13 @@
         both = apart(*lefts, inverse[k], inverse[k + 1])
         return {k: both[:, :width], k + 1: both[:, width:]}
 
-    def ready(at, many, places, of, extra=()):
+    def ready(at, many, places, of):
         links = []
         for a, b in places:
             tail = of[b][of[b].shape[0] - many * width :]
             links.append(narrow(named(at, b, a, tail, many)))
         narrow_a = [narrow(of[a]) for a, _ in places]
-        lefts = narrow_a
-        if extra:
-            lefts = [jnp.concatenate(both, axis=0) for both in zip(narrow_a, extra)]
-        both = apart(*lefts, *links)
+        both = apart(*narrow_a, *links)
         return narrow_a, [both[:, :width], both[:, width:]], links
 
     def ready_down(p, of):
@@ -148,10 +145,9 @@
         down[a] = narrow(of_a)
         down[b] = narrow(of_b)
 
-    def ready_up(p, of, extra=()):
+    def ready_up(p, of):
         places = [(last - 2 * (p + i), last - 2 * (p + i) - 1) for i in range(2)]
-        narrow_a, through, links = ready(upper_at, upper_slots, places, of, extra)
-        size = upper_slots * width
+        narrow_a, through, links = ready(upper_at, upper_slots, places, of)
         for i, (a, b) in enumerate(places):
             free_a = -of[a][:width]
             free_b = through[i][:width] - of[b][:width]
@@ -161,11 +157,11 @@
                 free_b = free_b + inner - named(upper_at, b, b, of[b], upper_slots)
             else:
                 upp_pair[p + i, :, :width] = narrow_a[i][width:]
-                upp_pair[p + i, :, width:] = narrow(through[i][width:size])
+                upp_pair[p + i, :, width:] = narrow(through[i][width:])
                 upp_second[p + i] = narrow(of[b][width:])
             fixed[a] = free_a
             fixed[b] = free_b
-        return links, [value[size:] for value in through]
+        return links
 
     def go_up(p, passed):
         a = last - 2 * p
@@ -213,21 +209,17 @@
     for p in range(1, pairs):
         go_down(p)
         if p % 2 == 1 and p - 1 < middle:
-            links += ready_up(p - 1, of_upp)[0]
+            links += ready_up(p - 1, of_upp)
     far = near + width
     payload[:near] = down[last]
-    passed = []
     for p in range(middle, pairs, 2):
         a = last - 2 * p
-        of_upp = scaled(a - 1, upper_part) | scaled(a - 3, upper_part)
-        passed += ready_up(p, of_upp, (down[a], down[a - 2]))[1]
-    early = []
-    for p in range(0, middle, 2):
+        links += ready_up(p, scaled(a - 1, upper_part) | scaled(a - 3, upper_part))
+    for p in range(0, pairs, 2):
         a = last - 2 * p
-        both = apart(down[a], down[a - 2], links[p], links[p + 1])
-        early += [both[:, :width], both[:, width:]]
-    for p, value in enumerate(early + passed):
-        go_up(p, value)
+        passed = apart(down[a], down[a - 2], links[p], links[p + 1])
+        go_up(p, passed[:, :width])
+        go_up(p + 1, passed[:, width:])
 
     payload[near + far :] = response[last, near:]
     payload[near : near + far] = response[0]

time: 19.8 us -> 19.8 us (level)
  no operation moved by 1% of the time
where the time goes in v16:
time: 19.8 us; the launch traced here: 19.6 us
  starting transfers between devices  8.98 us (45%)
  Pallas kernels  7.39 us (37%)
  waiting for transfers between devices  2.55 us (13%)
  between operations  0.69 us (3%)
    ppermute x2, starting transfers between devices, swaps(): return lax.ppermute(block, axis, pairs)  5.5 us
    pallas_call x1, Pallas kernels, on_device(): pl.pallas_call(sweep_kernel, out_shape=(wide, jax.ShapeDtypeStruct((rows...  3.63 us
    ppermute x2, starting transfers between devices, trade(): return lax.ppermute(block, axis, [(i, i ^ bit) for i in range(count)])  3.48 us
    ppermute x2, waiting for transfers between devices, trade(): return lax.ppermute(block, axis, [(i, i ^ bit) for i in range(count)])  1.89 us
    pallas_call x1, Pallas kernels, on_device(): pl.pallas_call(local, out_shape=(wide, wide, jax.ShapeDtypeStruct(masks,...  1.21 us
    pallas_call x1, Pallas kernels, on_device(): pl.pallas_call(fold, out_shape=(wide, jax.ShapeDtypeStruct((rows, width,...  1.09 us
    pallas_call x1, Pallas kernels, on_device(): pl.pallas_call(halo, out_shape=wide, in_specs=[VMEM] * 5, out_specs=VMEM,...  0.88 us
    ppermute x2, waiting for transfers between devices, swaps(): return lax.ppermute(block, axis, pairs)  0.66 us
  transfers between devices with their start and end apart: 4, of which 3 were waited for; matrix products, arithmetic and copies ran while one was open for 0% of the time, Pallas kernels for 12%

profile of v16, /device:TPU:0, one launch (start us, length us, event | category | flops | bytes accessed | tf_op | source)
XLA Modules:
  0.0 19.6 jit_solution(6239254638877830999)
XLA Ops:
  0.6 3.6 %sweeps.1 = (f32[8,32,128]{2,1,0:T(8,128)S(1)}, bf16[9,288,128]{2,1,0:T(8,128)(2,1)S(1)}, bf16[576,128]{1,0:T(8,128)(2,1)S(1)}) custom-call(f32[8,32,128]{2,1,0:T(8,128)} %rhs_far.1, bf16[8,128,128]{2,1,0:T(8,128)(2,1)} %inverse_far.1, bf16[8,3,128,128]{3,2,1,0:T(8,128)(2,1)} %refs_8_.1, bf16[8,3,128,128]{3,2,1,0:T(8,128)(2,1)} %refs_9_.1, s32[3,8]{1,0:T(4,128)} %bitcast.3, ...), custom_call_target="tpu_custom_call" | custom-call | tf_op jit(solution)/shard_map/sweeps/pallas_call | solution.py:497
  4.3 0.5 %collective-permute-start = (bf16[576,128]{1,0:T(8,128)(2,1)S(1)}, bf16[576,128]{1,0:T(8,128)(2,1)S(1)}, u32[]{:S(2)}, u32[]{:S(2)}) collective-permute-start(bf16[576,128]{1,0:T(8,128)(2,1)S(1)} %get-tuple-element.22.refs_0_), channel_id=1, source_target_pairs={{0,8},{8,0},{16,24},{24,16},{1,9},{9,1},{17,25},{25,17},{2,10},{10... | collective-permute-start | bytes 442376 | tf_op jit(solution)/shard_map/ppermute | solution.py:463
  4.8 1.0 %collective-permute-done.refs_1_ = bf16[576,128]{1,0:T(8,128)(2,1)S(1)} collective-permute-done((bf16[576,128]{1,0:T(8,128)(2,1)S(1)}, bf16[576,128]{1,0:T(8,128)(2,1)S(1)}, u32[]{:S(2)}, u32[]{:S(2)}) %collective-permute-start) | collective-permute-done | bytes 147488 | tf_op jit(solution)/shard_map/ppermute | solution.py:463
  5.8 0.3 %compose.1 = (bf16[160,128]{1,0:T(8,128)(2,1)S(1)}, bf16[448,128]{1,0:T(8,128)(2,1)S(1)}, bf16[128,128]{1,0:T(8,128)(2,1)S(1)}, bf16[32,128]{1,0:T(8,128)(2,1)S(1)}) custom-call(bf16[576,128]{1,0:T(8,128)(2,1)S(1)} %get-tuple-element.22.refs_0_, bf16[576,128]{1,0:T(8,128)(2,1)S(1)} %collective-permute-done.refs_1_), custom_call_target="tpu_custom_call" | custom-call | tf_op jit(solution)/shard_map/compose/pallas_call | solution.py:544
  6.1 3.0 %collective-permute-start.1 = (bf16[160,128]{1,0:T(8,128)(2,1)S(1)}, bf16[160,128]{1,0:T(8,128)(2,1)S(1)}, u32[]{:S(2)}, u32[]{:S(2)}) collective-permute-start(bf16[160,128]{1,0:T(8,128)(2,1)S(1)} %get-tuple-element.24), channel_id=1, source_target_pairs={{0,16},{8,24},{16,0},{24,8},{1,17},{9,25},{17,1},{25,9},{2,18},{10... | collective-permute-start | bytes 122888 | tf_op jit(solution)/shard_map/ppermute | solution.py:463
  9.0 0.0 copy-start
  9.0 0.0 copy-start.1
  9.0 1.1 %fold.1 = (f32[8,32,128]{2,1,0:T(8,128)S(1)}, bf16[8,128,128]{2,1,0:T(8,128)(2,1)S(1)}, bf16[160,128]{1,0:T(8,128)(2,1)S(1)}, bf16[160,128]{1,0:T(8,128)(2,1)S(1)}, bf16[8,128,128]{2,1,0:T(8,128)(2,1)S(1)}) custom-call(f32[8,32,128]{2,1,0:T(8,128)S(1)} %get-tuple-element.25.refs_0_, bf16[9,288,128]{2,1,0:T(8,128)(2,1)S(1)} %get-tuple-element.26.refs_1_, ...), custom_call_target="tpu_custom_call" | custom-call | tf_op jit(solution)/shard_map/fold/pallas_call | solution.py:564
  10.1 0.9 %collective-permute-done.1.refs_1_.refs_5_ = bf16[160,128]{1,0:T(8,128)(2,1)S(1)} collective-permute-done((bf16[160,128]{1,0:T(8,128)(2,1)S(1)}, bf16[160,128]{1,0:T(8,128)(2,1)S(1)}, u32[]{:S(2)}, u32[]{:S(2)}) %collective-permute-start.1) | collective-permute-done | bytes 40992 | tf_op jit(solution)/shard_map/ppermute | solution.py:463
  11.0 0.3 %chain.1 = (f32[8,32,128]{2,1,0:T(8,128)S(1)}, bf16[8,32,128]{2,1,0:T(8,128)(2,1)S(1)}, bf16[32,128]{1,0:T(8,128)(2,1)S(1)}, bf16[4,32,128]{2,1,0:T(8,128)(2,1)S(1)}, bf16[4,32,128]{2,1,0:T(8,128)(2,1)S(1)}) custom-call(bf16[32,128]{1,0:T(8,128)(2,1)S(1)} %get-tuple-element.23.refs_0_, bf16[160,128]{1,0:T(8,128)(2,1)S(1)} %collective-permute-done.1.refs_1_.refs_5_, ...), custom_call_target="tpu_custom_call" | custom-call | tf_op jit(solution)/shard_map/chain/pallas_call | solution.py:583
  11.3 0.7 %collective-permute-start.2 = (bf16[4,32,128]{2,1,0:T(8,128)(2,1)S(1)}, bf16[4,32,128]{2,1,0:T(8,128)(2,1)S(1)}, u32[]{:S(2)}, u32[]{:S(2)}) collective-permute-start(bf16[4,32,128]{2,1,0:T(8,128)(2,1)S(1)} %get-tuple-element.39), channel_id=1, source_target_pairs={{1,2},{2,1},{3,4},{4,3},{5,6},{6,5},{9,10},{10,9},{11,12},{12,11},... | collective-permute-start | bytes 98312 | tf_op jit(solution)/shard_map/ppermute | solution.py:471
  12.0 4.8 %collective-permute-start.3 = (bf16[4,32,128]{2,1,0:T(8,128)(2,1)S(1)}, bf16[4,32,128]{2,1,0:T(8,128)(2,1)S(1)}, u32[]{:S(2)}, u32[]{:S(2)}) collective-permute-start(bf16[4,32,128]{2,1,0:T(8,128)(2,1)S(1)} %get-tuple-element.40), channel_id=1, source_target_pairs={{0,1},{1,0},{2,3},{3,2},{4,5},{5,4},{6,7},{7,6},{8,9},{9,8},{10,11... | collective-permute-start | bytes 98312 | tf_op jit(solution)/shard_map/ppermute | solution.py:471
  16.8 0.0 copy-done
  16.8 0.0 copy-done.1
  16.8 0.0 copy-start.2
  16.8 1.2 %local_product.1 = (f32[8,32,128]{2,1,0:T(8,128)S(1)}, f32[8,32,128]{2,1,0:T(8,128)}, bf16[8,1,8,32,128]{4,3,2,1,0:T(8,128)(2,1)S(1)}) custom-call(bf16[8,32,128]{2,1,0:T(8,128)(2,1)S(1)} %get-tuple-element.30.refs_0_, bf16[32,128]{1,0:T(8,128)(2,1)S(1)} %get-tuple-element.31.refs_1_, bf16[160,128]{1,0:T(8,128)(2,1)S(1)} %get-tuple-element.32.refs_2_, ...), custom_call_target="tpu_custom_call" | custom-call | tf_op jit(solution)/shard_map/local_product/pallas_call | solution.py:605
  18.1 0.0 collective-permute-done.2.refs_1_
  18.1 0.7 %collective-permute-done.3.refs_2_ = bf16[4,32,128]{2,1,0:T(8,128)(2,1)S(1)} collective-permute-done((bf16[4,32,128]{2,1,0:T(8,128)(2,1)S(1)}, bf16[4,32,128]{2,1,0:T(8,128)(2,1)S(1)}, u32[]{:S(2)}, u32[]{:S(2)}) %collective-permute-start.3) | collective-permute-done | bytes 32800 | tf_op jit(solution)/shard_map/ppermute | solution.py:471
  18.7 0.0 copy-done.2
  18.7 0.9 %halo_product.1 = f32[8,32,128]{2,1,0:T(8,128)} custom-call(f32[8,32,128]{2,1,0:T(8,128)S(1)} %get-tuple-element.38.refs_0_, bf16[4,32,128]{2,1,0:T(8,128)(2,1)S(1)} %collective-permute-done.2.refs_1_, bf16[4,32,128]{2,1,0:T(8,128)(2,1)S(1)} %collective-permute-done.3.refs_2_, bf16[8,2,128,128]{3,2,1,0:T(8,128)(2,1)S(1)} %copy-done.2, ...), custom_call_target="tpu_custom_call" | custom-call | tf_op jit(solution)/shard_map/halo_product/pallas_call | solution.py:635
Async XLA Ops:
  4.3 1.5 %collective-permute-start = (bf16[576,128]{1,0:T(8,128)(2,1)S(1)}, bf16[576,128]{1,0:T(8,128)(2,1)S(1)}, u32[]{:S(2)}, u32[]{:S(2)}) collective-permute-start(bf16[576,128]{1,0:T(8,128)(2,1)S(1)} %get-tuple-element.22.refs_0_), channel_id=1, source_target_pairs={{0,8},{8,0},{16,24},{24,16},{1,9},{9,1},{17,25},{25,17},{2,10},{10... | collective-permute-start | bytes 442376 | tf_op jit(solution)/shard_map/ppermute | solution.py:463
  6.1 4.9 %collective-permute-start.1 = (bf16[160,128]{1,0:T(8,128)(2,1)S(1)}, bf16[160,128]{1,0:T(8,128)(2,1)S(1)}, u32[]{:S(2)}, u32[]{:S(2)}) collective-permute-start(bf16[160,128]{1,0:T(8,128)(2,1)S(1)} %get-tuple-element.24), channel_id=1, source_target_pairs={{0,16},{8,24},{16,0},{24,8},{1,17},{9,25},{17,1},{25,9},{2,18},{10... | collective-permute-start | bytes 122888 | tf_op jit(solution)/shard_map/ppermute | solution.py:463
  9.0 7.8 %copy-start = (bf16[8,3,128,128]{3,2,1,0:T(8,128)(2,1)S(1)}, bf16[8,3,128,128]{3,2,1,0:T(8,128)(2,1)}, u32[]{:S(2)}) copy-start(bf16[8,3,128,128]{3,2,1,0:T(8,128)(2,1)} %refs_8_.1) | copy-start | bytes 2359300
  9.0 7.8 %copy-start.1 = (bf16[8,3,128,128]{3,2,1,0:T(8,128)(2,1)S(1)}, bf16[8,3,128,128]{3,2,1,0:T(8,128)(2,1)}, u32[]{:S(2)}) copy-start(bf16[8,3,128,128]{3,2,1,0:T(8,128)(2,1)} %refs_9_.1) | copy-start | bytes 2359300
  11.3 6.7 %collective-permute-start.2 = (bf16[4,32,128]{2,1,0:T(8,128)(2,1)S(1)}, bf16[4,32,128]{2,1,0:T(8,128)(2,1)S(1)}, u32[]{:S(2)}, u32[]{:S(2)}) collective-permute-start(bf16[4,32,128]{2,1,0:T(8,128)(2,1)S(1)} %get-tuple-element.39), channel_id=1, source_target_pairs={{1,2},{2,1},{3,4},{4,3},{5,6},{6,5},{9,10},{10,9},{11,12},{12,11},... | collective-permute-start | bytes 98312 | tf_op jit(solution)/shard_map/ppermute | solution.py:471
  12.0 6.7 %collective-permute-start.3 = (bf16[4,32,128]{2,1,0:T(8,128)(2,1)S(1)}, bf16[4,32,128]{2,1,0:T(8,128)(2,1)S(1)}, u32[]{:S(2)}, u32[]{:S(2)}) collective-permute-start(bf16[4,32,128]{2,1,0:T(8,128)(2,1)S(1)} %get-tuple-element.40), channel_id=1, source_target_pairs={{0,1},{1,0},{2,3},{3,2},{4,5},{5,4},{6,7},{7,6},{8,9},{9,8},{10,11... | collective-permute-start | bytes 98312 | tf_op jit(solution)/shard_map/ppermute | solution.py:471
  16.8 1.9 %copy-start.2 = (bf16[8,2,128,128]{3,2,1,0:T(8,128)(2,1)S(1)}, bf16[8,2,128,128]{3,2,1,0:T(8,128)(2,1)}, u32[]{:S(2)}) copy-start(bf16[8,2,128,128]{3,2,1,0:T(8,128)(2,1)} %refs_3_.3) | copy-start | bytes 1572868

commit v17 on v13

--- a/solution.py
+++ b/solution.py
@@ -53,10 +53,12 @@
     last = rows - 1
     half = rows // 2
     parts = [
-        (inverse_far, inverse),
-        (rhs_far, rhs),
         (lower_far.at[:half], lower.at[:half]),
+        (inverse_far.at[:half], inverse.at[:half]),
+        (rhs_far.at[:half], rhs.at[:half]),
         (lower_at_far, lower_at),
+        (inverse_far.at[half:], inverse.at[half:]),
+        (rhs_far.at[half:], rhs.at[half:]),
         (lower_far.at[half:], lower.at[half:]),
         (upper_far, upper),
         (upper_at_far, upper_at),
@@ -509,7 +511,7 @@
             pltpu.VMEM((rows + 1, near, width), jnp.bfloat16),
             pltpu.VMEM((rows, near, width), jnp.float32),
             pltpu.VMEM((rows, width, width), jnp.float32),
-            pltpu.SemaphoreType.DMA((7,)),
+            pltpu.SemaphoreType.DMA((9,)),
         ],
         compiler_params=SMALL,
         name="sweeps",

time: 19.8 us -> 19.7 us (level)
  no operation moved by 1% of the time
where the time goes in v17:
time: 19.7 us; the launch traced here: 19.5 us
  starting transfers between devices  8.97 us (46%)
  Pallas kernels  7.28 us (37%)
  waiting for transfers between devices  2.55 us (13%)
  between operations  0.68 us (3%)
    ppermute x2, starting transfers between devices, swaps(): return lax.ppermute(block, axis, pairs)  5.5 us
    pallas_call x1, Pallas kernels, on_device(): pl.pallas_call(sweep_kernel, out_shape=(wide, jax.ShapeDtypeStruct((rows...  3.52 us
    ppermute x2, starting transfers between devices, trade(): return lax.ppermute(block, axis, [(i, i ^ bit) for i in range(count)])  3.47 us
    ppermute x2, waiting for transfers between devices, trade(): return lax.ppermute(block, axis, [(i, i ^ bit) for i in range(count)])  1.89 us
    pallas_call x1, Pallas kernels, on_device(): pl.pallas_call(local, out_shape=(wide, wide, jax.ShapeDtypeStruct(masks,...  1.21 us
    pallas_call x1, Pallas kernels, on_device(): pl.pallas_call(fold, out_shape=(wide, jax.ShapeDtypeStruct((rows, width,...  1.09 us
    pallas_call x1, Pallas kernels, on_device(): pl.pallas_call(halo, out_shape=wide, in_specs=[VMEM] * 5, out_specs=VMEM,...  0.88 us
    ppermute x2, waiting for transfers between devices, swaps(): return lax.ppermute(block, axis, pairs)  0.66 us
  transfers between devices with their start and end apart: 4, of which 3 were waited for; matrix products, arithmetic and copies ran while one was open for 0% of the time, Pallas kernels for 12%

profile of v17, /device:TPU:0, one launch (start us, length us, event | category | flops | bytes accessed | tf_op | source)
XLA Modules:
  0.0 19.5 jit_solution(15827356242110250529)
XLA Ops:
  0.6 3.5 %sweeps.1 = (f32[8,32,128]{2,1,0:T(8,128)S(1)}, bf16[9,288,128]{2,1,0:T(8,128)(2,1)S(1)}, bf16[576,128]{1,0:T(8,128)(2,1)S(1)}) custom-call(f32[8,32,128]{2,1,0:T(8,128)} %rhs_far.1, bf16[8,128,128]{2,1,0:T(8,128)(2,1)} %inverse_far.1, bf16[8,3,128,128]{3,2,1,0:T(8,128)(2,1)} %refs_8_.1, bf16[8,3,128,128]{3,2,1,0:T(8,128)(2,1)} %refs_9_.1, s32[3,8]{1,0:T(4,128)} %bitcast.3, ...), custom_call_target="tpu_custom_call" | custom-call | tf_op jit(solution)/shard_map/sweeps/pallas_call | solution.py:491
  4.2 0.5 %collective-permute-start = (bf16[576,128]{1,0:T(8,128)(2,1)S(1)}, bf16[576,128]{1,0:T(8,128)(2,1)S(1)}, u32[]{:S(2)}, u32[]{:S(2)}) collective-permute-start(bf16[576,128]{1,0:T(8,128)(2,1)S(1)} %get-tuple-element.22.refs_0_), channel_id=1, source_target_pairs={{0,8},{8,0},{16,24},{24,16},{1,9},{9,1},{17,25},{25,17},{2,10},{10... | collective-permute-start | bytes 442376 | tf_op jit(solution)/shard_map/ppermute | solution.py:457
  4.7 1.0 %collective-permute-done.refs_1_ = bf16[576,128]{1,0:T(8,128)(2,1)S(1)} collective-permute-done((bf16[576,128]{1,0:T(8,128)(2,1)S(1)}, bf16[576,128]{1,0:T(8,128)(2,1)S(1)}, u32[]{:S(2)}, u32[]{:S(2)}) %collective-permute-start) | collective-permute-done | bytes 147488 | tf_op jit(solution)/shard_map/ppermute | solution.py:457
  5.7 0.3 %compose.1 = (bf16[160,128]{1,0:T(8,128)(2,1)S(1)}, bf16[448,128]{1,0:T(8,128)(2,1)S(1)}, bf16[128,128]{1,0:T(8,128)(2,1)S(1)}, bf16[32,128]{1,0:T(8,128)(2,1)S(1)}) custom-call(bf16[576,128]{1,0:T(8,128)(2,1)S(1)} %get-tuple-element.22.refs_0_, bf16[576,128]{1,0:T(8,128)(2,1)S(1)} %collective-permute-done.refs_1_), custom_call_target="tpu_custom_call" | custom-call | tf_op jit(solution)/shard_map/compose/pallas_call | solution.py:538
  6.0 3.0 %collective-permute-start.1 = (bf16[160,128]{1,0:T(8,128)(2,1)S(1)}, bf16[160,128]{1,0:T(8,128)(2,1)S(1)}, u32[]{:S(2)}, u32[]{:S(2)}) collective-permute-start(bf16[160,128]{1,0:T(8,128)(2,1)S(1)} %get-tuple-element.24), channel_id=1, source_target_pairs={{0,16},{8,24},{16,0},{24,8},{1,17},{9,25},{17,1},{25,9},{2,18},{10... | collective-permute-start | bytes 122888 | tf_op jit(solution)/shard_map/ppermute | solution.py:457
  8.9 0.0 copy-start
  8.9 0.0 copy-start.1
  8.9 1.1 %fold.1 = (f32[8,32,128]{2,1,0:T(8,128)S(1)}, bf16[8,128,128]{2,1,0:T(8,128)(2,1)S(1)}, bf16[160,128]{1,0:T(8,128)(2,1)S(1)}, bf16[160,128]{1,0:T(8,128)(2,1)S(1)}, bf16[8,128,128]{2,1,0:T(8,128)(2,1)S(1)}) custom-call(f32[8,32,128]{2,1,0:T(8,128)S(1)} %get-tuple-element.25.refs_0_, bf16[9,288,128]{2,1,0:T(8,128)(2,1)S(1)} %get-tuple-element.26.refs_1_, ...), custom_call_target="tpu_custom_call" | custom-call | tf_op jit(solution)/shard_map/fold/pallas_call | solution.py:558
  10.0 0.9 %collective-permute-done.1.refs_1_.refs_5_ = bf16[160,128]{1,0:T(8,128)(2,1)S(1)} collective-permute-done((bf16[160,128]{1,0:T(8,128)(2,1)S(1)}, bf16[160,128]{1,0:T(8,128)(2,1)S(1)}, u32[]{:S(2)}, u32[]{:S(2)}) %collective-permute-start.1) | collective-permute-done | bytes 40992 | tf_op jit(solution)/shard_map/ppermute | solution.py:457
  10.9 0.3 %chain.1 = (f32[8,32,128]{2,1,0:T(8,128)S(1)}, bf16[8,32,128]{2,1,0:T(8,128)(2,1)S(1)}, bf16[32,128]{1,0:T(8,128)(2,1)S(1)}, bf16[4,32,128]{2,1,0:T(8,128)(2,1)S(1)}, bf16[4,32,128]{2,1,0:T(8,128)(2,1)S(1)}) custom-call(bf16[32,128]{1,0:T(8,128)(2,1)S(1)} %get-tuple-element.23.refs_0_, bf16[160,128]{1,0:T(8,128)(2,1)S(1)} %collective-permute-done.1.refs_1_.refs_5_, ...), custom_call_target="tpu_custom_call" | custom-call | tf_op jit(solution)/shard_map/chain/pallas_call | solution.py:577
  11.2 0.7 %collective-permute-start.2 = (bf16[4,32,128]{2,1,0:T(8,128)(2,1)S(1)}, bf16[4,32,128]{2,1,0:T(8,128)(2,1)S(1)}, u32[]{:S(2)}, u32[]{:S(2)}) collective-permute-start(bf16[4,32,128]{2,1,0:T(8,128)(2,1)S(1)} %get-tuple-element.39), channel_id=1, source_target_pairs={{1,2},{2,1},{3,4},{4,3},{5,6},{6,5},{9,10},{10,9},{11,12},{12,11},... | collective-permute-start | bytes 98312 | tf_op jit(solution)/shard_map/ppermute | solution.py:465
  11.9 4.8 %collective-permute-start.3 = (bf16[4,32,128]{2,1,0:T(8,128)(2,1)S(1)}, bf16[4,32,128]{2,1,0:T(8,128)(2,1)S(1)}, u32[]{:S(2)}, u32[]{:S(2)}) collective-permute-start(bf16[4,32,128]{2,1,0:T(8,128)(2,1)S(1)} %get-tuple-element.40), channel_id=1, source_target_pairs={{0,1},{1,0},{2,3},{3,2},{4,5},{5,4},{6,7},{7,6},{8,9},{9,8},{10,11... | collective-permute-start | bytes 98312 | tf_op jit(solution)/shard_map/ppermute | solution.py:465
  16.7 0.0 copy-done
  16.7 0.0 copy-done.1
  16.7 0.0 copy-start.2
  16.7 1.2 %local_product.1 = (f32[8,32,128]{2,1,0:T(8,128)S(1)}, f32[8,32,128]{2,1,0:T(8,128)}, bf16[8,1,8,32,128]{4,3,2,1,0:T(8,128)(2,1)S(1)}) custom-call(bf16[8,32,128]{2,1,0:T(8,128)(2,1)S(1)} %get-tuple-element.30.refs_0_, bf16[32,128]{1,0:T(8,128)(2,1)S(1)} %get-tuple-element.31.refs_1_, bf16[160,128]{1,0:T(8,128)(2,1)S(1)} %get-tuple-element.32.refs_2_, ...), custom_call_target="tpu_custom_call" | custom-call | tf_op jit(solution)/shard_map/local_product/pallas_call | solution.py:599
  17.9 0.0 collective-permute-done.2.refs_1_
  18.0 0.7 %collective-permute-done.3.refs_2_ = bf16[4,32,128]{2,1,0:T(8,128)(2,1)S(1)} collective-permute-done((bf16[4,32,128]{2,1,0:T(8,128)(2,1)S(1)}, bf16[4,32,128]{2,1,0:T(8,128)(2,1)S(1)}, u32[]{:S(2)}, u32[]{:S(2)}) %collective-permute-start.3) | collective-permute-done | bytes 32800 | tf_op jit(solution)/shard_map/ppermute | solution.py:465
  18.6 0.0 copy-done.2
  18.6 0.9 %halo_product.1 = f32[8,32,128]{2,1,0:T(8,128)} custom-call(f32[8,32,128]{2,1,0:T(8,128)S(1)} %get-tuple-element.38.refs_0_, bf16[4,32,128]{2,1,0:T(8,128)(2,1)S(1)} %collective-permute-done.2.refs_1_, bf16[4,32,128]{2,1,0:T(8,128)(2,1)S(1)} %collective-permute-done.3.refs_2_, bf16[8,2,128,128]{3,2,1,0:T(8,128)(2,1)S(1)} %copy-done.2, ...), custom_call_target="tpu_custom_call" | custom-call | tf_op jit(solution)/shard_map/halo_product/pallas_call | solution.py:629
Async XLA Ops:
  4.2 1.5 %collective-permute-start = (bf16[576,128]{1,0:T(8,128)(2,1)S(1)}, bf16[576,128]{1,0:T(8,128)(2,1)S(1)}, u32[]{:S(2)}, u32[]{:S(2)}) collective-permute-start(bf16[576,128]{1,0:T(8,128)(2,1)S(1)} %get-tuple-element.22.refs_0_), channel_id=1, source_target_pairs={{0,8},{8,0},{16,24},{24,16},{1,9},{9,1},{17,25},{25,17},{2,10},{10... | collective-permute-start | bytes 442376 | tf_op jit(solution)/shard_map/ppermute | solution.py:457
  6.0 4.9 %collective-permute-start.1 = (bf16[160,128]{1,0:T(8,128)(2,1)S(1)}, bf16[160,128]{1,0:T(8,128)(2,1)S(1)}, u32[]{:S(2)}, u32[]{:S(2)}) collective-permute-start(bf16[160,128]{1,0:T(8,128)(2,1)S(1)} %get-tuple-element.24), channel_id=1, source_target_pairs={{0,16},{8,24},{16,0},{24,8},{1,17},{9,25},{17,1},{25,9},{2,18},{10... | collective-permute-start | bytes 122888 | tf_op jit(solution)/shard_map/ppermute | solution.py:457
  8.9 7.8 %copy-start = (bf16[8,3,128,128]{3,2,1,0:T(8,128)(2,1)S(1)}, bf16[8,3,128,128]{3,2,1,0:T(8,128)(2,1)}, u32[]{:S(2)}) copy-start(bf16[8,3,128,128]{3,2,1,0:T(8,128)(2,1)} %refs_8_.1) | copy-start | bytes 2359300
  8.9 7.8 %copy-start.1 = (bf16[8,3,128,128]{3,2,1,0:T(8,128)(2,1)S(1)}, bf16[8,3,128,128]{3,2,1,0:T(8,128)(2,1)}, u32[]{:S(2)}) copy-start(bf16[8,3,128,128]{3,2,1,0:T(8,128)(2,1)} %refs_9_.1) | copy-start | bytes 2359300
  11.2 6.7 %collective-permute-start.2 = (bf16[4,32,128]{2,1,0:T(8,128)(2,1)S(1)}, bf16[4,32,128]{2,1,0:T(8,128)(2,1)S(1)}, u32[]{:S(2)}, u32[]{:S(2)}) collective-permute-start(bf16[4,32,128]{2,1,0:T(8,128)(2,1)S(1)} %get-tuple-element.39), channel_id=1, source_target_pairs={{1,2},{2,1},{3,4},{4,3},{5,6},{6,5},{9,10},{10,9},{11,12},{12,11},... | collective-permute-start | bytes 98312 | tf_op jit(solution)/shard_map/ppermute | solution.py:465
  11.9 6.7 %collective-permute-start.3 = (bf16[4,32,128]{2,1,0:T(8,128)(2,1)S(1)}, bf16[4,32,128]{2,1,0:T(8,128)(2,1)S(1)}, u32[]{:S(2)}, u32[]{:S(2)}) collective-permute-start(bf16[4,32,128]{2,1,0:T(8,128)(2,1)S(1)} %get-tuple-element.40), channel_id=1, source_target_pairs={{0,1},{1,0},{2,3},{3,2},{4,5},{5,4},{6,7},{7,6},{8,9},{9,8},{10,11... | collective-permute-start | bytes 98312 | tf_op jit(solution)/shard_map/ppermute | solution.py:465
  16.7 1.9 %copy-start.2 = (bf16[8,2,128,128]{3,2,1,0:T(8,128)(2,1)S(1)}, bf16[8,2,128,128]{3,2,1,0:T(8,128)(2,1)}, u32[]{:S(2)}) copy-start(bf16[8,2,128,128]{3,2,1,0:T(8,128)(2,1)} %refs_3_.3) | copy-start | bytes 1572868

commit v18 on v17

--- a/solution.py
+++ b/solution.py
@@ -50,6 +50,7 @@
     slots = lower.shape[1]
     upper_slots = upper.shape[1]
     near = count + width
+    far = near + width
     last = rows - 1
     half = rows // 2
     parts = [
@@ -190,8 +191,14 @@
             free_b = free_b + first[near:, width:] - second[near:]
         for k, value, free in ((a, of_a, free_a), (b, of_b, free_b)):
             base[k] = value[:count]
-            response[k, :near] = narrow(value)
-            response[k, near:] = narrow(free)
+            value, free = narrow(value), narrow(free)
+            response[k, :near] = value
+            response[k, near:] = free
+            if k == last:
+                payload[far + near :] = free
+            if k == 0:
+                payload[near : 2 * near] = value
+                payload[2 * near : near + far] = free
 
     pairs = rows // 2
     for copy in copies[:4]:
@@ -207,16 +214,12 @@
         go_down(p)
         if p % 2 == 1:
             links += ready_up(p - 1)
-    far = near + width
     payload[:near] = down[last]
     for p in range(0, pairs, 2):
         a = last - 2 * p
         passed = apart(down[a], down[a - 2], links[p], links[p + 1])
         go_up(p, passed[:, :width])
         go_up(p + 1, passed[:, width:])
-
-    payload[near + far :] = response[last, near:]
-    payload[near : near + far] = response[0]
 
 
 def compose_kernel(axis, bit, final, mine, theirs, *refs):

time: 19.7 us -> 19.7 us (level)
  no operation moved by 1% of the time
where the time goes in v18:
time: 19.7 us; the launch traced here: 19.5 us
  starting transfers between devices  8.97 us (46%)
  Pallas kernels  7.26 us (37%)
  waiting for transfers between devices  2.55 us (13%)
  between operations  0.68 us (3%)
    ppermute x2, starting transfers between devices, swaps(): return lax.ppermute(block, axis, pairs)  5.5 us
    pallas_call x1, Pallas kernels, on_device(): pl.pallas_call(sweep_kernel, out_shape=(wide, jax.ShapeDtypeStruct((rows...  3.49 us
    ppermute x2, starting transfers between devices, trade(): return lax.ppermute(block, axis, [(i, i ^ bit) for i in range(count)])  3.47 us
    ppermute x2, waiting for transfers between devices, trade(): return lax.ppermute(block, axis, [(i, i ^ bit) for i in range(count)])  1.89 us
    pallas_call x1, Pallas kernels, on_device(): pl.pallas_call(local, out_shape=(wide, wide, jax.ShapeDtypeStruct(masks,...  1.21 us
    pallas_call x1, Pallas kernels, on_device(): pl.pallas_call(fold, out_shape=(wide, jax.ShapeDtypeStruct((rows, width,...  1.09 us
    pallas_call x1, Pallas kernels, on_device(): pl.pallas_call(halo, out_shape=wide, in_specs=[VMEM] * 5, out_specs=VMEM,...  0.88 us
    ppermute x2, waiting for transfers between devices, swaps(): return lax.ppermute(block, axis, pairs)  0.66 us
  transfers between devices with their start and end apart: 4, of which 3 were waited for; matrix products, arithmetic and copies ran while one was open for 0% of the time, Pallas kernels for 12%

profile of v18, /device:TPU:0, one launch (start us, length us, event | category | flops | bytes accessed | tf_op | source)
XLA Modules:
  0.0 19.5 jit_solution(9199058961289361703)
XLA Ops:
  0.6 3.5 %sweeps.1 = (f32[8,32,128]{2,1,0:T(8,128)S(1)}, bf16[9,288,128]{2,1,0:T(8,128)(2,1)S(1)}, bf16[576,128]{1,0:T(8,128)(2,1)S(1)}) custom-call(f32[8,32,128]{2,1,0:T(8,128)} %rhs_far.1, bf16[8,128,128]{2,1,0:T(8,128)(2,1)} %inverse_far.1, bf16[8,3,128,128]{3,2,1,0:T(8,128)(2,1)} %refs_8_.1, bf16[8,3,128,128]{3,2,1,0:T(8,128)(2,1)} %refs_9_.1, s32[3,8]{1,0:T(4,128)} %bitcast.3, ...), custom_call_target="tpu_custom_call" | custom-call | tf_op jit(solution)/shard_map/sweeps/pallas_call | solution.py:494
  4.1 0.5 %collective-permute-start = (bf16[576,128]{1,0:T(8,128)(2,1)S(1)}, bf16[576,128]{1,0:T(8,128)(2,1)S(1)}, u32[]{:S(2)}, u32[]{:S(2)}) collective-permute-start(bf16[576,128]{1,0:T(8,128)(2,1)S(1)} %get-tuple-element.22.refs_0_), channel_id=1, source_target_pairs={{0,8},{8,0},{16,24},{24,16},{1,9},{9,1},{17,25},{25,17},{2,10},{10... | collective-permute-start | bytes 442376 | tf_op jit(solution)/shard_map/ppermute | solution.py:460
  4.6 1.0 %collective-permute-done.refs_1_ = bf16[576,128]{1,0:T(8,128)(2,1)S(1)} collective-permute-done((bf16[576,128]{1,0:T(8,128)(2,1)S(1)}, bf16[576,128]{1,0:T(8,128)(2,1)S(1)}, u32[]{:S(2)}, u32[]{:S(2)}) %collective-permute-start) | collective-permute-done | bytes 147488 | tf_op jit(solution)/shard_map/ppermute | solution.py:460
  5.6 0.3 %compose.1 = (bf16[160,128]{1,0:T(8,128)(2,1)S(1)}, bf16[448,128]{1,0:T(8,128)(2,1)S(1)}, bf16[128,128]{1,0:T(8,128)(2,1)S(1)}, bf16[32,128]{1,0:T(8,128)(2,1)S(1)}) custom-call(bf16[576,128]{1,0:T(8,128)(2,1)S(1)} %get-tuple-element.22.refs_0_, bf16[576,128]{1,0:T(8,128)(2,1)S(1)} %collective-permute-done.refs_1_), custom_call_target="tpu_custom_call" | custom-call | tf_op jit(solution)/shard_map/compose/pallas_call | solution.py:541
  5.9 3.0 %collective-permute-start.1 = (bf16[160,128]{1,0:T(8,128)(2,1)S(1)}, bf16[160,128]{1,0:T(8,128)(2,1)S(1)}, u32[]{:S(2)}, u32[]{:S(2)}) collective-permute-start(bf16[160,128]{1,0:T(8,128)(2,1)S(1)} %get-tuple-element.24), channel_id=1, source_target_pairs={{0,16},{8,24},{16,0},{24,8},{1,17},{9,25},{17,1},{25,9},{2,18},{10... | collective-permute-start | bytes 122888 | tf_op jit(solution)/shard_map/ppermute | solution.py:460
  8.9 0.0 copy-start
  8.9 0.0 copy-start.1
  8.9 1.1 %fold.1 = (f32[8,32,128]{2,1,0:T(8,128)S(1)}, bf16[8,128,128]{2,1,0:T(8,128)(2,1)S(1)}, bf16[160,128]{1,0:T(8,128)(2,1)S(1)}, bf16[160,128]{1,0:T(8,128)(2,1)S(1)}, bf16[8,128,128]{2,1,0:T(8,128)(2,1)S(1)}) custom-call(f32[8,32,128]{2,1,0:T(8,128)S(1)} %get-tuple-element.25.refs_0_, bf16[9,288,128]{2,1,0:T(8,128)(2,1)S(1)} %get-tuple-element.26.refs_1_, ...), custom_call_target="tpu_custom_call" | custom-call | tf_op jit(solution)/shard_map/fold/pallas_call | solution.py:561
  10.0 0.9 %collective-permute-done.1.refs_1_.refs_5_ = bf16[160,128]{1,0:T(8,128)(2,1)S(1)} collective-permute-done((bf16[160,128]{1,0:T(8,128)(2,1)S(1)}, bf16[160,128]{1,0:T(8,128)(2,1)S(1)}, u32[]{:S(2)}, u32[]{:S(2)}) %collective-permute-start.1) | collective-permute-done | bytes 40992 | tf_op jit(solution)/shard_map/ppermute | solution.py:460
  10.9 0.3 %chain.1 = (f32[8,32,128]{2,1,0:T(8,128)S(1)}, bf16[8,32,128]{2,1,0:T(8,128)(2,1)S(1)}, bf16[32,128]{1,0:T(8,128)(2,1)S(1)}, bf16[4,32,128]{2,1,0:T(8,128)(2,1)S(1)}, bf16[4,32,128]{2,1,0:T(8,128)(2,1)S(1)}) custom-call(bf16[32,128]{1,0:T(8,128)(2,1)S(1)} %get-tuple-element.23.refs_0_, bf16[160,128]{1,0:T(8,128)(2,1)S(1)} %collective-permute-done.1.refs_1_.refs_5_, ...), custom_call_target="tpu_custom_call" | custom-call | tf_op jit(solution)/shard_map/chain/pallas_call | solution.py:580
  11.2 0.7 %collective-permute-start.2 = (bf16[4,32,128]{2,1,0:T(8,128)(2,1)S(1)}, bf16[4,32,128]{2,1,0:T(8,128)(2,1)S(1)}, u32[]{:S(2)}, u32[]{:S(2)}) collective-permute-start(bf16[4,32,128]{2,1,0:T(8,128)(2,1)S(1)} %get-tuple-element.39), channel_id=1, source_target_pairs={{1,2},{2,1},{3,4},{4,3},{5,6},{6,5},{9,10},{10,9},{11,12},{12,11},... | collective-permute-start | bytes 98312 | tf_op jit(solution)/shard_map/ppermute | solution.py:468
  11.9 4.8 %collective-permute-start.3 = (bf16[4,32,128]{2,1,0:T(8,128)(2,1)S(1)}, bf16[4,32,128]{2,1,0:T(8,128)(2,1)S(1)}, u32[]{:S(2)}, u32[]{:S(2)}) collective-permute-start(bf16[4,32,128]{2,1,0:T(8,128)(2,1)S(1)} %get-tuple-element.40), channel_id=1, source_target_pairs={{0,1},{1,0},{2,3},{3,2},{4,5},{5,4},{6,7},{7,6},{8,9},{9,8},{10,11... | collective-permute-start | bytes 98312 | tf_op jit(solution)/shard_map/ppermute | solution.py:468
  16.7 0.0 copy-done
  16.7 0.0 copy-done.1
  16.7 0.0 copy-start.2
  16.7 1.2 %local_product.1 = (f32[8,32,128]{2,1,0:T(8,128)S(1)}, f32[8,32,128]{2,1,0:T(8,128)}, bf16[8,1,8,32,128]{4,3,2,1,0:T(8,128)(2,1)S(1)}) custom-call(bf16[8,32,128]{2,1,0:T(8,128)(2,1)S(1)} %get-tuple-element.30.refs_0_, bf16[32,128]{1,0:T(8,128)(2,1)S(1)} %get-tuple-element.31.refs_1_, bf16[160,128]{1,0:T(8,128)(2,1)S(1)} %get-tuple-element.32.refs_2_, ...), custom_call_target="tpu_custom_call" | custom-call | tf_op jit(solution)/shard_map/local_product/pallas_call | solution.py:602
  17.9 0.0 collective-permute-done.2.refs_1_
  17.9 0.7 %collective-permute-done.3.refs_2_ = bf16[4,32,128]{2,1,0:T(8,128)(2,1)S(1)} collective-permute-done((bf16[4,32,128]{2,1,0:T(8,128)(2,1)S(1)}, bf16[4,32,128]{2,1,0:T(8,128)(2,1)S(1)}, u32[]{:S(2)}, u32[]{:S(2)}) %collective-permute-start.3) | collective-permute-done | bytes 32800 | tf_op jit(solution)/shard_map/ppermute | solution.py:468
  18.6 0.0 copy-done.2
  18.6 0.9 %halo_product.1 = f32[8,32,128]{2,1,0:T(8,128)} custom-call(f32[8,32,128]{2,1,0:T(8,128)S(1)} %get-tuple-element.38.refs_0_, bf16[4,32,128]{2,1,0:T(8,128)(2,1)S(1)} %collective-permute-done.2.refs_1_, bf16[4,32,128]{2,1,0:T(8,128)(2,1)S(1)} %collective-permute-done.3.refs_2_, bf16[8,2,128,128]{3,2,1,0:T(8,128)(2,1)S(1)} %copy-done.2, ...), custom_call_target="tpu_custom_call" | custom-call | tf_op jit(solution)/shard_map/halo_product/pallas_call | solution.py:632
Async XLA Ops:
  4.1 1.5 %collective-permute-start = (bf16[576,128]{1,0:T(8,128)(2,1)S(1)}, bf16[576,128]{1,0:T(8,128)(2,1)S(1)}, u32[]{:S(2)}, u32[]{:S(2)}) collective-permute-start(bf16[576,128]{1,0:T(8,128)(2,1)S(1)} %get-tuple-element.22.refs_0_), channel_id=1, source_target_pairs={{0,8},{8,0},{16,24},{24,16},{1,9},{9,1},{17,25},{25,17},{2,10},{10... | collective-permute-start | bytes 442376 | tf_op jit(solution)/shard_map/ppermute | solution.py:460
  5.9 4.9 %collective-permute-start.1 = (bf16[160,128]{1,0:T(8,128)(2,1)S(1)}, bf16[160,128]{1,0:T(8,128)(2,1)S(1)}, u32[]{:S(2)}, u32[]{:S(2)}) collective-permute-start(bf16[160,128]{1,0:T(8,128)(2,1)S(1)} %get-tuple-element.24), channel_id=1, source_target_pairs={{0,16},{8,24},{16,0},{24,8},{1,17},{9,25},{17,1},{25,9},{2,18},{10... | collective-permute-start | bytes 122888 | tf_op jit(solution)/shard_map/ppermute | solution.py:460
  8.9 7.8 %copy-start = (bf16[8,3,128,128]{3,2,1,0:T(8,128)(2,1)S(1)}, bf16[8,3,128,128]{3,2,1,0:T(8,128)(2,1)}, u32[]{:S(2)}) copy-start(bf16[8,3,128,128]{3,2,1,0:T(8,128)(2,1)} %refs_8_.1) | copy-start | bytes 2359300
  8.9 7.8 %copy-start.1 = (bf16[8,3,128,128]{3,2,1,0:T(8,128)(2,1)S(1)}, bf16[8,3,128,128]{3,2,1,0:T(8,128)(2,1)}, u32[]{:S(2)}) copy-start(bf16[8,3,128,128]{3,2,1,0:T(8,128)(2,1)} %refs_9_.1) | copy-start | bytes 2359300
  11.2 6.7 %collective-permute-start.2 = (bf16[4,32,128]{2,1,0:T(8,128)(2,1)S(1)}, bf16[4,32,128]{2,1,0:T(8,128)(2,1)S(1)}, u32[]{:S(2)}, u32[]{:S(2)}) collective-permute-start(bf16[4,32,128]{2,1,0:T(8,128)(2,1)S(1)} %get-tuple-element.39), channel_id=1, source_target_pairs={{1,2},{2,1},{3,4},{4,3},{5,6},{6,5},{9,10},{10,9},{11,12},{12,11},... | collective-permute-start | bytes 98312 | tf_op jit(solution)/shard_map/ppermute | solution.py:468
  11.9 6.7 %collective-permute-start.3 = (bf16[4,32,128]{2,1,0:T(8,128)(2,1)S(1)}, bf16[4,32,128]{2,1,0:T(8,128)(2,1)S(1)}, u32[]{:S(2)}, u32[]{:S(2)}) collective-permute-start(bf16[4,32,128]{2,1,0:T(8,128)(2,1)S(1)} %get-tuple-element.40), channel_id=1, source_target_pairs={{0,1},{1,0},{2,3},{3,2},{4,5},{5,4},{6,7},{7,6},{8,9},{9,8},{10,11... | collective-permute-start | bytes 98312 | tf_op jit(solution)/shard_map/ppermute | solution.py:468
  16.7 1.9 %copy-start.2 = (bf16[8,2,128,128]{3,2,1,0:T(8,128)(2,1)S(1)}, bf16[8,2,128,128]{3,2,1,0:T(8,128)(2,1)}, u32[]{:S(2)}) copy-start(bf16[8,2,128,128]{3,2,1,0:T(8,128)(2,1)} %refs_3_.3) | copy-start | bytes 1572868

commit v19 on v18

--- a/solution.py
+++ b/solution.py
@@ -153,6 +153,8 @@
             exact[b] = of_b
         down[a] = narrow(of_a)
         down[b] = narrow(of_b)
+        if b == last:
+            payload[:near] = narrow(of_b)
 
     def ready_up(p):
         of_a, narrow_a, of_b, through, links = ready(
@@ -214,7 +216,6 @@
         go_down(p)
         if p % 2 == 1:
             links += ready_up(p - 1)
-    payload[:near] = down[last]
     for p in range(0, pairs, 2):
         a = last - 2 * p
         passed = apart(down[a], down[a - 2], links[p], links[p + 1])

time: 19.7 us -> 19.6 us (level)
  no operation moved by 1% of the time
where the time goes in v19:
time: 19.6 us; the launch traced here: 19.5 us
  starting transfers between devices  8.98 us (46%)
  Pallas kernels  7.23 us (37%)
  waiting for transfers between devices  2.55 us (13%)
  between operations  0.68 us (3%)
    ppermute x2, starting transfers between devices, swaps(): return lax.ppermute(block, axis, pairs)  5.5 us
    ppermute x2, starting transfers between devices, trade(): return lax.ppermute(block, axis, [(i, i ^ bit) for i in range(count)])  3.48 us
    pallas_call x1, Pallas kernels, on_device(): pl.pallas_call(sweep_kernel, out_shape=(wide, jax.ShapeDtypeStruct((rows...  3.47 us
    ppermute x2, waiting for transfers between devices, trade(): return lax.ppermute(block, axis, [(i, i ^ bit) for i in range(count)])  1.89 us
    pallas_call x1, Pallas kernels, on_device(): pl.pallas_call(local, out_shape=(wide, wide, jax.ShapeDtypeStruct(masks,...  1.21 us
    pallas_call x1, Pallas kernels, on_device(): pl.pallas_call(fold, out_shape=(wide, jax.ShapeDtypeStruct((rows, width,...  1.09 us
    pallas_call x1, Pallas kernels, on_device(): pl.pallas_call(halo, out_shape=wide, in_specs=[VMEM] * 5, out_specs=VMEM,...  0.88 us
    ppermute x2, waiting for transfers between devices, swaps(): return lax.ppermute(block, axis, pairs)  0.66 us
  transfers between devices with their start and end apart: 4, of which 3 were waited for; matrix products, arithmetic and copies ran while one was open for 0% of the time, Pallas kernels for 12%

profile of v19, /device:TPU:0, one launch (start us, length us, event | category | flops | bytes accessed | tf_op | source)
XLA Modules:
  0.0 19.5 jit_solution(10518494065472377622)
XLA Ops:
  0.6 3.5 %sweeps.1 = (f32[8,32,128]{2,1,0:T(8,128)S(1)}, bf16[9,288,128]{2,1,0:T(8,128)(2,1)S(1)}, bf16[576,128]{1,0:T(8,128)(2,1)S(1)}) custom-call(f32[8,32,128]{2,1,0:T(8,128)} %rhs_far.1, bf16[8,128,128]{2,1,0:T(8,128)(2,1)} %inverse_far.1, bf16[8,3,128,128]{3,2,1,0:T(8,128)(2,1)} %refs_8_.1, bf16[8,3,128,128]{3,2,1,0:T(8,128)(2,1)} %refs_9_.1, s32[3,8]{1,0:T(4,128)} %bitcast.3, ...), custom_call_target="tpu_custom_call" | custom-call | tf_op jit(solution)/shard_map/sweeps/pallas_call | solution.py:495
  4.1 0.5 %collective-permute-start = (bf16[576,128]{1,0:T(8,128)(2,1)S(1)}, bf16[576,128]{1,0:T(8,128)(2,1)S(1)}, u32[]{:S(2)}, u32[]{:S(2)}) collective-permute-start(bf16[576,128]{1,0:T(8,128)(2,1)S(1)} %get-tuple-element.22.refs_0_), channel_id=1, source_target_pairs={{0,8},{8,0},{16,24},{24,16},{1,9},{9,1},{17,25},{25,17},{2,10},{10... | collective-permute-start | bytes 442376 | tf_op jit(solution)/shard_map/ppermute | solution.py:461
  4.6 1.0 %collective-permute-done.refs_1_ = bf16[576,128]{1,0:T(8,128)(2,1)S(1)} collective-permute-done((bf16[576,128]{1,0:T(8,128)(2,1)S(1)}, bf16[576,128]{1,0:T(8,128)(2,1)S(1)}, u32[]{:S(2)}, u32[]{:S(2)}) %collective-permute-start) | collective-permute-done | bytes 147488 | tf_op jit(solution)/shard_map/ppermute | solution.py:461
  5.6 0.3 %compose.1 = (bf16[160,128]{1,0:T(8,128)(2,1)S(1)}, bf16[448,128]{1,0:T(8,128)(2,1)S(1)}, bf16[128,128]{1,0:T(8,128)(2,1)S(1)}, bf16[32,128]{1,0:T(8,128)(2,1)S(1)}) custom-call(bf16[576,128]{1,0:T(8,128)(2,1)S(1)} %get-tuple-element.22.refs_0_, bf16[576,128]{1,0:T(8,128)(2,1)S(1)} %collective-permute-done.refs_1_), custom_call_target="tpu_custom_call" | custom-call | tf_op jit(solution)/shard_map/compose/pallas_call | solution.py:542
  5.9 3.0 %collective-permute-start.1 = (bf16[160,128]{1,0:T(8,128)(2,1)S(1)}, bf16[160,128]{1,0:T(8,128)(2,1)S(1)}, u32[]{:S(2)}, u32[]{:S(2)}) collective-permute-start(bf16[160,128]{1,0:T(8,128)(2,1)S(1)} %get-tuple-element.24), channel_id=1, source_target_pairs={{0,16},{8,24},{16,0},{24,8},{1,17},{9,25},{17,1},{25,9},{2,18},{10... | collective-permute-start | bytes 122888 | tf_op jit(solution)/shard_map/ppermute | solution.py:461
  8.9 0.0 copy-start
  8.9 0.0 copy-start.1
  8.9 1.1 %fold.1 = (f32[8,32,128]{2,1,0:T(8,128)S(1)}, bf16[8,128,128]{2,1,0:T(8,128)(2,1)S(1)}, bf16[160,128]{1,0:T(8,128)(2,1)S(1)}, bf16[160,128]{1,0:T(8,128)(2,1)S(1)}, bf16[8,128,128]{2,1,0:T(8,128)(2,1)S(1)}) custom-call(f32[8,32,128]{2,1,0:T(8,128)S(1)} %get-tuple-element.25.refs_0_, bf16[9,288,128]{2,1,0:T(8,128)(2,1)S(1)} %get-tuple-element.26.refs_1_, ...), custom_call_target="tpu_custom_call" | custom-call | tf_op jit(solution)/shard_map/fold/pallas_call | solution.py:562
  10.0 0.9 %collective-permute-done.1.refs_1_.refs_5_ = bf16[160,128]{1,0:T(8,128)(2,1)S(1)} collective-permute-done((bf16[160,128]{1,0:T(8,128)(2,1)S(1)}, bf16[160,128]{1,0:T(8,128)(2,1)S(1)}, u32[]{:S(2)}, u32[]{:S(2)}) %collective-permute-start.1) | collective-permute-done | bytes 40992 | tf_op jit(solution)/shard_map/ppermute | solution.py:461
  10.9 0.3 %chain.1 = (f32[8,32,128]{2,1,0:T(8,128)S(1)}, bf16[8,32,128]{2,1,0:T(8,128)(2,1)S(1)}, bf16[32,128]{1,0:T(8,128)(2,1)S(1)}, bf16[4,32,128]{2,1,0:T(8,128)(2,1)S(1)}, bf16[4,32,128]{2,1,0:T(8,128)(2,1)S(1)}) custom-call(bf16[32,128]{1,0:T(8,128)(2,1)S(1)} %get-tuple-element.23.refs_0_, bf16[160,128]{1,0:T(8,128)(2,1)S(1)} %collective-permute-done.1.refs_1_.refs_5_, ...), custom_call_target="tpu_custom_call" | custom-call | tf_op jit(solution)/shard_map/chain/pallas_call | solution.py:581
  11.2 0.7 %collective-permute-start.2 = (bf16[4,32,128]{2,1,0:T(8,128)(2,1)S(1)}, bf16[4,32,128]{2,1,0:T(8,128)(2,1)S(1)}, u32[]{:S(2)}, u32[]{:S(2)}) collective-permute-start(bf16[4,32,128]{2,1,0:T(8,128)(2,1)S(1)} %get-tuple-element.39), channel_id=1, source_target_pairs={{1,2},{2,1},{3,4},{4,3},{5,6},{6,5},{9,10},{10,9},{11,12},{12,11},... | collective-permute-start | bytes 98312 | tf_op jit(solution)/shard_map/ppermute | solution.py:469
  11.8 4.8 %collective-permute-start.3 = (bf16[4,32,128]{2,1,0:T(8,128)(2,1)S(1)}, bf16[4,32,128]{2,1,0:T(8,128)(2,1)S(1)}, u32[]{:S(2)}, u32[]{:S(2)}) collective-permute-start(bf16[4,32,128]{2,1,0:T(8,128)(2,1)S(1)} %get-tuple-element.40), channel_id=1, source_target_pairs={{0,1},{1,0},{2,3},{3,2},{4,5},{5,4},{6,7},{7,6},{8,9},{9,8},{10,11... | collective-permute-start | bytes 98312 | tf_op jit(solution)/shard_map/ppermute | solution.py:469
  16.7 0.0 copy-done
  16.7 0.0 copy-done.1
  16.7 0.0 copy-start.2
  16.7 1.2 %local_product.1 = (f32[8,32,128]{2,1,0:T(8,128)S(1)}, f32[8,32,128]{2,1,0:T(8,128)}, bf16[8,1,8,32,128]{4,3,2,1,0:T(8,128)(2,1)S(1)}) custom-call(bf16[8,32,128]{2,1,0:T(8,128)(2,1)S(1)} %get-tuple-element.30.refs_0_, bf16[32,128]{1,0:T(8,128)(2,1)S(1)} %get-tuple-element.31.refs_1_, bf16[160,128]{1,0:T(8,128)(2,1)S(1)} %get-tuple-element.32.refs_2_, ...), custom_call_target="tpu_custom_call" | custom-call | tf_op jit(solution)/shard_map/local_product/pallas_call | solution.py:603
  17.9 0.0 collective-permute-done.2.refs_1_
  17.9 0.7 %collective-permute-done.3.refs_2_ = bf16[4,32,128]{2,1,0:T(8,128)(2,1)S(1)} collective-permute-done((bf16[4,32,128]{2,1,0:T(8,128)(2,1)S(1)}, bf16[4,32,128]{2,1,0:T(8,128)(2,1)S(1)}, u32[]{:S(2)}, u32[]{:S(2)}) %collective-permute-start.3) | collective-permute-done | bytes 32800 | tf_op jit(solution)/shard_map/ppermute | solution.py:469
  18.6 0.0 copy-done.2
  18.6 0.9 %halo_product.1 = f32[8,32,128]{2,1,0:T(8,128)} custom-call(f32[8,32,128]{2,1,0:T(8,128)S(1)} %get-tuple-element.38.refs_0_, bf16[4,32,128]{2,1,0:T(8,128)(2,1)S(1)} %collective-permute-done.2.refs_1_, bf16[4,32,128]{2,1,0:T(8,128)(2,1)S(1)} %collective-permute-done.3.refs_2_, bf16[8,2,128,128]{3,2,1,0:T(8,128)(2,1)S(1)} %copy-done.2, ...), custom_call_target="tpu_custom_call" | custom-call | tf_op jit(solution)/shard_map/halo_product/pallas_call | solution.py:633
Async XLA Ops:
  4.1 1.5 %collective-permute-start = (bf16[576,128]{1,0:T(8,128)(2,1)S(1)}, bf16[576,128]{1,0:T(8,128)(2,1)S(1)}, u32[]{:S(2)}, u32[]{:S(2)}) collective-permute-start(bf16[576,128]{1,0:T(8,128)(2,1)S(1)} %get-tuple-element.22.refs_0_), channel_id=1, source_target_pairs={{0,8},{8,0},{16,24},{24,16},{1,9},{9,1},{17,25},{25,17},{2,10},{10... | collective-permute-start | bytes 442376 | tf_op jit(solution)/shard_map/ppermute | solution.py:461
  5.9 4.9 %collective-permute-start.1 = (bf16[160,128]{1,0:T(8,128)(2,1)S(1)}, bf16[160,128]{1,0:T(8,128)(2,1)S(1)}, u32[]{:S(2)}, u32[]{:S(2)}) collective-permute-start(bf16[160,128]{1,0:T(8,128)(2,1)S(1)} %get-tuple-element.24), channel_id=1, source_target_pairs={{0,16},{8,24},{16,0},{24,8},{1,17},{9,25},{17,1},{25,9},{2,18},{10... | collective-permute-start | bytes 122888 | tf_op jit(solution)/shard_map/ppermute | solution.py:461
  8.9 7.8 %copy-start = (bf16[8,3,128,128]{3,2,1,0:T(8,128)(2,1)S(1)}, bf16[8,3,128,128]{3,2,1,0:T(8,128)(2,1)}, u32[]{:S(2)}) copy-start(bf16[8,3,128,128]{3,2,1,0:T(8,128)(2,1)} %refs_8_.1) | copy-start | bytes 2359300
  8.9 7.8 %copy-start.1 = (bf16[8,3,128,128]{3,2,1,0:T(8,128)(2,1)S(1)}, bf16[8,3,128,128]{3,2,1,0:T(8,128)(2,1)}, u32[]{:S(2)}) copy-start(bf16[8,3,128,128]{3,2,1,0:T(8,128)(2,1)} %refs_9_.1) | copy-start | bytes 2359300
  11.2 6.7 %collective-permute-start.2 = (bf16[4,32,128]{2,1,0:T(8,128)(2,1)S(1)}, bf16[4,32,128]{2,1,0:T(8,128)(2,1)S(1)}, u32[]{:S(2)}, u32[]{:S(2)}) collective-permute-start(bf16[4,32,128]{2,1,0:T(8,128)(2,1)S(1)} %get-tuple-element.39), channel_id=1, source_target_pairs={{1,2},{2,1},{3,4},{4,3},{5,6},{6,5},{9,10},{10,9},{11,12},{12,11},... | collective-permute-start | bytes 98312 | tf_op jit(solution)/shard_map/ppermute | solution.py:469
  11.8 6.7 %collective-permute-start.3 = (bf16[4,32,128]{2,1,0:T(8,128)(2,1)S(1)}, bf16[4,32,128]{2,1,0:T(8,128)(2,1)S(1)}, u32[]{:S(2)}, u32[]{:S(2)}) collective-permute-start(bf16[4,32,128]{2,1,0:T(8,128)(2,1)S(1)} %get-tuple-element.40), channel_id=1, source_target_pairs={{0,1},{1,0},{2,3},{3,2},{4,5},{5,4},{6,7},{7,6},{8,9},{9,8},{10,11... | collective-permute-start | bytes 98312 | tf_op jit(solution)/shard_map/ppermute | solution.py:469
  16.7 1.9 %copy-start.2 = (bf16[8,2,128,128]{3,2,1,0:T(8,128)(2,1)S(1)}, bf16[8,2,128,128]{3,2,1,0:T(8,128)(2,1)}, u32[]{:S(2)}) copy-start(bf16[8,2,128,128]{3,2,1,0:T(8,128)(2,1)} %refs_3_.3) | copy-start | bytes 1572868
